TPU v7x, 32 devices: a whole 2x2x4 slice. The times are simulated.
32 devices in a mesh: dp: 8 (over y, x, core), band: 4 (over z).
Axes of the slice: x: 2, y: 2, z: 4, core: 2. Of those that a mesh axis runs over, the one named last changes fastest.
Arguments:
- tokens: bfloat16 [16, 1024, 1152], P('dp', 'band'), may hold values from -6 to 6
- condition: bfloat16 [16, 1152], P('dp'), may hold values from -6 to 6
- patch_grid: int32 [16, 2], P('dp'), may hold values from 16 to 64, as said below
- ada_weight: bfloat16 [1152, 6912], P('band'), may hold values from -0.1875 to 0.1875
- ada_bias: bfloat16 [6912], P('band'), may hold values from -3 to 3
- qkv_weight: bfloat16 [1152, 3456], P('band'), may hold values from -0.25 to 0.25
- query_bias: bfloat16 [1152], P('band'), may hold values from -3 to 3
- value_bias: bfloat16 [1152], P('band'), may hold values from -3 to 3
- proj_weight: bfloat16 [1152, 1152], P('band'), may hold values from -0.75 to 0.75
- proj_bias: bfloat16 [1152], P('band'), may hold values from -2 to 2
- inner_weight: bfloat16 [1152, 4608], P('band'), may hold values from -0.1875 to 0.1875
- inner_bias: bfloat16 [4608], P('band'), may hold values from -3 to 3
- outer_weight: bfloat16 [4608, 1152], P('band'), may hold values from -0.09375 to 0.09375
- outer_bias: bfloat16 [1152], P('band'), may hold values from -2 to 2
- cotangent: bfloat16 [16, 1024, 1152], P('dp', 'band'), may hold values from -6 to 6
Outputs:
- block_out: bfloat16 [16, 1024, 1152], P('dp', 'band')
- grad_tokens: float32 [16, 1024, 1152], P('dp', 'band')
- grad_condition: float32 [16, 1152], P('dp')
- grad_ada_weight: float32 [1152, 6912], P('band')
- grad_ada_bias: float32 [6912], P('band')
- grad_qkv_weight: float32 [1152, 3456], P('band')
- grad_query_bias: float32 [1152], P('band')
- grad_value_bias: float32 [1152], P('band')
- grad_proj_weight: float32 [1152, 1152], P('band')
- grad_proj_bias: float32 [1152], P('band')
- grad_inner_weight: float32 [1152, 4608], P('band')
- grad_inner_bias: float32 [4608], P('band')
- grad_outer_weight: float32 [4608, 1152], P('band')
- grad_outer_bias: float32 [1152], P('band')
Inputs may be any that keep to these rules, and one draw needn't show every extreme that they name: `patch_grid`: each image's grid is either 4 * 4 rows by 64 columns or 24 rows by 40 columns; each kind covers exactly half of the images, which ones is drawn.
All inputs are finite; a program needn't handle non-finite values.
Results may differ from a plain program's by a relative error of at most 0.02.
The roundings to bfloat16 on the way count: a program that leaves them out, or rounds other values in their place, can miss the bound.
Values may be sent and summed in bfloat16 or wider, within the bound.
A program may use at most 320 MiB of HBM per device.

v0:
```python
from functools import partial

import jax
import jax.numpy as jnp
from jax import lax
from jax.sharding import PartitionSpec as P

HEAD_DIM = 72


def slot_layout(patch_grid, start, count, band_slots, band_count):
    slot_ids = start + jnp.arange(count, dtype=jnp.int32)
    band_ids = slot_ids // band_slots
    within = slot_ids % band_slots
    grid_rows = patch_grid[:, 0:1]
    grid_cols = patch_grid[:, 1:2]
    band_rows = grid_rows // band_count
    is_valid = within < band_rows * grid_cols
    row_index = band_ids * band_rows + within // grid_cols
    col_index = within % grid_cols
    return (row_index, col_index, is_valid)


def position_table(row_index, col_index, width):
    quarter = width // 4
    frequency = 10000.0 ** (-jnp.arange(quarter, dtype=jnp.float32) / quarter)
    rows_angle = row_index.astype(jnp.float32)[..., None] * frequency
    cols_angle = col_index.astype(jnp.float32)[..., None] * frequency
    return jnp.concatenate(
        [jnp.sin(rows_angle), jnp.cos(rows_angle), jnp.sin(cols_angle), jnp.cos(cols_angle)], -1
    )


def normalize(values):
    average = jnp.mean(values, -1, keepdims=True)
    centered = values - average
    variance = jnp.mean(centered * centered, -1, keepdims=True)
    inverse = lax.rsqrt(variance + 1e-06)
    return (centered * inverse, inverse)


def norm_back(grad_normed, normed, inverse):
    first = jnp.mean(grad_normed, -1, keepdims=True)
    second = jnp.mean(grad_normed * normed, -1, keepdims=True)
    return inverse * (grad_normed - first - normed * second)


def contract(operand, grad_rows):
    return lax.dot_general(
        operand, grad_rows, (((0, 1), (0, 1)), ((), ())), preferred_element_type=jnp.float32
    )


def split_heads(rows):
    return rows.reshape(rows.shape[0], rows.shape[1], rows.shape[2] // HEAD_DIM, HEAD_DIM)


def score_block(query_rows, key_rows, key_valid):
    scores = jnp.einsum(
        "iqhd,ikhd->ihqk",
        split_heads(query_rows),
        split_heads(key_rows),
        preferred_element_type=jnp.float32,
    )
    scores = scores * HEAD_DIM ** (-0.5)
    return jnp.where(key_valid[:, None, None, :], scores, -1e30)


def attention_forward(query_rows, key_rows, value_rows, key_valid):
    scores = score_block(query_rows, key_rows, key_valid)
    row_top = jnp.max(scores, -1, keepdims=True)
    exponent = jnp.exp(scores - row_top)
    row_total = jnp.sum(exponent, -1, keepdims=True)
    soft_weights = (exponent / row_total).astype(jnp.bfloat16)
    mixed_rows = jnp.einsum(
        "ihqk,ikhd->iqhd", soft_weights, split_heads(value_rows), preferred_element_type=jnp.float32
    )
    return (
        mixed_rows.reshape(query_rows.shape[:2] + (value_rows.shape[2],)).astype(jnp.bfloat16),
        row_top + jnp.log(row_total),
    )


def attention_backward(query_rows, key_rows, value_rows, log_total, grad_mixed, key_valid):
    soft_weights = jnp.exp(score_block(query_rows, key_rows, key_valid) - log_total)
    grad_heads = split_heads(grad_mixed)
    grad_soft = jnp.einsum(
        "iqhd,ikhd->ihqk", grad_heads, split_heads(value_rows), preferred_element_type=jnp.float32
    )
    row_inner = jnp.sum(soft_weights * grad_soft, -1, keepdims=True)
    grad_scores = (soft_weights * (grad_soft - row_inner)).astype(jnp.bfloat16)
    score_scale = HEAD_DIM ** (-0.5)
    grad_query = score_scale * jnp.einsum(
        "ihqk,ikhd->iqhd", grad_scores, split_heads(key_rows), preferred_element_type=jnp.float32
    )
    grad_key = score_scale * jnp.einsum(
        "ihqk,iqhd->ikhd", grad_scores, split_heads(query_rows), preferred_element_type=jnp.float32
    )
    grad_value = jnp.einsum(
        "ihqk,iqhd->ikhd",
        soft_weights.astype(jnp.bfloat16),
        grad_heads,
        preferred_element_type=jnp.float32,
    )
    return (
        grad_query.reshape(query_rows.shape),
        grad_key.reshape(key_rows.shape),
        grad_value.reshape(value_rows.shape),
    )


def total_over_images(ada_part, ada_bias_part, shares):
    return (
        lax.psum(ada_part.astype(jnp.bfloat16), "dp").astype(jnp.float32),
        lax.psum(ada_bias_part.astype(jnp.bfloat16), "dp").astype(jnp.float32),
        lax.psum(shares[0].astype(jnp.bfloat16), "dp").astype(jnp.float32),
        lax.psum(shares[1].astype(jnp.bfloat16), "dp").astype(jnp.float32),
        lax.psum(shares[2].astype(jnp.bfloat16), "dp").astype(jnp.float32),
        lax.psum(shares[3].astype(jnp.bfloat16), "dp").astype(jnp.float32),
        lax.psum(shares[4].astype(jnp.bfloat16), "dp").astype(jnp.float32),
        lax.psum(shares[5].astype(jnp.bfloat16), "dp").astype(jnp.float32),
        lax.psum(shares[6].astype(jnp.bfloat16), "dp").astype(jnp.float32),
        lax.psum(shares[7].astype(jnp.bfloat16), "dp").astype(jnp.float32),
        lax.psum(shares[8].astype(jnp.bfloat16), "dp").astype(jnp.float32),
    )


def own_piece(vector, count, band_place):
    return lax.dynamic_slice_in_dim(vector, band_place * count, count, 0)


def body(
    tokens,
    condition,
    patch_grid,
    ada_weight,
    ada_bias,
    qkv_weight,
    query_bias,
    value_bias,
    proj_weight,
    proj_bias,
    inner_weight,
    inner_bias,
    outer_weight,
    outer_bias,
    cotangent,
):
    band_count = lax.axis_size("band")
    images, band_slots, width = tokens.shape
    slots = band_slots * band_count
    band_place = lax.axis_index("band")
    gathered = (
        lax.all_gather(ada_weight, "band", axis=0, tiled=True),
        lax.all_gather(ada_bias, "band", axis=0, tiled=True),
        lax.all_gather(qkv_weight, "band", axis=0, tiled=True),
        lax.all_gather(query_bias, "band", axis=0, tiled=True),
        lax.all_gather(value_bias, "band", axis=0, tiled=True),
        lax.all_gather(proj_weight, "band", axis=0, tiled=True),
        lax.all_gather(proj_bias, "band", axis=0, tiled=True),
        lax.all_gather(inner_weight, "band", axis=0, tiled=True),
        lax.all_gather(inner_bias, "band", axis=0, tiled=True),
        lax.all_gather(outer_weight, "band", axis=0, tiled=True),
        lax.all_gather(outer_bias, "band", axis=0, tiled=True),
    )
    (
        ada_full,
        ada_bias_full,
        qkv_full,
        query_bias_full,
        value_bias_full,
        proj_full,
        proj_bias_full,
        inner_full,
        inner_bias_full,
        outer_full,
        outer_bias_full,
    ) = gathered
    row_index, col_index, is_valid = slot_layout(
        patch_grid, band_place * band_slots, band_slots, band_slots, band_count
    )
    whole_valid = slot_layout(patch_grid, 0, slots, band_slots, band_count)[2]
    condition_f = condition.astype(jnp.float32)
    activated = jax.nn.silu(condition_f).astype(jnp.bfloat16)
    modulation = jnp.dot(activated, ada_full, preferred_element_type=jnp.float32) + ada_bias_full
    blocks = [
        modulation[:, None, block_index * width : (block_index + 1) * width]
        for block_index in range(6)
    ]
    shift_one, scale_one, gate_one, shift_two, scale_two, gate_two = blocks
    residual = tokens.astype(jnp.float32) + position_table(row_index, col_index, width)
    normed_one, inverse_one = normalize(residual)
    attn_in = (normed_one * (1.0 + scale_one) + shift_one).astype(jnp.bfloat16)
    projected = jnp.dot(attn_in, qkv_full, preferred_element_type=jnp.float32)
    query_rows = (projected[..., :width] + query_bias_full).astype(jnp.bfloat16)
    key_rows = projected[..., width : 2 * width].astype(jnp.bfloat16)
    value_rows = (projected[..., 2 * width :] + value_bias_full).astype(jnp.bfloat16)
    gathered_keys, gathered_values = (
        lax.all_gather(key_rows, "band", axis=1, tiled=True),
        lax.all_gather(value_rows, "band", axis=1, tiled=True),
    )
    mixed_rows, band_total = attention_forward(
        query_rows, gathered_keys, gathered_values, whole_valid
    )
    attended = jnp.dot(mixed_rows, proj_full, preferred_element_type=jnp.float32) + proj_bias_full
    middle = residual + gate_one * attended
    normed_two, inverse_two = normalize(middle)
    mlp_in = (normed_two * (1.0 + scale_two) + shift_two).astype(jnp.bfloat16)
    hidden_pre = jnp.dot(mlp_in, inner_full, preferred_element_type=jnp.float32) + inner_bias_full
    hidden_act = jax.nn.gelu(hidden_pre, approximate=True).astype(jnp.bfloat16)
    mlp_out = jnp.dot(hidden_act, outer_full, preferred_element_type=jnp.float32) + outer_bias_full
    block_out = (middle + gate_two * mlp_out).astype(jnp.bfloat16)
    grad_out = cotangent.astype(jnp.float32) * is_valid[..., None].astype(jnp.float32)
    grad_gate_two = jnp.sum(grad_out * mlp_out, 1)
    grad_mlp = (gate_two * grad_out).astype(jnp.bfloat16)
    gelu_back = jax.vjp(partial(jax.nn.gelu, approximate=True), hidden_pre)[1]
    grad_outer = contract(hidden_act, grad_mlp)
    grad_outer_bias = jnp.sum(grad_mlp.astype(jnp.float32), (0, 1))
    grad_hidden = jnp.dot(grad_mlp, outer_full.T, preferred_element_type=jnp.float32)
    grad_pre = gelu_back(grad_hidden)[0].astype(jnp.bfloat16)
    grad_inner = contract(mlp_in, grad_pre)
    grad_inner_bias = jnp.sum(grad_pre.astype(jnp.float32), (0, 1))
    grad_mlp_in = jnp.dot(grad_pre, inner_full.T, preferred_element_type=jnp.float32)
    grad_shift_two = jnp.sum(grad_mlp_in, 1)
    grad_scale_two = jnp.sum(grad_mlp_in * normed_two, 1)
    grad_middle = grad_out + norm_back(grad_mlp_in * (1.0 + scale_two), normed_two, inverse_two)
    grad_gate_one = jnp.sum(grad_middle * attended, 1)
    grad_attended = (gate_one * grad_middle).astype(jnp.bfloat16)
    grad_proj = contract(mixed_rows, grad_attended)
    grad_proj_bias = jnp.sum(grad_attended.astype(jnp.float32), (0, 1))
    grad_mixed = jnp.dot(grad_attended, proj_full.T, preferred_element_type=jnp.float32).astype(
        jnp.bfloat16
    )
    band_dq, key_terms, value_terms = attention_backward(
        query_rows, gathered_keys, gathered_values, band_total, grad_mixed, whole_valid
    )
    key_sum, value_sum = (
        lax.psum_scatter(
            key_terms.astype(jnp.bfloat16), "band", scatter_dimension=1, tiled=True
        ).astype(jnp.float32),
        lax.psum_scatter(
            value_terms.astype(jnp.bfloat16), "band", scatter_dimension=1, tiled=True
        ).astype(jnp.float32),
    )
    grad_query = band_dq.astype(jnp.bfloat16)
    grad_key = key_sum.astype(jnp.bfloat16)
    grad_value = value_sum.astype(jnp.bfloat16)
    grad_qkv = jnp.concatenate([grad_query, grad_key, grad_value], -1)
    grad_qkv_weight = contract(attn_in, grad_qkv)
    grad_attn_in = jnp.dot(grad_qkv, qkv_full.T, preferred_element_type=jnp.float32)
    grad_query_bias = jnp.sum(grad_query.astype(jnp.float32), (0, 1))
    grad_value_bias = jnp.sum(grad_value.astype(jnp.float32), (0, 1))
    grad_shift_one = jnp.sum(grad_attn_in, 1)
    grad_scale_one = jnp.sum(grad_attn_in * normed_one, 1)
    grad_tokens = grad_middle + norm_back(grad_attn_in * (1.0 + scale_one), normed_one, inverse_one)
    partial_mod = jnp.concatenate(
        [
            grad_shift_one,
            grad_scale_one,
            grad_gate_one,
            grad_shift_two,
            grad_scale_two,
            grad_gate_two,
        ],
        -1,
    )
    grad_mod = lax.psum(partial_mod.astype(jnp.bfloat16), "band")
    grad_act = jnp.dot(grad_mod, ada_full.T, preferred_element_type=jnp.float32)
    silu_back = jax.vjp(jax.nn.silu, condition_f)[1]
    grad_condition = silu_back(grad_act)[0]
    row_count = ada_weight.shape[0]
    own_rows = lax.dynamic_slice_in_dim(activated, band_place * row_count, row_count, 1)
    ada_part = lax.dot_general(
        own_rows, grad_mod, (((0,), (0,)), ((), ())), preferred_element_type=jnp.float32
    )
    ada_bias_part = own_piece(
        jnp.sum(grad_mod.astype(jnp.float32), 0), ada_bias.shape[0], band_place
    )
    partials = (
        grad_qkv_weight,
        grad_query_bias,
        grad_value_bias,
        grad_proj,
        grad_proj_bias,
        grad_inner,
        grad_inner_bias,
        grad_outer,
        grad_outer_bias,
    )
    shares = (
        lax.psum_scatter(
            partials[0].astype(jnp.bfloat16), "band", scatter_dimension=0, tiled=True
        ).astype(jnp.float32),
        lax.psum_scatter(
            partials[1].astype(jnp.bfloat16), "band", scatter_dimension=0, tiled=True
        ).astype(jnp.float32),
        lax.psum_scatter(
            partials[2].astype(jnp.bfloat16), "band", scatter_dimension=0, tiled=True
        ).astype(jnp.float32),
        lax.psum_scatter(
            partials[3].astype(jnp.bfloat16), "band", scatter_dimension=0, tiled=True
        ).astype(jnp.float32),
        lax.psum_scatter(
            partials[4].astype(jnp.bfloat16), "band", scatter_dimension=0, tiled=True
        ).astype(jnp.float32),
        lax.psum_scatter(
            partials[5].astype(jnp.bfloat16), "band", scatter_dimension=0, tiled=True
        ).astype(jnp.float32),
        lax.psum_scatter(
            partials[6].astype(jnp.bfloat16), "band", scatter_dimension=0, tiled=True
        ).astype(jnp.float32),
        lax.psum_scatter(
            partials[7].astype(jnp.bfloat16), "band", scatter_dimension=0, tiled=True
        ).astype(jnp.float32),
        lax.psum_scatter(
            partials[8].astype(jnp.bfloat16), "band", scatter_dimension=0, tiled=True
        ).astype(jnp.float32),
    )
    totals = total_over_images(ada_part, ada_bias_part, shares)
    return (
        block_out,
        grad_tokens,
        grad_condition,
        totals[0],
        totals[1],
        totals[2],
        totals[3],
        totals[4],
        totals[5],
        totals[6],
        totals[7],
        totals[8],
        totals[9],
        totals[10],
    )


def solution(mesh):
    placed = (
        P("dp", "band", None),
        P("dp", None),
        P("dp", None),
        P("band", None),
        P("band"),
        P("band", None),
        P("band"),
        P("band"),
        P("band", None),
        P("band"),
        P("band", None),
        P("band"),
        P("band", None),
        P("band"),
        P("dp", "band", None),
    )
    return jax.shard_map(
        body,
        mesh=mesh,
        in_specs=placed,
        out_specs=(
            P("dp", "band", None),
            P("dp", "band", None),
            P("dp", None),
            P("band", None),
            P("band"),
            P("band", None),
            P("band"),
            P("band"),
            P("band", None),
            P("band"),
            P("band", None),
            P("band"),
            P("band", None),
            P("band"),
        ),
        check_vma=False,
    )
```

profile of v0, /device:TPU:1, one launch (start us, length us, event | category | flops | bytes accessed | tf_op | source)
XLA Modules:
  0.0 2051.3 jit_solution(2868996950987715143)
XLA Ops:
  12.1 16.4 all-reduce.13
  29.4 5.5 multiply_cosine_fusion
  40.3 244.7 %all-gather.9.cloned.1.call-done = bf16[1152,6912]{1,0:T(8,128)(2,1)} async-done(((bf16[288,6912]{1,0:T(8,128)(2,1)}), bf16[1152,6912]{1,0:T(8,128)(2,1)}) %all-gather.9.cloned.1.call-update) | async-done | bytes 15925264 | tf_op jit(solution)/shard_map/all_gather | solution.py:154
  285.0 7.7 convolution_add_fusion
  293.3 134.2 %all-gather.11.cloned.1.call-done = bf16[1152,3456]{1,0:T(8,128)(2,1)} async-done(((bf16[288,3456]{1,0:T(8,128)(2,1)}), bf16[1152,3456]{1,0:T(8,128)(2,1)}) %all-gather.11.cloned.1.call-update) | async-done | bytes 7962640 | tf_op jit(solution)/shard_map/all_gather | solution.py:156
  427.5 7.9 fusion.28
  439.2 2.8 slice.74
  444.0 10.5 all-gather
  458.7 68.3 %all-gather.13.cloned.1.call-done = bf16[2,1024,1152]{2,1,0:T(8,128)(2,1)} async-done(((bf16[2,256,1152]{2,1,0:T(8,128)(2,1)}), bf16[2,1024,1152]{2,1,0:T(8,128)(2,1)}) %all-gather.13.cloned.1.call-update) | async-done | bytes 4718608 | tf_op jit(solution)/shard_map/all_gather | solution.py:200
  527.0 6.6 copy.66
  533.6 83.2 %all-gather.15.cloned.1.call-done = bf16[2,1024,1152]{2,1,0:T(8,128)(2,1)} async-done(((bf16[2,256,1152]{2,1,0:T(8,128)(2,1)}), bf16[2,1024,1152]{2,1,0:T(8,128)(2,1)}) %all-gather.15.cloned.1.call-update) | async-done | bytes 4718608 | tf_op jit(solution)/shard_map/all_gather | solution.py:199
  616.8 6.6 copy.68
  623.4 16.6 fusion.68
  639.9 14.4 fusion
  654.4 16.2 fusion.41
  671.9 5.6 fusion.64
  679.9 178.5 %all-gather.19.cloned.1.call-done = bf16[1152,4608]{1,0:T(8,128)(2,1)} async-done(((bf16[288,4608]{1,0:T(8,128)(2,1)}), bf16[1152,4608]{1,0:T(8,128)(2,1)}) %all-gather.19.cloned.1.call-update) | async-done | bytes 10616848 | tf_op jit(solution)/shard_map/all_gather | solution.py:161
  858.5 13.6 fusion.15
  872.0 172.3 %all-gather.21.cloned.1.call-done = bf16[4608,1152]{1,0:T(8,128)(2,1)} async-done(((bf16[1152,1152]{1,0:T(8,128)(2,1)}), bf16[4608,1152]{1,0:T(8,128)(2,1)}) %all-gather.21.cloned.1.call-update) | async-done | bytes 10616848 | tf_op jit(solution)/shard_map/all_gather | solution.py:163
  1044.3 17.6 fusion.70
  1061.9 9.9 fusion.13
  1071.9 12.5 multiply_reduce_fusion.1
  1084.4 3.3 fusion.63
  1088.7 2.9 convolution_convert_fusion.1
  1093.2 15.6 fusion.34
  1108.8 6.7 copy.72
  1115.6 25.4 %multiply_reduce_fusion = (f32[2,16,256]{2,1,0:T(8,128)}, f32[2,16,256,1024]{3,2,1,0:T(8,128)}) fusion(f32[2,16,256,1024]{3,2,1,0:T(8,128)} %get-tuple-element.86, f32[2,16,256]{2,1,0:T(8,128)} %log_add_fusion, bf16[2,256,16,72]{1,3,2,0:T(8,128)(2,1)S(1)} %bitcast.94, bf16[2,1024,16,72]{1,3,2,0:T(8,128)(2,1)} %bitcast.90), kind=kOutput, calls=%fused_computation.1 | convolution fusion | flops 1233117184 | bytes 73072640 | tf_op jit(solution)/shard_map/iqhd,ikhd->ihqk/dot_general | solution.py:87
  1141.1 28.2 %multiply_convert_fusion = bf16[2,16,256,1024]{3,2,1,0:T(8,128)(2,1)} fusion(f32[2,16,256,1024]{3,2,1,0:T(8,128)} %get-tuple-element.89, f32[2,16,256,1024]{3,2,1,0:T(8,128)} %get-tuple-element.86, f32[2,16,256]{2,1,0:T(8,128)} %get-tuple-element.88, f32[2,16,256]{2,1,0:T(8,128)} %log_add_fusion), kind=kLoop, calls=%fused_computation | loop fusion | flops 33554432 | bytes 83951616 | tf_op jit(solution)/shard_map/convert_element_type | solution.py:91
  1169.2 11.0 multiply_convert_fusion.1
  1180.2 6.7 copy.71
  1188.2 4.5 fusion.30
  1194.0 13.4 fusion.3
  1208.1 11.1 fusion.2
  1219.3 10.9 fusion.69
  1231.6 55.6 %reduce-scatter.7.cloned.1.call-done = bf16[2,256,1152]{2,1,0:T(8,128)(2,1)} async-done(((bf16[2,1024,1152]{2,1,0:T(8,128)(2,1)}), bf16[2,256,1152]{2,1,0:T(8,128)(2,1)}) %reduce-scatter.7.cloned.1.call-update) | async-done | bytes 1179664 | tf_op jit(solution)/shard_map/reduce_scatter | solution.py:238
  1287.1 9.9 fusion.8
  1299.6 9.3 multiply_reduce_fusion.4
  1311.7 19.9 all-reduce.12
  1331.7 10.4 fusion.46
  1342.1 3.3 convolution_convert_fusion
  1345.3 181.9 %reduce-scatter.17.cloned.1.call-done = bf16[1152,1152]{1,0:T(8,128)(2,1)} async-done(((bf16[4608,1152]{1,0:T(8,128)(2,1)}), bf16[1152,1152]{1,0:T(8,128)(2,1)}) %reduce-scatter.17.cloned.1.call-update) | async-done | bytes 2654224 | tf_op jit(solution)/shard_map/reduce_scatter | solution.py:312
  1527.3 183.5 %reduce-scatter.15.cloned.1.call-done = bf16[288,4608]{1,0:T(8,128)(2,1)} async-done(((bf16[1152,4608]{1,0:T(8,128)(2,1)}), bf16[288,4608]{1,0:T(8,128)(2,1)}) %reduce-scatter.15.cloned.1.call-update) | async-done | bytes 2654224 | tf_op jit(solution)/shard_map/reduce_scatter | solution.py:306
  1710.8 141.9 %reduce-scatter.11.cloned.1.call-done = bf16[288,3456]{1,0:T(8,128)(2,1)} async-done(((bf16[1152,3456]{1,0:T(8,128)(2,1)}), bf16[288,3456]{1,0:T(8,128)(2,1)}) %reduce-scatter.11.cloned.1.call-update) | async-done | bytes 1990672 | tf_op jit(solution)/shard_map/reduce_scatter | solution.py:291
  1854.5 21.8 %all-reduce.10 = (bf16[1728]{0:T(1024)(128)(2,1)S(1)}, bf16[288]{0:T(512)(128)(2,1)S(1)}, bf16[288]{0:T(512)(128)(2,1)S(1)}, bf16[288]{0:T(512)(128)(2,1)S(1)}, ...) all-reduce(bf16[1728]{0:T(1024)(128)(2,1)S(1)} %dynamic_slice.11, ...), channel_id=1, replica_groups=mesh['dp'=8,'band'=4] {'dp'}, use_global_device_ids=true, to_apply=%region_22.23 | all-reduce | flops 4032 | bytes 16128 | tf_op jit(solution)/shard_map/psum | solution.py:115
  1879.8 147.4 %all-reduce.16.cloned.1.call-done = (bf16[288,6912]{1,0:T(8,128)(2,1)}, bf16[288,3456]{1,0:T(8,128)(2,1)}, bf16[288,1152]{1,0:T(8,128)(2,1)}, bf16[288,4608]{1,0:T(8,128)(2,1)}, bf16[1152,1152]{1,0:T(8,128)(2,1)}) async-done(((bf16[288,6912]{1,0:T(8,128)(2,1)}, bf16[288,3456]{1,0:T(8,128)(2,1)}, bf16[288,1152]{1,0:T(8,128)(2,1)}, bf16[288,4608]{1,0:T(8,128)(2,1)}, bf16[1152,1152]{1,0:T(8,128)(2,1)}), ...) | async-done | bytes 11943952 | tf_op jit(solution)/shard_map/psum | solution.py:114
  2029.5 6.0 convert_element_type.256
  2038.6 3.0 convert_element_type.268
  2041.6 2.7 convert_element_type.271
  (223 shorter events, 45.7 us)
Async XLA Ops:
  7.2 21.4 %copy-start.53 = (s32[2,2]{1,0:T(2,128)S(1)}, s32[2,2]{1,0:T(2,128)}, u32[]{:S(2)}) copy-start(s32[2,2]{1,0:T(2,128)} %param.17) | copy-start | bytes 52
  7.3 277.8 %all-gather.9.cloned.1.call-start = ((), (), s32[]{:S(2)}) async-start(), calls=%async_computation.6 | async-start | bytes 19906560 | tf_op jit(solution)/shard_map/all_gather | solution.py:154
  8.0 419.5 %all-gather.11.cloned.1.call-start = ((), (), s32[]{:S(2)}) async-start(), calls=%async_computation.7 | async-start | bytes 9953280 | tf_op jit(solution)/shard_map/all_gather | solution.py:156
  8.7 518.2 %all-gather.13.cloned.1.call-start = ((), (), s32[]{:S(2)}) async-start(), calls=%async_computation.8 | async-start | bytes 5898240 | tf_op jit(solution)/shard_map/all_gather | solution.py:200
  39.8 632.1 %copy-start = (f32[2,256,1152]{2,1,0:T(8,128)}, f32[2,256,1152]{2,1,0:T(8,128)S(1)}, u32[]{:S(2)}) copy-start(f32[2,256,1152]{2,1,0:T(8,128)S(1)} %get-tuple-element.55) | copy-start | bytes 7077892
  39.9 245.2 %copy-start.25 = (bf16[2,1152]{1,0:T(2,128)(2,1)S(1)}, bf16[2,1152]{1,0:T(2,128)(2,1)}, u32[]{:S(2)}) copy-start(bf16[2,1152]{1,0:T(2,128)(2,1)} %param.16) | copy-start | bytes 13828
  39.9 387.6 %copy-start.29 = (f32[2,256]{1,0:T(2,128)}, f32[2,256]{1,0:T(2,128)S(1)}, u32[]{:S(2)}) copy-start(f32[2,256]{1,0:T(2,128)S(1)} %broadcast_multiply_fusion.5) | copy-start | bytes 6148
  40.3 387.3 %copy-start.39 = (f32[2,256]{1,0:T(2,128)}, f32[2,256]{1,0:T(2,128)S(1)}, u32[]{:S(2)}) copy-start(f32[2,256]{1,0:T(2,128)S(1)} %add_rsqrt_fusion.1) | copy-start | bytes 6148
  293.3 142.1 %copy-start.19 = (f32[2,1152]{1,0:T(2,128)}, f32[2,1152]{1,0:T(2,128)S(1)}, u32[]{:S(2)}) copy-start(f32[2,1152]{1,0:T(2,128)S(1)} %get-tuple-element.71) | copy-start | bytes 27652
  293.3 142.1 %copy-start.36 = (f32[2,1152]{1,0:T(2,128)}, f32[2,1152]{1,0:T(2,128)S(1)}, u32[]{:S(2)}) copy-start(f32[2,1152]{1,0:T(2,128)S(1)} %get-tuple-element.70) | copy-start | bytes 27652
  439.1 177.6 %all-gather.15.cloned.1.call-start = ((), (), s32[]{:S(2)}) async-start(), calls=%async_computation.9 | async-start | bytes 5898240 | tf_op jit(solution)/shard_map/all_gather | solution.py:199
  442.0 229.9 %all-gather.17.cloned.1.call-start = ((), (), s32[]{:S(2)}) async-start(), calls=%async_computation.10 | async-start | bytes 3317760 | tf_op jit(solution)/shard_map/all_gather | solution.py:159
  442.6 415.8 %all-gather.19.cloned.1.call-start = ((), (), s32[]{:S(2)}) async-start(), calls=%async_computation.11 | async-start | bytes 13271040 | tf_op jit(solution)/shard_map/all_gather | solution.py:161
  443.2 601.1 %all-gather.21.cloned.1.call-start = ((), (), s32[]{:S(2)}) async-start(), calls=%async_computation.12 | async-start | bytes 13271040 | tf_op jit(solution)/shard_map/all_gather | solution.py:163
  444.0 787.6 %reduce-scatter.9.cloned.1.call-start = ((), (), s32[]{:S(2)}) async-start(), calls=%async_computation.14 | async-start | bytes 5898240 | tf_op jit(solution)/shard_map/reduce_scatter | solution.py:241
  458.7 164.7 %copy-start.2 = (bf16[2,256,1152]{1,2,0:T(8,128)(2,1)}, bf16[2,256,1152]{1,2,0:T(8,128)(2,1)S(1)}, u32[]{:S(2)}) copy-start(bf16[2,256,1152]{1,2,0:T(8,128)(2,1)S(1)} %copy.67) | copy-start | bytes 3538948
  639.9 14.4 copy-start.17
  654.4 17.5 copy-start.23
  654.4 17.5 copy-start.42
  677.5 180.9 %copy-start.37 = (f32[2,1152]{1,0:T(2,128)S(1)}, f32[2,1152]{1,0:T(2,128)}, u32[]{:S(2)}) copy-start(f32[2,1152]{1,0:T(2,128)} %get-tuple-element.68) | copy-start | bytes 27652
  679.3 192.7 %copy-start.45 = (f32[2,256]{1,0:T(2,128)}, f32[2,256]{1,0:T(2,128)S(1)}, u32[]{:S(2)}) copy-start(f32[2,256]{1,0:T(2,128)S(1)} %add_rsqrt_fusion) | copy-start | bytes 6148
  858.4 185.9 %copy-start.13 = (bf16[2,256,1152]{2,1,0:T(8,128)(2,1)S(1)}, bf16[2,256,1152]{2,1,0:T(8,128)(2,1)}, u32[]{:S(2)}) copy-start(bf16[2,256,1152]{2,1,0:T(8,128)(2,1)} %param.29) | copy-start | bytes 3538948
  858.4 185.9 %copy-start.21 = (f32[2,1152]{1,0:T(2,128)S(1)}, f32[2,1152]{1,0:T(2,128)}, u32[]{:S(2)}) copy-start(f32[2,1152]{1,0:T(2,128)} %get-tuple-element.67) | copy-start | bytes 27652
  858.4 185.9 %copy-start.27 = (f32[4608]{0:T(1024)S(1)}, f32[4608]{0:T(1024)}, u32[]{:S(2)}) copy-start(f32[4608]{0:T(1024)} %reshape.436) | copy-start | bytes 55300
  858.4 185.9 %copy-start.43 = (f32[2,256]{1,0:T(2,128)S(1)}, f32[2,256]{1,0:T(2,128)}, u32[]{:S(2)}) copy-start(f32[2,256]{1,0:T(2,128)} %compare_convert_fusion) | copy-start | bytes 6148
  1061.9 9.9 copy-start.5
  1061.9 9.9 copy-start.22
  1061.9 10.0 copy-start.28
  1061.9 10.0 copy-start.41
  1061.9 10.0 copy-start.44
  1061.9 10.0 copy-start.46
  1061.9 10.0 copy-start.59
  1071.9 12.5 copy-start.24
  1115.6 171.6 %reduce-scatter.7.cloned.1.call-start = ((), (), s32[]{:S(2)}) async-start(), calls=%async_computation.13 | async-start | bytes 5898240 | tf_op jit(solution)/shard_map/reduce_scatter | solution.py:238
  1141.0 28.2 %copy-start.3 = (bf16[2,256,1152]{1,2,0:T(8,128)(2,1)S(1)}, bf16[2,256,1152]{1,2,0:T(8,128)(2,1)}, u32[]{:S(2)}) copy-start(bf16[2,256,1152]{1,2,0:T(8,128)(2,1)} %copy-done.2) | copy-start | bytes 3538948
  1187.0 158.4 %reduce-scatter.13.cloned.1.call-start = ((), (), s32[]{:S(2)}) async-start(), calls=%async_computation.16 | async-start | bytes 3317760 | tf_op jit(solution)/shard_map/reduce_scatter | solution.py:300
  1192.7 334.6 %reduce-scatter.17.cloned.1.call-start = ((), (), s32[]{:S(2)}) async-start(), calls=%async_computation.18 | async-start | bytes 13271040 | tf_op jit(solution)/shard_map/reduce_scatter | solution.py:312
  1207.4 503.4 %reduce-scatter.15.cloned.1.call-start = ((), (), s32[]{:S(2)}) async-start(), calls=%async_computation.17 | async-start | bytes 13271040 | tf_op jit(solution)/shard_map/reduce_scatter | solution.py:306
  1219.2 633.4 %reduce-scatter.11.cloned.1.call-start = ((), (), s32[]{:S(2)}) async-start(), calls=%async_computation.15 | async-start | bytes 9953280 | tf_op jit(solution)/shard_map/reduce_scatter | solution.py:291
  1219.3 67.9 %copy-start.20 = (f32[2,1152]{1,0:T(2,128)S(1)}, f32[2,1152]{1,0:T(2,128)}, u32[]{:S(2)}) copy-start(f32[2,1152]{1,0:T(2,128)} %copy-done.19) | copy-start | bytes 27652
  1230.2 57.0 %copy-start.1 = (f32[2,256,1152]{2,1,0:T(8,128)S(1)}, f32[2,256,1152]{2,1,0:T(8,128)}, u32[]{:S(2)}) copy-start(f32[2,256,1152]{2,1,0:T(8,128)} %copy-done) | copy-start | bytes 7077892
  1230.2 57.0 %copy-start.30 = (f32[2,256]{1,0:T(2,128)S(1)}, f32[2,256]{1,0:T(2,128)}, u32[]{:S(2)}) copy-start(f32[2,256]{1,0:T(2,128)} %copy-done.29) | copy-start | bytes 6148
  1297.1 730.2 %all-reduce.16.cloned.1.call-start = ((), (), s32[]{:S(2)}) async-start(), calls=%async_computation.19 | async-start | bytes 23887872 | tf_op jit(solution)/shard_map/psum | solution.py:114
  1299.6 9.4 copy-start.6
  1299.6 9.4 copy-start.10
  1299.6 9.4 copy-start.40
  1309.2 22.5 %copy-start.26 = (bf16[2,1152]{1,0:T(2,128)(2,1)S(1)}, bf16[2,1152]{1,0:T(2,128)(2,1)}, u32[]{:S(2)}) copy-start(bf16[2,1152]{1,0:T(2,128)(2,1)} %param.16) | copy-start | bytes 13828
  2029.5 6.0 copy-start.11
  (27 other events, 68.1 us)
Sparse Core Ops, SparseCore 0:
  9.7 275.3 all-gather.8
  286.6 140.8 all-gather.10
  439.3 87.6 all-gather.12
  529.0 87.7 all-gather.14
  618.2 53.6 all-gather.16
  673.3 185.0 all-gather.18
  860.0 184.2 all-gather.20
  1115.7 83.2 reduce-scatter.8
  1201.3 85.7 reduce-scatter.6
  1289.9 54.9 reduce-scatter.12
  1347.2 180.0 reduce-scatter.16
  1529.6 181.1 reduce-scatter.14
  1713.7 138.8 reduce-scatter.10
  1858.3 168.9 all-reduce.15
where the time goes:
time: 2060 us; the launch traced here: 2050 us
  waiting for transfers between devices  1600 us (78%)
  matrix products  235 us (11%)
  other arithmetic  83.5 us (4%)
  blocking collectives  68.6 us (3%)
  local copies, waits for them, and re-layouts  49.4 us (2%)
    all_gather x1, waiting for transfers between devices, body(): lax.all_gather(ada_weight, 'band', axis=0, tiled=True)  245 us
    reduce_scatter x1, waiting for transfers between devices, body(): lax.psum_scatter(partials[5].astype(jnp.bfloat16), 'band', scatter_dimens...  184 us
    reduce_scatter x1, waiting for transfers between devices, body(): lax.psum_scatter(partials[7].astype(jnp.bfloat16), 'band', scatter_dimens...  182 us
    all_gather x1, waiting for transfers between devices, body(): lax.all_gather(inner_weight, 'band', axis=0, tiled=True)  178 us
    all_gather x1, waiting for transfers between devices, body(): lax.all_gather(outer_weight, 'band', axis=0, tiled=True)  172 us
    psum x1, waiting for transfers between devices, total_over_images(): lax.psum(ada_part.astype(jnp.bfloat16), 'dp').astype(jnp.float32)  147 us
    reduce_scatter x1, waiting for transfers between devices, body(): lax.psum_scatter(partials[0].astype(jnp.bfloat16), 'band', scatter_dimens...  142 us
    all_gather x1, waiting for transfers between devices, body(): lax.all_gather(qkv_weight, 'band', axis=0, tiled=True)  134 us
  transfers between devices with their start and end apart: 14, of which 12 were waited for; matrix products, arithmetic and copies ran while one was open for 13% of the time, Pallas kernels for 0%

commit v1 on v0

v1 whole, which is shorter than its diff:
```python
import functools
from functools import partial

import jax
import jax.numpy as jnp
from jax import lax
from jax.experimental import pallas as pl
from jax.experimental.pallas import tpu as pltpu
from jax.sharding import PartitionSpec as P

HEAD_DIM = 72

MESH = pl.DeviceIdType.MESH
NB=4
def place():
    dp = lax.axis_index("dp"); band = lax.axis_index("band")
    return dp, band
def gather_kernel(width, qp_in, inner_in, outer_in, tok_in, cot_in, mod_in,
                  qp_out, inner_out, outer_out, tok_out, cot_out, mod_out,
                  z_send, z_recv, a_send, a_recv, b_send, b_recv, c_send, c_recv,
                  t_send, t_recv, m_send, m_recv, local_sem, h_sem, bq, bi, bo, bt):
    dp, band = place()
    core = lax.rem(dp, 2); px = lax.rem(dp // 2, 2); py = lax.rem(dp // 4, 2)
    base = dp - core
    kind = py * 2 + px
    sib = dp + 1 - 2 * core
    xdp = dp + 2 - 4 * px
    ydp = dp + 4 - 8 * py
    dev = lambda d, b: {"dp": d, "band": b}
    barrier = pltpu.get_barrier_semaphore()
    peers = [dev(xdp, band), dev(ydp, band), dev(sib, band)]
    for k in range(1, NB):
        ob = lax.rem(band + k, NB)
        peers += [dev(dp, ob), dev(sib, ob)]
    for q in peers:
        pl.semaphore_signal(barrier, inc=1, device_id=q, device_id_type=MESH)
    pl.semaphore_wait(barrier, len(peers))

    def rc(src, dst, ss, rs, to):
        return pltpu.make_async_remote_copy(src_ref=src, dst_ref=dst, send_sem=ss, recv_sem=rs, device_id=to, device_id_type=MESH)
    ins = (qp_in, inner_in, outer_in); outs = (qp_out, inner_out, outer_out)
    def cols(t, n=1):
        return pl.ds(pl.multiple_of(t * width, 128), n * width)
    def unit(ph, b, t, h):
        return outs[ph].at[b, t, h] if ph == 2 else outs[ph].at[b, h, :, cols(t)]
    def own(ph):
        return ins[ph].at[kind, core] if ph == 2 else ins[ph].at[core, :, cols(kind)]
    def pair(ph, b, h, y):
        return outs[ph].at[b, pl.ds(2 * y, 2), h] if ph == 2 else outs[ph].at[b, h, :, cols(2 * y, 2)]
    def row(ph, b, h):
        return outs[ph].at[b, :, h] if ph == 2 else outs[ph].at[b, h]
    sends = []
    def go(c):
        c.start(); sends.append(c)
    slot = lax.rem(band, 2)
    def move(which, src, dst):
        for i in range(2):
            to_core = band // 2; to_band = 2 * core + i
            home = jnp.logical_and(to_core == core, to_band == band)
            @pl.when(home)
            def _():
                pltpu.make_async_copy(src.at[i], bt.at[which], h_sem.at[which]).start()
                pltpu.make_async_copy(src.at[i], bt.at[which], h_sem.at[which]).wait()
                pltpu.make_async_copy(bt.at[which], dst.at[slot], t_recv.at[which, slot]).start()
            @pl.when(jnp.logical_not(home))
            def _():
                rc(src.at[i], dst.at[slot], t_send.at[which, i], t_recv.at[which, slot], dev(base + to_core, to_band)).start()
    def move_wait(which, src, dst):
        for i in range(2):
            to_core = band // 2; to_band = 2 * core + i
            home = jnp.logical_and(to_core == core, to_band == band)
            @pl.when(jnp.logical_not(home))
            def _():
                rc(src.at[i], dst.at[slot], t_send.at[which, i], t_recv.at[which, slot], dev(base + to_core, to_band)).wait_send()
        for s in range(2):
            pltpu.make_async_copy(src.at[s], dst.at[s], t_recv.at[which, s]).wait()
    def mods():
        for i in range(2):
            for c in range(2):
                home = jnp.logical_and(c == core, 2 * core + i == band)
                @pl.when(home)
                def _():
                    pltpu.make_async_copy(mod_in.at[i], mod_out.at[band], m_recv.at[band]).start()
                @pl.when(jnp.logical_not(home))
                def _():
                    rc(mod_in.at[i], mod_out.at[band], m_send.at[i, c], m_recv.at[band], dev(base + c, 2 * core + i)).start()
    def mods_wait():
        for i in range(2):
            for c in range(2):
                home = jnp.logical_and(c == core, 2 * core + i == band)
                @pl.when(jnp.logical_not(home))
                def _():
                    rc(mod_in.at[i], mod_out.at[band], m_send.at[i, c], m_recv.at[band], dev(base + c, 2 * core + i)).wait_send()
        for b in range(NB):
            pltpu.make_async_copy(mod_in.at[0], mod_out.at[b], m_recv.at[b]).wait()
    def zstart(ph):
        for k in (1, 3, 2):
            ob = lax.rem(band + k, NB)
            go(rc(own(ph), unit(ph, band, kind, core), z_send.at[ph, k], z_recv.at[ph, k], dev(dp, ob)))
    mods()
    move(0, tok_in, tok_out)
    zstart(0)
    bounce = (bq, bi, bo)
    for ph in range(3):
        pltpu.make_async_copy(ins[ph], bounce[ph], local_sem.at[ph]).start()
    for ph in range(3):
        pltpu.make_async_copy(ins[ph], bounce[ph], local_sem.at[ph]).wait()
        pltpu.make_async_copy(bounce[ph], outs[ph].at[band], local_sem.at[ph]).start()
    steps = [(ph, k) for ph in range(3) for k in (1, 3, 2)]
    n = len(steps)
    frm = lambda k: lax.rem(band + NB - k, NB)
    other = lambda v: 1 - v
    for s in range(n + 3):
        if s < n:
            ph, k = steps[s]; b = frm(k)
            u = unit(ph, b, kind, core)
            rc(u, u, z_send.at[ph, k], z_recv.at[ph, k], dev(dp, band)).wait_recv()
            go(rc(u, u, a_send.at[s], a_recv.at[s], dev(xdp if s % 2 == 0 else ydp, band)))
            if k == 3 and ph < 2:
                zstart(ph + 1)
            if k == 2 and ph == 2:
                move(1, cot_in, cot_out)
        r = s - 1
        if 0 <= r < n:
            ph, k = steps[r]; b = frm(k)
            got = py * 2 + other(px) if r % 2 == 0 else other(py) * 2 + px
            u = unit(ph, b, got, core)
            rc(u, u, a_send.at[r], a_recv.at[r], dev(xdp, band)).wait_recv()
            if r % 2 == 0:
                v = pair(ph, b, core, py)
                go(rc(v, v, b_send.at[r, 0], b_recv.at[r, 0], dev(ydp, band)))
            else:
                for j in range(2):
                    v = unit(ph, b, j * 2 + px, core)
                    go(rc(v, v, b_send.at[r, j], b_recv.at[r, j], dev(xdp, band)))
        r = s - 2
        if 0 <= r < n:
            ph, k = steps[r]; b = frm(k)
            if r % 2 == 0:
                v = pair(ph, b, core, other(py))
                rc(v, v, b_send.at[r, 0], b_recv.at[r, 0], dev(ydp, band)).wait_recv()
            else:
                for j in range(2):
                    v = unit(ph, b, j * 2 + other(px), core)
                    rc(v, v, b_send.at[r, j], b_recv.at[r, j], dev(xdp, band)).wait_recv()
            w = row(ph, b, core)
            go(rc(w, w, c_send.at[r], c_recv.at[r], dev(sib, band)))
        r = s - 3
        if 0 <= r < n:
            ph, k = steps[r]; b = frm(k)
            w = row(ph, b, other(core))
            rc(w, w, c_send.at[r], c_recv.at[r], dev(sib, band)).wait_recv()
    for ph in range(3):
        pltpu.make_async_copy(bounce[ph], outs[ph].at[band], local_sem.at[ph]).wait()
    mods_wait()
    move_wait(0, tok_in, tok_out)
    move_wait(1, cot_in, cot_out)
    for c in sends: c.wait_send()

def gather_weights(qp, inner, outer, tok, cot, mod, width):
    half = qp.shape[0] // 2
    ff = qp.shape[1]
    bf = jnp.bfloat16
    qp = qp.reshape(2, half, ff); inner = inner.reshape(2, half, ff); outer = outer.reshape(4, 2, half, width)
    D = pltpu.SemaphoreType.DMA
    outs = pl.pallas_call(
        functools.partial(gather_kernel, width),
        out_shape=[jax.ShapeDtypeStruct((NB,) + qp.shape, bf), jax.ShapeDtypeStruct((NB,) + inner.shape, bf),
                   jax.ShapeDtypeStruct((NB,) + outer.shape, bf),
                   jax.ShapeDtypeStruct(tok.shape, bf), jax.ShapeDtypeStruct(cot.shape, bf),
                   jax.ShapeDtypeStruct((NB,) + mod.shape[1:], jnp.float32)],
        in_specs=[pl.BlockSpec(memory_space=pl.ANY)] * 6,
        out_specs=[pl.BlockSpec(memory_space=pl.ANY)] * 6,
        scratch_shapes=[D((3, 4)), D((3, 4)), D((9,)), D((9,)), D((9, 2)), D((9, 2)), D((9,)), D((9,)),
                        D((2, 2)), D((2, 2)), D((2, 2)), D((4,)), D((3,)), D((2,)),
                        pltpu.VMEM(qp.shape, bf), pltpu.VMEM(inner.shape, bf), pltpu.VMEM(outer.shape, bf),
                        pltpu.VMEM((2,) + tok.shape[1:], bf)],
        compiler_params=pltpu.CompilerParams(collective_id=0, has_side_effects=True, vmem_limit_bytes=32*2**20),
        name="gather_weights",
    )(qp, inner, outer, tok, cot, mod)
    return outs


def normalize(values):
    average = jnp.mean(values, -1, keepdims=True)
    centered = values - average
    variance = jnp.mean(centered * centered, -1, keepdims=True)
    inverse = lax.rsqrt(variance + 1e-06)
    return (centered * inverse, inverse)


def norm_back(grad_normed, normed, inverse):
    first = jnp.mean(grad_normed, -1, keepdims=True)
    second = jnp.mean(grad_normed * normed, -1, keepdims=True)
    return inverse * (grad_normed - first - normed * second)


def contract(operand, grad_rows):
    return lax.dot_general(
        operand, grad_rows, (((0, 1), (0, 1)), ((), ())), preferred_element_type=jnp.float32
    )


def split_heads(rows):
    return rows.reshape(rows.shape[0], rows.shape[1], rows.shape[2] // HEAD_DIM, HEAD_DIM)


def score_block(query_rows, key_rows, key_valid):
    scores = jnp.einsum(
        "iqhd,ikhd->ihqk",
        split_heads(query_rows),
        split_heads(key_rows),
        preferred_element_type=jnp.float32,
    )
    scores = scores * HEAD_DIM ** (-0.5)
    return jnp.where(key_valid[:, None, None, :], scores, -1e30)


def attention_forward(query_rows, key_rows, value_rows, key_valid):
    scores = score_block(query_rows, key_rows, key_valid)
    row_top = jnp.max(scores, -1, keepdims=True)
    exponent = jnp.exp(scores - row_top)
    row_total = jnp.sum(exponent, -1, keepdims=True)
    soft_weights = (exponent / row_total).astype(jnp.bfloat16)
    mixed_rows = jnp.einsum(
        "ihqk,ikhd->iqhd", soft_weights, split_heads(value_rows), preferred_element_type=jnp.float32
    )
    return (
        mixed_rows.reshape(query_rows.shape[:2] + (value_rows.shape[2],)).astype(jnp.bfloat16),
        row_top + jnp.log(row_total),
    )


def attention_backward(query_rows, key_rows, value_rows, log_total, grad_mixed, key_valid):
    soft_weights = jnp.exp(score_block(query_rows, key_rows, key_valid) - log_total)
    grad_heads = split_heads(grad_mixed)
    grad_soft = jnp.einsum(
        "iqhd,ikhd->ihqk", grad_heads, split_heads(value_rows), preferred_element_type=jnp.float32
    )
    row_inner = jnp.sum(soft_weights * grad_soft, -1, keepdims=True)
    grad_scores = (soft_weights * (grad_soft - row_inner)).astype(jnp.bfloat16)
    score_scale = HEAD_DIM ** (-0.5)
    grad_query = score_scale * jnp.einsum(
        "ihqk,ikhd->iqhd", grad_scores, split_heads(key_rows), preferred_element_type=jnp.float32
    )
    grad_key = score_scale * jnp.einsum(
        "ihqk,iqhd->ikhd", grad_scores, split_heads(query_rows), preferred_element_type=jnp.float32
    )
    grad_value = jnp.einsum(
        "ihqk,iqhd->ikhd",
        soft_weights.astype(jnp.bfloat16),
        grad_heads,
        preferred_element_type=jnp.float32,
    )
    return (
        grad_query.reshape(query_rows.shape),
        grad_key.reshape(key_rows.shape),
        grad_value.reshape(value_rows.shape),
    )


def pair_perm(dp_count, band_count):
    return [
        (dp * band_count + band, (dp ^ 1) * band_count + band)
        for dp in range(dp_count)
        for band in range(band_count)
    ]


def home_perm_back(dp_count, band_count, turn):
    pairs = []
    for dp in range(dp_count):
        for band in range(band_count):
            to_dp = dp - dp % 2 + band // 2
            to_band = 2 * (dp % 2) + (band + turn) % 2
            pairs.append((dp * band_count + band, to_dp * band_count + to_band))
    return pairs


def send_home(rows, band, perms):
    odd = lax.rem(band, 2) == 1
    first = jnp.where(odd, rows[1], rows[0])
    second = jnp.where(odd, rows[0], rows[1])
    got = [lax.ppermute(part, ("dp", "band"), perm) for part, perm in zip((first, second), perms)]
    return jnp.stack([jnp.where(odd, got[1], got[0]), jnp.where(odd, got[0], got[1])])


def position_rows(row_index, col_index, width):
    quarter = width // 4
    frequency = 10000.0 ** (-jnp.arange(quarter, dtype=jnp.float32) / quarter)
    angles = jnp.arange(128, dtype=jnp.float32)[:, None] * frequency
    table = jnp.concatenate([jnp.sin(angles), jnp.cos(angles)], -1)
    places = jnp.arange(128, dtype=jnp.int32)
    pick = lambda index: jnp.dot(
        (index[:, None] == places).astype(jnp.float32), table, precision=lax.Precision.HIGHEST
    )
    return jnp.concatenate([pick(row_index), pick(col_index)], -1)


def rows_dot(left, right):
    return lax.dot_general(left, right, (((0,), (0,)), ((), ())), preferred_element_type=jnp.float32)


def back_dot(left, right):
    return lax.dot_general(left, right, (((1,), (1,)), ((), ())), preferred_element_type=jnp.float32)


def own_piece(vector, count, band_place):
    return lax.dynamic_slice_in_dim(vector, band_place * count, count, 0)


def body(
    tokens,
    condition,
    patch_grid,
    ada_weight,
    ada_bias,
    qkv_weight,
    query_bias,
    value_bias,
    proj_weight,
    proj_bias,
    inner_weight,
    inner_bias,
    outer_weight,
    outer_bias,
    cotangent,
):
    both = ("dp", "band")
    dp_count = lax.axis_size("dp")
    band_count = lax.axis_size("band")
    images, band_slots, width = tokens.shape
    band = lax.axis_index("band")
    dp = lax.axis_index("dp")
    core = lax.rem(dp, 2)
    hidden = inner_weight.shape[1]
    part_rows = qkv_weight.shape[0]
    siblings = pair_perm(dp_count, band_count)
    homes = [home_perm_back(dp_count, band_count, turn) for turn in range(2)]

    condition_f = condition.astype(jnp.float32)
    activated = jax.nn.silu(condition_f).astype(jnp.bfloat16)
    own_activated = lax.dynamic_slice_in_dim(activated, band * part_rows, part_rows, 1)
    share = jnp.dot(own_activated, ada_weight, preferred_element_type=jnp.float32)
    share = share + lax.dynamic_update_slice_in_dim(
        jnp.zeros((ada_weight.shape[1],), jnp.float32),
        ada_bias.astype(jnp.float32),
        band * ada_bias.shape[0],
        0,
    )
    biases = jnp.concatenate([query_bias, value_bias, proj_bias, inner_bias, outer_bias])
    bias_count = biases.shape[0]
    mod_count = share.shape[1]
    note = jnp.concatenate(
        [
            share,
            jnp.broadcast_to(biases.astype(jnp.float32), (images, bias_count)),
            patch_grid.astype(jnp.float32),
        ],
        1,
    )
    note_rows = -(-note.shape[1] // 1024) * 8
    note = jnp.pad(note, ((0, 0), (0, note_rows * 128 - note.shape[1])))
    note = note.reshape(images, note_rows, 128)
    first_weight = jnp.concatenate([qkv_weight, proj_weight], 1)
    first_full, inner_full, outer_full, tokens_here, cotangent_here, notes = gather_weights(
        first_weight, inner_weight, outer_weight, tokens, cotangent, note, width
    )
    first_full = first_full.reshape(width, -1)
    inner_full = inner_full.reshape(width, hidden)
    outer_full = outer_full.reshape(hidden, width)
    qkv_full = first_full[:, : 3 * width]
    proj_full = first_full[:, 3 * width :]
    notes = notes.reshape(band_count, -1)
    modulation = jnp.sum(notes[:, :mod_count], 0)
    pieces = []
    at = mod_count
    for piece in (query_bias, value_bias, proj_bias, inner_bias, outer_bias):
        pieces.append(notes[:, at : at + piece.shape[0]].reshape(-1))
        at += piece.shape[0]
    query_bias_full, value_bias_full, proj_bias_full, inner_bias_full, outer_bias_full = pieces
    grid_rows = notes[0, at].astype(jnp.int32)
    grid_cols = notes[0, at + 1].astype(jnp.int32)

    rows = images * band_slots
    ids = core * rows + jnp.arange(rows, dtype=jnp.int32)
    within = ids % band_slots
    band_rows = grid_rows // band_count
    is_valid = within < band_rows * grid_cols
    row_index = ids // band_slots * band_rows + within // grid_cols
    col_index = within % grid_cols
    key_valid = jnp.concatenate([is_valid, is_valid])

    shift_one, scale_one, gate_one, shift_two, scale_two, gate_two = [
        modulation[index * width : (index + 1) * width] for index in range(6)
    ]
    residual = tokens_here.reshape(rows, width).astype(jnp.float32) + position_rows(
        row_index, col_index, width
    )
    normed_one, inverse_one = normalize(residual)
    attn_in = (normed_one * (1.0 + scale_one) + shift_one).astype(jnp.bfloat16)
    projected = jnp.dot(attn_in, qkv_full, preferred_element_type=jnp.float32)
    query_rows = (projected[:, :width] + query_bias_full).astype(jnp.bfloat16)
    key_value = (
        projected[:, width:] + jnp.concatenate([jnp.zeros((width,), jnp.float32), value_bias_full])
    ).astype(jnp.bfloat16)
    other_key_value = lax.ppermute(key_value, both, siblings)
    keys = jnp.concatenate([key_value[:, :width], other_key_value[:, :width]])
    values = jnp.concatenate([key_value[:, width:], other_key_value[:, width:]])
    mixed_rows, band_total = attention_forward(
        query_rows[None], keys[None], values[None], key_valid[None]
    )
    mixed_rows = mixed_rows[0]
    attended = jnp.dot(mixed_rows, proj_full, preferred_element_type=jnp.float32) + proj_bias_full
    middle = residual + gate_one * attended
    normed_two, inverse_two = normalize(middle)
    mlp_in = (normed_two * (1.0 + scale_two) + shift_two).astype(jnp.bfloat16)
    hidden_pre = jnp.dot(mlp_in, inner_full, preferred_element_type=jnp.float32) + inner_bias_full
    hidden_act = jax.nn.gelu(hidden_pre, approximate=True).astype(jnp.bfloat16)
    mlp_out = jnp.dot(hidden_act, outer_full, preferred_element_type=jnp.float32) + outer_bias_full
    block_out = (middle + gate_two * mlp_out).astype(jnp.bfloat16)
    block_home = send_home(block_out.reshape(images, band_slots, width), band, homes)

    grad_out = cotangent_here.reshape(rows, width).astype(jnp.float32) * is_valid[:, None].astype(
        jnp.float32
    )
    grad_gate_two = jnp.sum(grad_out * mlp_out, 0)
    grad_mlp = (gate_two * grad_out).astype(jnp.bfloat16)
    gelu_back = jax.vjp(partial(jax.nn.gelu, approximate=True), hidden_pre)[1]
    grad_outer = rows_dot(hidden_act, grad_mlp).astype(jnp.bfloat16)
    grad_outer_bias = jnp.sum(grad_mlp.astype(jnp.float32), 0)
    grad_hidden = back_dot(grad_mlp, outer_full)
    grad_pre = gelu_back(grad_hidden)[0].astype(jnp.bfloat16)
    grad_inner = rows_dot(mlp_in, grad_pre).astype(jnp.bfloat16)
    grad_inner_bias = jnp.sum(grad_pre.astype(jnp.float32), 0)
    grad_mlp_in = back_dot(grad_pre, inner_full)
    grad_shift_two = jnp.sum(grad_mlp_in, 0)
    grad_scale_two = jnp.sum(grad_mlp_in * normed_two, 0)
    grad_middle = grad_out + norm_back(grad_mlp_in * (1.0 + scale_two), normed_two, inverse_two)
    grad_gate_one = jnp.sum(grad_middle * attended, 0)
    grad_attended = (gate_one * grad_middle).astype(jnp.bfloat16)
    grad_proj = rows_dot(mixed_rows, grad_attended).astype(jnp.bfloat16)
    grad_proj_bias = jnp.sum(grad_attended.astype(jnp.float32), 0)
    grad_mixed = back_dot(grad_attended, proj_full).astype(jnp.bfloat16)
    band_dq, key_terms, value_terms = attention_backward(
        query_rows[None], keys[None], values[None], band_total, grad_mixed[None], key_valid[None]
    )
    terms = jnp.concatenate([key_terms[0], value_terms[0]], -1)
    other_terms = lax.ppermute(terms[rows:].astype(jnp.bfloat16), both, siblings)
    grad_key_value = (terms[:rows] + other_terms.astype(jnp.float32)).astype(jnp.bfloat16)
    grad_query = band_dq[0].astype(jnp.bfloat16)
    grad_qkv = jnp.concatenate([grad_query, grad_key_value], -1)
    grad_qkv_weight = rows_dot(attn_in, grad_qkv).astype(jnp.bfloat16)
    grad_attn_in = back_dot(grad_qkv, qkv_full)
    grad_query_bias = jnp.sum(grad_query.astype(jnp.float32), 0)
    grad_value_bias = jnp.sum(grad_key_value[:, width:].astype(jnp.float32), 0)
    grad_shift_one = jnp.sum(grad_attn_in, 0)
    grad_scale_one = jnp.sum(grad_attn_in * normed_one, 0)
    grad_tokens = grad_middle + norm_back(grad_attn_in * (1.0 + scale_one), normed_one, inverse_one)
    tokens_home = send_home(
        grad_tokens.astype(jnp.bfloat16).reshape(images, band_slots, width), band, homes
    ).astype(jnp.float32)

    part_mod = jnp.concatenate(
        [grad_shift_one, grad_scale_one, grad_gate_one, grad_shift_two, grad_scale_two, grad_gate_two]
    )
    grad_mod = (part_mod + lax.ppermute(part_mod, both, siblings)).astype(jnp.bfloat16)
    every_mod = lax.all_gather(grad_mod, both, axis=0).reshape(dp_count // 2, 2, band_count, -1)
    every_mod = every_mod[:, 0].reshape(dp_count * images, -1)
    every_activated = lax.all_gather(own_activated, "dp", axis=0, tiled=True)
    grad_ada = rows_dot(every_activated, every_mod)
    grad_ada_bias = own_piece(jnp.sum(every_mod.astype(jnp.float32), 0), ada_bias.shape[0], band)
    own_mod = lax.dynamic_slice_in_dim(every_mod, images * dp, images, 0)
    grad_act = lax.all_gather(back_dot(own_mod, ada_weight), "band", axis=1, tiled=True)
    grad_condition = jax.vjp(jax.nn.silu, condition_f)[1](grad_act)[0]

    def total(piece):
        scattered = lax.psum_scatter(piece, ("band", "dp"), scatter_dimension=0, tiled=True)
        return lax.all_gather(scattered, "dp", axis=0, tiled=True).astype(jnp.float32)

    bias_grads = lax.psum(
        jnp.concatenate(
            [grad_query_bias, grad_value_bias, grad_proj_bias, grad_inner_bias, grad_outer_bias]
        ),
        both,
    )
    bias_parts = []
    at = 0
    for piece in (query_bias, value_bias, proj_bias, inner_bias, outer_bias):
        whole = piece.shape[0] * band_count
        bias_parts.append(own_piece(bias_grads[at : at + whole], piece.shape[0], band))
        at += whole
    return (
        block_home,
        tokens_home,
        grad_condition,
        grad_ada,
        grad_ada_bias,
        total(grad_qkv_weight),
        bias_parts[0],
        bias_parts[1],
        total(grad_proj),
        bias_parts[2],
        total(grad_inner),
        bias_parts[3],
        total(grad_outer),
        bias_parts[4],
    )


def solution(mesh):
    placed = (
        P("dp", "band", None),
        P("dp", None),
        P("dp", None),
        P("band", None),
        P("band"),
        P("band", None),
        P("band"),
        P("band"),
        P("band", None),
        P("band"),
        P("band", None),
        P("band"),
        P("band", None),
        P("band"),
        P("dp", "band", None),
    )
    return jax.shard_map(
        body,
        mesh=mesh,
        in_specs=placed,
        out_specs=(
            P("dp", "band", None),
            P("dp", "band", None),
            P("dp", None),
            P("band", None),
            P("band"),
            P("band", None),
            P("band"),
            P("band"),
            P("band", None),
            P("band"),
            P("band", None),
            P("band"),
            P("band", None),
            P("band"),
        ),
        check_vma=False,
    )
```

time: 2060 us -> 1240 us (0.60)
  waiting for transfers between devices: 1600 us -> 34.8 us
  blocking collectives: 68.6 us -> 430 us
  Pallas kernels: 0 us -> 171 us
  starting transfers between devices: 0.82 us -> 96.9 us
  local copies, waits for them, and re-layouts: 49.4 us -> 129 us
    all_gather x7 -> x3, waiting for transfers between devices: 882 us -> 0.01 us  [total(): lax.all_gather(scattered, 'dp', axis=0, tiled=True).astype(jnp.float32)]
    reduce_scatter x6 -> x1, waiting for transfers between devices: 563 us -> 0.02 us  [total(): lax.psum_scatter(piece, ('band', 'dp'), scatter_dimension=0, tiled=True)]
    unnamed x1, blocking collectives: 16.4 us -> 282 us
    pallas_call x0 -> x1, Pallas kernels: none -> 171 us  [gather_weights(): pl.pallas_call(functools.partial(gather_kernel, width), out_shape=[jax.Sh...]
    psum x1 -> x0, waiting for transfers between devices: 147 us -> none  [total_over_images(): lax.psum(ada_part.astype(jnp.bfloat16), 'dp').astype(jnp.float32)]
    all_gather x1 -> x4, blocking collectives: 10.5 us -> 107 us  [the longest x1 70.2 us: body(): lax.all_gather(grad_mod, both, axis=0)]
    unnamed x0 -> x20, starting transfers between devices: none -> 75.5 us
    unnamed x144 -> x185, local copies, waits for them, and re-layouts: 10.6 us -> 72.9 us
  transfers between devices with their start and end apart: 14 -> 31, of which waited for: 12 -> 5; matrix products, arithmetic and copies ran while one was open for 13% -> 49% of each run, Pallas kernels for 0% -> 0%
where the time goes in v1:
time: 1240 us; the launch traced here: 1220 us
  blocking collectives  430 us (35%)
  matrix products  231 us (19%)
  Pallas kernels  171 us (14%)
  local copies, waits for them, and re-layouts  129 us (10%)
  other arithmetic  104 us (8%)
  starting transfers between devices  96.9 us (8%)
  waiting for transfers between devices  34.8 us (3%)
  between operations  20.1 us (2%)
    unnamed x1, blocking collectives  282 us
    pallas_call x1, Pallas kernels, gather_weights(): pl.pallas_call(functools.partial(gather_kernel, width), out_shape=[jax.Sh...  171 us
    unnamed x20, starting transfers between devices  75.5 us
    unnamed x185, local copies, waits for them, and re-layouts  72.9 us
    all_gather x1, blocking collectives, body(): lax.all_gather(grad_mod, both, axis=0)  70.2 us
    dot_general x5, matrix products, back_dot(): lax.dot_general(left, right, (((1,), (1,)), ((), ())), preferred_element_...  48 us
    psum x1, blocking collectives, body(): lax.psum(jnp.concatenate([grad_query_bias, grad_value_bias, grad_proj_bia...  40.1 us
    dot_general x5, matrix products, rows_dot(): lax.dot_general(left, right, (((0,), (0,)), ((), ())), preferred_element_...  39.9 us
  transfers between devices with their start and end apart: 31, of which 5 were waited for; matrix products, arithmetic and copies ran while one was open for 49% of the time, Pallas kernels for 0%

profile of v1, /device:TPU:1, one launch (start us, length us, event | category | flops | bytes accessed | tf_op | source)
XLA Modules:
  0.0 1215.6 jit_solution(8971417102134573569)
XLA Ops:
  20.6 170.8 %gather_weights.1 = (bf16[4,2,144,4608]{3,2,1,0:T(8,128)(2,1)}, bf16[4,2,144,4608]{3,2,1,0:T(8,128)(2,1)}, bf16[4,4,2,144,1152]{4,3,2,1,0:T(8,128)(2,1)}, bf16[2...) custom-call(bf16[2,144,4608]{2,1,0:T(8,128)(2,1)S(1)} %bitcast.116, ...), custom_call_target="tpu_custom_call" | custom-call | tf_op jit(solution)/shard_map/gather_weights/pallas_call | solution.py:166
  217.4 7.8 fusion.19
  252.0 4.1 pad_maximum_fusion.3
  256.1 4.3 copy.69
  260.4 14.2 %fusion.9 = (f32[16,512]{1,0:T(8,128)S(1)}, f32[16,512,1024]{2,1,0:T(8,128)}) fusion(pred[1024]{0:T(1024)(128)(4,1)} %pad_add_fusion, bf16[512,16,72]{0,2,1:T(8,128)(2,1)S(1)} %bitcast.129, bf16[1024,16,72]{0,2,1:T(8,128)(2,1)S(1)} %bitcast.127), kind=kOutput, calls=%fused_computation.14 | convolution fusion | flops 1233117184 | bytes 37127168 | tf_op jit(solution)/shard_map/iqhd,ikhd->ihqk/dot_general | solution.py:209
  274.6 14.9 %fusion.3 = f32[16,512]{1,0:T(8,128)S(1)} fusion(f32[16,512]{1,0:T(8,128)S(1)} %get-tuple-element.127, f32[16,512,1024]{2,1,0:T(8,128)} %get-tuple-element.128, pred[1024]{0:T(1024)(128)(4,1)S(1)} %copy-done.43), kind=kLoop, calls=%fused_computation.6 | loop fusion | flops 33546240 | bytes 33620992 | tf_op jit(solution)/shard_map/reduce_sum | solution.py:223
  290.0 14.5 %fusion.29 = bf16[16,72,512]{2,1,0:T(8,128)(2,1)S(1)} fusion(bf16[1024,16,72]{0,2,1:T(8,128)(2,1)S(1)} %bitcast.133, f32[16,512]{1,0:T(8,128)S(1)} %fusion.3, f32[16,512]{1,0:T(8,128)S(1)} %get-tuple-element.127, f32[16,512,1024]{2,1,0:T(8,128)} %get-tuple-element.128, pred[1024]{0:T(1024)(128)(4,1)S(1)} %copy-done.43), kind=kOutput, calls=%fused_computation.81 | convolution fusion | flops 1250492416 | bytes 37159936 | tf_op jit(solution)/shard_map/ihqk,ikhd->iqhd/dot_general | solution.py:225
  304.6 5.6 fusion.64
  310.6 9.2 fusion.60
  319.9 14.2 %convolution_convert_fusion = bf16[4608,1152]{1,0:T(8,128)(2,1)} fusion(f32[512,1152]{0,1:T(8,128)S(1)} %copy-done.23, f32[512]{0:T(512)S(1)} %copy-done.66, f32[1152]{0:T(1024)S(1)} %copy-done.46, f32[512,4608]{1,0:T(8,128)} %fusion.60, f32[4608]{0:T(1024)S(1)} %copy-done.52), kind=kOutput, calls=%fused_computation.8 | convolution fusion | flops 5466488832 | bytes 22438400 | tf_op jit(solution)/shard_map/dot_general | solution.py:301
  335.3 16.0 %convert_reduce_fusion = (f32[4608]{0:T(1024)}, bf16[512,4608]{1,0:T(8,128)(2,1)S(1)}) fusion(f32[512,4608]{1,0:T(8,128)} %fusion.60, f32[4608]{0:T(1024)} %add.277, bf16[512,1152]{1,0:T(8,128)(2,1)S(1)} %bitcast.147, bf16[4608,1152]{1,0:T(8,128)(2,1)} %bitcast.165), kind=kOutput, calls=%fused_computation.26 | convolution fusion | flops 5490077184 | bytes 25989120 | tf_op jit(solution)/shard_map/dot_general | solution.py:305
  351.3 13.1 %fusion.72 = (f32[1152]{0:T(1024)}, f32[512,1152]{1,0:T(8,128)}) fusion(bf16[512,4608]{1,0:T(8,128)(2,1)S(1)} %get-tuple-element.83, bf16[1152,4608]{1,0:T(8,128)(2,1)} %bitcast.139), kind=kOutput, calls=%fused_computation.193 | convolution fusion | flops 5436406784 | bytes 17699328 | tf_op jit(solution)/shard_map/dot_general | solution.py:305
  371.2 19.4 %convert_reduce_fusion.2 = (f32[1152]{0:T(1024)}, bf16[512,1152]{0,1:T(8,128)(2,1)}, f32[512,1152]{0,1:T(8,128)}, f32[1152]{0:T(1024)}, bf16[512,1152]{0,1:T(8,128)(2,1)}) fusion(f32[1152]{0:T(1024)S(1)} %copy-done.60, f32[512]{0:T(512)S(1)} %broadcast_multiply_fusion.3, f32[512,1152]{0,1:T(8,128)S(1)} %get-tuple-element.90, f32[512]{0:T(512)S(1)} %copy-done.38, ...), kind=kOutput, calls=%fused_computation.54 | convolution fusion | flops 5470615552 | bytes 31906816 | tf_op jit(solution)/shard_map/dot_general | solution.py:420
  390.6 5.0 convolution_convert_fusion.4
  397.6 24.5 %multiply_reduce_fusion = (f32[16,512]{1,0:T(8,128)}, f32[16,512,1024]{2,1,0:T(8,128)}) fusion(f32[16,512]{1,0:T(8,128)} %log_add_fusion, f32[16,512,1024]{2,1,0:T(8,128)} %get-tuple-element.128, pred[1024]{0:T(1024)(128)(4,1)} %pad_add_fusion, bf16[512,16,72]{0,2,1:T(8,128)(2,1)S(1)} %bitcast.143, bf16[1024,16,72]{0,2,1:T(8,128)(2,1)S(1)} %bitcast.134), kind=kOutput, calls=%fused_computation.1 | convolution fusion | flops 1249894400 | bytes 70714368 | tf_op jit(solution)/shard_map/iqhd,ikhd->ihqk/dot_general | solution.py:237
  422.1 29.0 %multiply_convert_fusion = bf16[16,512,1024]{2,1,0:T(8,128)(2,1)} fusion(f32[16,512,1024]{2,1,0:T(8,128)} %get-tuple-element.131, f32[16,512]{1,0:T(8,128)} %get-tuple-element.130, f32[16,512]{1,0:T(8,128)} %log_add_fusion, f32[16,512,1024]{2,1,0:T(8,128)} %get-tuple-element.128, pred[1024]{0:T(1024)(128)(4,1)} %pad_add_fusion), kind=kLoop, calls=%fused_computation | loop fusion | flops 50331648 | bytes 83952640 | tf_op jit(solution)/shard_map/convert_element_type | solution.py:241
  451.2 8.9 broadcast_multiply_fusion
  460.1 18.9 %fusion.5 = f32[16,72,1024]{2,1,0:T(8,128)} fusion(bf16[512,16,72]{0,2,1:T(8,128)(2,1)} %bitcast.144, f32[16,512]{1,0:T(8,128)S(1)} %copy-done.28, f32[16,512,1024]{2,1,0:T(8,128)} %get-tuple-element.128, pred[1024]{0:T(1024)(128)(4,1)S(1)} %copy-done.44), kind=kOutput, calls=%fused_computation.10 | convolution fusion | flops 1241513984 | bytes 39486464 | tf_op jit(solution)/shard_map/ihqk,iqhd->ikhd/dot_general | solution.py:249
  486.6 12.1 convert_reduce_fusion.4
  498.7 11.0 convolution_convert_fusion.1
  514.6 7.0 convolution_convert_fusion.2
  521.7 282.4 %fusion.61 = (bf16[48,3456]{1,0:T(8,128)(2,1)S(1)}, bf16[48,1152]{1,0:T(8,128)(2,1)S(1)}, bf16[40,4608]{1,0:T(8,128)(2,1)S(1)}) fusion(bf16[1152,3456]{1,0:T(8,128)(2,1)} %convolution_convert_fusion.2, bf16[1152,1152]{1,0:T(8,128)(2,1)} %convolution_convert_fusion.3, bf16[1152,4608]{1,0:T(8,128)(2,1)} %convolution_convert_fusion.1), kind=kCustom, calls=%all-reduce-scatter.3 | all-reduce-scatter fusion | flops 12976130 | bytes 22045184
  807.2 6.5 collective-permute-start.14
  821.9 10.7 collective-permute-start.8
  838.8 9.1 collective-permute-done.9
  847.9 34.7 %concatenate.63 = bf16[420,3456]{1,0:T(8,128)(2,1)} concatenate(bf16[36,3456]{1,0:T(8,128)(2,1)} %copy-done.32, bf16[48,3456]{1,0:T(8,128)(2,1)} %collective-permute-done.13, bf16[48,3456]{1,0:T(8,128)(2,1)} %collective-permute-done.12, bf16[48,3456]{1,0:T(8,128)(2,1)} %copy-done.31, bf16[48,3456]{1,0:T(8,128)(2,1)} %copy-done.30, bf16[48,3456]{1,0:T(8,128)(2,1)} %collective-permute-done.9, ...), dimensions={0} | concatenate | bytes 5806080
  886.4 6.4 collective-permute-start.24
  892.8 5.4 collective-permute-start.25
  898.2 4.0 collective-permute-start.26
  902.9 10.9 collective-permute-done.26
  913.8 16.3 %concatenate.65 = bf16[164,4608]{1,0:T(8,128)(2,1)} concatenate(bf16[4,4608]{1,0:T(4,128)(2,1)S(1)} %collective-permute-done.26, bf16[40,4608]{1,0:T(8,128)(2,1)} %collective-permute-done.25, bf16[40,4608]{1,0:T(8,128)(2,1)} %collective-permute-done.24, bf16[40,4608]{1,0:T(8,128)(2,1)S(1)} %collective-permute-done.23, bf16[40,4608]{1,0:T(8,128)(2,1)S(1)} %get-tuple-element.79), dimensions={0} | concatenate | bytes 3022848
  936.9 8.0 collective-permute-start.2
  944.9 11.7 all-gather.3
  956.7 8.1 collective-permute-done.2
  971.6 8.1 collective-permute-start.16
  982.1 4.0 collective-permute-start.18
  986.1 10.7 fusion.71
  1008.6 40.1 %psum.7 = f32[9216]{0:T(1024)S(1)} all-reduce(f32[9216]{0:T(1024)S(1)} %constant_dynamic-update-slice_fusion.10), channel_id=1, replica_groups=mesh['dp'=8,'band'=4] {'dp','band'}, use_global_device_ids=true, to_apply=%region_25.26 | all-reduce | flops 9216 | bytes 73728 | tf_op jit(solution)/shard_map/psum | solution.py:481
  1054.0 70.2 %all-gather.1 = bf16[32,1,6912]{2,1,0:T(2,128)(2,1)S(1)} all-gather(bf16[1,1,6912]{2,1,0:T(2,128)(2,1)S(1)} %reshape.353), channel_id=2, replica_groups=mesh['dp'=8,'band'=4] {'dp','band'}, dimensions={0}, use_global_device_ids=true | all-gather | bytes 456192 | tf_op jit(solution)/shard_map/all_gather | solution.py:468
  1130.3 10.2 all-gather.2
  1141.9 7.5 collective-permute-start.4
  1151.9 4.5 fusion.73
  1157.7 6.6 collective-permute-start.20
  1170.0 4.6 concatenate.64
  1174.7 15.0 %all-gather.5 = bf16[8,36,1152]{2,1,0:T(8,128)(2,1)S(1)} all-gather(bf16[1,36,1152]{2,1,0:T(8,128)(2,1)S(1)} %dynamic-slice_bitcast_fusion.2), channel_id=1, replica_groups=mesh['dp'=8,'band'=4] {'dp'}, dimensions={0}, use_global_device_ids=true | all-gather | bytes 746496 | tf_op jit(solution)/shard_map/all_gather | solution.py:479
  1194.1 4.2 reshape.365
  1198.3 4.8 reshape.367
  1203.1 4.5 convert_element_type.261
  (331 shorter events, 161.9 us)
Async XLA Ops:
  8.0 998.7 %reduce-scatter.8.cloned.1.call-start = ((), (), s32[]{:S(2)}) async-start(), calls=%async_computation.1 | async-start | bytes 10948608 | tf_op jit(solution)/shard_map/reduce_scatter | solution.py:478
  215.2 95.3 %copy-start.34 = (f32[1152]{0:T(1024)}, f32[1152]{0:T(1024)S(1)}, u32[]{:S(2)}) copy-start(f32[1152]{0:T(1024)S(1)} %get-tuple-element.118) | copy-start | bytes 13828
  228.8 16.0 %collective-permute-start = (bf16[512,2304]{1,0:T(8,128)(2,1)}, bf16[512,2304]{1,0:T(8,128)(2,1)}, u32[]{:S(2)}, u32[]{:S(2)}) collective-permute-start(bf16[512,2304]{1,0:T(8,128)(2,1)} %fusion.25), channel_id=1, source_target_pairs={{0,4},{1,5},{2,6},{3,7},{4,0},{5,1},{6,2},{7,3},{8,12},{9,13},{10,... | collective-permute-start | bytes 7077896 | tf_op jit(solution)/shard_map/ppermute | solution.py:407
  233.5 26.9 %copy-start.12 = (bf16[512,1152]{0,1:T(8,128)(2,1)}, bf16[512,1152]{0,1:T(8,128)(2,1)S(1)}, u32[]{:S(2)}) copy-start(bf16[512,1152]{0,1:T(8,128)(2,1)S(1)} %copy.70) | copy-start | bytes 3538948
  260.4 14.2 %copy-start.43 = (pred[1024]{0:T(1024)(128)(4,1)S(1)}, pred[1024]{0:T(1024)(128)(4,1)}, u32[]{:S(2)}) copy-start(pred[1024]{0:T(1024)(128)(4,1)} %pad_add_fusion) | copy-start | bytes 3076
  274.5 15.5 %copy-start.14 = (bf16[1024,1152]{0,1:T(8,128)(2,1)S(1)}, bf16[1024,1152]{0,1:T(8,128)(2,1)}, u32[]{:S(2)}) copy-start(bf16[1024,1152]{0,1:T(8,128)(2,1)} %copy.69) | copy-start | bytes 7077892
  290.0 14.5 %copy-start.9 = (f32[512,1152]{0,1:T(8,128)S(1)}, f32[512,1152]{0,1:T(8,128)}, u32[]{:S(2)}) copy-start(f32[512,1152]{0,1:T(8,128)} %copy-done.8) | copy-start | bytes 7077892
  290.0 14.5 %copy-start.59 = (f32[1152]{0:T(1024)S(1)}, f32[1152]{0:T(1024)}, u32[]{:S(2)}) copy-start(f32[1152]{0:T(1024)} %get-tuple-element.122) | copy-start | bytes 13828
  290.0 14.5 %copy-start.62 = (f32[1152]{0:T(1024)S(1)}, f32[1152]{0:T(1024)}, u32[]{:S(2)}) copy-start(f32[1152]{0:T(1024)} %add.269) | copy-start | bytes 13828
  310.2 61.0 %copy-start.7 = (f32[512,1152]{0,1:T(8,128)}, f32[512,1152]{0,1:T(8,128)S(1)}, u32[]{:S(2)}) copy-start(f32[512,1152]{0,1:T(8,128)S(1)} %get-tuple-element.90) | copy-start | bytes 7077892
  334.1 860.1 %all-gather.13.cloned.1.call-start = ((), (), s32[]{:S(2)}) async-start(), calls=%async_computation.3 | async-start | bytes 2488320 | tf_op jit(solution)/shard_map/all_gather | solution.py:479
  397.3 24.8 %copy-start.19 = (bf16[512,1152]{0,1:T(8,128)(2,1)}, bf16[512,1152]{0,1:T(8,128)(2,1)S(1)}, u32[]{:S(2)}) copy-start(bf16[512,1152]{0,1:T(8,128)(2,1)S(1)} %copy.76) | copy-start | bytes 3538948
  422.1 29.0 %copy-start.13 = (bf16[512,1152]{0,1:T(8,128)(2,1)S(1)}, bf16[512,1152]{0,1:T(8,128)(2,1)}, u32[]{:S(2)}) copy-start(bf16[512,1152]{0,1:T(8,128)(2,1)} %copy-done.12) | copy-start | bytes 3538948
  460.1 18.9 %copy-start.4 = (f32[16,72,1024]{2,1,0:T(8,128)}, f32[16,72,1024]{2,1,0:T(8,128)S(1)}, u32[]{:S(2)}) copy-start(f32[16,72,1024]{2,1,0:T(8,128)S(1)} %broadcast_multiply_fusion) | copy-start | bytes 14155780
  482.7 27.1 %collective-permute-start.3 = (bf16[512,2304]{0,1:T(8,128)(2,1)}, bf16[512,2304]{0,1:T(8,128)(2,1)}, u32[]{:S(2)}, u32[]{:S(2)}) collective-permute-start(bf16[512,2304]{0,1:T(8,128)(2,1)} %fusion.24), channel_id=1, source_target_pairs={{0,4},{1,5},{2,6},{3,7},{4,0},{5,1},{6,2},{7,3},{8,12},{9,13},{10,... | collective-permute-start | bytes 7077896 | tf_op jit(solution)/shard_map/ppermute | solution.py:449
  486.6 23.2 %slice-start = ((s8[4718592]{0:T(1024)(128)(4,1)}), s8[524288]{0:T(1024)(128)(4,1)S(1)}, s32[]{:S(2)}) async-start(s8[4718592]{0:T(1024)(128)(4,1)} %bitcast.124), calls=%async_computation.5 | async-start | bytes 1048576
  521.7 313.0 %copy-start.68 = (u32[32]{0:T(128)S(1)}, u32[32]{0:T(128)}, u32[]{:S(2)}) copy-start(u32[32]{0:T(128)} %constant.144) | copy-start | bytes 388
  804.1 17.7 %collective-permute-start.10 = (bf16[48,3456]{1,0:T(8,128)(2,1)S(1)}, bf16[48,3456]{1,0:T(8,128)(2,1)S(1)}, u32[]{:S(2)}, u32[]{:S(2)}) collective-permute-start(bf16[48,3456]{1,0:T(8,128)(2,1)S(1)} %get-tuple-element.77), channel_id=1, source_target_pairs={{0,16},{4,20},{8,24},{12,28},{16,1},{20,5},{24,9},{28,13},{1,17},{... | collective-permute-start | bytes 995336
  805.4 27.2 %collective-permute-start.11 = (bf16[48,3456]{1,0:T(8,128)(2,1)S(1)}, bf16[48,3456]{1,0:T(8,128)(2,1)S(1)}, u32[]{:S(2)}, u32[]{:S(2)}) collective-permute-start(bf16[48,3456]{1,0:T(8,128)(2,1)S(1)} %get-tuple-element.77), channel_id=1, source_target_pairs={{0,20},{4,24},{8,28},{12,1},{16,5},{20,9},{24,13},{28,17},{1,21},{... | collective-permute-start | bytes 995336
  807.2 11.6 collective-permute-start.14
  813.7 22.2 %collective-permute-start.12 = (bf16[48,3456]{1,0:T(8,128)(2,1)S(1)}, bf16[48,3456]{1,0:T(8,128)(2,1)}, u32[]{:S(2)}, u32[]{:S(2)}) collective-permute-start(bf16[48,3456]{1,0:T(8,128)(2,1)S(1)} %get-tuple-element.77), channel_id=1, source_target_pairs={{0,24},{4,28},{8,1},{12,5},{16,9},{20,13},{24,17},{28,21},{1,25},{... | collective-permute-start | bytes 995336
  815.7 20.1 %collective-permute-start.13 = (bf16[48,3456]{1,0:T(8,128)(2,1)S(1)}, bf16[48,3456]{1,0:T(8,128)(2,1)}, u32[]{:S(2)}, u32[]{:S(2)}) collective-permute-start(bf16[48,3456]{1,0:T(8,128)(2,1)S(1)} %get-tuple-element.77), channel_id=1, source_target_pairs={{0,28},{4,1},{8,5},{12,9},{16,13},{20,17},{24,21},{28,25},{1,29},{... | collective-permute-start | bytes 995336
  818.8 15.8 %copy-start.32 = (bf16[36,3456]{1,0:T(8,128)(2,1)}, bf16[36,3456]{1,0:T(8,128)(2,1)S(1)}, u32[]{:S(2)}) copy-start(bf16[36,3456]{1,0:T(8,128)(2,1)S(1)} %collective-permute-done.14) | copy-start | bytes 746500
  818.8 17.1 %collective-permute-start.7 = (bf16[48,3456]{1,0:T(8,128)(2,1)S(1)}, bf16[48,3456]{1,0:T(8,128)(2,1)}, u32[]{:S(2)}, u32[]{:S(2)}) collective-permute-start(bf16[48,3456]{1,0:T(8,128)(2,1)S(1)} %get-tuple-element.77), channel_id=1, source_target_pairs={{0,4},{4,8},{8,12},{12,16},{16,20},{20,24},{24,28},{28,1},{1,5},{5... | collective-permute-start | bytes 995336
  821.9 16.9 %collective-permute-start.8 = (bf16[48,3456]{1,0:T(8,128)(2,1)S(1)}, bf16[48,3456]{1,0:T(8,128)(2,1)}, u32[]{:S(2)}, u32[]{:S(2)}) collective-permute-start(bf16[48,3456]{1,0:T(8,128)(2,1)S(1)} %get-tuple-element.77), channel_id=1, source_target_pairs={{0,8},{4,12},{8,16},{12,20},{16,24},{20,28},{24,1},{28,5},{1,9},{5... | collective-permute-start | bytes 995336
  832.6 15.3 %collective-permute-start.9 = (bf16[48,3456]{1,0:T(8,128)(2,1)S(1)}, bf16[48,3456]{1,0:T(8,128)(2,1)}, u32[]{:S(2)}, u32[]{:S(2)}) collective-permute-start(bf16[48,3456]{1,0:T(8,128)(2,1)S(1)} %get-tuple-element.77), channel_id=1, source_target_pairs={{0,12},{4,16},{8,20},{12,24},{16,28},{20,1},{24,5},{28,9},{1,13},{... | collective-permute-start | bytes 995336
  884.4 314.0 %all-gather.15.cloned.1.call-start = ((), (), s32[]{:S(2)}) async-start(), calls=%async_computation.4 | async-start | bytes 3317760 | tf_op jit(solution)/shard_map/all_gather | solution.py:479
  884.4 29.4 %collective-permute-start.23 = (bf16[40,4608]{1,0:T(8,128)(2,1)S(1)}, bf16[40,4608]{1,0:T(8,128)(2,1)S(1)}, u32[]{:S(2)}, u32[]{:S(2)}) collective-permute-start(bf16[40,4608]{1,0:T(8,128)(2,1)S(1)} %get-tuple-element.79), channel_id=1, source_target_pairs={{0,4},{4,8},{8,12},{12,16},{16,20},{20,24},{24,28},{28,1},{1,5},{5... | collective-permute-start | bytes 1105928
  886.4 27.5 %collective-permute-start.24 = (bf16[40,4608]{1,0:T(8,128)(2,1)S(1)}, bf16[40,4608]{1,0:T(8,128)(2,1)}, u32[]{:S(2)}, u32[]{:S(2)}) collective-permute-start(bf16[40,4608]{1,0:T(8,128)(2,1)S(1)} %get-tuple-element.79), channel_id=1, source_target_pairs={{0,8},{4,12},{8,16},{12,20},{16,24},{20,28},{24,1},{28,5},{1,9},{5... | collective-permute-start | bytes 1105928
  892.8 21.0 %collective-permute-start.25 = (bf16[40,4608]{1,0:T(8,128)(2,1)S(1)}, bf16[40,4608]{1,0:T(8,128)(2,1)}, u32[]{:S(2)}, u32[]{:S(2)}) collective-permute-start(bf16[40,4608]{1,0:T(8,128)(2,1)S(1)} %get-tuple-element.79), channel_id=1, source_target_pairs={{0,12},{4,16},{8,20},{12,24},{16,28},{20,1},{24,5},{28,9},{1,13},{... | collective-permute-start | bytes 1105928
  898.2 15.6 %collective-permute-start.26 = (bf16[4,4608]{1,0:T(4,128)(2,1)S(1)}, bf16[4,4608]{1,0:T(4,128)(2,1)S(1)}, u32[]{:S(2)}, u32[]{:S(2)}) collective-permute-start(bf16[4,4608]{1,0:T(4,128)(2,1)S(1)} %slice.186), channel_id=1, source_target_pairs={{0,16},{4,20},{8,24},{12,28},{16,1},{20,5},{24,9},{28,13},{1,17},{... | collective-permute-start | bytes 110600
  930.2 14.8 %copy-start.57 = (bf16[2,288]{1,0:T(2,128)(2,1)S(1)}, bf16[2,288]{1,0:T(2,128)(2,1)}, u32[]{:S(2)}) copy-start(bf16[2,288]{1,0:T(2,128)(2,1)} %copy-done.56) | copy-start | bytes 3460
  932.0 271.1 %all-gather.11.cloned.1.call-start = ((), (), s32[]{:S(2)}) async-start(), calls=%async_computation.2 | async-start | bytes 2985984 | tf_op jit(solution)/shard_map/all_gather | solution.py:479
  934.5 22.3 %collective-permute-start.1 = (bf16[256,1152]{0,1:T(8,128)(2,1)}, bf16[256,1152]{0,1:T(8,128)(2,1)}, u32[]{:S(2)}, u32[]{:S(2)}) collective-permute-start(bf16[256,1152]{0,1:T(8,128)(2,1)} %get-tuple-element.105), channel_id=1, source_target_pairs={{0,1},{1,0},{2,5},{3,4},{4,3},{5,2},{6,7},{7,6},{8,9},{9,8},{10,13... | collective-permute-start | bytes 1769480 | tf_op jit(solution)/shard_map/ppermute | solution.py:284
  936.9 28.0 %collective-permute-start.2 = (bf16[256,1152]{0,1:T(8,128)(2,1)}, bf16[256,1152]{0,1:T(8,128)(2,1)}, u32[]{:S(2)}, u32[]{:S(2)}) collective-permute-start(bf16[256,1152]{0,1:T(8,128)(2,1)} %get-tuple-element.106), channel_id=1, source_target_pairs={{0,0},{1,1},{2,4},{3,5},{4,2},{5,3},{6,6},{7,7},{8,8},{9,9},{10,12... | collective-permute-start | bytes 1769480 | tf_op jit(solution)/shard_map/ppermute | solution.py:284
  969.7 179.7 %collective-permute-start.15 = (bf16[48,1152]{1,0:T(8,128)(2,1)S(1)}, bf16[48,1152]{1,0:T(8,128)(2,1)S(1)}, u32[]{:S(2)}, u32[]{:S(2)}) collective-permute-start(bf16[48,1152]{1,0:T(8,128)(2,1)S(1)} %get-tuple-element.78), channel_id=1, source_target_pairs={{0,4},{4,8},{8,12},{12,16},{16,20},{20,24},{24,28},{28,1},{1,5},{5... | collective-permute-start | bytes 331784
  971.6 184.8 %collective-permute-start.16 = (bf16[48,1152]{1,0:T(8,128)(2,1)S(1)}, bf16[48,1152]{1,0:T(8,128)(2,1)S(1)}, u32[]{:S(2)}, u32[]{:S(2)}) collective-permute-start(bf16[48,1152]{1,0:T(8,128)(2,1)S(1)} %get-tuple-element.78), channel_id=1, source_target_pairs={{0,8},{4,12},{8,16},{12,20},{16,24},{20,28},{24,1},{28,5},{1,9},{5... | collective-permute-start | bytes 331784
  979.7 178.0 %collective-permute-start.17 = (bf16[48,1152]{1,0:T(8,128)(2,1)S(1)}, bf16[48,1152]{1,0:T(8,128)(2,1)}, u32[]{:S(2)}, u32[]{:S(2)}) collective-permute-start(bf16[48,1152]{1,0:T(8,128)(2,1)S(1)} %get-tuple-element.78), channel_id=1, source_target_pairs={{0,12},{4,16},{8,20},{12,24},{16,28},{20,1},{24,5},{28,9},{1,13},{... | collective-permute-start | bytes 331784
  982.1 182.3 %collective-permute-start.18 = (bf16[48,1152]{1,0:T(8,128)(2,1)S(1)}, bf16[48,1152]{1,0:T(8,128)(2,1)}, u32[]{:S(2)}, u32[]{:S(2)}) collective-permute-start(bf16[48,1152]{1,0:T(8,128)(2,1)S(1)} %get-tuple-element.78), channel_id=1, source_target_pairs={{0,16},{4,20},{8,24},{12,28},{16,1},{20,5},{24,9},{28,13},{1,17},{... | collective-permute-start | bytes 331784
  1006.7 42.0 %copy-start.22 = (bf16[512,1152]{0,1:T(8,128)(2,1)S(1)}, bf16[512,1152]{0,1:T(8,128)(2,1)}, u32[]{:S(2)}) copy-start(bf16[512,1152]{0,1:T(8,128)(2,1)} %get-tuple-element.94) | copy-start | bytes 3538948
  1006.8 45.3 %collective-permute-start.6 = (f32[6912]{0:T(1024)S(1)}, f32[6912]{0:T(1024)S(1)}, u32[]{:S(2)}, u32[]{:S(2)}) collective-permute-start(f32[6912]{0:T(1024)S(1)} %constant_dynamic-update-slice_fusion.8), channel_id=1, source_target_pairs={{0,4},{1,5},{2,6},{3,7},{4,0},{5,1},{6,2},{7,3},{8,12},{9,13},{10,... | collective-permute-start | bytes 82952 | tf_op jit(solution)/shard_map/ppermute | solution.py:467
  1052.2 89.1 %collective-permute-start.22 = (bf16[36,1152]{1,0:T(8,128)(2,1)S(1)}, bf16[36,1152]{1,0:T(8,128)(2,1)S(1)}, u32[]{:S(2)}, u32[]{:S(2)}) collective-permute-start(bf16[36,1152]{1,0:T(8,128)(2,1)S(1)} %slice.185), channel_id=1, source_target_pairs={{0,1},{4,5},{8,9},{12,13},{16,17},{20,21},{24,25},{28,29},{1,2},{5... | collective-permute-start | bytes 248840
  1127.0 13.6 %copy-start.42 = (bf16[2,1152]{1,0:T(2,128)(2,1)S(1)}, bf16[2,1152]{1,0:T(2,128)(2,1)}, u32[]{:S(2)}) copy-start(bf16[2,1152]{1,0:T(2,128)(2,1)} %param.16) | copy-start | bytes 13828
  1141.9 49.0 %collective-permute-start.4 = (bf16[256,1152]{0,1:T(8,128)(2,1)S(1)}, bf16[256,1152]{0,1:T(8,128)(2,1)S(1)}, u32[]{:S(2)}, u32[]{:S(2)}) collective-permute-start(bf16[256,1152]{0,1:T(8,128)(2,1)S(1)} %get-tuple-element.101), channel_id=1, source_target_pairs={{0,1},{1,0},{2,5},{3,4},{4,3},{5,2},{6,7},{7,6},{8,9},{9,8},{10,13... | collective-permute-start | bytes 1769480 | tf_op jit(solution)/shard_map/ppermute | solution.py:284
  1149.4 41.5 %collective-permute-start.5 = (bf16[256,1152]{0,1:T(8,128)(2,1)S(1)}, bf16[256,1152]{0,1:T(8,128)(2,1)}, u32[]{:S(2)}, u32[]{:S(2)}) collective-permute-start(bf16[256,1152]{0,1:T(8,128)(2,1)S(1)} %get-tuple-element.102), channel_id=1, source_target_pairs={{0,0},{1,1},{2,4},{3,5},{4,2},{5,3},{6,6},{7,7},{8,8},{9,9},{10,12... | collective-permute-start | bytes 1769480 | tf_op jit(solution)/shard_map/ppermute | solution.py:284
  1156.4 10.1 collective-permute-start.19
  1157.7 8.8 collective-permute-start.20
  1164.4 5.7 collective-permute-start.21
  (61 other events, 334.1 us)
Sparse Core Ops, SparseCore 0:
  334.2 139.5 reduce-scatter.7
Sparse Core Ops, SparseCore 1:
  884.5 49.5 all-gather.12
  936.4 33.0 all-gather.14
  1006.9 29.9 all-gather.10

commit v2 on v1

--- a/solution.py
+++ b/solution.py
@@ -181,6 +181,427 @@
     return outs
 
 
+LANES = 128
+PACK_ROWS = 128
+
+
+def pack_heads(source, first, heads_ref, row0, rows, tail):
+    heads = heads_ref.shape[0]
+
+    @pl.loop(0, rows // PACK_ROWS)
+    def _(step):
+        at = pl.multiple_of(step * PACK_ROWS, PACK_ROWS)
+        block = source[pl.ds(at, PACK_ROWS), first : first + heads * HEAD_DIM]
+        end = tail(at)
+        for h in range(heads):
+            part = block[:, h * HEAD_DIM : (h + 1) * HEAD_DIM]
+            heads_ref[h, pl.ds(row0 + at, PACK_ROWS), :] = jnp.concatenate([part, end], 1)
+
+
+def unpack_heads(heads_ref, row0, rows, target, first):
+    heads = heads_ref.shape[0]
+
+    @pl.loop(0, rows // PACK_ROWS)
+    def _(step):
+        at = pl.multiple_of(step * PACK_ROWS, PACK_ROWS)
+        parts = [heads_ref[h, pl.ds(row0 + at, PACK_ROWS), :][:, :HEAD_DIM] for h in range(heads)]
+        target[pl.ds(at, PACK_ROWS), first : first + heads * HEAD_DIM] = jnp.concatenate(parts, 1)
+
+
+def flat_tail(value):
+    def tail(at):
+        lane = lax.broadcasted_iota(jnp.int32, (PACK_ROWS, LANES - HEAD_DIM), 1)
+        return jnp.where(lane == 0, value, 0.0).astype(jnp.bfloat16)
+
+    return tail
+
+
+def key_tail(valid_count, band_slots):
+    def tail(at):
+        shape = (PACK_ROWS, LANES - HEAD_DIM)
+        lane = lax.broadcasted_iota(jnp.int32, shape, 1)
+        slot = lax.rem(at + lax.broadcasted_iota(jnp.int32, shape, 0), band_slots)
+        return jnp.where(jnp.logical_and(lane == 0, slot >= valid_count), -1e30, 0.0).astype(jnp.bfloat16)
+
+    return tail
+
+
+def lanes_dot(left, right):
+    return lax.dot_general(left, right, (((1,), (1,)), ((), ())), preferred_element_type=jnp.float32)
+
+
+def rows_dot(left, right):
+    return lax.dot_general(left, right, (((0,), (0,)), ((), ())), preferred_element_type=jnp.float32)
+
+
+SCORE_SCALE = HEAD_DIM ** (-0.5)
+
+
+def attend_kernel(band_slots, count_ref, q_ref, own_ref, far_ref, out_ref, top_ref, qh, kh, vh):
+    rows, width = q_ref.shape
+    heads = qh.shape[0]
+    pack_heads(q_ref, 0, qh, 0, rows, flat_tail(1.0))
+    for row0, ref in ((0, own_ref), (rows, far_ref)):
+        pack_heads(ref, 0, kh, row0, rows, key_tail(count_ref[0], band_slots))
+        pack_heads(ref, width, vh, row0, rows, flat_tail(0.0))
+
+    @pl.loop(0, heads)
+    def _(h):
+        for block in range(2):
+            at = pl.ds(block * rows // 2, rows // 2)
+            scores = lanes_dot(kh[h], qh[h, at, :]) * SCORE_SCALE
+            top = jnp.max(scores, 0, keepdims=True)
+            weights = jnp.exp(scores - top)
+            total = jnp.sum(weights, 0, keepdims=True)
+            low = (weights * (1.0 / total)).astype(jnp.bfloat16)
+            mixed = rows_dot(vh[h], low)
+            qh[h, at, :] = jnp.transpose(mixed).astype(jnp.bfloat16)
+            top_ref[h, :, at] = jnp.broadcast_to(top + jnp.log(total), (8, rows // 2))
+
+    unpack_heads(qh, 0, rows, out_ref, 0)
+
+
+def attend(count, query, own, far, band_slots):
+    rows, width = query.shape
+    heads = width // HEAD_DIM
+    bf = jnp.bfloat16
+    vmem = pl.BlockSpec(memory_space=pltpu.VMEM)
+    return pl.pallas_call(
+        partial(attend_kernel, band_slots),
+        out_shape=[
+            jax.ShapeDtypeStruct((rows, width), bf),
+            jax.ShapeDtypeStruct((heads, 8, rows), jnp.float32),
+        ],
+        in_specs=[pl.BlockSpec(memory_space=pltpu.SMEM), vmem, vmem, vmem],
+        out_specs=[vmem, vmem],
+        scratch_shapes=[
+            pltpu.VMEM((heads, rows, LANES), bf),
+            pltpu.VMEM((heads, 2 * rows, LANES), bf),
+            pltpu.VMEM((heads, 2 * rows, LANES), bf),
+        ],
+        compiler_params=pltpu.CompilerParams(vmem_limit_bytes=48 * 2**20),
+        cost_estimate=pl.CostEstimate(
+            flops=8 * rows * rows * width, bytes_accessed=16 * rows * width, transcendentals=2 * heads * rows * rows
+        ),
+        name="attend",
+    )(count, query, own, far)
+
+
+def attend_head(h, qh, kh, vh, gh, top_ref):
+    query = qh[h]
+    key = kh[h]
+    grad = gh[h]
+    probs = jnp.exp(lanes_dot(key, query) * SCORE_SCALE - top_ref[h, 0:1, :])
+    grad_probs = lanes_dot(vh[h], grad)
+    inner = jnp.sum(probs * grad_probs, 0, keepdims=True)
+    grad_scores = (probs * (grad_probs - inner)).astype(jnp.bfloat16)
+    vh[h] = jnp.dot(
+        probs.astype(jnp.bfloat16), grad, preferred_element_type=jnp.float32
+    ).astype(jnp.bfloat16)
+    grad_query = rows_dot(key, grad_scores)
+    kh[h] = (
+        SCORE_SCALE * jnp.dot(grad_scores, query, preferred_element_type=jnp.float32)
+    ).astype(jnp.bfloat16)
+    qh[h] = (SCORE_SCALE * jnp.transpose(grad_query)).astype(jnp.bfloat16)
+
+
+def attend_back_kernel(band_slots, count_ref, q_ref, own_ref, far_ref, grad_ref, top_ref,
+                       dq_ref, down_ref, dfar_ref, qh, kh, vh, gh):
+    rows, width = q_ref.shape
+    heads = qh.shape[0]
+    pack_heads(q_ref, 0, qh, 0, rows, flat_tail(1.0))
+    pack_heads(grad_ref, 0, gh, 0, rows, flat_tail(0.0))
+    for row0, ref in ((0, own_ref), (rows, far_ref)):
+        pack_heads(ref, 0, kh, row0, rows, key_tail(count_ref[0], band_slots))
+        pack_heads(ref, width, vh, row0, rows, flat_tail(0.0))
+
+    @pl.loop(0, heads)
+    def _(h):
+        attend_head(h, qh, kh, vh, gh, top_ref)
+
+    unpack_heads(qh, 0, rows, dq_ref, 0)
+    for row0, ref in ((0, down_ref), (rows, dfar_ref)):
+        unpack_heads(kh, row0, rows, ref, 0)
+        unpack_heads(vh, row0, rows, ref, width)
+
+
+def attend_back(count, query, own, far, grad, top, band_slots):
+    rows, width = query.shape
+    heads = width // HEAD_DIM
+    bf = jnp.bfloat16
+    vmem = pl.BlockSpec(memory_space=pltpu.VMEM)
+    return pl.pallas_call(
+        partial(attend_back_kernel, band_slots),
+        out_shape=[
+            jax.ShapeDtypeStruct((rows, width), bf),
+            jax.ShapeDtypeStruct((rows, 2 * width), bf),
+            jax.ShapeDtypeStruct((rows, 2 * width), bf),
+        ],
+        in_specs=[pl.BlockSpec(memory_space=pltpu.SMEM)] + [vmem] * 5,
+        out_specs=[vmem] * 3,
+        scratch_shapes=[
+            pltpu.VMEM((heads, rows, LANES), bf),
+            pltpu.VMEM((heads, 2 * rows, LANES), bf),
+            pltpu.VMEM((heads, 2 * rows, LANES), bf),
+            pltpu.VMEM((heads, rows, LANES), bf),
+        ],
+        compiler_params=pltpu.CompilerParams(vmem_limit_bytes=56 * 2**20),
+        cost_estimate=pl.CostEstimate(
+            flops=20 * rows * rows * width, bytes_accessed=32 * rows * width, transcendentals=2 * heads * rows * rows
+        ),
+        name="attend_back",
+    )(count, query, own, far, grad, top)
+
+
+def compass():
+    dp = lax.axis_index("dp")
+    band = lax.axis_index("band")
+    core = lax.rem(dp, 2)
+    px = lax.rem(dp // 2, 2)
+    py = lax.rem(dp // 4, 2)
+    return dict(
+        dp=dp, band=band, core=core, px=px, py=py, kind=2 * py + px,
+        sib=dp + 1 - 2 * core, xdp=dp + 2 - 4 * px, ydp=dp + 4 - 8 * py,
+    )
+
+
+def add_rows(total, term):
+    rows = total.shape[0]
+
+    @pl.loop(0, rows // 16)
+    def _(step):
+        at = pl.ds(pl.multiple_of(step * 16, 16), 16)
+        total[at, :] = (
+            total[at, :].astype(jnp.float32) + term[at, :].astype(jnp.float32)
+        ).astype(jnp.bfloat16)
+
+
+def reduce_barrier(me):
+    barrier = pltpu.get_barrier_semaphore()
+    peers = [(me["xdp"], me["band"]), (me["ydp"], me["band"]), (me["sib"], me["band"])]
+    peers += [(me["dp"], lax.rem(me["band"] + k, NB)) for k in range(1, NB)]
+    for dp, band in peers:
+        pl.semaphore_signal(
+            barrier, inc=1, device_id={"dp": dp, "band": band}, device_id_type=MESH
+        )
+    pl.semaphore_wait(barrier, len(peers))
+
+
+REDUCE_ORDER = (1, 3, 2, 0)
+
+
+def reduce_scratch(phases, half, width):
+    bf = jnp.bfloat16
+    n = phases * NB
+    D = pltpu.SemaphoreType.DMA
+    return dict(
+        acc=pltpu.VMEM((n, 4, half, width), bf),
+        recv_a=pltpu.VMEM((n, 4, half, width), bf),
+        recv_b=pltpu.VMEM((n, 2, half, width), bf),
+        recv_c=pltpu.VMEM((n, half, width), bf),
+        recv_z=pltpu.VMEM((phases, NB, half, width), bf),
+        a_send=D((n,)), a_recv=D((n,)), a_own=D((n,)),
+        b_send=D((n, 2)), b_recv=D((n,)), c_send=D((n,)), c_recv=D((n,)),
+        z_send=D((phases, NB)), z_recv=D((phases, NB)),
+        d_send=D((phases, 4)), d_recv=D((phases, 4)), d_own=D((phases,)),
+    )
+
+
+def reduce_steps(me, phases, source, out, sc, last):
+    dp, band, core, px, py, kind = (me[k] for k in ("dp", "band", "core", "px", "py", "kind"))
+    here = lambda d: {"dp": d, "band": band}
+    chunks = [(phase, k) for phase in range(phases) for k in REDUCE_ORDER]
+    n = len(chunks)
+    flip = lambda v: 1 - v
+    sends = []
+
+    def remote(src, dst, ss, rs, to):
+        return pltpu.make_async_remote_copy(
+            src_ref=src, dst_ref=dst, send_sem=ss, recv_sem=rs, device_id=to, device_id_type=MESH
+        )
+
+    def go(copy):
+        copy.start()
+        sends.append(copy)
+
+    def start_a(s):
+        phase, k = chunks[s]
+        b = lax.rem(band + k, NB)
+        for t in range(4):
+            remote(
+                source(phase, b, t, flip(core)), sc["recv_a"].at[s, t],
+                sc["a_send"].at[s], sc["a_recv"].at[s], here(me["sib"]),
+            ).start()
+            pltpu.make_async_copy(
+                source(phase, b, t, core), sc["acc"].at[s, t], sc["a_own"].at[s]
+            ).start()
+
+    def first(s, j, send):
+        if s % 2 == 0:
+            return 2 * j + (flip(px) if send else px)
+        return 2 * (flip(py) if send else py) + j
+
+    def second(s, send):
+        if s % 2 == 0:
+            return 2 * (flip(py) if send else py) + px
+        return 2 * py + (flip(px) if send else px)
+
+    def a_to_b(s):
+        acc, got = sc["acc"], sc["recv_a"]
+        pltpu.make_async_copy(got.at[s], acc.at[s], sc["a_own"].at[s]).wait()
+        whole = remote(got.at[s], got.at[s], sc["a_send"].at[s], sc["a_recv"].at[s], here(me["sib"]))
+        whole.wait_recv()
+        to = here(me["xdp"] if s % 2 == 0 else me["ydp"])
+        for j in range(2):
+            t = first(s, j, True)
+            add_rows(acc.at[s, t], got.at[s, t])
+            go(remote(acc.at[s, t], sc["recv_b"].at[s, j], sc["b_send"].at[s, j], sc["b_recv"].at[s], to))
+        for j in range(2):
+            t = first(s, j, False)
+            add_rows(acc.at[s, t], got.at[s, t])
+        whole.wait_send()
+
+    def b_to_c(s):
+        acc, got = sc["acc"], sc["recv_b"]
+        remote(got.at[s], got.at[s], sc["b_send"].at[s, 0], sc["b_recv"].at[s], here(me["xdp"])).wait_recv()
+        to = here(me["ydp"] if s % 2 == 0 else me["xdp"])
+        away = flip(py) if s % 2 == 0 else flip(px)
+        stay = py if s % 2 == 0 else px
+        add_rows(acc.at[s, second(s, True)], got.at[s, away])
+        go(remote(acc.at[s, second(s, True)], sc["recv_c"].at[s], sc["c_send"].at[s], sc["c_recv"].at[s], to))
+        add_rows(acc.at[s, kind], got.at[s, stay])
+
+    def c_to_z(s):
+        acc, got = sc["acc"], sc["recv_c"]
+        phase, k = chunks[s]
+        remote(got.at[s], got.at[s], sc["c_send"].at[s], sc["c_recv"].at[s], here(me["xdp"])).wait_recv()
+        add_rows(acc.at[s, kind], got.at[s])
+        if k != 0:
+            b = lax.rem(band + k, NB)
+            go(remote(
+                acc.at[s, kind], sc["recv_z"].at[phase, k], sc["z_send"].at[phase, k],
+                sc["z_recv"].at[phase, k], {"dp": dp, "band": b},
+            ))
+
+    def z_to_d(phase):
+        s = phase * NB + NB - 1
+        acc, got = sc["acc"], sc["recv_z"]
+        for k in range(1, NB):
+            remote(
+                got.at[phase, k], got.at[phase, k], sc["z_send"].at[phase, k],
+                sc["z_recv"].at[phase, k], here(dp),
+            ).wait_recv()
+        rows = acc.shape[2]
+
+        @pl.loop(0, rows // 16)
+        def _(step):
+            at = pl.ds(pl.multiple_of(step * 16, 16), 16)
+            total = acc[s, kind, at, :].astype(jnp.float32)
+            for k in range(1, NB):
+                total = total + got[phase, k, at, :].astype(jnp.float32)
+            got[phase, 0, at, :] = total.astype(jnp.bfloat16)
+
+        unit = out[phase].at[kind, core]
+        own = pltpu.make_async_copy(got.at[phase, 0], unit, sc["d_own"].at[phase])
+        own.start()
+        go(remote(
+            got.at[phase, 0], unit, sc["d_send"].at[phase, 0], sc["d_recv"].at[phase, 0],
+            here(me["xdp"] if phase % 2 == 0 else me["ydp"]),
+        ))
+        own.wait()
+
+    def d_second(phase):
+        even = phase % 2 == 0
+        mate = 2 * py + flip(px) if even else 2 * flip(py) + px
+        unit = out[phase].at[mate, core]
+        remote(unit, unit, sc["d_send"].at[phase, 0], sc["d_recv"].at[phase, 0], here(me["xdp"])).wait_recv()
+        if even:
+            pair = out[phase].at[pl.ds(2 * py, 2), core]
+            go(remote(pair, pair, sc["d_send"].at[phase, 1], sc["d_recv"].at[phase, 1], here(me["ydp"])))
+        else:
+            for j in range(2):
+                unit = out[phase].at[2 * j + px, core]
+                go(remote(unit, unit, sc["d_send"].at[phase, 1 + j], sc["d_recv"].at[phase, 1 + j], here(me["xdp"])))
+
+    def d_third(phase):
+        if phase % 2 == 0:
+            pair = out[phase].at[pl.ds(2 * flip(py), 2), core]
+            remote(pair, pair, sc["d_send"].at[phase, 1], sc["d_recv"].at[phase, 1], here(me["ydp"])).wait_recv()
+        else:
+            for j in range(2):
+                unit = out[phase].at[2 * j + flip(px), core]
+                remote(unit, unit, sc["d_send"].at[phase, 1 + j], sc["d_recv"].at[phase, 1 + j], here(me["xdp"])).wait_recv()
+        row = out[phase].at[:, core]
+        go(remote(row, row, sc["d_send"].at[phase, 3], sc["d_recv"].at[phase, 3], here(me["sib"])))
+
+    def d_last(phase):
+        row = out[phase].at[:, flip(core)]
+        remote(row, row, sc["d_send"].at[phase, 3], sc["d_recv"].at[phase, 3], here(me["sib"])).wait_recv()
+
+    def finish():
+        for copy in sends:
+            copy.wait_send()
+
+    steps = [lambda: [start_a(s) for s in range(n)]]
+    late = {}
+    for phase in range(phases):
+        end = (phase + 1) * NB - 1
+        for lag, do in ((4, z_to_d), (5, d_second), (6, d_third), (7, d_last)):
+            late.setdefault(end + lag, []).append(partial(do, phase))
+    for s in range(n + 8):
+        batch = []
+        if s < n:
+            batch.append(partial(a_to_b, s))
+        if 0 <= s - 1 < n:
+            batch.append(partial(b_to_c, s - 1))
+        if 0 <= s - 2 < n:
+            batch.append(partial(c_to_z, s - 2))
+        batch += late.get(s, [])
+        if batch:
+            steps.append(lambda batch=batch: [do() for do in batch])
+    steps.append(finish)
+    return steps
+
+
+def reduce_kernel(counts, names, *refs):
+    me = compass()
+    phases = len(counts)
+    grads = []
+    at = 0
+    for count in counts:
+        grads.append(refs[at : at + count])
+        at += count
+    out = refs[at : at + phases]
+    sc = dict(zip(names, refs[at + phases :]))
+
+    def source(phase, b, t, h):
+        if len(grads[phase]) == 1:
+            return grads[phase][0].at[b, t, h]
+        return grads[phase][t].at[b, h]
+
+    reduce_barrier(me)
+    for step in reduce_steps(me, phases, source, out, sc, None):
+        step()
+
+
+def reduce_grads(grads, collective_id):
+    phases = len(grads)
+    half, width = grads[0][0].shape[-2:]
+    counts = tuple(len(phase) for phase in grads)
+    scratch = reduce_scratch(phases, half, width)
+    return pl.pallas_call(
+        partial(reduce_kernel, counts, tuple(scratch)),
+        out_shape=[jax.ShapeDtypeStruct((4, 2, half, width), jnp.bfloat16)] * phases,
+        in_specs=[pl.BlockSpec(memory_space=pl.ANY)] * sum(counts),
+        out_specs=[pl.BlockSpec(memory_space=pl.ANY)] * phases,
+        scratch_shapes=list(scratch.values()),
+        compiler_params=pltpu.CompilerParams(
+            collective_id=collective_id, has_side_effects=True, vmem_limit_bytes=56 * 2**20
+        ),
+        name="reduce_grads",
+    )(*[unit for phase in grads for unit in phase])
+
+
 def normalize(values):
     average = jnp.mean(values, -1, keepdims=True)
     centered = values - average
@@ -193,70 +614,6 @@
     first = jnp.mean(grad_normed, -1, keepdims=True)
     second = jnp.mean(grad_normed * normed, -1, keepdims=True)
     return inverse * (grad_normed - first - normed * second)
-
-
-def contract(operand, grad_rows):
-    return lax.dot_general(
-        operand, grad_rows, (((0, 1), (0, 1)), ((), ())), preferred_element_type=jnp.float32
-    )
-
-
-def split_heads(rows):
-    return rows.reshape(rows.shape[0], rows.shape[1], rows.shape[2] // HEAD_DIM, HEAD_DIM)
-
-
-def score_block(query_rows, key_rows, key_valid):
-    scores = jnp.einsum(
-        "iqhd,ikhd->ihqk",
-        split_heads(query_rows),
-        split_heads(key_rows),
-        preferred_element_type=jnp.float32,
-    )
-    scores = scores * HEAD_DIM ** (-0.5)
-    return jnp.where(key_valid[:, None, None, :], scores, -1e30)
-
-
-def attention_forward(query_rows, key_rows, value_rows, key_valid):
-    scores = score_block(query_rows, key_rows, key_valid)
-    row_top = jnp.max(scores, -1, keepdims=True)
-    exponent = jnp.exp(scores - row_top)
-    row_total = jnp.sum(exponent, -1, keepdims=True)
-    soft_weights = (exponent / row_total).astype(jnp.bfloat16)
-    mixed_rows = jnp.einsum(
-        "ihqk,ikhd->iqhd", soft_weights, split_heads(value_rows), preferred_element_type=jnp.float32
-    )
-    return (
-        mixed_rows.reshape(query_rows.shape[:2] + (value_rows.shape[2],)).astype(jnp.bfloat16),
-        row_top + jnp.log(row_total),
-    )
-
-
-def attention_backward(query_rows, key_rows, value_rows, log_total, grad_mixed, key_valid):
-    soft_weights = jnp.exp(score_block(query_rows, key_rows, key_valid) - log_total)
-    grad_heads = split_heads(grad_mixed)
-    grad_soft = jnp.einsum(
-        "iqhd,ikhd->ihqk", grad_heads, split_heads(value_rows), preferred_element_type=jnp.float32
-    )
-    row_inner = jnp.sum(soft_weights * grad_soft, -1, keepdims=True)
-    grad_scores = (soft_weights * (grad_soft - row_inner)).astype(jnp.bfloat16)
-    score_scale = HEAD_DIM ** (-0.5)
-    grad_query = score_scale * jnp.einsum(
-        "ihqk,ikhd->iqhd", grad_scores, split_heads(key_rows), preferred_element_type=jnp.float32
-    )
-    grad_key = score_scale * jnp.einsum(
-        "ihqk,iqhd->ikhd", grad_scores, split_heads(query_rows), preferred_element_type=jnp.float32
-    )
-    grad_value = jnp.einsum(
-        "ihqk,iqhd->ikhd",
-        soft_weights.astype(jnp.bfloat16),
-        grad_heads,
-        preferred_element_type=jnp.float32,
-    )
-    return (
-        grad_query.reshape(query_rows.shape),
-        grad_key.reshape(key_rows.shape),
-        grad_value.reshape(value_rows.shape),
-    )
 
 
 def pair_perm(dp_count, band_count):
@@ -297,12 +654,11 @@
     return jnp.concatenate([pick(row_index), pick(col_index)], -1)
 
 
-def rows_dot(left, right):
-    return lax.dot_general(left, right, (((0,), (0,)), ((), ())), preferred_element_type=jnp.float32)
-
-
-def back_dot(left, right):
-    return lax.dot_general(left, right, (((1,), (1,)), ((), ())), preferred_element_type=jnp.float32)
+def over_groups(piece, dp_count):
+    if dp_count == 8:
+        return piece
+    groups = [[rank + 8 * group for group in range(dp_count // 8)] for rank in range(8)]
+    return lax.psum(piece.astype(jnp.float32), "dp", axis_index_groups=groups)
 
 
 def own_piece(vector, count, band_place):
@@ -389,7 +745,6 @@
     is_valid = within < band_rows * grid_cols
     row_index = ids // band_slots * band_rows + within // grid_cols
     col_index = within % grid_cols
-    key_valid = jnp.concatenate([is_valid, is_valid])
 
     shift_one, scale_one, gate_one, shift_two, scale_two, gate_two = [
         modulation[index * width : (index + 1) * width] for index in range(6)
@@ -405,12 +760,8 @@
         projected[:, width:] + jnp.concatenate([jnp.zeros((width,), jnp.float32), value_bias_full])
     ).astype(jnp.bfloat16)
     other_key_value = lax.ppermute(key_value, both, siblings)
-    keys = jnp.concatenate([key_value[:, :width], other_key_value[:, :width]])
-    values = jnp.concatenate([key_value[:, width:], other_key_value[:, width:]])
-    mixed_rows, band_total = attention_forward(
-        query_rows[None], keys[None], values[None], key_valid[None]
-    )
-    mixed_rows = mixed_rows[0]
+    valid_count = (band_rows * grid_cols).reshape(1)
+    mixed_rows, tops = attend(valid_count, query_rows, key_value, other_key_value, band_slots)
     attended = jnp.dot(mixed_rows, proj_full, preferred_element_type=jnp.float32) + proj_bias_full
     middle = residual + gate_one * attended
     normed_two, inverse_two = normalize(middle)
@@ -427,13 +778,20 @@
     grad_gate_two = jnp.sum(grad_out * mlp_out, 0)
     grad_mlp = (gate_two * grad_out).astype(jnp.bfloat16)
     gelu_back = jax.vjp(partial(jax.nn.gelu, approximate=True), hidden_pre)[1]
-    grad_outer = rows_dot(hidden_act, grad_mlp).astype(jnp.bfloat16)
+    blocks = (band_count, 2, part_rows // 2, width)
+    grad_outer = rows_dot(hidden_act, grad_mlp).astype(jnp.bfloat16).reshape(
+        band_count, 4, 2, part_rows // 2, width
+    )
     grad_outer_bias = jnp.sum(grad_mlp.astype(jnp.float32), 0)
-    grad_hidden = back_dot(grad_mlp, outer_full)
+    grad_hidden = lanes_dot(grad_mlp, outer_full)
     grad_pre = gelu_back(grad_hidden)[0].astype(jnp.bfloat16)
-    grad_inner = rows_dot(mlp_in, grad_pre).astype(jnp.bfloat16)
+    grad_inner = [
+        rows_dot(mlp_in, grad_pre[:, t * width : (t + 1) * width]).astype(jnp.bfloat16).reshape(blocks)
+        for t in range(4)
+    ]
+    outer_sum, inner_sum = reduce_grads([[grad_outer], grad_inner], 1)
     grad_inner_bias = jnp.sum(grad_pre.astype(jnp.float32), 0)
-    grad_mlp_in = back_dot(grad_pre, inner_full)
+    grad_mlp_in = lanes_dot(grad_pre, inner_full)
     grad_shift_two = jnp.sum(grad_mlp_in, 0)
     grad_scale_two = jnp.sum(grad_mlp_in * normed_two, 0)
     grad_middle = grad_out + norm_back(grad_mlp_in * (1.0 + scale_two), normed_two, inverse_two)
@@ -441,17 +799,21 @@
     grad_attended = (gate_one * grad_middle).astype(jnp.bfloat16)
     grad_proj = rows_dot(mixed_rows, grad_attended).astype(jnp.bfloat16)
     grad_proj_bias = jnp.sum(grad_attended.astype(jnp.float32), 0)
-    grad_mixed = back_dot(grad_attended, proj_full).astype(jnp.bfloat16)
-    band_dq, key_terms, value_terms = attention_backward(
-        query_rows[None], keys[None], values[None], band_total, grad_mixed[None], key_valid[None]
-    )
-    terms = jnp.concatenate([key_terms[0], value_terms[0]], -1)
-    other_terms = lax.ppermute(terms[rows:].astype(jnp.bfloat16), both, siblings)
-    grad_key_value = (terms[:rows] + other_terms.astype(jnp.float32)).astype(jnp.bfloat16)
-    grad_query = band_dq[0].astype(jnp.bfloat16)
+    grad_mixed = lanes_dot(grad_attended, proj_full).astype(jnp.bfloat16)
+    grad_query, own_terms, far_terms = attend_back(
+        valid_count, query_rows, key_value, other_key_value, grad_mixed, tops, band_slots
+    )
+    other_terms = lax.ppermute(far_terms, both, siblings)
+    grad_key_value = (own_terms.astype(jnp.float32) + other_terms.astype(jnp.float32)).astype(
+        jnp.bfloat16
+    )
     grad_qkv = jnp.concatenate([grad_query, grad_key_value], -1)
-    grad_qkv_weight = rows_dot(attn_in, grad_qkv).astype(jnp.bfloat16)
-    grad_attn_in = back_dot(grad_qkv, qkv_full)
+    grad_first = [
+        rows_dot(attn_in, part).astype(jnp.bfloat16).reshape(blocks)
+        for part in (grad_query, grad_key_value[:, :width], grad_key_value[:, width:])
+    ]
+    (first_sum,) = reduce_grads([grad_first + [grad_proj.reshape(blocks)]], 2)
+    grad_attn_in = lanes_dot(grad_qkv, qkv_full)
     grad_query_bias = jnp.sum(grad_query.astype(jnp.float32), 0)
     grad_value_bias = jnp.sum(grad_key_value[:, width:].astype(jnp.float32), 0)
     grad_shift_one = jnp.sum(grad_attn_in, 0)
@@ -471,13 +833,21 @@
     grad_ada = rows_dot(every_activated, every_mod)
     grad_ada_bias = own_piece(jnp.sum(every_mod.astype(jnp.float32), 0), ada_bias.shape[0], band)
     own_mod = lax.dynamic_slice_in_dim(every_mod, images * dp, images, 0)
-    grad_act = lax.all_gather(back_dot(own_mod, ada_weight), "band", axis=1, tiled=True)
+    grad_act = lax.all_gather(lanes_dot(own_mod, ada_weight), "band", axis=1, tiled=True)
     grad_condition = jax.vjp(jax.nn.silu, condition_f)[1](grad_act)[0]
 
-    def total(piece):
-        scattered = lax.psum_scatter(piece, ("band", "dp"), scatter_dimension=0, tiled=True)
-        return lax.all_gather(scattered, "dp", axis=0, tiled=True).astype(jnp.float32)
-
+    def side_by_side(units):
+        return jnp.concatenate([unit.reshape(part_rows, width) for unit in units], 1).astype(jnp.float32)
+
+    first_sum, inner_sum, outer_sum = [
+        over_groups(piece, dp_count) for piece in (first_sum, inner_sum, outer_sum)
+    ]
+    weight_sums = dict(
+        qkv=side_by_side([first_sum[t] for t in range(3)]),
+        proj=first_sum[3].reshape(part_rows, width).astype(jnp.float32),
+        inner=side_by_side([inner_sum[t] for t in range(4)]),
+        outer=outer_sum.reshape(4 * part_rows, width).astype(jnp.float32),
+    )
     bias_grads = lax.psum(
         jnp.concatenate(
             [grad_query_bias, grad_value_bias, grad_proj_bias, grad_inner_bias, grad_outer_bias]
@@ -496,14 +866,14 @@
         grad_condition,
         grad_ada,
         grad_ada_bias,
-        total(grad_qkv_weight),
+        weight_sums["qkv"],
         bias_parts[0],
         bias_parts[1],
-        total(grad_proj),
+        weight_sums["proj"],
         bias_parts[2],
-        total(grad_inner),
+        weight_sums["inner"],
         bias_parts[3],
-        total(grad_outer),
+        weight_sums["outer"],
         bias_parts[4],
     )
 

time: 1240 us -> 887 us (0.72)
  the two profiles are of different devices: /device:TPU:1 before, /device:TPU:0 now
where the time goes in v2:
time: 887 us; the launch traced here: 877 us
  Pallas kernels  494 us (56%)
  matrix products  141 us (16%)
  blocking collectives  136 us (15%)
  other arithmetic  50.7 us (6%)
  local copies, waits for them, and re-layouts  40.1 us (5%)
  starting transfers between devices  11.6 us (1%)
    pallas_call x2, Pallas kernels, reduce_grads(): pl.pallas_call(partial(reduce_kernel, counts, tuple(scratch)), out_shape=...  236 us
    pallas_call x1, Pallas kernels, gather_weights(): pl.pallas_call(functools.partial(gather_kernel, width), out_shape=[jax.Sh...  171 us
    all_gather x1, blocking collectives, body(): lax.all_gather(grad_mod, both, axis=0)  74.1 us
    pallas_call x1, Pallas kernels, attend_back(): pl.pallas_call(partial(attend_back_kernel, band_slots), out_shape=[jax.Sh...  47.8 us
    dot_general x10, matrix products, rows_dot(): lax.dot_general(left, right, (((0,), (0,)), ((), ())), preferred_element_...  44.8 us
    dot_general x5, matrix products, lanes_dot(): lax.dot_general(left, right, (((1,), (1,)), ((), ())), preferred_element_...  44 us
    psum x1, blocking collectives, body(): lax.psum(jnp.concatenate([grad_query_bias, grad_value_bias, grad_proj_bia...  39.7 us
    pallas_call x1, Pallas kernels, attend(): pl.pallas_call(partial(attend_kernel, band_slots), out_shape=[jax.ShapeDt...  39.3 us
  transfers between devices with their start and end apart: 7, of which 0 were waited for; matrix products, arithmetic and copies ran while one was open for 5% of the time, Pallas kernels for 32%

profile of v2, /device:TPU:0, one launch (start us, length us, event | category | flops | bytes accessed | tf_op | source)
XLA Modules:
  0.0 876.7 jit_solution(7525882790318844933)
XLA Ops:
  2.9 3.5 concatenate.42
  7.4 2.9 convolution_add_fusion
  13.2 170.8 %gather_weights.1 = (bf16[4,2,144,4608]{3,2,1,0:T(8,128)(2,1)}, bf16[4,2,144,4608]{3,2,1,0:T(8,128)(2,1)}, bf16[4,4,2,144,1152]{4,3,2,1,0:T(8,128)(2,1)}, bf16[2...) custom-call(bf16[2,144,4608]{2,1,0:T(8,128)(2,1)S(1)} %bitcast.101, ...), custom_call_target="tpu_custom_call" | custom-call | tf_op jit(solution)/shard_map/gather_weights/pallas_call | solution.py:166
  192.9 2.8 fusion.27
  195.7 2.7 copy.55
  198.5 2.5 fusion.26
  201.0 2.6 convert_reduce_fusion.1
  207.3 3.9 add_convert_fusion.4
  211.2 7.9 fusion.9
  227.9 8.7 all-gather.3
  239.6 39.3 %attend.1 = (bf16[512,1152]{1,0:T(8,128)(2,1)S(1)}, f32[16,8,512]{2,1,0:T(8,128)S(1)}) custom-call(s32[1]{0:T(128)} %bitcast.6.count_ref, bf16[512,1152]{1,0:T(8,128)(2,1)S(1)} %fusion.15.q_ref, bf16[512,2304]{1,0:T(8,128)(2,1)} %fusion.11.own_ref, bf16[512,2304]{1,0:T(8,128)(2,1)} %collective-permute-done.far_ref), custom_call_target="tpu_custom_call" | custom-call | flops 2415919104 | bytes 9437184 | tf_op jit(solution)/shard_map/attend/pallas_call | solution.py:269
  279.0 5.2 fusion.50
  285.3 13.1 %fusion.59 = f32[512,4608]{1,0:T(8,128)} fusion(bf16[512,1152]{0,1:T(8,128)(2,1)S(1)} %add_convert_fusion.3, bf16[1152,4608]{1,0:T(8,128)(2,1)} %bitcast.107), kind=kOutput, calls=%fused_computation.176 | convolution fusion | flops 5435817984 | bytes 21233664 | tf_op jit(solution)/shard_map/dot_general | solution.py:769
  298.4 18.2 %convert_reduce_fusion = (f32[4608]{0:T(1024)}, bf16[512,4608]{1,0:T(8,128)(2,1)}) fusion(f32[512,4608]{1,0:T(8,128)} %fusion.59, f32[4608]{0:T(1024)S(1)} %copy-done.44, bf16[512,1152]{1,0:T(8,128)(2,1)} %bitcast.133, bf16[4608,1152]{1,0:T(8,128)(2,1)} %bitcast.149), kind=kOutput, calls=%fused_computation.10 | convolution fusion | flops 5490077184 | bytes 25989120 | tf_op jit(solution)/shard_map/dot_general | solution.py:230
  316.7 9.8 %fusion.58 = (f32[1152]{0:T(1024)}, f32[512,1152]{1,0:T(8,128)}) fusion(bf16[512,4608]{1,0:T(8,128)(2,1)} %get-tuple-element.91, bf16[1152,4608]{1,0:T(8,128)(2,1)S(1)} %bitcast.110), kind=kOutput, calls=%fused_computation.175 | convolution fusion | flops 5436406784 | bytes 17699328 | tf_op jit(solution)/shard_map/dot_general | solution.py:230
  326.4 3.0 copy.60
  329.5 3.1 multiply_reduce_fusion.1
  333.7 18.8 %convert_reduce_fusion.2 = (f32[1152]{0:T(1024)}, bf16[512,1152]{0,1:T(8,128)(2,1)}, f32[512,1152]{0,1:T(8,128)}, f32[1152]{0:T(1024)}, bf16[512,1152]{0,1:T(8,128)(2,1)}) fusion(f32[1152]{0:T(1024)} %get-tuple-element.134, f32[512]{0:T(512)} %broadcast_multiply_fusion.2, f32[512,1152]{0,1:T(8,128)S(1)} %get-tuple-element.96, ...), kind=kOutput, calls=%fused_computation.43 | convolution fusion | flops 5470615552 | bytes 31906816 | tf_op jit(solution)/shard_map/dot_general | solution.py:771
  352.6 5.1 convolution_convert_fusion.9.grad_ref
  357.7 4.7 convolution_convert_fusion.5
  362.5 11.9 %convolution_convert_fusion = bf16[4608,1152]{1,0:T(8,128)(2,1)} fusion(f32[512,1152]{0,1:T(8,128)S(1)} %copy-done.17, f32[512]{0:T(512)S(1)} %copy-done.54, f32[1152]{0:T(1024)S(1)} %copy-done.35, f32[512,4608]{1,0:T(8,128)S(1)} %bitcast.117, f32[4608]{0:T(1024)S(1)} %copy-done.45), kind=kOutput, calls=%fused_computation | convolution fusion | flops 5466488832 | bytes 22438400 | tf_op jit(solution)/shard_map/dot_general | solution.py:234
  374.4 3.2 convolution_convert_fusion.4
  377.6 3.2 convolution_convert_fusion.3
  380.8 3.2 convolution_convert_fusion.2
  384.0 3.3 convolution_convert_fusion.1
  388.2 47.8 %attend_back.1 = (bf16[512,1152]{1,0:T(8,128)(2,1)}, bf16[512,2304]{1,0:T(8,128)(2,1)}, bf16[512,2304]{1,0:T(8,128)(2,1)}) custom-call(s32[1]{0:T(128)} %bitcast.6.count_ref, bf16[512,1152]{1,0:T(8,128)(2,1)} %copy-done.4, bf16[512,2304]{1,0:T(8,128)(2,1)} %fusion.11.own_ref, bf16[512,2304]{1,0:T(8,128)(2,1)} %collective-permute-done.far_ref, ...), custom_call_target="tpu_custom_call" | custom-call | flops 6039797760 | bytes 18874368 | tf_op jit(solution)/shard_map/attend_back/pallas_call | solution.py:333
  435.9 3.8 collective-permute-start.3
  439.7 4.5 convolution_convert_fusion.8
  444.2 141.0 %reduce_grads.3 = (bf16[4,2,144,1152]{3,2,1,0:T(8,128)(2,1)}, bf16[4,2,144,1152]{3,2,1,0:T(8,128)(2,1)}) custom-call(bf16[4,4,2,144,1152]{4,3,2,1,0:T(8,128)(2,1)} %bitcast.115, bf16[4,2,144,1152]{3,2,1,0:T(8,128)(2,1)} %bitcast.125, bf16[4,2,144,1152]{3,2,1,0:T(8,128)(2,1)} %bitcast.126, bf16[4,2,144,1152]{3,2,1,0:T(8,128)(2,1)} %bitcast.127, ...), custom_call_target="tpu_custom_call" | custom-call | tf_op jit(solution)/shard_map/reduce_grads/pallas_call | solution.py:592
  585.2 4.6 bitcast_convert_fusion
  591.6 2.7 maximum_convert_fusion
  596.4 2.3 add_convert_fusion
  598.7 9.8 %fusion.57 = (f32[1152]{0:T(1024)S(1)}, f32[512,1152]{1,0:T(8,128)}) fusion(bf16[1152,4608]{1,0:T(8,128)(2,1)} %bitcast.148, bf16[512,2304]{1,0:T(8,128)(2,1)S(1)} %add_convert_fusion, bf16[512,1152]{1,0:T(8,128)(2,1)S(1)} %copy-done.25), kind=kOutput, calls=%fused_computation.174 | convolution fusion | flops 4084530176 | bytes 13865472 | tf_op jit(solution)/shard_map/dot_general | solution.py:230
  608.5 3.2 convolution_convert_fusion.7
  611.7 3.2 convolution_convert_fusion.6
  615.2 3.3 copy.61
  618.5 2.7 multiply_reduce_fusion.3
  621.5 2.8 multiply_reduce_fusion.2
  626.0 5.9 collective-permute-start.5
  632.1 95.3 %reduce_grads.2 = bf16[4,2,144,1152]{3,2,1,0:T(8,128)(2,1)} custom-call(bf16[4,2,144,1152]{3,2,1,0:T(8,128)(2,1)} %bitcast.119, bf16[4,2,144,1152]{3,2,1,0:T(8,128)(2,1)} %bitcast.120, bf16[4,2,144,1152]{3,2,1,0:T(8,128)(2,1)} %bitcast.121, bf16[4,2,144,1152]{3,2,1,0:T(8,128)(2,1)} %bitcast.118), custom_call_target="tpu_custom_call" | custom-call | tf_op jit(solution)/shard_map/reduce_grads/pallas_call | solution.py:592
  727.5 1.9 fusion.52
  729.5 39.7 %psum.7 = f32[9216]{0:T(1024)S(1)} all-reduce(f32[9216]{0:T(1024)S(1)} %constant_dynamic-update-slice_fusion.10), channel_id=1, replica_groups=mesh['dp'=8,'band'=4] {'dp','band'}, use_global_device_ids=true, to_apply=%region_21.22 | all-reduce | flops 9216 | bytes 73728 | tf_op jit(solution)/shard_map/psum | solution.py:851
  770.5 2.2 maximum_convert_fusion.1
  776.0 74.1 %all-gather.1 = bf16[32,1,6912]{2,1,0:T(2,128)(2,1)S(1)} all-gather(bf16[1,1,6912]{2,1,0:T(2,128)(2,1)S(1)} %reshape.297), channel_id=2, replica_groups=mesh['dp'=8,'band'=4] {'dp','band'}, dimensions={0}, use_global_device_ids=true | all-gather | bytes 456192 | tf_op jit(solution)/shard_map/all_gather | solution.py:830
  850.1 2.6 reduce.4
  853.0 4.5 fusion.60
  858.6 13.1 %all-gather.2 = f32[4,288,2]{1,2,0:T(2,128)S(1)} all-gather(f32[1,288,2]{1,2,0:T(2,128)S(1)} %convolution_bitcast_fusion), channel_id=1, replica_groups=mesh['dp'=8,'band'=4] {'band'}, dimensions={0}, use_global_device_ids=true | all-gather | bytes 11520 | tf_op jit(solution)/shard_map/all_gather | solution.py:836
  874.5 2.0 copy.66
  (231 shorter events, 47.2 us)
Async XLA Ops:
  0.6 9.7 %copy-start.19 = (bf16[288,3456]{1,0:T(8,128)(2,1)S(1)}, bf16[288,3456]{1,0:T(8,128)(2,1)}, u32[]{:S(2)}) copy-start(bf16[288,3456]{1,0:T(8,128)(2,1)} %param.20) | copy-start | bytes 5971972
  6.5 5.3 copy-start.46
  7.3 4.5 copy-start.2
  7.3 4.5 copy-start.3
  184.0 5.5 copy-start.26
  187.3 20.0 %copy-start.27 = (f32[1152]{0:T(1024)}, f32[1152]{0:T(1024)S(1)}, u32[]{:S(2)}) copy-start(f32[1152]{0:T(1024)S(1)} %get-tuple-element.133) | copy-start | bytes 13828
  211.2 7.9 copy-start.20
  219.1 4.9 copy-start.42
  219.1 5.6 copy-start.41
  222.8 5.1 copy-start.47
  222.8 16.8 %collective-permute-start = (bf16[512,2304]{1,0:T(8,128)(2,1)}, bf16[512,2304]{1,0:T(8,128)(2,1)}, u32[]{:S(2)}, u32[]{:S(2)}) collective-permute-start(bf16[512,2304]{1,0:T(8,128)(2,1)} %fusion.11.own_ref), channel_id=1, source_target_pairs={{0,4},{1,5},{2,6},{3,7},{4,0},{5,1},{6,2},{7,3},{8,12},{9,13},{10,... | collective-permute-start | bytes 7077896 | tf_op jit(solution)/shard_map/ppermute | solution.py:762
  239.5 39.4 %copy-start.4 = (bf16[512,1152]{1,0:T(8,128)(2,1)}, bf16[512,1152]{1,0:T(8,128)(2,1)S(1)}, u32[]{:S(2)}) copy-start(bf16[512,1152]{1,0:T(8,128)(2,1)S(1)} %fusion.15.q_ref) | copy-start | bytes 3538948
  239.5 39.4 %copy-start.6 = (f32[512,1152]{0,1:T(8,128)S(1)}, f32[512,1152]{0,1:T(8,128)}, u32[]{:S(2)}) copy-start(f32[512,1152]{0,1:T(8,128)} %get-tuple-element.98) | copy-start | bytes 7077892
  239.5 39.4 %copy-start.49 = (f32[1152]{0:T(1024)S(1)}, f32[1152]{0:T(1024)}, u32[]{:S(2)}) copy-start(f32[1152]{0:T(1024)} %get-tuple-element.134) | copy-start | bytes 13828
  239.6 39.4 %copy-start.50 = (f32[1152]{0:T(1024)S(1)}, f32[1152]{0:T(1024)}, u32[]{:S(2)}) copy-start(f32[1152]{0:T(1024)} %add.253) | copy-start | bytes 13828
  278.9 5.2 copy-start.5
  285.2 13.2 %copy-start.13 = (bf16[512,1152]{0,1:T(8,128)(2,1)}, bf16[512,1152]{0,1:T(8,128)(2,1)S(1)}, u32[]{:S(2)}) copy-start(bf16[512,1152]{0,1:T(8,128)(2,1)S(1)} %add_convert_fusion.3) | copy-start | bytes 3538948
  285.2 13.1 %copy-start.44 = (f32[4608]{0:T(1024)S(1)}, f32[4608]{0:T(1024)}, u32[]{:S(2)}) copy-start(f32[4608]{0:T(1024)} %add.261) | copy-start | bytes 55300
  285.3 31.4 %slice-start = ((s8[10616832]{0:T(1024)(128)(4,1)}), s8[4194304]{0:T(1024)(128)(4,1)S(1)}, s32[]{:S(2)}) async-start(s8[10616832]{0:T(1024)(128)(4,1)} %bitcast.108), calls=%async_computation | async-start | bytes 8388608
  298.4 18.3 %slice-start.1 = ((s8[10616832]{0:T(1024)(128)(4,1)}), s8[4194304]{0:T(1024)(128)(4,1)S(1)}, s32[]{:S(2)}) async-start(s8[10616832]{0:T(1024)(128)(4,1)} %bitcast.108), calls=%async_computation.1 | async-start | bytes 8388608
  298.4 18.3 %slice-start.2 = ((s8[10616832]{0:T(1024)(128)(4,1)}), s8[2228224]{0:T(1024)(128)(4,1)S(1)}, s32[]{:S(2)}) async-start(s8[10616832]{0:T(1024)(128)(4,1)} %bitcast.108), calls=%async_computation.2 | async-start | bytes 4456448
  352.5 9.9 %slice-start.3 = ((s8[9437184]{0:T(1024)(128)(4,1)}), s8[4194304]{0:T(1024)(128)(4,1)S(1)}, s32[]{:S(2)}) async-start(s8[9437184]{0:T(1024)(128)(4,1)} %bitcast.116), calls=%async_computation.3 | async-start | bytes 8388608
  352.6 9.9 %slice-start.4 = ((s8[9437184]{0:T(1024)(128)(4,1)}), s8[4194304]{0:T(1024)(128)(4,1)S(1)}, s32[]{:S(2)}) async-start(s8[9437184]{0:T(1024)(128)(4,1)} %bitcast.116), calls=%async_computation.4 | async-start | bytes 8388608
  357.7 4.8 slice-start.5
  357.7 4.8 copy-start.17
  357.7 4.8 copy-start.35
  357.7 4.8 copy-start.45
  357.7 4.8 copy-start.54
  357.7 16.7 %slice-start.6 = ((s8[4718592]{0:T(1024)(128)(4,1)}), s8[524288]{0:T(1024)(128)(4,1)S(1)}, s32[]{:S(2)}) async-start(s8[4718592]{0:T(1024)(128)(4,1)} %bitcast.151), calls=%async_computation.6 | async-start | bytes 1048576
  362.5 11.9 %copy-start.14 = (bf16[512,1152]{0,1:T(8,128)(2,1)S(1)}, bf16[512,1152]{0,1:T(8,128)(2,1)}, u32[]{:S(2)}) copy-start(bf16[512,1152]{0,1:T(8,128)(2,1)} %copy-done.13) | copy-start | bytes 3538948
  362.5 11.9 %slice-start.7 = ((s8[4718592]{0:T(1024)(128)(4,1)}), s8[4194304]{0:T(1024)(128)(4,1)S(1)}, s32[]{:S(2)}) async-start(s8[4718592]{0:T(1024)(128)(4,1)} %bitcast.151), calls=%async_computation.7 | async-start | bytes 8388608
  387.4 206.9 %collective-permute-start.1 = (bf16[256,1152]{0,1:T(8,128)(2,1)S(1)}, bf16[256,1152]{0,1:T(8,128)(2,1)S(1)}, u32[]{:S(2)}, u32[]{:S(2)}) collective-permute-start(bf16[256,1152]{0,1:T(8,128)(2,1)S(1)} %get-tuple-element.117), channel_id=1, source_target_pairs={{0,1},{1,0},{2,5},{3,4},{4,3},{5,2},{6,7},{7,6},{8,9},{9,8},{10,13... | collective-permute-start | bytes 1769480 | tf_op jit(solution)/shard_map/ppermute | solution.py:641
  387.4 206.8 %collective-permute-start.2 = (bf16[256,1152]{0,1:T(8,128)(2,1)S(1)}, bf16[256,1152]{0,1:T(8,128)(2,1)S(1)}, u32[]{:S(2)}, u32[]{:S(2)}) collective-permute-start(bf16[256,1152]{0,1:T(8,128)(2,1)S(1)} %get-tuple-element.118), channel_id=1, source_target_pairs={{0,0},{1,1},{2,4},{3,5},{4,2},{5,3},{6,6},{7,7},{8,8},{9,9},{10,12... | collective-permute-start | bytes 1769480 | tf_op jit(solution)/shard_map/ppermute | solution.py:641
  388.1 51.6 %copy-start.21 = (bf16[512,1152]{0,1:T(8,128)(2,1)S(1)}, bf16[512,1152]{0,1:T(8,128)(2,1)}, u32[]{:S(2)}) copy-start(bf16[512,1152]{0,1:T(8,128)(2,1)} %copy-done.20) | copy-start | bytes 3538948
  435.9 160.1 %collective-permute-start.3 = (bf16[512,2304]{1,0:T(8,128)(2,1)}, bf16[512,2304]{1,0:T(8,128)(2,1)}, u32[]{:S(2)}, u32[]{:S(2)}) collective-permute-start(bf16[512,2304]{1,0:T(8,128)(2,1)} %get-tuple-element.37), channel_id=1, source_target_pairs={{0,4},{1,5},{2,6},{3,7},{4,0},{5,1},{6,2},{7,3},{8,12},{9,13},{10,... | collective-permute-start | bytes 7077896 | tf_op jit(solution)/shard_map/ppermute | solution.py:806
  585.2 4.6 copy-start.24
  585.2 6.1 copy-start.15
  598.7 9.8 %copy-start.22 = (bf16[512,1152]{0,1:T(8,128)(2,1)S(1)}, bf16[512,1152]{0,1:T(8,128)(2,1)}, u32[]{:S(2)}) copy-start(bf16[512,1152]{0,1:T(8,128)(2,1)} %copy-done.20) | copy-start | bytes 3538948
  624.3 7.6 copy-start.39
  624.3 7.7 copy-start.52
  624.3 7.7 copy-start.38
  624.4 7.7 copy-start.53
  625.5 247.7 %collective-permute-start.4 = (bf16[256,1152]{0,1:T(8,128)(2,1)}, bf16[256,1152]{0,1:T(8,128)(2,1)S(1)}, u32[]{:S(2)}, u32[]{:S(2)}) collective-permute-start(bf16[256,1152]{0,1:T(8,128)(2,1)} %get-tuple-element.113), channel_id=1, source_target_pairs={{0,1},{1,0},{2,5},{3,4},{4,3},{5,2},{6,7},{7,6},{8,9},{9,8},{10,13... | collective-permute-start | bytes 1769480 | tf_op jit(solution)/shard_map/ppermute | solution.py:641
  626.0 247.2 %collective-permute-start.5 = (bf16[256,1152]{0,1:T(8,128)(2,1)}, bf16[256,1152]{0,1:T(8,128)(2,1)}, u32[]{:S(2)}, u32[]{:S(2)}) collective-permute-start(bf16[256,1152]{0,1:T(8,128)(2,1)} %get-tuple-element.114), channel_id=1, source_target_pairs={{0,0},{1,1},{2,4},{3,5},{4,2},{5,3},{6,6},{7,7},{8,8},{9,9},{10,12... | collective-permute-start | bytes 1769480 | tf_op jit(solution)/shard_map/ppermute | solution.py:641
  632.1 143.9 %collective-permute-start.6 = (f32[6912]{0:T(1024)S(1)}, f32[6912]{0:T(1024)S(1)}, u32[]{:S(2)}, u32[]{:S(2)}) collective-permute-start(f32[6912]{0:T(1024)S(1)} %constant_dynamic-update-slice_fusion.8), channel_id=1, source_target_pairs={{0,4},{1,5},{2,6},{3,7},{4,0},{5,1},{6,2},{7,3},{8,12},{9,13},{10,... | collective-permute-start | bytes 82952 | tf_op jit(solution)/shard_map/ppermute | solution.py:829
  772.7 80.3 %copy-start.29 = (bf16[16,288]{1,0:T(8,128)(2,1)S(1)}, bf16[16,288]{1,0:T(8,128)(2,1)}, u32[]{:S(2)}) copy-start(bf16[16,288]{1,0:T(8,128)(2,1)} %reshape.302) | copy-start | bytes 27652
  853.0 4.5 copy-start.9
  857.5 15.1 %copy-start.30 = (bf16[2,1152]{1,0:T(2,128)(2,1)S(1)}, bf16[2,1152]{1,0:T(2,128)(2,1)}, u32[]{:S(2)}) copy-start(bf16[2,1152]{1,0:T(2,128)(2,1)} %param.16) | copy-start | bytes 13828
  (22 other events, 58.1 us)

commit v3 on v2

--- a/solution.py
+++ b/solution.py
@@ -305,54 +305,6 @@
     qh[h] = (SCORE_SCALE * jnp.transpose(grad_query)).astype(jnp.bfloat16)
 
 
-def attend_back_kernel(band_slots, count_ref, q_ref, own_ref, far_ref, grad_ref, top_ref,
-                       dq_ref, down_ref, dfar_ref, qh, kh, vh, gh):
-    rows, width = q_ref.shape
-    heads = qh.shape[0]
-    pack_heads(q_ref, 0, qh, 0, rows, flat_tail(1.0))
-    pack_heads(grad_ref, 0, gh, 0, rows, flat_tail(0.0))
-    for row0, ref in ((0, own_ref), (rows, far_ref)):
-        pack_heads(ref, 0, kh, row0, rows, key_tail(count_ref[0], band_slots))
-        pack_heads(ref, width, vh, row0, rows, flat_tail(0.0))
-
-    @pl.loop(0, heads)
-    def _(h):
-        attend_head(h, qh, kh, vh, gh, top_ref)
-
-    unpack_heads(qh, 0, rows, dq_ref, 0)
-    for row0, ref in ((0, down_ref), (rows, dfar_ref)):
-        unpack_heads(kh, row0, rows, ref, 0)
-        unpack_heads(vh, row0, rows, ref, width)
-
-
-def attend_back(count, query, own, far, grad, top, band_slots):
-    rows, width = query.shape
-    heads = width // HEAD_DIM
-    bf = jnp.bfloat16
-    vmem = pl.BlockSpec(memory_space=pltpu.VMEM)
-    return pl.pallas_call(
-        partial(attend_back_kernel, band_slots),
-        out_shape=[
-            jax.ShapeDtypeStruct((rows, width), bf),
-            jax.ShapeDtypeStruct((rows, 2 * width), bf),
-            jax.ShapeDtypeStruct((rows, 2 * width), bf),
-        ],
-        in_specs=[pl.BlockSpec(memory_space=pltpu.SMEM)] + [vmem] * 5,
-        out_specs=[vmem] * 3,
-        scratch_shapes=[
-            pltpu.VMEM((heads, rows, LANES), bf),
-            pltpu.VMEM((heads, 2 * rows, LANES), bf),
-            pltpu.VMEM((heads, 2 * rows, LANES), bf),
-            pltpu.VMEM((heads, rows, LANES), bf),
-        ],
-        compiler_params=pltpu.CompilerParams(vmem_limit_bytes=56 * 2**20),
-        cost_estimate=pl.CostEstimate(
-            flops=20 * rows * rows * width, bytes_accessed=32 * rows * width, transcendentals=2 * heads * rows * rows
-        ),
-        name="attend_back",
-    )(count, query, own, far, grad, top)
-
-
 def compass():
     dp = lax.axis_index("dp")
     band = lax.axis_index("band")
@@ -385,6 +337,11 @@
             barrier, inc=1, device_id={"dp": dp, "band": band}, device_id_type=MESH
         )
     pl.semaphore_wait(barrier, len(peers))
+
+
+def run_all(batch):
+    for do in batch:
+        do()
 
 
 REDUCE_ORDER = (1, 3, 2, 0)
@@ -407,7 +364,7 @@
     )
 
 
-def reduce_steps(me, phases, source, out, sc, last):
+def reduce_steps(me, phases, source, out, sc, beside=()):
     dp, band, core, px, py, kind = (me[k] for k in ("dp", "band", "core", "px", "py", "kind"))
     here = lambda d: {"dp": d, "band": band}
     chunks = [(phase, k) for phase in range(phases) for k in REDUCE_ORDER]
@@ -420,9 +377,9 @@
             src_ref=src, dst_ref=dst, send_sem=ss, recv_sem=rs, device_id=to, device_id_type=MESH
         )
 
-    def go(copy):
-        copy.start()
-        sends.append(copy)
+    def go(make):
+        make().start()
+        sends.append(make)
 
     def start_a(s):
         phase, k = chunks[s]
@@ -446,16 +403,49 @@
             return 2 * (flip(py) if send else py) + px
         return 2 * py + (flip(px) if send else px)
 
+    def send_b(s, j):
+        return remote(
+            sc["acc"].at[s, first(s, j, True)], sc["recv_b"].at[s, j], sc["b_send"].at[s, j],
+            sc["b_recv"].at[s], here(me["xdp"] if s % 2 == 0 else me["ydp"]),
+        )
+
+    def send_c(s):
+        return remote(
+            sc["acc"].at[s, second(s, True)], sc["recv_c"].at[s], sc["c_send"].at[s],
+            sc["c_recv"].at[s], here(me["ydp"] if s % 2 == 0 else me["xdp"]),
+        )
+
+    def send_z(s):
+        phase, k = chunks[s]
+        return remote(
+            sc["acc"].at[s, kind], sc["recv_z"].at[phase, k], sc["z_send"].at[phase, k],
+            sc["z_recv"].at[phase, k], {"dp": dp, "band": lax.rem(band + k, NB)},
+        )
+
+    def send_d(phase, slot):
+        ss, rs = sc["d_send"].at[phase, slot], sc["d_recv"].at[phase, slot]
+        even = phase % 2 == 0
+        if slot == 0:
+            unit = out[phase].at[kind, core]
+            return remote(sc["recv_z"].at[phase, 0], unit, ss, rs, here(me["xdp"] if even else me["ydp"]))
+        if slot == 3:
+            row = out[phase].at[:, core]
+            return remote(row, row, ss, rs, here(me["sib"]))
+        if even:
+            pair = out[phase].at[pl.ds(2 * py, 2), core]
+            return remote(pair, pair, ss, rs, here(me["ydp"]))
+        unit = out[phase].at[2 * (slot - 1) + px, core]
+        return remote(unit, unit, ss, rs, here(me["xdp"]))
+
     def a_to_b(s):
         acc, got = sc["acc"], sc["recv_a"]
         pltpu.make_async_copy(got.at[s], acc.at[s], sc["a_own"].at[s]).wait()
         whole = remote(got.at[s], got.at[s], sc["a_send"].at[s], sc["a_recv"].at[s], here(me["sib"]))
         whole.wait_recv()
-        to = here(me["xdp"] if s % 2 == 0 else me["ydp"])
         for j in range(2):
             t = first(s, j, True)
             add_rows(acc.at[s, t], got.at[s, t])
-            go(remote(acc.at[s, t], sc["recv_b"].at[s, j], sc["b_send"].at[s, j], sc["b_recv"].at[s], to))
+            go(partial(send_b, s, j))
         for j in range(2):
             t = first(s, j, False)
             add_rows(acc.at[s, t], got.at[s, t])
@@ -464,11 +454,10 @@
     def b_to_c(s):
         acc, got = sc["acc"], sc["recv_b"]
         remote(got.at[s], got.at[s], sc["b_send"].at[s, 0], sc["b_recv"].at[s], here(me["xdp"])).wait_recv()
-        to = here(me["ydp"] if s % 2 == 0 else me["xdp"])
         away = flip(py) if s % 2 == 0 else flip(px)
         stay = py if s % 2 == 0 else px
         add_rows(acc.at[s, second(s, True)], got.at[s, away])
-        go(remote(acc.at[s, second(s, True)], sc["recv_c"].at[s], sc["c_send"].at[s], sc["c_recv"].at[s], to))
+        go(partial(send_c, s))
         add_rows(acc.at[s, kind], got.at[s, stay])
 
     def c_to_z(s):
@@ -477,11 +466,7 @@
         remote(got.at[s], got.at[s], sc["c_send"].at[s], sc["c_recv"].at[s], here(me["xdp"])).wait_recv()
         add_rows(acc.at[s, kind], got.at[s])
         if k != 0:
-            b = lax.rem(band + k, NB)
-            go(remote(
-                acc.at[s, kind], sc["recv_z"].at[phase, k], sc["z_send"].at[phase, k],
-                sc["z_recv"].at[phase, k], {"dp": dp, "band": b},
-            ))
+            go(partial(send_z, s))
 
     def z_to_d(phase):
         s = phase * NB + NB - 1
@@ -504,10 +489,7 @@
         unit = out[phase].at[kind, core]
         own = pltpu.make_async_copy(got.at[phase, 0], unit, sc["d_own"].at[phase])
         own.start()
-        go(remote(
-            got.at[phase, 0], unit, sc["d_send"].at[phase, 0], sc["d_recv"].at[phase, 0],
-            here(me["xdp"] if phase % 2 == 0 else me["ydp"]),
-        ))
+        go(partial(send_d, phase, 0))
         own.wait()
 
     def d_second(phase):
@@ -515,13 +497,8 @@
         mate = 2 * py + flip(px) if even else 2 * flip(py) + px
         unit = out[phase].at[mate, core]
         remote(unit, unit, sc["d_send"].at[phase, 0], sc["d_recv"].at[phase, 0], here(me["xdp"])).wait_recv()
-        if even:
-            pair = out[phase].at[pl.ds(2 * py, 2), core]
-            go(remote(pair, pair, sc["d_send"].at[phase, 1], sc["d_recv"].at[phase, 1], here(me["ydp"])))
-        else:
-            for j in range(2):
-                unit = out[phase].at[2 * j + px, core]
-                go(remote(unit, unit, sc["d_send"].at[phase, 1 + j], sc["d_recv"].at[phase, 1 + j], here(me["xdp"])))
+        for slot in (1,) if even else (1, 2):
+            go(partial(send_d, phase, slot))
 
     def d_third(phase):
         if phase % 2 == 0:
@@ -531,18 +508,17 @@
             for j in range(2):
                 unit = out[phase].at[2 * j + flip(px), core]
                 remote(unit, unit, sc["d_send"].at[phase, 1 + j], sc["d_recv"].at[phase, 1 + j], here(me["xdp"])).wait_recv()
-        row = out[phase].at[:, core]
-        go(remote(row, row, sc["d_send"].at[phase, 3], sc["d_recv"].at[phase, 3], here(me["sib"])))
+        go(partial(send_d, phase, 3))
 
     def d_last(phase):
         row = out[phase].at[:, flip(core)]
         remote(row, row, sc["d_send"].at[phase, 3], sc["d_recv"].at[phase, 3], here(me["sib"])).wait_recv()
 
     def finish():
-        for copy in sends:
-            copy.wait_send()
-
-    steps = [lambda: [start_a(s) for s in range(n)]]
+        for make in sends:
+            make().wait_send()
+
+    steps = [partial(run_all, [partial(start_a, s) for s in range(n)])]
     late = {}
     for phase in range(phases):
         end = (phase + 1) * NB - 1
@@ -556,50 +532,290 @@
             batch.append(partial(b_to_c, s - 1))
         if 0 <= s - 2 < n:
             batch.append(partial(c_to_z, s - 2))
+        if s < len(beside):
+            batch.append(beside[s])
         batch += late.get(s, [])
         if batch:
-            steps.append(lambda batch=batch: [do() for do in batch])
+            steps.append(partial(run_all, batch))
     steps.append(finish)
     return steps
 
 
-def reduce_kernel(counts, names, *refs):
-    me = compass()
-    phases = len(counts)
+def reduce_sources(counts, refs):
     grads = []
     at = 0
     for count in counts:
         grads.append(refs[at : at + count])
         at += count
-    out = refs[at : at + phases]
-    sc = dict(zip(names, refs[at + phases :]))
 
     def source(phase, b, t, h):
         if len(grads[phase]) == 1:
             return grads[phase][0].at[b, t, h]
         return grads[phase][t].at[b, h]
 
+    return source
+
+
+def small_scratch(mod_rows, bias_rows, cond_rows, cond_cols):
+    D = pltpu.SemaphoreType.DMA
+    f32 = jnp.float32
+    return dict(
+        s_core=pltpu.VMEM((mod_rows + bias_rows, 128), f32),
+        s_every=pltpu.VMEM((NB, 4, mod_rows, 128), jnp.bfloat16),
+        s_bias=pltpu.VMEM((3, bias_rows, 128), f32),
+        s_got=pltpu.VMEM((2 + NB, bias_rows, 128), f32),
+        s_flat=pltpu.VMEM((8, mod_rows, 128), f32),
+        s_cond=pltpu.VMEM((NB, cond_rows, cond_cols), f32),
+        s_send=D((8,)), s_recv=D((8,)), sz_send=D((2, NB)), sz_recv=D((2, NB)),
+        sc_send=D((NB,)), sc_recv=D((NB,)),
+    )
+
+
+def small_steps(me, mods, images, small_ref, ada_ref, every_ref, bias_ref, cond_ref, sc):
+    dp, band, core, px, py, kind = (me[k] for k in ("dp", "band", "core", "px", "py", "kind"))
+    here = lambda d: {"dp": d, "band": band}
+    every, bias, got, cond = sc["s_every"], sc["s_bias"], sc["s_got"], sc["s_cond"]
+    mod_rows = every.shape[2]
+    flip = lambda v: 1 - v
+
+    def remote(src, dst, ss, rs, to):
+        return pltpu.make_async_remote_copy(
+            src_ref=src, dst_ref=dst, send_sem=ss, recv_sem=rs, device_id=to, device_id_type=MESH
+        )
+
+    def plain(index, src, dst, to):
+        return remote(src, dst, sc["s_send"].at[index], sc["s_recv"].at[index], to)
+
+    def core_copy():
+        return plain(0, small_ref, sc["s_core"], here(me["sib"]))
+
+    def x_copies(mine):
+        unit = every.at[band, kind if mine else 2 * py + flip(px)]
+        return [
+            plain(1, unit, unit, here(me["xdp"])),
+            plain(2, bias.at[0], got.at[0], here(me["xdp"])),
+        ]
+
+    def y_copies(mine):
+        pair = every.at[band, pl.ds(2 * (py if mine else flip(py)), 2)]
+        return [
+            plain(3, pair, pair, here(me["ydp"])),
+            plain(4, bias.at[1], got.at[1], here(me["ydp"])),
+        ]
+
+    def z_copies(k, mine):
+        to = {"dp": dp, "band": lax.rem(band + k, NB)}
+        block = every.at[band if mine else lax.rem(band + NB - k, NB)]
+        return [
+            remote(block, block, sc["sz_send"].at[0, k], sc["sz_recv"].at[0, k], to),
+            remote(bias.at[2], got.at[2 + k], sc["sz_send"].at[1, k], sc["sz_recv"].at[1, k], to),
+        ]
+
+    def cond_copy(k, mine):
+        to = {"dp": dp, "band": lax.rem(band + k, NB)}
+        block = cond.at[band if mine else lax.rem(band + NB - k, NB)]
+        return remote(block, block, sc["sc_send"].at[k], sc["sc_recv"].at[k], to)
+
+    def begin():
+        core_copy().start()
+
+    def cores():
+        core_copy().wait()
+        total = small_ref[...] + sc["s_core"][...]
+        every[band, kind] = total[:mod_rows].astype(jnp.bfloat16)
+        bias[0] = total[mod_rows:]
+        for copy in x_copies(True):
+            copy.start()
+
+    def over_x():
+        for copy in x_copies(True):
+            copy.wait_send()
+        for copy in x_copies(False):
+            copy.wait_recv()
+        bias[1] = bias[0] + got[0]
+        for copy in y_copies(True):
+            copy.start()
+
+    def over_y():
+        for copy in y_copies(True):
+            copy.wait_send()
+        for copy in y_copies(False):
+            copy.wait_recv()
+        bias[2] = bias[1] + got[1]
+        for k in range(1, NB):
+            for copy in z_copies(k, True):
+                copy.start()
+
+    def over_z():
+        for k in range(1, NB):
+            for copy in z_copies(k, True):
+                copy.wait_send()
+            for copy in z_copies(k, False):
+                copy.wait_recv()
+        bias_ref[...] = bias[2] + got[3] + got[4] + got[5]
+        every_ref[...] = every[...]
+        flat = sc["s_flat"]
+        for i in range(images):
+            flat[i] = every[images * core + i, kind].astype(jnp.float32)
+        parts = mods // 128
+        lead = flat.shape[0]
+        total = jnp.zeros((lead, ada_ref.shape[0]), jnp.float32)
+        for r in range(parts):
+            left = jnp.concatenate(
+                [flat[i, r : r + 1, :] for i in range(images)]
+                + [jnp.zeros((lead - images, 128), jnp.float32)]
+            ).astype(jnp.bfloat16)
+            total = total + lanes_dot(left, ada_ref[:, r * 128 : (r + 1) * 128])
+        pad = cond.shape[2] - total.shape[1]
+        cond[band] = jnp.concatenate([total, jnp.zeros((lead, pad), jnp.float32)], 1)
+        for k in range(1, NB):
+            cond_copy(k, True).start()
+
+    def conditions():
+        for k in range(1, NB):
+            cond_copy(k, True).wait_send()
+            cond_copy(k, False).wait_recv()
+        cond_ref[...] = cond[...]
+
+    return [begin, cores, over_x, over_y, over_z, conditions]
+
+
+def reduce_last_kernel(counts, mods, images, names, *refs):
+    me = compass()
+    phases = len(counts)
+    at = sum(counts)
+    source = reduce_sources(counts, refs)
+    small_ref, ada_ref = refs[at : at + 2]
+    out = refs[at + 2 : at + 2 + phases]
+    every_ref, bias_ref, cond_ref = refs[at + 2 + phases : at + 5 + phases]
+    sc = dict(zip(names, refs[at + 5 + phases :]))
     reduce_barrier(me)
-    for step in reduce_steps(me, phases, source, out, sc, None):
+    small = small_steps(me, mods, images, small_ref, ada_ref, every_ref, bias_ref, cond_ref, sc)
+    small[0]()
+    for step in reduce_steps(me, phases, source, out, sc, small[1:]):
         step()
 
 
-def reduce_grads(grads, collective_id):
+def reduce_last(grads, mod_part, bias_part, ada_weight, images, collective_id):
     phases = len(grads)
     half, width = grads[0][0].shape[-2:]
     counts = tuple(len(phase) for phase in grads)
-    scratch = reduce_scratch(phases, half, width)
-    return pl.pallas_call(
-        partial(reduce_kernel, counts, tuple(scratch)),
-        out_shape=[jax.ShapeDtypeStruct((4, 2, half, width), jnp.bfloat16)] * phases,
-        in_specs=[pl.BlockSpec(memory_space=pl.ANY)] * sum(counts),
-        out_specs=[pl.BlockSpec(memory_space=pl.ANY)] * phases,
+    mod_rows, bias_rows = mod_part.shape[0], bias_part.shape[0]
+    cond_cols = -(-ada_weight.shape[0] // 128) * 128
+    scratch = dict(**reduce_scratch(phases, half, width), **small_scratch(mod_rows, bias_rows, 8, cond_cols))
+    any_, vmem = pl.BlockSpec(memory_space=pl.ANY), pl.BlockSpec(memory_space=pltpu.VMEM)
+    outs = pl.pallas_call(
+        partial(reduce_last_kernel, counts, ada_weight.shape[1], images, tuple(scratch)),
+        out_shape=[jax.ShapeDtypeStruct((4, 2, half, width), jnp.bfloat16)] * phases
+        + [
+            jax.ShapeDtypeStruct((NB, 4, mod_rows, 128), jnp.bfloat16),
+            jax.ShapeDtypeStruct((bias_rows, 128), jnp.float32),
+            jax.ShapeDtypeStruct((NB, 8, cond_cols), jnp.float32),
+        ],
+        in_specs=[any_] * sum(counts) + [vmem] * 2,
+        out_specs=[any_] * phases + [vmem] * 3,
         scratch_shapes=list(scratch.values()),
         compiler_params=pltpu.CompilerParams(
             collective_id=collective_id, has_side_effects=True, vmem_limit_bytes=56 * 2**20
         ),
-        name="reduce_grads",
-    )(*[unit for phase in grads for unit in phase])
+        name="reduce_last",
+    )(*[unit for phase in grads for unit in phase], jnp.concatenate([mod_part, bias_part]), ada_weight)
+    return outs[:phases], outs[phases], outs[phases + 1], outs[phases + 2]
+
+
+def reduce_attend_kernel(counts, band_slots, names, *refs):
+    me = compass()
+    phases = len(counts)
+    at = sum(counts)
+    source = reduce_sources(counts, refs)
+    count_ref, q_ref, own_ref, far_ref, grad_ref, top_ref = refs[at : at + 6]
+    at += 6
+    out = refs[at : at + phases]
+    dq_ref, down_ref, dfar_ref = refs[at + phases : at + phases + 3]
+    sc = dict(zip(names, refs[at + phases + 3 :]))
+    qh, kh, vh, gh, stage, stage_sem = (sc[k] for k in ("qh", "kh", "vh", "gh", "stage", "stage_sem"))
+    rows, width = q_ref.shape
+    heads = qh.shape[0]
+    reduce_barrier(me)
+    steps = reduce_steps(me, phases, source, out, sc)
+    steps[0]()
+    keys, plain, ones = key_tail(count_ref[0], band_slots), flat_tail(0.0), flat_tail(1.0)
+    loads = [(q_ref, 0, qh, 0, ones), (grad_ref, 0, gh, 0, plain)]
+    for row0, ref in ((0, own_ref), (rows, far_ref)):
+        loads += [(ref, 0, kh, row0, keys), (ref, width, vh, row0, plain)]
+
+    def load(i):
+        ref, column = loads[i][:2]
+        return pltpu.make_async_copy(ref.at[:, pl.ds(column, width)], stage.at[i % 2], stage_sem.at[i % 2])
+
+    load(0).start()
+    for i, (ref, column, heads_ref, row0, tail) in enumerate(loads):
+        if i + 1 < len(loads):
+            load(i + 1).start()
+        load(i).wait()
+        pack_heads(stage.at[i % 2], 0, heads_ref, row0, rows, tail)
+    rest = steps[1:]
+
+    @pl.loop(0, heads)
+    def _(h):
+        attend_head(h, qh, kh, vh, gh, top_ref)
+        for i, step in enumerate(rest[:heads]):
+            pl.when(h == i)(step)
+
+    stores = [(qh, 0, dq_ref, 0)]
+    for row0, ref in ((0, down_ref), (rows, dfar_ref)):
+        stores += [(kh, row0, ref, 0), (vh, row0, ref, width)]
+
+    def store(i):
+        ref, column = stores[i][2:]
+        return pltpu.make_async_copy(stage.at[i % 2], ref.at[:, pl.ds(column, width)], stage_sem.at[i % 2])
+
+    for i, (heads_ref, row0, ref, column) in enumerate(stores):
+        if i >= 2:
+            store(i - 2).wait()
+        unpack_heads(heads_ref, row0, rows, stage.at[i % 2], 0)
+        store(i).start()
+    for i in (len(stores) - 2, len(stores) - 1):
+        store(i).wait()
+    for step in rest[heads:]:
+        step()
+
+
+def reduce_attend(grads, count, query, own, far, grad, top, band_slots, collective_id):
+    phases = len(grads)
+    half, width = grads[0][0].shape[-2:]
+    counts = tuple(len(phase) for phase in grads)
+    rows = query.shape[0]
+    heads = width // HEAD_DIM
+    bf = jnp.bfloat16
+    scratch = reduce_scratch(phases, half, width)
+    scratch.update(
+        qh=pltpu.VMEM((heads, rows, LANES), bf),
+        kh=pltpu.VMEM((heads, 2 * rows, LANES), bf),
+        vh=pltpu.VMEM((heads, 2 * rows, LANES), bf),
+        gh=pltpu.VMEM((heads, rows, LANES), bf),
+        stage=pltpu.VMEM((2, rows, width), bf),
+        stage_sem=pltpu.SemaphoreType.DMA((2,)),
+    )
+    any_, vmem = pl.BlockSpec(memory_space=pl.ANY), pl.BlockSpec(memory_space=pltpu.VMEM)
+    smem = pl.BlockSpec(memory_space=pltpu.SMEM)
+    outs = pl.pallas_call(
+        partial(reduce_attend_kernel, counts, band_slots, tuple(scratch)),
+        out_shape=[jax.ShapeDtypeStruct((4, 2, half, width), bf)] * phases
+        + [
+            jax.ShapeDtypeStruct((rows, width), bf),
+            jax.ShapeDtypeStruct((rows, 2 * width), bf),
+            jax.ShapeDtypeStruct((rows, 2 * width), bf),
+        ],
+        in_specs=[any_] * sum(counts) + [smem] + [any_] * 4 + [vmem],
+        out_specs=[any_] * (phases + 3),
+        scratch_shapes=list(scratch.values()),
+        compiler_params=pltpu.CompilerParams(
+            collective_id=collective_id, has_side_effects=True, vmem_limit_bytes=60 * 2**20
+        ),
+        name="reduce_attend",
+    )(*[unit for phase in grads for unit in phase], count, query, own, far, grad, top)
+    return outs[:phases], outs[phases], outs[phases + 1], outs[phases + 2]
 
 
 def normalize(values):
@@ -659,6 +875,13 @@
         return piece
     groups = [[rank + 8 * group for group in range(dp_count // 8)] for rank in range(8)]
     return lax.psum(piece.astype(jnp.float32), "dp", axis_index_groups=groups)
+
+
+def every_group(piece, dp_count):
+    if dp_count == 8:
+        return piece[None]
+    groups = [[rank + 8 * group for group in range(dp_count // 8)] for rank in range(8)]
+    return lax.all_gather(piece, "dp", axis_index_groups=groups)
 
 
 def own_piece(vector, count, band_place):
@@ -711,6 +934,7 @@
         [
             share,
             jnp.broadcast_to(biases.astype(jnp.float32), (images, bias_count)),
+            condition_f,
             patch_grid.astype(jnp.float32),
         ],
         1,
@@ -735,6 +959,8 @@
         pieces.append(notes[:, at : at + piece.shape[0]].reshape(-1))
         at += piece.shape[0]
     query_bias_full, value_bias_full, proj_bias_full, inner_bias_full, outer_bias_full = pieces
+    condition_here = notes[0, at : at + width]
+    at += width
     grid_rows = notes[0, at].astype(jnp.int32)
     grid_cols = notes[0, at + 1].astype(jnp.int32)
 
@@ -789,7 +1015,6 @@
         rows_dot(mlp_in, grad_pre[:, t * width : (t + 1) * width]).astype(jnp.bfloat16).reshape(blocks)
         for t in range(4)
     ]
-    outer_sum, inner_sum = reduce_grads([[grad_outer], grad_inner], 1)
     grad_inner_bias = jnp.sum(grad_pre.astype(jnp.float32), 0)
     grad_mlp_in = lanes_dot(grad_pre, inner_full)
     grad_shift_two = jnp.sum(grad_mlp_in, 0)
@@ -800,8 +1025,9 @@
     grad_proj = rows_dot(mixed_rows, grad_attended).astype(jnp.bfloat16)
     grad_proj_bias = jnp.sum(grad_attended.astype(jnp.float32), 0)
     grad_mixed = lanes_dot(grad_attended, proj_full).astype(jnp.bfloat16)
-    grad_query, own_terms, far_terms = attend_back(
-        valid_count, query_rows, key_value, other_key_value, grad_mixed, tops, band_slots
+    (outer_sum, inner_sum), grad_query, own_terms, far_terms = reduce_attend(
+        [[grad_outer], grad_inner], valid_count, query_rows, key_value, other_key_value, grad_mixed, tops,
+        band_slots, 1,
     )
     other_terms = lax.ppermute(far_terms, both, siblings)
     grad_key_value = (own_terms.astype(jnp.float32) + other_terms.astype(jnp.float32)).astype(
@@ -812,7 +1038,6 @@
         rows_dot(attn_in, part).astype(jnp.bfloat16).reshape(blocks)
         for part in (grad_query, grad_key_value[:, :width], grad_key_value[:, width:])
     ]
-    (first_sum,) = reduce_grads([grad_first + [grad_proj.reshape(blocks)]], 2)
     grad_attn_in = lanes_dot(grad_qkv, qkv_full)
     grad_query_bias = jnp.sum(grad_query.astype(jnp.float32), 0)
     grad_value_bias = jnp.sum(grad_key_value[:, width:].astype(jnp.float32), 0)
@@ -826,14 +1051,24 @@
     part_mod = jnp.concatenate(
         [grad_shift_one, grad_scale_one, grad_gate_one, grad_shift_two, grad_scale_two, grad_gate_two]
     )
-    grad_mod = (part_mod + lax.ppermute(part_mod, both, siblings)).astype(jnp.bfloat16)
-    every_mod = lax.all_gather(grad_mod, both, axis=0).reshape(dp_count // 2, 2, band_count, -1)
-    every_mod = every_mod[:, 0].reshape(dp_count * images, -1)
-    every_activated = lax.all_gather(own_activated, "dp", axis=0, tiled=True)
+    part_mod = jnp.concatenate([part_mod, 0.5 * condition_here]).reshape(-1, 128)
+    part_mod = jnp.pad(part_mod, ((0, -part_mod.shape[0] % 16), (0, 0)))
+    part_bias = jnp.concatenate(
+        [grad_query_bias, grad_value_bias, grad_proj_bias, grad_inner_bias, grad_outer_bias]
+    ).reshape(-1, 128)
+    (first_sum,), every, bias_grads, grad_act = reduce_last(
+        [grad_first + [grad_proj.reshape(blocks)]], part_mod, part_bias, ada_weight, images, 2
+    )
+    every = every_group(every, dp_count)
+    bias_grads = over_groups(bias_grads, dp_count).reshape(-1)
+    every = jnp.swapaxes(every, 1, 2).reshape(dp_count * images, -1)
+    every_mod = every[:, :mod_count]
+    every_condition = every[:, mod_count : mod_count + width]
+    every_activated = jax.nn.silu(every_condition.astype(jnp.float32)).astype(jnp.bfloat16)
+    every_activated = lax.dynamic_slice_in_dim(every_activated, band * part_rows, part_rows, 1)
     grad_ada = rows_dot(every_activated, every_mod)
     grad_ada_bias = own_piece(jnp.sum(every_mod.astype(jnp.float32), 0), ada_bias.shape[0], band)
-    own_mod = lax.dynamic_slice_in_dim(every_mod, images * dp, images, 0)
-    grad_act = lax.all_gather(lanes_dot(own_mod, ada_weight), "band", axis=1, tiled=True)
+    grad_act = jnp.swapaxes(grad_act[:, :images, :part_rows], 0, 1).reshape(images, width)
     grad_condition = jax.vjp(jax.nn.silu, condition_f)[1](grad_act)[0]
 
     def side_by_side(units):
@@ -847,12 +1082,6 @@
         proj=first_sum[3].reshape(part_rows, width).astype(jnp.float32),
         inner=side_by_side([inner_sum[t] for t in range(4)]),
         outer=outer_sum.reshape(4 * part_rows, width).astype(jnp.float32),
-    )
-    bias_grads = lax.psum(
-        jnp.concatenate(
-            [grad_query_bias, grad_value_bias, grad_proj_bias, grad_inner_bias, grad_outer_bias]
-        ),
-        both,
     )
     bias_parts = []
     at = 0

time: 887 us -> 784 us (0.88)
  the two profiles are of different devices: /device:TPU:0 before, /device:TPU:1 now
where the time goes in v3:
time: 784 us; the launch traced here: 777 us
  Pallas kernels  476 us (61%)
  matrix products  143 us (18%)
  local copies, waits for them, and re-layouts  55.4 us (7%)
  other arithmetic  47.1 us (6%)
  waiting for transfers between devices  32.9 us (4%)
  starting transfers between devices  18.6 us (2%)
    pallas_call x1, Pallas kernels, reduce_attend(): pl.pallas_call(partial(reduce_attend_kernel, counts, band_slots, tuple(sc...  173 us
    pallas_call x1, Pallas kernels, gather_weights(): pl.pallas_call(functools.partial(gather_kernel, width), out_shape=[jax.Sh...  171 us
    pallas_call x1, Pallas kernels, reduce_last(): pl.pallas_call(partial(reduce_last_kernel, counts, ada_weight.shape[1], i...  93.3 us
    dot_general x10, matrix products, rows_dot(): lax.dot_general(left, right, (((0,), (0,)), ((), ())), preferred_element_...  47.2 us
    dot_general x4, matrix products, lanes_dot(): lax.dot_general(left, right, (((1,), (1,)), ((), ())), preferred_element_...  43.4 us
    pallas_call x1, Pallas kernels, attend(): pl.pallas_call(partial(attend_kernel, band_slots), out_shape=[jax.ShapeDt...  38.6 us
    ppermute x4, waiting for transfers between devices, send_home(): lax.ppermute(part, ('dp', 'band'), perm)  32.9 us
    dot_general x1, matrix products, body(): jnp.dot(hidden_act, outer_full, preferred_element_type=jnp.float32)  18.9 us
  transfers between devices with their start and end apart: 6, of which 4 were waited for; matrix products, arithmetic and copies ran while one was open for 4% of the time, Pallas kernels for 0%

profile of v3, /device:TPU:1, one launch (start us, length us, event | category | flops | bytes accessed | tf_op | source)
XLA Modules:
  0.0 776.7 jit_solution(11244632338948841487)
XLA Ops:
  2.7 3.5 concatenate.58
  7.3 3.0 convolution_add_fusion
  13.2 171.1 %gather_weights.1 = (bf16[4,2,144,4608]{3,2,1,0:T(8,128)(2,1)}, bf16[4,2,144,4608]{3,2,1,0:T(8,128)(2,1)}, bf16[4,4,2,144,1152]{4,3,2,1,0:T(8,128)(2,1)}, bf16[2...) custom-call(bf16[2,144,4608]{2,1,0:T(8,128)(2,1)S(1)} %bitcast.111, ...), custom_call_target="tpu_custom_call" | custom-call | tf_op jit(solution)/shard_map/gather_weights/pallas_call | solution.py:166
  192.7 2.8 fusion.28
  195.5 2.7 copy.43
  198.2 2.5 fusion.26
  201.3 2.6 convert_reduce_fusion.1
  207.8 3.9 add_convert_fusion.4
  212.8 7.4 fusion.9
  220.5 2.7 copy-done.14
  235.7 38.6 %attend.1 = (bf16[512,1152]{1,0:T(8,128)(2,1)S(1)}, f32[16,8,512]{2,1,0:T(8,128)S(1)}) custom-call(s32[1]{0:T(128)} %bitcast.6.count_ref.refs_5_, bf16[512,1152]{1,0:T(8,128)(2,1)S(1)} %fusion.15.q_ref.refs_6_, bf16[512,2304]{1,0:T(8,128)(2,1)S(1)} %fusion.11.own_ref.refs_7_, bf16[512,2304]{1,0:T(8,128)(2,1)} %collective-permute-done.far_ref.refs_8_), custom_call_target="tpu_custom_call" | custom-call | flops 2415919104 | bytes 9437184 | tf_op jit(solution)/shard_map/attend/pallas_call | solution.py:269
  274.4 5.6 fusion.56
  281.1 13.0 %fusion.64 = f32[512,4608]{1,0:T(8,128)} fusion(bf16[512,1152]{0,1:T(8,128)(2,1)S(1)} %add_convert_fusion.3, bf16[1152,4608]{1,0:T(8,128)(2,1)} %bitcast.117), kind=kOutput, calls=%fused_computation.182 | convolution fusion | flops 5435817984 | bytes 21233664 | tf_op jit(solution)/shard_map/dot_general | solution.py:995
  294.2 17.8 %convert_reduce_fusion = (f32[4608]{0:T(1024)}, bf16[512,4608]{1,0:T(8,128)(2,1)}) fusion(f32[512,4608]{1,0:T(8,128)} %fusion.64, f32[4608]{0:T(1024)S(1)} %copy-done.41, bf16[512,1152]{1,0:T(8,128)(2,1)} %bitcast.144, bf16[4608,1152]{1,0:T(8,128)(2,1)} %bitcast.170), kind=kOutput, calls=%fused_computation.10 | convolution fusion | flops 5490077184 | bytes 25989120 | tf_op jit(solution)/shard_map/dot_general | solution.py:230
  311.9 10.2 %fusion.63 = (f32[1152]{0:T(1024)}, f32[512,1152]{1,0:T(8,128)}) fusion(bf16[512,4608]{1,0:T(8,128)(2,1)} %get-tuple-element.85, bf16[1152,4608]{1,0:T(8,128)(2,1)S(1)} %bitcast.120), kind=kOutput, calls=%fused_computation.181 | convolution fusion | flops 5436406784 | bytes 17699328 | tf_op jit(solution)/shard_map/dot_general | solution.py:230
  322.1 4.6 convolution_convert_fusion.5
  326.7 3.2 convolution_convert_fusion.6
  329.9 3.2 convolution_convert_fusion.7
  333.1 3.2 convolution_convert_fusion.8
  336.3 3.1 copy.47
  339.5 3.3 multiply_reduce_fusion.1
  343.9 14.0 %convolution_convert_fusion = bf16[4608,1152]{1,0:T(8,128)(2,1)} fusion(f32[512,1152]{0,1:T(8,128)S(1)} %copy-done.18, f32[512]{0:T(512)S(1)} %copy-done.48, f32[1152]{0:T(1024)S(1)} %copy-done.37, f32[512,4608]{1,0:T(8,128)} %fusion.64, f32[4608]{0:T(1024)S(1)} %copy-done.42), kind=kOutput, calls=%fused_computation | convolution fusion | flops 5466488832 | bytes 22438400 | tf_op jit(solution)/shard_map/dot_general | solution.py:234
  358.0 18.9 %convert_reduce_fusion.2 = (f32[1152]{0:T(1024)}, bf16[512,1152]{0,1:T(8,128)(2,1)}, f32[512,1152]{0,1:T(8,128)}, f32[1152]{0:T(1024)}, bf16[512,1152]{0,1:T(8,128)(2,1)S(1)}) fusion(f32[1152]{0:T(1024)} %get-tuple-element.128, f32[512]{0:T(512)} %broadcast_multiply_fusion.2, f32[512,1152]{0,1:T(8,128)S(1)} %get-tuple-element.90, f32[512]{0:T(512)} %copy-done.34, ...), kind=kOutput, calls=%fused_computation.42 | convolution fusion | flops 5470615552 | bytes 31906816 | tf_op jit(solution)/shard_map/dot_general | solution.py:997
  376.9 5.1 convolution_convert_fusion.9.refs_9_
  382.0 3.3 convolution_convert_fusion.1
  385.4 173.3 %reduce_attend.1 = (bf16[4,2,144,1152]{3,2,1,0:T(8,128)(2,1)}, bf16[4,2,144,1152]{3,2,1,0:T(8,128)(2,1)}, bf16[512,1152]{1,0:T(8,128)(2,1)}, bf16[512,2304]{1,0:T(8,128)(2,1)}, bf16[512,2304]{1,0:T(8,128)(2,1)}) custom-call(bf16[4,4,2,144,1152]{4,3,2,1,0:T(8,128)(2,1)} %bitcast.125, bf16[4,2,144,1152]{3,2,1,0:T(8,128)(2,1)} %bitcast.136, ...), custom_call_target="tpu_custom_call" | custom-call | tf_op jit(solution)/shard_map/reduce_attend/pallas_call | solution.py:802
  558.8 4.6 convolution_convert_fusion.4
  563.4 2.9 bitcast_convert_fusion
  568.0 2.1 collective-permute-start.2
  571.8 2.9 maximum_convert_fusion
  574.8 7.3 collective-permute-done.1
  582.1 12.6 %collective-permute-done.2 = bf16[256,1152]{0,1:T(8,128)(2,1)S(1)} collective-permute-done((bf16[256,1152]{0,1:T(8,128)(2,1)S(1)}, bf16[256,1152]{0,1:T(8,128)(2,1)S(1)}, u32[]{:S(2)}, u32[]{:S(2)}) %collective-permute-start.2) | collective-permute-done | bytes 589856 | tf_op jit(solution)/shard_map/ppermute | solution.py:857
  596.9 2.3 add_convert_fusion
  599.4 10.3 %fusion.62 = (f32[1152]{0:T(1024)}, f32[512,1152]{1,0:T(8,128)}) fusion(bf16[1152,4608]{1,0:T(8,128)(2,1)} %bitcast.169, bf16[512,2304]{1,0:T(8,128)(2,1)S(1)} %add_convert_fusion, bf16[512,1152]{1,0:T(8,128)(2,1)S(1)} %copy-done.25), kind=kOutput, calls=%fused_computation.180 | convolution fusion | flops 4084530176 | bytes 13865472 | tf_op jit(solution)/shard_map/dot_general | solution.py:230
  609.7 3.2 convolution_convert_fusion.2
  612.9 3.2 convolution_convert_fusion.3
  616.1 3.3 copy.48
  619.4 3.3 multiply_reduce_fusion.3
  623.4 3.4 multiply_reduce_fusion.2
  626.8 5.3 concatenate.73
  633.6 93.3 %reduce_last.1 = (bf16[4,2,144,1152]{3,2,1,0:T(8,128)(2,1)}, bf16[4,4,64,128]{3,2,1,0:T(8,128)(2,1)}, f32[72,128]{1,0:T(8,128)}, f32[4,8,384]{2,1,0:T(8,128)}) custom-call(bf16[4,2,144,1152]{3,2,1,0:T(8,128)(2,1)} %bitcast.127, bf16[4,2,144,1152]{3,2,1,0:T(8,128)(2,1)} %bitcast.129, bf16[4,2,144,1152]{3,2,1,0:T(8,128)(2,1)} %bitcast.128, ...), custom_call_target="tpu_custom_call" | custom-call | tf_op jit(solution)/shard_map/reduce_last/pallas_call | solution.py:707
  729.0 1.9 fusion.58
  731.2 4.6 fusion.31
  738.6 12.9 %collective-permute-start.4 = (bf16[256,1152]{0,1:T(8,128)(2,1)S(1)}, bf16[256,1152]{0,1:T(8,128)(2,1)S(1)}, u32[]{:S(2)}, u32[]{:S(2)}) collective-permute-start(bf16[256,1152]{0,1:T(8,128)(2,1)S(1)} %get-tuple-element.107), channel_id=1, source_target_pairs={{0,1},{1,0},{2,5},{3,4},{4,3},{5,2},{6,7},{7,6},{8,9},{9,8},{10,13... | collective-permute-start | bytes 1769480 | tf_op jit(solution)/shard_map/ppermute | solution.py:857
  758.9 2.2 maximum_convert_fusion.1
  761.1 4.2 collective-permute-done.4
  765.2 8.8 %collective-permute-done.5 = bf16[256,1152]{0,1:T(8,128)(2,1)S(1)} collective-permute-done((bf16[256,1152]{0,1:T(8,128)(2,1)S(1)}, bf16[256,1152]{0,1:T(8,128)(2,1)S(1)}, u32[]{:S(2)}, u32[]{:S(2)}) %collective-permute-start.5) | collective-permute-done | bytes 589856 | tf_op jit(solution)/shard_map/ppermute | solution.py:857
  774.2 2.0 copy.54
  (195 shorter events, 54.1 us)
Async XLA Ops:
  6.3 4.1 copy-start.20
  7.3 4.6 copy-start.4
  7.3 4.6 copy-start.5
  184.4 4.9 copy-start.26
  198.2 3.1 copy-start.12
  198.2 3.1 copy-start.13
  223.2 12.5 %copy-start = (bf16[512,2304]{1,0:T(8,128)(2,1)}, bf16[512,2304]{1,0:T(8,128)(2,1)S(1)}, u32[]{:S(2)}) copy-start(bf16[512,2304]{1,0:T(8,128)(2,1)S(1)} %fusion.11.own_ref.refs_7_) | copy-start | bytes 7077892
  223.2 12.5 %collective-permute-start = (bf16[512,2304]{1,0:T(8,128)(2,1)S(1)}, bf16[512,2304]{1,0:T(8,128)(2,1)}, u32[]{:S(2)}, u32[]{:S(2)}) collective-permute-start(bf16[512,2304]{1,0:T(8,128)(2,1)S(1)} %fusion.11.own_ref.refs_7_), channel_id=1, source_target_pairs={{0,4},{1,5},{2,6},{3,7},{4,0},{5,1},{6,2},{7,3},{8,12},{9,13},{10,... | collective-permute-start | bytes 7077896 | tf_op jit(solution)/shard_map/ppermute | solution.py:988
  235.6 38.7 %copy-start.1 = (bf16[512,1152]{1,0:T(8,128)(2,1)}, bf16[512,1152]{1,0:T(8,128)(2,1)S(1)}, u32[]{:S(2)}) copy-start(bf16[512,1152]{1,0:T(8,128)(2,1)S(1)} %fusion.15.q_ref.refs_6_) | copy-start | bytes 3538948
  235.7 38.7 %copy-start.9 = (f32[512,1152]{0,1:T(8,128)S(1)}, f32[512,1152]{0,1:T(8,128)}, u32[]{:S(2)}) copy-start(f32[512,1152]{0,1:T(8,128)} %get-tuple-element.92) | copy-start | bytes 7077892
  235.7 38.7 %copy-start.45 = (f32[1152]{0:T(1024)S(1)}, f32[1152]{0:T(1024)}, u32[]{:S(2)}) copy-start(f32[1152]{0:T(1024)} %get-tuple-element.128) | copy-start | bytes 13828
  235.7 38.7 %copy-start.46 = (f32[1152]{0:T(1024)S(1)}, f32[1152]{0:T(1024)}, u32[]{:S(2)}) copy-start(f32[1152]{0:T(1024)} %add.252) | copy-start | bytes 13828
  274.3 5.6 copy-start.6
  274.4 5.6 copy-start.7
  280.3 13.8 %copy-start.43 = (f32[512]{0:T(512)}, f32[512]{0:T(512)S(1)}, u32[]{:S(2)}) copy-start(f32[512]{0:T(512)S(1)} %add_rsqrt_fusion) | copy-start | bytes 6148
  281.1 13.0 %copy-start.41 = (f32[4608]{0:T(1024)S(1)}, f32[4608]{0:T(1024)}, u32[]{:S(2)}) copy-start(f32[4608]{0:T(1024)} %add.260) | copy-start | bytes 55300
  281.1 30.8 %slice-start = ((s8[10616832]{0:T(1024)(128)(4,1)}), s8[4194304]{0:T(1024)(128)(4,1)S(1)}, s32[]{:S(2)}) async-start(s8[10616832]{0:T(1024)(128)(4,1)} %bitcast.118), calls=%async_computation | async-start | bytes 8388608
  294.1 17.8 %slice-start.1 = ((s8[10616832]{0:T(1024)(128)(4,1)}), s8[4194304]{0:T(1024)(128)(4,1)S(1)}, s32[]{:S(2)}) async-start(s8[10616832]{0:T(1024)(128)(4,1)} %bitcast.118), calls=%async_computation.1 | async-start | bytes 8388608
  294.1 17.8 %slice-start.2 = ((s8[10616832]{0:T(1024)(128)(4,1)}), s8[2228224]{0:T(1024)(128)(4,1)S(1)}, s32[]{:S(2)}) async-start(s8[10616832]{0:T(1024)(128)(4,1)} %bitcast.118), calls=%async_computation.2 | async-start | bytes 4456448
  322.1 4.6 copy-start.49
  336.3 3.1 copy-start.35
  336.3 3.1 copy-start.44
  339.5 4.5 copy-start.18
  339.5 4.5 copy-start.37
  339.5 4.5 copy-start.42
  339.5 4.5 copy-start.48
  376.9 5.1 copy-start.8
  376.9 5.2 copy-start.50
  385.4 173.4 %copy-start.22 = (bf16[512,1152]{0,1:T(8,128)(2,1)S(1)}, bf16[512,1152]{0,1:T(8,128)(2,1)}, u32[]{:S(2)}) copy-start(bf16[512,1152]{0,1:T(8,128)(2,1)} %copy-done.21) | copy-start | bytes 3538948
  558.7 37.7 %collective-permute-start.3 = (bf16[512,2304]{1,0:T(8,128)(2,1)}, bf16[512,2304]{1,0:T(8,128)(2,1)}, u32[]{:S(2)}, u32[]{:S(2)}) collective-permute-start(bf16[512,2304]{1,0:T(8,128)(2,1)} %get-tuple-element.41), channel_id=1, source_target_pairs={{0,4},{1,5},{2,6},{3,7},{4,0},{5,1},{6,2},{7,3},{8,12},{9,13},{10,... | collective-permute-start | bytes 7077896 | tf_op jit(solution)/shard_map/ppermute | solution.py:1032
  558.8 4.6 copy-start.16
  563.4 6.7 copy-start.24
  566.3 5.3 copy-start.15
  566.4 15.7 %collective-permute-start.1 = (bf16[256,1152]{0,1:T(8,128)(2,1)S(1)}, bf16[256,1152]{0,1:T(8,128)(2,1)S(1)}, u32[]{:S(2)}, u32[]{:S(2)}) collective-permute-start(bf16[256,1152]{0,1:T(8,128)(2,1)S(1)} %get-tuple-element.111), channel_id=1, source_target_pairs={{0,1},{1,0},{2,5},{3,4},{4,3},{5,2},{6,7},{7,6},{8,9},{9,8},{10,13... | collective-permute-start | bytes 1769480 | tf_op jit(solution)/shard_map/ppermute | solution.py:857
  568.0 26.7 %collective-permute-start.2 = (bf16[256,1152]{0,1:T(8,128)(2,1)S(1)}, bf16[256,1152]{0,1:T(8,128)(2,1)S(1)}, u32[]{:S(2)}, u32[]{:S(2)}) collective-permute-start(bf16[256,1152]{0,1:T(8,128)(2,1)S(1)} %get-tuple-element.112), channel_id=1, source_target_pairs={{0,0},{1,1},{2,4},{3,5},{4,2},{5,3},{6,6},{7,7},{8,8},{9,9},{10,12... | collective-permute-start | bytes 1769480 | tf_op jit(solution)/shard_map/ppermute | solution.py:857
  599.4 10.3 %copy-start.23 = (bf16[512,1152]{0,1:T(8,128)(2,1)S(1)}, bf16[512,1152]{0,1:T(8,128)(2,1)}, u32[]{:S(2)}) copy-start(bf16[512,1152]{0,1:T(8,128)(2,1)} %copy-done.21) | copy-start | bytes 3538948
  616.1 3.3 copy-start.10
  616.1 3.3 copy-start.32
  616.1 3.3 copy-start.33
  616.1 6.6 copy-start.30
  619.4 3.3 copy-start.47
  619.4 3.4 copy-start.40
  619.4 3.4 copy-start.39
  619.4 4.0 copy-start.11
  619.4 4.0 copy-start.19
  731.2 6.7 copy-start.29
  738.6 26.6 %collective-permute-start.4 = (bf16[256,1152]{0,1:T(8,128)(2,1)S(1)}, bf16[256,1152]{0,1:T(8,128)(2,1)S(1)}, u32[]{:S(2)}, u32[]{:S(2)}) collective-permute-start(bf16[256,1152]{0,1:T(8,128)(2,1)S(1)} %get-tuple-element.107), channel_id=1, source_target_pairs={{0,1},{1,0},{2,5},{3,4},{4,3},{5,2},{6,7},{7,6},{8,9},{9,8},{10,13... | collective-permute-start | bytes 1769480 | tf_op jit(solution)/shard_map/ppermute | solution.py:857
  751.5 22.5 %collective-permute-start.5 = (bf16[256,1152]{0,1:T(8,128)(2,1)S(1)}, bf16[256,1152]{0,1:T(8,128)(2,1)S(1)}, u32[]{:S(2)}, u32[]{:S(2)}) collective-permute-start(bf16[256,1152]{0,1:T(8,128)(2,1)S(1)} %get-tuple-element.108), channel_id=1, source_target_pairs={{0,0},{1,1},{2,4},{3,5},{4,2},{5,3},{6,6},{7,7},{8,8},{9,9},{10,12... | collective-permute-start | bytes 1769480 | tf_op jit(solution)/shard_map/ppermute | solution.py:857
  (12 other events, 22.8 us)

commit v4 on v3

--- a/solution.py
+++ b/solution.py
@@ -10,175 +10,23 @@
 
 HEAD_DIM = 72
 
+
 MESH = pl.DeviceIdType.MESH
-NB=4
-def place():
-    dp = lax.axis_index("dp"); band = lax.axis_index("band")
-    return dp, band
-def gather_kernel(width, qp_in, inner_in, outer_in, tok_in, cot_in, mod_in,
-                  qp_out, inner_out, outer_out, tok_out, cot_out, mod_out,
-                  z_send, z_recv, a_send, a_recv, b_send, b_recv, c_send, c_recv,
-                  t_send, t_recv, m_send, m_recv, local_sem, h_sem, bq, bi, bo, bt):
-    dp, band = place()
-    core = lax.rem(dp, 2); px = lax.rem(dp // 2, 2); py = lax.rem(dp // 4, 2)
-    base = dp - core
-    kind = py * 2 + px
-    sib = dp + 1 - 2 * core
-    xdp = dp + 2 - 4 * px
-    ydp = dp + 4 - 8 * py
-    dev = lambda d, b: {"dp": d, "band": b}
-    barrier = pltpu.get_barrier_semaphore()
-    peers = [dev(xdp, band), dev(ydp, band), dev(sib, band)]
-    for k in range(1, NB):
-        ob = lax.rem(band + k, NB)
-        peers += [dev(dp, ob), dev(sib, ob)]
-    for q in peers:
-        pl.semaphore_signal(barrier, inc=1, device_id=q, device_id_type=MESH)
-    pl.semaphore_wait(barrier, len(peers))
-
-    def rc(src, dst, ss, rs, to):
-        return pltpu.make_async_remote_copy(src_ref=src, dst_ref=dst, send_sem=ss, recv_sem=rs, device_id=to, device_id_type=MESH)
-    ins = (qp_in, inner_in, outer_in); outs = (qp_out, inner_out, outer_out)
-    def cols(t, n=1):
-        return pl.ds(pl.multiple_of(t * width, 128), n * width)
-    def unit(ph, b, t, h):
-        return outs[ph].at[b, t, h] if ph == 2 else outs[ph].at[b, h, :, cols(t)]
-    def own(ph):
-        return ins[ph].at[kind, core] if ph == 2 else ins[ph].at[core, :, cols(kind)]
-    def pair(ph, b, h, y):
-        return outs[ph].at[b, pl.ds(2 * y, 2), h] if ph == 2 else outs[ph].at[b, h, :, cols(2 * y, 2)]
-    def row(ph, b, h):
-        return outs[ph].at[b, :, h] if ph == 2 else outs[ph].at[b, h]
-    sends = []
-    def go(c):
-        c.start(); sends.append(c)
-    slot = lax.rem(band, 2)
-    def move(which, src, dst):
-        for i in range(2):
-            to_core = band // 2; to_band = 2 * core + i
-            home = jnp.logical_and(to_core == core, to_band == band)
-            @pl.when(home)
-            def _():
-                pltpu.make_async_copy(src.at[i], bt.at[which], h_sem.at[which]).start()
-                pltpu.make_async_copy(src.at[i], bt.at[which], h_sem.at[which]).wait()
-                pltpu.make_async_copy(bt.at[which], dst.at[slot], t_recv.at[which, slot]).start()
-            @pl.when(jnp.logical_not(home))
-            def _():
-                rc(src.at[i], dst.at[slot], t_send.at[which, i], t_recv.at[which, slot], dev(base + to_core, to_band)).start()
-    def move_wait(which, src, dst):
-        for i in range(2):
-            to_core = band // 2; to_band = 2 * core + i
-            home = jnp.logical_and(to_core == core, to_band == band)
-            @pl.when(jnp.logical_not(home))
-            def _():
-                rc(src.at[i], dst.at[slot], t_send.at[which, i], t_recv.at[which, slot], dev(base + to_core, to_band)).wait_send()
-        for s in range(2):
-            pltpu.make_async_copy(src.at[s], dst.at[s], t_recv.at[which, s]).wait()
-    def mods():
-        for i in range(2):
-            for c in range(2):
-                home = jnp.logical_and(c == core, 2 * core + i == band)
-                @pl.when(home)
-                def _():
-                    pltpu.make_async_copy(mod_in.at[i], mod_out.at[band], m_recv.at[band]).start()
-                @pl.when(jnp.logical_not(home))
-                def _():
-                    rc(mod_in.at[i], mod_out.at[band], m_send.at[i, c], m_recv.at[band], dev(base + c, 2 * core + i)).start()
-    def mods_wait():
-        for i in range(2):
-            for c in range(2):
-                home = jnp.logical_and(c == core, 2 * core + i == band)
-                @pl.when(jnp.logical_not(home))
-                def _():
-                    rc(mod_in.at[i], mod_out.at[band], m_send.at[i, c], m_recv.at[band], dev(base + c, 2 * core + i)).wait_send()
-        for b in range(NB):
-            pltpu.make_async_copy(mod_in.at[0], mod_out.at[b], m_recv.at[b]).wait()
-    def zstart(ph):
-        for k in (1, 3, 2):
-            ob = lax.rem(band + k, NB)
-            go(rc(own(ph), unit(ph, band, kind, core), z_send.at[ph, k], z_recv.at[ph, k], dev(dp, ob)))
-    mods()
-    move(0, tok_in, tok_out)
-    zstart(0)
-    bounce = (bq, bi, bo)
-    for ph in range(3):
-        pltpu.make_async_copy(ins[ph], bounce[ph], local_sem.at[ph]).start()
-    for ph in range(3):
-        pltpu.make_async_copy(ins[ph], bounce[ph], local_sem.at[ph]).wait()
-        pltpu.make_async_copy(bounce[ph], outs[ph].at[band], local_sem.at[ph]).start()
-    steps = [(ph, k) for ph in range(3) for k in (1, 3, 2)]
-    n = len(steps)
-    frm = lambda k: lax.rem(band + NB - k, NB)
-    other = lambda v: 1 - v
-    for s in range(n + 3):
-        if s < n:
-            ph, k = steps[s]; b = frm(k)
-            u = unit(ph, b, kind, core)
-            rc(u, u, z_send.at[ph, k], z_recv.at[ph, k], dev(dp, band)).wait_recv()
-            go(rc(u, u, a_send.at[s], a_recv.at[s], dev(xdp if s % 2 == 0 else ydp, band)))
-            if k == 3 and ph < 2:
-                zstart(ph + 1)
-            if k == 2 and ph == 2:
-                move(1, cot_in, cot_out)
-        r = s - 1
-        if 0 <= r < n:
-            ph, k = steps[r]; b = frm(k)
-            got = py * 2 + other(px) if r % 2 == 0 else other(py) * 2 + px
-            u = unit(ph, b, got, core)
-            rc(u, u, a_send.at[r], a_recv.at[r], dev(xdp, band)).wait_recv()
-            if r % 2 == 0:
-                v = pair(ph, b, core, py)
-                go(rc(v, v, b_send.at[r, 0], b_recv.at[r, 0], dev(ydp, band)))
-            else:
-                for j in range(2):
-                    v = unit(ph, b, j * 2 + px, core)
-                    go(rc(v, v, b_send.at[r, j], b_recv.at[r, j], dev(xdp, band)))
-        r = s - 2
-        if 0 <= r < n:
-            ph, k = steps[r]; b = frm(k)
-            if r % 2 == 0:
-                v = pair(ph, b, core, other(py))
-                rc(v, v, b_send.at[r, 0], b_recv.at[r, 0], dev(ydp, band)).wait_recv()
-            else:
-                for j in range(2):
-                    v = unit(ph, b, j * 2 + other(px), core)
-                    rc(v, v, b_send.at[r, j], b_recv.at[r, j], dev(xdp, band)).wait_recv()
-            w = row(ph, b, core)
-            go(rc(w, w, c_send.at[r], c_recv.at[r], dev(sib, band)))
-        r = s - 3
-        if 0 <= r < n:
-            ph, k = steps[r]; b = frm(k)
-            w = row(ph, b, other(core))
-            rc(w, w, c_send.at[r], c_recv.at[r], dev(sib, band)).wait_recv()
-    for ph in range(3):
-        pltpu.make_async_copy(bounce[ph], outs[ph].at[band], local_sem.at[ph]).wait()
-    mods_wait()
-    move_wait(0, tok_in, tok_out)
-    move_wait(1, cot_in, cot_out)
-    for c in sends: c.wait_send()
-
-def gather_weights(qp, inner, outer, tok, cot, mod, width):
-    half = qp.shape[0] // 2
-    ff = qp.shape[1]
-    bf = jnp.bfloat16
-    qp = qp.reshape(2, half, ff); inner = inner.reshape(2, half, ff); outer = outer.reshape(4, 2, half, width)
-    D = pltpu.SemaphoreType.DMA
-    outs = pl.pallas_call(
-        functools.partial(gather_kernel, width),
-        out_shape=[jax.ShapeDtypeStruct((NB,) + qp.shape, bf), jax.ShapeDtypeStruct((NB,) + inner.shape, bf),
-                   jax.ShapeDtypeStruct((NB,) + outer.shape, bf),
-                   jax.ShapeDtypeStruct(tok.shape, bf), jax.ShapeDtypeStruct(cot.shape, bf),
-                   jax.ShapeDtypeStruct((NB,) + mod.shape[1:], jnp.float32)],
-        in_specs=[pl.BlockSpec(memory_space=pl.ANY)] * 6,
-        out_specs=[pl.BlockSpec(memory_space=pl.ANY)] * 6,
-        scratch_shapes=[D((3, 4)), D((3, 4)), D((9,)), D((9,)), D((9, 2)), D((9, 2)), D((9,)), D((9,)),
-                        D((2, 2)), D((2, 2)), D((2, 2)), D((4,)), D((3,)), D((2,)),
-                        pltpu.VMEM(qp.shape, bf), pltpu.VMEM(inner.shape, bf), pltpu.VMEM(outer.shape, bf),
-                        pltpu.VMEM((2,) + tok.shape[1:], bf)],
-        compiler_params=pltpu.CompilerParams(collective_id=0, has_side_effects=True, vmem_limit_bytes=32*2**20),
-        name="gather_weights",
-    )(qp, inner, outer, tok, cot, mod)
-    return outs
+NB = 4
+
+
+def normalize(values):
+    average = jnp.mean(values, -1, keepdims=True)
+    centered = values - average
+    variance = jnp.mean(centered * centered, -1, keepdims=True)
+    inverse = lax.rsqrt(variance + 1e-06)
+    return (centered * inverse, inverse)
+
+
+def norm_back(grad_normed, normed, inverse):
+    first = jnp.mean(grad_normed, -1, keepdims=True)
+    second = jnp.mean(grad_normed * normed, -1, keepdims=True)
+    return inverse * (grad_normed - first - normed * second)
 
 
 LANES = 128
@@ -237,54 +85,18 @@
 SCORE_SCALE = HEAD_DIM ** (-0.5)
 
 
-def attend_kernel(band_slots, count_ref, q_ref, own_ref, far_ref, out_ref, top_ref, qh, kh, vh):
-    rows, width = q_ref.shape
-    heads = qh.shape[0]
-    pack_heads(q_ref, 0, qh, 0, rows, flat_tail(1.0))
-    for row0, ref in ((0, own_ref), (rows, far_ref)):
-        pack_heads(ref, 0, kh, row0, rows, key_tail(count_ref[0], band_slots))
-        pack_heads(ref, width, vh, row0, rows, flat_tail(0.0))
-
-    @pl.loop(0, heads)
-    def _(h):
-        for block in range(2):
-            at = pl.ds(block * rows // 2, rows // 2)
-            scores = lanes_dot(kh[h], qh[h, at, :]) * SCORE_SCALE
-            top = jnp.max(scores, 0, keepdims=True)
-            weights = jnp.exp(scores - top)
-            total = jnp.sum(weights, 0, keepdims=True)
-            low = (weights * (1.0 / total)).astype(jnp.bfloat16)
-            mixed = rows_dot(vh[h], low)
-            qh[h, at, :] = jnp.transpose(mixed).astype(jnp.bfloat16)
-            top_ref[h, :, at] = jnp.broadcast_to(top + jnp.log(total), (8, rows // 2))
-
-    unpack_heads(qh, 0, rows, out_ref, 0)
-
-
-def attend(count, query, own, far, band_slots):
-    rows, width = query.shape
-    heads = width // HEAD_DIM
-    bf = jnp.bfloat16
-    vmem = pl.BlockSpec(memory_space=pltpu.VMEM)
-    return pl.pallas_call(
-        partial(attend_kernel, band_slots),
-        out_shape=[
-            jax.ShapeDtypeStruct((rows, width), bf),
-            jax.ShapeDtypeStruct((heads, 8, rows), jnp.float32),
-        ],
-        in_specs=[pl.BlockSpec(memory_space=pltpu.SMEM), vmem, vmem, vmem],
-        out_specs=[vmem, vmem],
-        scratch_shapes=[
-            pltpu.VMEM((heads, rows, LANES), bf),
-            pltpu.VMEM((heads, 2 * rows, LANES), bf),
-            pltpu.VMEM((heads, 2 * rows, LANES), bf),
-        ],
-        compiler_params=pltpu.CompilerParams(vmem_limit_bytes=48 * 2**20),
-        cost_estimate=pl.CostEstimate(
-            flops=8 * rows * rows * width, bytes_accessed=16 * rows * width, transcendentals=2 * heads * rows * rows
-        ),
-        name="attend",
-    )(count, query, own, far)
+def attend_block(h, qh, kh, vh, top_ref):
+    rows = qh.shape[1]
+    for block in range(2):
+        at = pl.ds(block * rows // 2, rows // 2)
+        scores = lanes_dot(kh[h], qh[h, at, :]) * SCORE_SCALE
+        top = jnp.max(scores, 0, keepdims=True)
+        weights = jnp.exp(scores - top)
+        total = jnp.sum(weights, 0, keepdims=True)
+        low = (weights * (1.0 / total)).astype(jnp.bfloat16)
+        mixed = rows_dot(vh[h], low)
+        qh[h, at, :] = jnp.transpose(mixed).astype(jnp.bfloat16)
+        top_ref[h, :, at] = jnp.broadcast_to(top + jnp.log(total), (8, rows // 2))
 
 
 def attend_head(h, qh, kh, vh, gh, top_ref):
@@ -818,18 +630,424 @@
     return outs[:phases], outs[phases], outs[phases + 1], outs[phases + 2]
 
 
-def normalize(values):
-    average = jnp.mean(values, -1, keepdims=True)
-    centered = values - average
-    variance = jnp.mean(centered * centered, -1, keepdims=True)
-    inverse = lax.rsqrt(variance + 1e-06)
-    return (centered * inverse, inverse)
-
-
-def norm_back(grad_normed, normed, inverse):
-    first = jnp.mean(grad_normed, -1, keepdims=True)
-    second = jnp.mean(grad_normed * normed, -1, keepdims=True)
-    return inverse * (grad_normed - first - normed * second)
+GATHER_ORDER = (1, 3, 2)
+MOD_BLOCKS = 6
+BLOCK = 128
+
+
+def forward_scratch(half, ff, width, rows, note_rows, images):
+    bf, f32 = jnp.bfloat16, jnp.float32
+    D = pltpu.SemaphoreType.DMA
+    heads = width // HEAD_DIM
+    V = pltpu.VMEM
+    return dict(
+        qp=V((NB, 2, half, ff), bf), bounce_i=V((2, half, ff), bf), bounce_o=V((4, 2, half, width), bf),
+        bounce_t=V((rows // images, width), bf), tok=V((images, rows // images, width), bf),
+        notes=V((NB, note_rows, 128), f32), vec=V((16, width), f32),
+        residual=V((rows, width), f32), attn_in=V((rows, width), bf), query=V((rows, width), bf),
+        own=V((rows, 2 * width), bf), far=V((rows, 2 * width), bf), mixed=V((rows, width), bf),
+        attended=V((rows, width), f32), mlp_in=V((rows, width), bf), tops=V((heads, 8, rows), f32),
+        qh=V((heads, rows, LANES), bf), kh=V((heads, 2 * rows, LANES), bf), vh=V((heads, 2 * rows, LANES), bf),
+        z_send=D((3, NB)), z_recv=D((3, NB)), a_send=D((9,)), a_recv=D((9,)), b_send=D((9, 2)), b_recv=D((9, 2)),
+        c_send=D((9,)), c_recv=D((9,)), t_send=D((2, 2)), t_recv=D((2, 2)), m_send=D((2, 2)), m_recv=D((NB,)),
+        local=D((4,)), kv_send=D((1,)), kv_recv=D((1,)), done=D((12,)),
+    )
+
+
+def gather_steps(me, width, ins, outs, tok_in, tok_out, cot_in, cot_out, note_in, note_out, sc):
+    dp, band, core, px, py, kind = (me[k] for k in ("dp", "band", "core", "px", "py", "kind"))
+    base = dp - core
+    dev = lambda d, b: {"dp": d, "band": b}
+    here = lambda d: dev(d, band)
+    flip = lambda v: 1 - v
+    order = [(ph, k) for ph in range(3) for k in GATHER_ORDER]
+    sends = []
+
+    def remote(src, dst, ss, rs, to):
+        return pltpu.make_async_remote_copy(
+            src_ref=src, dst_ref=dst, send_sem=ss, recv_sem=rs, device_id=to, device_id_type=MESH
+        )
+
+    def go(make):
+        make().start()
+        sends.append(make)
+
+    def cols(t, n=1):
+        return pl.ds(pl.multiple_of(t * width, 128), n * width)
+
+    def unit(ph, b, t, h):
+        return outs[ph].at[b, t, h] if ph == 2 else outs[ph].at[b, h, :, cols(t)]
+
+    def pair(ph, b, h, y):
+        return outs[ph].at[b, pl.ds(2 * y, 2), h] if ph == 2 else outs[ph].at[b, h, :, cols(2 * y, 2)]
+
+    def row(ph, b, h):
+        return outs[ph].at[b, :, h] if ph == 2 else outs[ph].at[b, h]
+
+    def came(k):
+        return lax.rem(band + NB - k, NB)
+
+    def send_z(ph, k):
+        src = ins[ph].at[kind, core] if ph == 2 else ins[ph].at[core, :, cols(kind)]
+        return remote(
+            src, unit(ph, band, kind, core), sc["z_send"].at[ph, k], sc["z_recv"].at[ph, k],
+            dev(dp, lax.rem(band + k, NB)),
+        )
+
+    def send_a(s):
+        ph, k = order[s]
+        u = unit(ph, came(k), kind, core)
+        return remote(u, u, sc["a_send"].at[s], sc["a_recv"].at[s], here(me["xdp"] if s % 2 == 0 else me["ydp"]))
+
+    def b_copy(s, j, mine):
+        ph, k = order[s]
+        if s % 2 == 0:
+            u = pair(ph, came(k), core, py if mine else flip(py))
+            to = me["ydp"]
+        else:
+            u = unit(ph, came(k), 2 * j + (px if mine else flip(px)), core)
+            to = me["xdp"]
+        return remote(u, u, sc["b_send"].at[s, j], sc["b_recv"].at[s, j], here(to))
+
+    def c_copy(s, mine):
+        ph, k = order[s]
+        u = row(ph, came(k), core if mine else flip(core))
+        return remote(u, u, sc["c_send"].at[s], sc["c_recv"].at[s], here(me["sib"]))
+
+    def z_start(ph):
+        for k in GATHER_ORDER:
+            go(partial(send_z, ph, k))
+
+    def z_wait(s):
+        ph, k = order[s]
+        u = unit(ph, came(k), kind, core)
+        remote(u, u, sc["z_send"].at[ph, k], sc["z_recv"].at[ph, k], here(dp)).wait_recv()
+        go(partial(send_a, s))
+        if k == GATHER_ORDER[1] and ph < 2:
+            z_start(ph + 1)
+        if k == GATHER_ORDER[2] and ph == 2:
+            move(1, cot_in, cot_out, sc["bounce_t"])
+
+    def a_wait(s):
+        ph, k = order[s]
+        got = 2 * py + flip(px) if s % 2 == 0 else 2 * flip(py) + px
+        u = unit(ph, came(k), got, core)
+        remote(u, u, sc["a_send"].at[s], sc["a_recv"].at[s], here(me["xdp"])).wait_recv()
+        for j in range(1 if s % 2 == 0 else 2):
+            go(partial(b_copy, s, j, True))
+
+    def b_wait(s):
+        for j in range(1 if s % 2 == 0 else 2):
+            b_copy(s, j, False).wait_recv()
+        go(partial(c_copy, s, True))
+
+    def c_wait(s):
+        c_copy(s, False).wait_recv()
+
+    slot = lax.rem(band, 2)
+
+    def image_copy(which, src, dst, i):
+        to = dev(base + band // 2, 2 * core + i)
+        return remote(src.at[i], dst.at[slot], sc["t_send"].at[which, i], sc["t_recv"].at[which, slot], to)
+
+    def at_home(i):
+        return jnp.logical_and(band // 2 == core, 2 * core + i == band)
+
+    def move(which, src, dst, bounce=None):
+        for i in range(2):
+
+            @pl.when(at_home(i))
+            def _():
+                if bounce is None:
+                    pltpu.make_async_copy(src.at[i], dst.at[slot], sc["t_recv"].at[which, slot]).start()
+                else:
+                    inward = pltpu.make_async_copy(src.at[i], bounce, sc["local"].at[3])
+                    inward.start()
+                    inward.wait()
+                    pltpu.make_async_copy(bounce, dst.at[slot], sc["t_recv"].at[which, slot]).start()
+
+            @pl.when(jnp.logical_not(at_home(i)))
+            def _():
+                image_copy(which, src, dst, i).start()
+
+    def move_wait(which, src, dst):
+        for i in range(2):
+
+            @pl.when(jnp.logical_not(at_home(i)))
+            def _():
+                image_copy(which, src, dst, i).wait_send()
+
+        for s in range(2):
+            pltpu.make_async_copy(dst.at[s], dst.at[s], sc["t_recv"].at[which, s]).wait()
+
+    def note_copy(i, c):
+        return remote(
+            note_in.at[i], note_out.at[band], sc["m_send"].at[i, c], sc["m_recv"].at[band],
+            dev(base + c, 2 * core + i),
+        )
+
+    def note_home(i, c):
+        return jnp.logical_and(c == core, 2 * core + i == band)
+
+    def begin():
+        for i in range(2):
+            for c in range(2):
+
+                @pl.when(note_home(i, c))
+                def _():
+                    pltpu.make_async_copy(note_in.at[i], note_out.at[band], sc["m_recv"].at[band]).start()
+
+                @pl.when(jnp.logical_not(note_home(i, c)))
+                def _():
+                    note_copy(i, c).start()
+
+        move(0, tok_in, tok_out)
+        z_start(0)
+        for ph, dst in enumerate((outs[0].at[band], sc["bounce_i"], sc["bounce_o"])):
+            pltpu.make_async_copy(ins[ph], dst, sc["local"].at[ph]).start()
+
+    def arrived():
+        for i in range(2):
+            for c in range(2):
+
+                @pl.when(jnp.logical_not(note_home(i, c)))
+                def _():
+                    note_copy(i, c).wait_send()
+
+        for b in range(NB):
+            pltpu.make_async_copy(note_in.at[0], note_out.at[b], sc["m_recv"].at[b]).wait()
+        move_wait(0, tok_in, tok_out)
+
+    def place():
+        for ph, dst in ((1, sc["bounce_i"]), (2, sc["bounce_o"])):
+            pltpu.make_async_copy(ins[ph], dst, sc["local"].at[ph]).wait()
+            pltpu.make_async_copy(dst, outs[ph].at[band], sc["local"].at[ph]).start()
+
+    def first_here():
+        pltpu.make_async_copy(ins[0], outs[0].at[band], sc["local"].at[0]).wait()
+
+    def finish():
+        for ph, src in ((1, sc["bounce_i"]), (2, sc["bounce_o"])):
+            pltpu.make_async_copy(src, outs[ph].at[band], sc["local"].at[ph]).wait()
+        move_wait(1, cot_in, cot_out)
+        for make in sends:
+            make().wait_send()
+
+    return dict(
+        begin=begin, arrived=arrived, place=place, first_here=first_here, finish=finish,
+        z=z_wait, a=a_wait, b=b_wait, c=c_wait,
+    )
+
+
+def forward_kernel(names, band_slots, *refs):
+    me = compass()
+    qp_in, inner_in, outer_in, tok_in, cot_in, note_in, table_ref = refs[:7]
+    (qp_out, inner_out, outer_out, cot_out, vec_out, residual_out, attn_out, query_out, own_out, far_out,
+     tops_out, mixed_out, attended_out, mlp_out) = refs[7:21]
+    sc = dict(zip(names, refs[21:]))
+    rows, width = sc["residual"].shape
+    heads = width // HEAD_DIM
+    core = me["core"]
+    qp, tok, notes, vec = sc["qp"], sc["tok"], sc["notes"], sc["vec"]
+
+    barrier = pltpu.get_barrier_semaphore()
+    peers = [(me["xdp"], me["band"]), (me["ydp"], me["band"]), (me["sib"], me["band"])]
+    for k in range(1, NB):
+        other = lax.rem(me["band"] + k, NB)
+        peers += [(me["dp"], other), (me["sib"], other)]
+    for d, b in peers:
+        pl.semaphore_signal(barrier, inc=1, device_id={"dp": d, "band": b}, device_id_type=MESH)
+    pl.semaphore_wait(barrier, len(peers))
+
+    g = gather_steps(
+        me, width, (qp_in, inner_in, outer_in), (qp, inner_out, outer_out), tok_in, tok, cot_in, cot_out,
+        note_in, notes, sc,
+    )
+    saves = []
+
+    def save(src, dst):
+        copy = pltpu.make_async_copy(src, dst, sc["done"].at[len(saves)])
+        copy.start()
+        saves.append(copy)
+
+    def run(text):
+        for word in text.split():
+            g[word[0]](int(word[1:]))
+
+    g["begin"]()
+    g["place"]()
+    g["arrived"]()
+    spread_notes(notes, vec, width)
+    grid_rows = notes[0, 63:64, 0:1]
+    grid_cols = notes[0, 63:64, 1:2]
+    band_rows = jnp.floor(grid_rows * 0.25)
+    valid_count = (band_rows * grid_cols).astype(jnp.int32)
+    lane = lax.broadcasted_iota(jnp.int32, (1, width), 1)
+    vec[15:16, :] = jnp.where(lane == 0, band_rows * grid_cols, 0.0)
+    save(vec, vec_out)
+
+    @pl.loop(0, rows // BLOCK)
+    def _(step):
+        at = pl.multiple_of(step * BLOCK, BLOCK)
+        sub = pl.ds(at, BLOCK)
+        per_image = band_slots // BLOCK
+        within = (
+            lax.rem(step, per_image) * BLOCK + lax.broadcasted_iota(jnp.int32, (BLOCK, 1), 0)
+        ).astype(jnp.float32)
+        down = jnp.floor((within + 0.5) / grid_cols)
+        place = (2 * core + step // per_image).astype(jnp.float32)
+        picks = []
+        for index in (place * band_rows + down, within - down * grid_cols):
+            lanes = lax.broadcasted_iota(jnp.int32, (BLOCK, 128), 1).astype(jnp.float32)
+            pick = jnp.where(lanes == index, 1.0, 0.0).astype(jnp.bfloat16)
+            part = [jnp.dot(pick, table_ref[i], preferred_element_type=jnp.float32) for i in range(3)]
+            picks.append(part[0] + (part[1] + part[2]))
+        token = tok[step // per_image, pl.ds(lax.rem(step, per_image) * BLOCK, BLOCK), :]
+        residual = token.astype(jnp.float32) + jnp.concatenate(picks, 1)
+        sc["residual"][sub, :] = residual
+        normed = normalize(residual)[0]
+        sc["attn_in"][sub, :] = (normed * (1.0 + vec[1:2, :]) + vec[0:1, :]).astype(jnp.bfloat16)
+
+    save(sc["residual"], residual_out)
+    save(sc["attn_in"], attn_out)
+    run("z0 z1 a0 z2 a1 b0 a2 b1 c0 b2 c1")
+    g["first_here"]()
+    run("z3 c2")
+    save(qp, qp_out)
+    tile = width // 3
+    full = NB * 2 * qp.shape[2]
+
+    def product(left_ref, first, step):
+        at = pl.ds(pl.multiple_of(first + step * tile, 128), tile)
+        return jnp.dot(
+            left_ref[...], qp[:, :, :, at].reshape(full, tile), preferred_element_type=jnp.float32
+        )
+
+    def here(step):
+        return pl.ds(pl.multiple_of(step * tile, 128), tile)
+
+    @pl.loop(0, 3)
+    def _(step):
+        sc["own"][:, here(step)] = product(sc["attn_in"], width, step).astype(jnp.bfloat16)
+
+    run("z4 a3")
+
+    @pl.loop(0, 3)
+    def _(step):
+        value = product(sc["attn_in"], 2 * width, step) + vec[7:8, here(step)]
+        sc["own"][:, here(step + 3)] = value.astype(jnp.bfloat16)
+
+    swap = pltpu.make_async_remote_copy(
+        src_ref=sc["own"], dst_ref=sc["far"], send_sem=sc["kv_send"].at[0], recv_sem=sc["kv_recv"].at[0],
+        device_id={"dp": me["sib"], "band": me["band"]}, device_id_type=MESH,
+    )
+    swap.start()
+    run("z5 a4 b3")
+
+    @pl.loop(0, 3)
+    def _(step):
+        value = product(sc["attn_in"], 0, step) + vec[6:7, here(step)]
+        sc["query"][:, here(step)] = value.astype(jnp.bfloat16)
+
+    save(sc["query"], query_out)
+    save(sc["own"], own_out)
+    qh, kh, vh = sc["qh"], sc["kh"], sc["vh"]
+    keys, plain = key_tail(valid_count, band_slots), flat_tail(0.0)
+    pack_heads(sc["query"], 0, qh, 0, rows, flat_tail(1.0))
+    pack_heads(sc["own"], 0, kh, 0, rows, keys)
+    pack_heads(sc["own"], width, vh, 0, rows, plain)
+    swap.wait()
+    save(sc["far"], far_out)
+    pack_heads(sc["far"], 0, kh, rows, rows, keys)
+    pack_heads(sc["far"], width, vh, rows, rows, plain)
+    beside = ["z6 a5 b4 c3", "", "z7 a6 b5 c4", "", "", "z8 a7 b6 c5", "", "", "a8 b7 c6", "", "", "b8 c7", "", "", "c8"]
+
+    @pl.loop(0, heads)
+    def _(h):
+        attend_block(h, qh, kh, vh, sc["tops"])
+        for i, text in enumerate(beside):
+            if text:
+                pl.when(h == i)(partial(run, text))
+
+    unpack_heads(qh, 0, rows, sc["mixed"], 0)
+    save(sc["tops"], tops_out)
+    save(sc["mixed"], mixed_out)
+
+    @pl.loop(0, 3)
+    def _(step):
+        sc["attended"][:, here(step)] = product(sc["mixed"], 3 * width, step) + vec[8:9, here(step)]
+
+    save(sc["attended"], attended_out)
+
+    @pl.loop(0, rows // BLOCK)
+    def _(step):
+        sub = pl.ds(pl.multiple_of(step * BLOCK, BLOCK), BLOCK)
+        middle = sc["residual"][sub, :] + vec[2:3, :] * sc["attended"][sub, :]
+        normed = normalize(middle)[0]
+        sc["mlp_in"][sub, :] = (normed * (1.0 + vec[4:5, :]) + vec[3:4, :]).astype(jnp.bfloat16)
+
+    save(sc["mlp_in"], mlp_out)
+    g["finish"]()
+    for copy in saves:
+        copy.wait()
+
+
+NOTE_COND, NOTE_GRID, NOTE_BIAS = 54, 63, 64
+
+
+def spread_notes(notes, vec, width):
+    lines = width // 128
+    share = notes.shape[0]
+    total = notes[0, 0:NOTE_GRID, :] + 0.0
+    for b in range(1, share):
+        total = total + notes[b, 0:NOTE_GRID, :]
+
+    def flat(block, first):
+        return jnp.concatenate([block[first + i : first + i + 1, :] for i in range(lines)], 1)
+
+    for index in range(MOD_BLOCKS):
+        vec[index : index + 1, :] = flat(total, index * lines)
+    small = width // share
+    for index in range(4):
+        parts = []
+        for b in range(share):
+            first = NOTE_BIAS + 3 * index
+            for i in range(3):
+                parts.append(notes[b, first + i : first + i + 1, : min(128, small - 128 * i)])
+        vec[6 + index : 7 + index, :] = jnp.concatenate(parts, 1)
+    for b in range(share):
+        block = notes[b, NOTE_BIAS + 12 : NOTE_BIAS + 12 + lines, :]
+        vec[10 + b : 11 + b, :] = flat(block, 0)
+    vec[14:15, :] = flat(notes[0, NOTE_COND : NOTE_COND + lines, :], 0)
+
+
+def forward_block(qp, inner, outer, tok, cot, note, table):
+    half, ff = qp.shape[0] // 2, qp.shape[1]
+    images, band_slots, width = tok.shape
+    rows = images * band_slots
+    heads = width // HEAD_DIM
+    bf, f32 = jnp.bfloat16, jnp.float32
+    S = jax.ShapeDtypeStruct
+    qp, inner = qp.reshape(2, half, ff), inner.reshape(2, half, ff)
+    outer = outer.reshape(4, 2, half, width)
+    scratch = forward_scratch(half, ff, width, rows, note.shape[1], images)
+    any_ = pl.BlockSpec(memory_space=pl.ANY)
+    return pl.pallas_call(
+        partial(forward_kernel, tuple(scratch), band_slots),
+        out_shape=[
+            S((NB, 2, half, ff), bf), S((NB, 2, half, ff), bf), S((NB, 4, 2, half, width), bf), S(cot.shape, bf),
+            S((16, width), f32), S((rows, width), f32), S((rows, width), bf), S((rows, width), bf),
+            S((rows, 2 * width), bf), S((rows, 2 * width), bf), S((heads, 8, rows), f32), S((rows, width), bf),
+            S((rows, width), f32), S((rows, width), bf),
+        ],
+        in_specs=[any_] * 6 + [pl.BlockSpec(memory_space=pltpu.VMEM)],
+        out_specs=[any_] * 14,
+        scratch_shapes=list(scratch.values()),
+        compiler_params=pltpu.CompilerParams(
+            collective_id=0, has_side_effects=True, vmem_limit_bytes=60 * 2**20
+        ),
+        name="forward_block",
+    )(qp, inner, outer, tok, cot, note, table)
 
 
 def pair_perm(dp_count, band_count):
@@ -858,16 +1076,17 @@
     return jnp.stack([jnp.where(odd, got[1], got[0]), jnp.where(odd, got[0], got[1])])
 
 
-def position_rows(row_index, col_index, width):
+def position_parts(width):
     quarter = width // 4
     frequency = 10000.0 ** (-jnp.arange(quarter, dtype=jnp.float32) / quarter)
     angles = jnp.arange(128, dtype=jnp.float32)[:, None] * frequency
-    table = jnp.concatenate([jnp.sin(angles), jnp.cos(angles)], -1)
-    places = jnp.arange(128, dtype=jnp.int32)
-    pick = lambda index: jnp.dot(
-        (index[:, None] == places).astype(jnp.float32), table, precision=lax.Precision.HIGHEST
-    )
-    return jnp.concatenate([pick(row_index), pick(col_index)], -1)
+    left = jnp.concatenate([jnp.sin(angles), jnp.cos(angles)], -1)
+    parts = []
+    for _ in range(3):
+        part = lax.reduce_precision(left, 8, 7)
+        parts.append(part.astype(jnp.bfloat16))
+        left = left - part
+    return jnp.stack(parts)
 
 
 def over_groups(piece, dp_count):
@@ -927,71 +1146,38 @@
         band * ada_bias.shape[0],
         0,
     )
-    biases = jnp.concatenate([query_bias, value_bias, proj_bias, inner_bias, outer_bias])
-    bias_count = biases.shape[0]
     mod_count = share.shape[1]
+    lines = lambda vector: jnp.pad(
+        vector.astype(jnp.float32), [(0, 0)] * (vector.ndim - 1) + [(0, -vector.shape[-1] % 128)]
+    )
+    spread = lambda vector: jnp.broadcast_to(lines(vector), (images, -(-vector.shape[0] // 128) * 128))
     note = jnp.concatenate(
-        [
-            share,
-            jnp.broadcast_to(biases.astype(jnp.float32), (images, bias_count)),
-            condition_f,
-            patch_grid.astype(jnp.float32),
-        ],
+        [share, condition_f, lines(patch_grid)]
+        + [spread(bias) for bias in (query_bias, value_bias, proj_bias, outer_bias, inner_bias)],
         1,
     )
-    note_rows = -(-note.shape[1] // 1024) * 8
-    note = jnp.pad(note, ((0, 0), (0, note_rows * 128 - note.shape[1])))
-    note = note.reshape(images, note_rows, 128)
+    note = jnp.pad(note, ((0, 0), (0, -note.shape[1] % 1024))).reshape(images, -1, 128)
     first_weight = jnp.concatenate([qkv_weight, proj_weight], 1)
-    first_full, inner_full, outer_full, tokens_here, cotangent_here, notes = gather_weights(
-        first_weight, inner_weight, outer_weight, tokens, cotangent, note, width
+    (first_full, inner_full, outer_full, cotangent_here, vectors, residual, attn_in, query_rows, key_value,
+     other_key_value, tops, mixed_rows, attended, mlp_in) = forward_block(
+        first_weight, inner_weight, outer_weight, tokens, cotangent, note, position_parts(width)
     )
     first_full = first_full.reshape(width, -1)
     inner_full = inner_full.reshape(width, hidden)
     outer_full = outer_full.reshape(hidden, width)
     qkv_full = first_full[:, : 3 * width]
     proj_full = first_full[:, 3 * width :]
-    notes = notes.reshape(band_count, -1)
-    modulation = jnp.sum(notes[:, :mod_count], 0)
-    pieces = []
-    at = mod_count
-    for piece in (query_bias, value_bias, proj_bias, inner_bias, outer_bias):
-        pieces.append(notes[:, at : at + piece.shape[0]].reshape(-1))
-        at += piece.shape[0]
-    query_bias_full, value_bias_full, proj_bias_full, inner_bias_full, outer_bias_full = pieces
-    condition_here = notes[0, at : at + width]
-    at += width
-    grid_rows = notes[0, at].astype(jnp.int32)
-    grid_cols = notes[0, at + 1].astype(jnp.int32)
-
+    scale_one, gate_one = vectors[1], vectors[2]
+    scale_two, gate_two = vectors[4], vectors[5]
+    outer_bias_full = vectors[9]
+    inner_bias_full = vectors[10:14].reshape(-1)
+    condition_here = vectors[14]
+    valid_count = vectors[15, :1].astype(jnp.int32)
     rows = images * band_slots
-    ids = core * rows + jnp.arange(rows, dtype=jnp.int32)
-    within = ids % band_slots
-    band_rows = grid_rows // band_count
-    is_valid = within < band_rows * grid_cols
-    row_index = ids // band_slots * band_rows + within // grid_cols
-    col_index = within % grid_cols
-
-    shift_one, scale_one, gate_one, shift_two, scale_two, gate_two = [
-        modulation[index * width : (index + 1) * width] for index in range(6)
-    ]
-    residual = tokens_here.reshape(rows, width).astype(jnp.float32) + position_rows(
-        row_index, col_index, width
-    )
+    is_valid = jnp.arange(rows, dtype=jnp.int32) % band_slots < valid_count
     normed_one, inverse_one = normalize(residual)
-    attn_in = (normed_one * (1.0 + scale_one) + shift_one).astype(jnp.bfloat16)
-    projected = jnp.dot(attn_in, qkv_full, preferred_element_type=jnp.float32)
-    query_rows = (projected[:, :width] + query_bias_full).astype(jnp.bfloat16)
-    key_value = (
-        projected[:, width:] + jnp.concatenate([jnp.zeros((width,), jnp.float32), value_bias_full])
-    ).astype(jnp.bfloat16)
-    other_key_value = lax.ppermute(key_value, both, siblings)
-    valid_count = (band_rows * grid_cols).reshape(1)
-    mixed_rows, tops = attend(valid_count, query_rows, key_value, other_key_value, band_slots)
-    attended = jnp.dot(mixed_rows, proj_full, preferred_element_type=jnp.float32) + proj_bias_full
     middle = residual + gate_one * attended
     normed_two, inverse_two = normalize(middle)
-    mlp_in = (normed_two * (1.0 + scale_two) + shift_two).astype(jnp.bfloat16)
     hidden_pre = jnp.dot(mlp_in, inner_full, preferred_element_type=jnp.float32) + inner_bias_full
     hidden_act = jax.nn.gelu(hidden_pre, approximate=True).astype(jnp.bfloat16)
     mlp_out = jnp.dot(hidden_act, outer_full, preferred_element_type=jnp.float32) + outer_bias_full

time: 784 us -> 705 us (0.90)
  local copies, waits for them, and re-layouts: 55.4 us -> 20.6 us
  matrix products: 143 us -> 118 us
  waiting for transfers between devices: 32.9 us -> 16.6 us
  other arithmetic: 47.1 us -> 34.9 us
  Pallas kernels: 476 us -> 488 us
    dot_general x4 -> x0, matrix products: 17.6 us -> none  [the longest x1 7.43 us: body(): projected = jnp.dot(attn_in, qkv_full, preferred_element_type=jnp.float32)]
    ppermute x4, waiting for transfers between devices: 32.9 us -> 16.6 us  [send_home(): lax.ppermute(part, ('dp', 'band'), perm)]
    pallas_call x1, Pallas kernels: 93.3 us -> 109 us  [reduce_last(): pl.pallas_call(partial(reduce_last_kernel, counts, ada_weight.shape[1], i...]
    dot_general x4 -> x0, local copies, waits for them, and re-layouts: 10.6 us -> none  [the longest x2 6.36 us: lanes_dot(): lax.dot_general(left, right, (((1,), (1,)), ((), ())), preferred_element_...]
    unnamed x120 -> x100, local copies, waits for them, and re-layouts: 12.8 us -> 2.41 us
    pallas_call x2 -> x1, Pallas kernels: 210 us -> 202 us  [forward_block(): pl.pallas_call(partial(forward_kernel, tuple(scratch), band_slots), out_s...]
  transfers between devices with their start and end apart: 6 -> 5, of which waited for: 4 -> 3; matrix products, arithmetic and copies ran while one was open for 4% -> 4% of each run, Pallas kernels for 0% -> 0%
where the time goes in v4:
time: 705 us; the launch traced here: 694 us
  Pallas kernels  488 us (69%)
  matrix products  118 us (17%)
  other arithmetic  34.9 us (5%)
  local copies, waits for them, and re-layouts  20.6 us (3%)
  waiting for transfers between devices  16.6 us (2%)
  starting transfers between devices  13.9 us (2%)
    pallas_call x1, Pallas kernels, forward_block(): pl.pallas_call(partial(forward_kernel, tuple(scratch), band_slots), out_s...  202 us
    pallas_call x1, Pallas kernels, reduce_attend(): pl.pallas_call(partial(reduce_attend_kernel, counts, band_slots, tuple(sc...  178 us
    pallas_call x1, Pallas kernels, reduce_last(): pl.pallas_call(partial(reduce_last_kernel, counts, ada_weight.shape[1], i...  109 us
    dot_general x10, matrix products, rows_dot(): lax.dot_general(left, right, (((0,), (0,)), ((), ())), preferred_element_...  46.6 us
    dot_general x4, matrix products, lanes_dot(): lax.dot_general(left, right, (((1,), (1,)), ((), ())), preferred_element_...  41 us
    ppermute x4, waiting for transfers between devices, send_home(): lax.ppermute(part, ('dp', 'band'), perm)  16.6 us
    dot_general x1, matrix products, body(): jnp.dot(hidden_act, outer_full, preferred_element_type=jnp.float32)  15.4 us
  transfers between devices with their start and end apart: 5, of which 3 were waited for; matrix products, arithmetic and copies ran while one was open for 4% of the time, Pallas kernels for 0%

profile of v4, /device:TPU:1, one launch (start us, length us, event | category | flops | bytes accessed | tf_op | source)
XLA Modules:
  0.0 694.4 jit_solution(5977012843599711665)
XLA Ops:
  3.0 3.0 fusion.9
  7.8 1.7 pad_maximum_fusion
  10.3 201.6 %forward_block.1 = (bf16[4,2,144,4608]{3,2,1,0:T(8,128)(2,1)}, bf16[4,2,144,4608]{3,2,1,0:T(8,128)(2,1)}, bf16[4,4,2,144,1152]{4,3,2,1,0:T(8,128)(2,1)}, bf16[2,...) custom-call(bf16[2,144,4608]{2,1,0:T(8,128)(2,1)} %bitcast.106, ...), custom_call_target="tpu_custom_call" | custom-call | tf_op jit(solution)/shard_map/forward_block/pallas_call | solution.py:1035
  211.9 1.6 multiply_reduce_fusion.10
  213.6 1.2 slice.138
  216.9 11.7 %fusion.42 = f32[512,4608]{1,0:T(8,128)} fusion(bf16[512,1152]{1,0:T(8,128)(2,1)} %get-tuple-element.40, bf16[1152,4608]{1,0:T(8,128)(2,1)} %bitcast.145), kind=kOutput, calls=%fused_computation.158 | convolution fusion | flops 5435817984 | bytes 21233664 | tf_op jit(solution)/shard_map/dot_general | solution.py:1181
  228.6 1.0 convert_reduce_fusion.1
  229.6 15.8 %convert_reduce_fusion = (f32[4608]{0:T(1024)}, bf16[512,4608]{1,0:T(8,128)(2,1)}) fusion(f32[512,4608]{1,0:T(8,128)} %fusion.42, f32[4608]{0:T(1024)S(1)} %add.138, bf16[512,1152]{1,0:T(8,128)(2,1)S(1)} %bitcast.127, bf16[4608,1152]{1,0:T(8,128)(2,1)S(1)} %bitcast.144), kind=kOutput, calls=%fused_computation.10 | convolution fusion | flops 5490077184 | bytes 25989120 | tf_op jit(solution)/shard_map/dot_general | solution.py:78
  245.4 4.7 convolution_convert_fusion.5
  250.1 3.2 convolution_convert_fusion.6
  253.3 3.2 convolution_convert_fusion.7
  256.6 3.2 convolution_convert_fusion.8
  260.0 2.4 fusion.39
  263.5 11.3 %multiply_reduce_fusion.1 = (f32[1152]{0:T(1024)}, f32[512]{0:T(512)S(1)}, f32[512]{0:T(512)S(1)}, f32[1152]{0:T(1024)}, f32[512,1152]{1,0:T(8,128)S(1)}) fusion(f32[512,1152]{1,0:T(8,128)S(1)} %get-tuple-element.82, f32[512]{0:T(512)S(1)} %add_rsqrt_fusion.1, f32[512]{0:T(512)S(1)} %get-tuple-element.120, f32[1152]{0:T(1024)S(1)} %get-tuple-element.70, ...), kind=kOutput, calls=%fused_computation.40 | convolution fusion | flops 5441123328 | bytes 20076032 | tf_op jit(solution)/shard_map/dot_general | solution.py:78
  274.9 15.4 %multiply_reduce_fusion = (f32[1152]{0:T(1024)}, bf16[512,1152]{1,0:T(8,128)(2,1)S(1)}, f32[1152]{0:T(1024)}, bf16[512,1152]{1,0:T(8,128)(2,1)S(1)}, f32[512,1152]{1,0:T(8,128)}, /*index=5*/bf16[512,1152]{1,0:T(8,128)(2,1)S(1)}) fusion(bf16[2,256,1152]{2,1,0:T(8,128)(2,1)S(1)} %copy-done.7, f32[512]{0:T(512)S(1)} %copy-done.27, ...), kind=kOutput, calls=%fused_computation.39 | convolution fusion | flops 5472385024 | bytes 31906816 | tf_op jit(solution)/shard_map/dot_general | solution.py:1183
  290.3 13.1 %convolution_convert_fusion = bf16[4608,1152]{1,0:T(8,128)(2,1)} fusion(bf16[512,1152]{1,0:T(8,128)(2,1)S(1)} %get-tuple-element.99, f32[512,4608]{1,0:T(8,128)} %fusion.42, f32[4608]{0:T(1024)S(1)} %copy-done.19), kind=kOutput, calls=%fused_computation | convolution fusion | flops 5464719360 | bytes 21252096 | tf_op jit(solution)/shard_map/dot_general | solution.py:82
  303.4 4.6 convolution_convert_fusion.9.refs_9_
  308.1 177.7 %reduce_attend.1 = (bf16[4,2,144,1152]{3,2,1,0:T(8,128)(2,1)}, bf16[4,2,144,1152]{3,2,1,0:T(8,128)(2,1)}, bf16[512,1152]{1,0:T(8,128)(2,1)}, bf16[512,2304]{1,0:T(8,128)(2,1)}, bf16[512,2304]{1,0:T(8,128)(2,1)}) custom-call(bf16[4,4,2,144,1152]{4,3,2,1,0:T(8,128)(2,1)} %bitcast.105, bf16[4,2,144,1152]{3,2,1,0:T(8,128)(2,1)} %bitcast.119, ...), custom_call_target="tpu_custom_call" | custom-call | tf_op jit(solution)/shard_map/reduce_attend/pallas_call | solution.py:614
  485.9 1.1 broadcast_select_fusion.3
  487.0 2.5 collective-permute-start
  489.5 9.3 %collective-permute-start.1 = (bf16[256,1152]{1,0:T(8,128)(2,1)}, bf16[256,1152]{1,0:T(8,128)(2,1)}, u32[]{:S(2)}, u32[]{:S(2)}) collective-permute-start(bf16[256,1152]{1,0:T(8,128)(2,1)} %get-tuple-element.107), channel_id=1, source_target_pairs={{0,0},{1,1},{2,4},{3,5},{4,2},{5,3},{6,6},{7,7},{8,8},{9,9},{10,12... | collective-permute-start | bytes 1769480 | tf_op jit(solution)/shard_map/ppermute | solution.py:1075
  498.8 4.9 convolution_convert_fusion.1
  503.7 4.6 bitcast_convert_fusion
  508.4 3.2 convolution_convert_fusion.4
  511.8 1.3 constant_dynamic-update-slice_fusion.7
  513.1 1.9 fusion.40
  515.0 2.9 maximum_convert_fusion
  517.9 1.7 collective-permute-done.1
  519.6 1.4 select_bitcast_fusion.3
  521.0 1.1 pad_maximum_fusion.1
  522.1 2.3 add_convert_fusion
  524.6 3.2 convolution_convert_fusion.2
  527.9 3.2 convolution_convert_fusion.3
  531.1 9.3 %multiply_reduce_fusion.3 = (f32[1152]{0:T(1024)}, f32[512]{0:T(512)S(1)}, f32[512]{0:T(512)S(1)}, f32[1152]{0:T(1024)}, f32[512,1152]{1,0:T(8,128)S(1)}) fusion(f32[512,1152]{1,0:T(8,128)S(1)} %copy-done, f32[512]{0:T(512)S(1)} %copy-done.22, f32[512]{0:T(512)S(1)} %copy-done.21, f32[1152]{0:T(1024)S(1)} %get-tuple-element.69, ...), kind=kOutput, calls=%fused_computation.42 | convolution fusion | flops 4089246720 | bytes 16242176 | tf_op jit(solution)/shard_map/dot_general | solution.py:78
  540.6 1.2 multiply_reduce_fusion.2
  541.8 4.6 concatenate.80
  546.4 1.4 select_maximum_fusion.refs_4_
  547.8 108.8 %reduce_last.1 = (bf16[4,2,144,1152]{3,2,1,0:T(8,128)(2,1)}, bf16[4,4,64,128]{3,2,1,0:T(8,128)(2,1)}, f32[72,128]{1,0:T(8,128)}, f32[4,8,384]{2,1,0:T(8,128)}) custom-call(bf16[4,2,144,1152]{3,2,1,0:T(8,128)(2,1)} %bitcast.108, bf16[4,2,144,1152]{3,2,1,0:T(8,128)(2,1)} %bitcast.110, bf16[4,2,144,1152]{3,2,1,0:T(8,128)(2,1)} %bitcast.109, ...), custom_call_target="tpu_custom_call" | custom-call | tf_op jit(solution)/shard_map/reduce_last/pallas_call | solution.py:519
  657.4 1.3 slice_bitcast_fusion
  658.8 1.9 fusion.41
  660.9 4.6 fusion.22
  665.5 1.2 bitcast_convert_fusion.1
  668.4 1.9 collective-permute-start.4
  673.7 1.4 dynamic_slice.30
  675.1 2.2 maximum_convert_fusion.1
  677.3 4.0 collective-permute-done.3
  681.3 10.9 %collective-permute-done.4 = bf16[256,1152]{1,0:T(8,128)(2,1)S(1)} collective-permute-done((bf16[256,1152]{1,0:T(8,128)(2,1)S(1)}, bf16[256,1152]{1,0:T(8,128)(2,1)S(1)}, u32[]{:S(2)}, u32[]{:S(2)}) %collective-permute-start.4) | collective-permute-done | bytes 589856 | tf_op jit(solution)/shard_map/ppermute | solution.py:1075
  692.3 1.6 maximum_convert_fusion.2
  (153 shorter events, 14.2 us)
Async XLA Ops:
  0.6 5.4 copy-start.10
  0.7 5.4 copy-start.32
  0.7 5.4 copy-start.28
  0.7 5.4 copy-start.29
  0.7 5.4 copy-start.30
  0.7 5.5 copy-start.31
  0.7 5.5 copy-start.26
  3.0 4.8 copy-start.4
  3.0 4.8 copy-start.8
  213.6 46.5 %copy-start.15 = (f32[1152]{0:T(1024)}, f32[1152]{0:T(1024)S(1)}, u32[]{:S(2)}) copy-start(f32[1152]{0:T(1024)S(1)} %get-tuple-element.73) | copy-start | bytes 13828
  213.6 49.8 %copy-start.23 = (f32[1152]{0:T(1024)}, f32[1152]{0:T(1024)S(1)}, u32[]{:S(2)}) copy-start(f32[1152]{0:T(1024)S(1)} %get-tuple-element.70) | copy-start | bytes 13828
  216.8 12.8 %copy-start.18 = (f32[4608]{0:T(1024)}, f32[4608]{0:T(1024)S(1)}, u32[]{:S(2)}) copy-start(f32[4608]{0:T(1024)S(1)} %add.138) | copy-start | bytes 55300
  216.8 12.8 %slice-start = ((s8[10616832]{0:T(1024)(128)(4,1)}), s8[4194304]{0:T(1024)(128)(4,1)S(1)}, s32[]{:S(2)}) async-start(s8[10616832]{0:T(1024)(128)(4,1)} %bitcast.142), calls=%async_computation | async-start | bytes 8388608
  216.8 11.7 %copy-start.6 = (bf16[2,256,1152]{2,1,0:T(8,128)(2,1)S(1)}, bf16[2,256,1152]{2,1,0:T(8,128)(2,1)}, u32[]{:S(2)}) copy-start(bf16[2,256,1152]{2,1,0:T(8,128)(2,1)} %get-tuple-element.43) | copy-start | bytes 3538948
  216.8 12.8 %slice-start.1 = ((s8[10616832]{0:T(1024)(128)(4,1)}), s8[4194304]{0:T(1024)(128)(4,1)S(1)}, s32[]{:S(2)}) async-start(s8[10616832]{0:T(1024)(128)(4,1)} %bitcast.142), calls=%async_computation.1 | async-start | bytes 8388608
  216.9 12.7 %slice-start.2 = ((s8[10616832]{0:T(1024)(128)(4,1)}), s8[2228224]{0:T(1024)(128)(4,1)S(1)}, s32[]{:S(2)}) async-start(s8[10616832]{0:T(1024)(128)(4,1)} %bitcast.142), calls=%async_computation.2 | async-start | bytes 4456448
  229.6 15.8 %copy-start.35 = (bf16[512,1152]{1,0:T(8,128)(2,1)S(1)}, bf16[512,1152]{1,0:T(8,128)(2,1)}, u32[]{:S(2)}) copy-start(bf16[512,1152]{1,0:T(8,128)(2,1)} %get-tuple-element.40) | copy-start | bytes 3538948
  245.4 4.7 copy-start.37
  253.3 3.2 copy-start.36
  256.6 3.2 copy-start
  260.0 2.4 copy-start.20
  260.0 3.4 slice-start.3
  260.0 3.4 slice-start.4
  263.4 11.4 %copy-start.7 = (bf16[2,256,1152]{2,1,0:T(8,128)(2,1)S(1)}, bf16[2,256,1152]{2,1,0:T(8,128)(2,1)}, u32[]{:S(2)}) copy-start(bf16[2,256,1152]{2,1,0:T(8,128)(2,1)} %get-tuple-element.43) | copy-start | bytes 3538948
  263.5 11.4 %copy-start.16 = (f32[1152]{0:T(1024)S(1)}, f32[1152]{0:T(1024)}, u32[]{:S(2)}) copy-start(f32[1152]{0:T(1024)} %copy-done.15) | copy-start | bytes 13828
  263.5 11.4 %copy-start.19 = (f32[4608]{0:T(1024)S(1)}, f32[4608]{0:T(1024)}, u32[]{:S(2)}) copy-start(f32[4608]{0:T(1024)} %copy-done.18) | copy-start | bytes 55300
  263.5 11.4 %copy-start.24 = (f32[1152]{0:T(1024)S(1)}, f32[1152]{0:T(1024)}, u32[]{:S(2)}) copy-start(f32[1152]{0:T(1024)} %get-tuple-element.71) | copy-start | bytes 13828
  263.5 11.4 %copy-start.27 = (f32[512]{0:T(512)S(1)}, f32[512]{0:T(512)}, u32[]{:S(2)}) copy-start(f32[512]{0:T(512)} %fusion.31) | copy-start | bytes 6148
  290.3 13.1 %copy-start.38 = (bf16[512,1152]{1,0:T(8,128)(2,1)}, bf16[512,1152]{1,0:T(8,128)(2,1)S(1)}, u32[]{:S(2)}) copy-start(bf16[512,1152]{1,0:T(8,128)(2,1)S(1)} %get-tuple-element.94) | copy-start | bytes 3538948
  485.8 36.3 %collective-permute-start.2 = (bf16[512,2304]{1,0:T(8,128)(2,1)}, bf16[512,2304]{1,0:T(8,128)(2,1)}, u32[]{:S(2)}, u32[]{:S(2)}) collective-permute-start(bf16[512,2304]{1,0:T(8,128)(2,1)} %get-tuple-element.51), channel_id=1, source_target_pairs={{0,4},{1,5},{2,6},{3,7},{4,0},{5,1},{6,2},{7,3},{8,12},{9,13},{10,... | collective-permute-start | bytes 7077896 | tf_op jit(solution)/shard_map/ppermute | solution.py:1218
  487.0 30.9 %collective-permute-start = (bf16[256,1152]{1,0:T(8,128)(2,1)}, bf16[256,1152]{1,0:T(8,128)(2,1)}, u32[]{:S(2)}, u32[]{:S(2)}) collective-permute-start(bf16[256,1152]{1,0:T(8,128)(2,1)} %get-tuple-element.106), channel_id=1, source_target_pairs={{0,1},{1,0},{2,5},{3,4},{4,3},{5,2},{6,7},{7,6},{8,9},{9,8},{10,13... | collective-permute-start | bytes 1769480 | tf_op jit(solution)/shard_map/ppermute | solution.py:1075
  489.5 30.1 %collective-permute-start.1 = (bf16[256,1152]{1,0:T(8,128)(2,1)}, bf16[256,1152]{1,0:T(8,128)(2,1)}, u32[]{:S(2)}, u32[]{:S(2)}) collective-permute-start(bf16[256,1152]{1,0:T(8,128)(2,1)} %get-tuple-element.107), channel_id=1, source_target_pairs={{0,0},{1,1},{2,4},{3,5},{4,2},{5,3},{6,6},{7,7},{8,8},{9,9},{10,12... | collective-permute-start | bytes 1769480 | tf_op jit(solution)/shard_map/ppermute | solution.py:1075
  503.7 4.6 copy-start.5
  503.7 4.6 copy-start.33
  517.9 4.2 copy-start.2
  522.1 2.5 copy-start.34
  527.8 3.2 copy-start.21
  527.8 3.2 copy-start.22
  531.1 9.3 %copy-start.12 = (f32[9216]{0:T(1024)S(1)}, f32[9216]{0:T(1024)}, u32[]{:S(2)}) copy-start(f32[9216]{0:T(1024)} %constant_dynamic-update-slice_fusion.7) | copy-start | bytes 110596
  531.1 9.3 %copy-start.25 = (f32[1152]{0:T(1024)S(1)}, f32[1152]{0:T(1024)}, u32[]{:S(2)}) copy-start(f32[1152]{0:T(1024)} %get-tuple-element.93) | copy-start | bytes 13828
  531.1 9.4 %copy-start.17 = (f32[4608]{0:T(1024)S(1)}, f32[4608]{0:T(1024)}, u32[]{:S(2)}) copy-start(f32[4608]{0:T(1024)} %get-tuple-element.76) | copy-start | bytes 55300
  531.1 9.4 %copy-start.14 = (f32[1152]{0:T(1024)S(1)}, f32[1152]{0:T(1024)}, u32[]{:S(2)}) copy-start(f32[1152]{0:T(1024)} %get-tuple-element.74) | copy-start | bytes 13828
  531.1 9.4 %copy-start.1 = (f32[512,1152]{1,0:T(8,128)S(1)}, f32[512,1152]{1,0:T(8,128)}, u32[]{:S(2)}) copy-start(f32[512,1152]{1,0:T(8,128)} %get-tuple-element.39) | copy-start | bytes 7077892
  531.1 9.4 %copy-start.3 = (f32[512,1152]{1,0:T(8,128)S(1)}, f32[512,1152]{1,0:T(8,128)}, u32[]{:S(2)}) copy-start(f32[512,1152]{1,0:T(8,128)} %get-tuple-element.95) | copy-start | bytes 7077892
  658.7 1.9 copy-start.9
  660.9 6.7 copy-start.11
  668.4 12.9 %collective-permute-start.3 = (bf16[256,1152]{1,0:T(8,128)(2,1)S(1)}, bf16[256,1152]{1,0:T(8,128)(2,1)S(1)}, u32[]{:S(2)}, u32[]{:S(2)}) collective-permute-start(bf16[256,1152]{1,0:T(8,128)(2,1)S(1)} %get-tuple-element.102), channel_id=1, source_target_pairs={{0,1},{1,0},{2,5},{3,4},{4,3},{5,2},{6,7},{7,6},{8,9},{9,8},{10,13... | collective-permute-start | bytes 1769480 | tf_op jit(solution)/shard_map/ppermute | solution.py:1075
  668.4 23.8 %collective-permute-start.4 = (bf16[256,1152]{1,0:T(8,128)(2,1)S(1)}, bf16[256,1152]{1,0:T(8,128)(2,1)S(1)}, u32[]{:S(2)}, u32[]{:S(2)}) collective-permute-start(bf16[256,1152]{1,0:T(8,128)(2,1)S(1)} %get-tuple-element.103), channel_id=1, source_target_pairs={{0,0},{1,1},{2,4},{3,5},{4,2},{5,3},{6,6},{7,7},{8,8},{9,9},{10,12... | collective-permute-start | bytes 1769480 | tf_op jit(solution)/shard_map/ppermute | solution.py:1075
  (1 other events, 1.3 us)

commit v5 on v4

--- a/solution.py
+++ b/solution.py
@@ -1,5 +1,5 @@
-import functools
 from functools import partial
+from types import SimpleNamespace
 
 import jax
 import jax.numpy as jnp
@@ -13,6 +13,10 @@
 
 MESH = pl.DeviceIdType.MESH
 NB = 4
+
+
+def device(dp, band):
+    return {"dp": dp, "band": band}
 
 
 def normalize(values):
@@ -123,7 +127,7 @@
     core = lax.rem(dp, 2)
     px = lax.rem(dp // 2, 2)
     py = lax.rem(dp // 4, 2)
-    return dict(
+    return SimpleNamespace(
         dp=dp, band=band, core=core, px=px, py=py, kind=2 * py + px,
         sib=dp + 1 - 2 * core, xdp=dp + 2 - 4 * px, ydp=dp + 4 - 8 * py,
     )
@@ -138,17 +142,6 @@
         total[at, :] = (
             total[at, :].astype(jnp.float32) + term[at, :].astype(jnp.float32)
         ).astype(jnp.bfloat16)
-
-
-def reduce_barrier(me):
-    barrier = pltpu.get_barrier_semaphore()
-    peers = [(me["xdp"], me["band"]), (me["ydp"], me["band"]), (me["sib"], me["band"])]
-    peers += [(me["dp"], lax.rem(me["band"] + k, NB)) for k in range(1, NB)]
-    for dp, band in peers:
-        pl.semaphore_signal(
-            barrier, inc=1, device_id={"dp": dp, "band": band}, device_id_type=MESH
-        )
-    pl.semaphore_wait(barrier, len(peers))
 
 
 def run_all(batch):
@@ -177,8 +170,8 @@
 
 
 def reduce_steps(me, phases, source, out, sc, beside=()):
-    dp, band, core, px, py, kind = (me[k] for k in ("dp", "band", "core", "px", "py", "kind"))
-    here = lambda d: {"dp": d, "band": band}
+    dp, band, core, px, py, kind = me.dp, me.band, me.core, me.px, me.py, me.kind
+    here = lambda d: device(d, band)
     chunks = [(phase, k) for phase in range(phases) for k in REDUCE_ORDER]
     n = len(chunks)
     flip = lambda v: 1 - v
@@ -198,11 +191,11 @@
         b = lax.rem(band + k, NB)
         for t in range(4):
             remote(
-                source(phase, b, t, flip(core)), sc["recv_a"].at[s, t],
-                sc["a_send"].at[s], sc["a_recv"].at[s], here(me["sib"]),
+                source(phase, b, t, flip(core)), sc.recv_a.at[s, t],
+                sc.a_send.at[s], sc.a_recv.at[s], here(me.sib),
             ).start()
             pltpu.make_async_copy(
-                source(phase, b, t, core), sc["acc"].at[s, t], sc["a_own"].at[s]
+                source(phase, b, t, core), sc.acc.at[s, t], sc.a_own.at[s]
             ).start()
 
     def first(s, j, send):
@@ -217,42 +210,42 @@
 
     def send_b(s, j):
         return remote(
-            sc["acc"].at[s, first(s, j, True)], sc["recv_b"].at[s, j], sc["b_send"].at[s, j],
-            sc["b_recv"].at[s], here(me["xdp"] if s % 2 == 0 else me["ydp"]),
+            sc.acc.at[s, first(s, j, True)], sc.recv_b.at[s, j], sc.b_send.at[s, j],
+            sc.b_recv.at[s], here(me.xdp if s % 2 == 0 else me.ydp),
         )
 
     def send_c(s):
         return remote(
-            sc["acc"].at[s, second(s, True)], sc["recv_c"].at[s], sc["c_send"].at[s],
-            sc["c_recv"].at[s], here(me["ydp"] if s % 2 == 0 else me["xdp"]),
+            sc.acc.at[s, second(s, True)], sc.recv_c.at[s], sc.c_send.at[s],
+            sc.c_recv.at[s], here(me.ydp if s % 2 == 0 else me.xdp),
         )
 
     def send_z(s):
         phase, k = chunks[s]
         return remote(
-            sc["acc"].at[s, kind], sc["recv_z"].at[phase, k], sc["z_send"].at[phase, k],
-            sc["z_recv"].at[phase, k], {"dp": dp, "band": lax.rem(band + k, NB)},
+            sc.acc.at[s, kind], sc.recv_z.at[phase, k], sc.z_send.at[phase, k],
+            sc.z_recv.at[phase, k], device(dp, lax.rem(band + k, NB)),
         )
 
     def send_d(phase, slot):
-        ss, rs = sc["d_send"].at[phase, slot], sc["d_recv"].at[phase, slot]
+        ss, rs = sc.d_send.at[phase, slot], sc.d_recv.at[phase, slot]
         even = phase % 2 == 0
         if slot == 0:
             unit = out[phase].at[kind, core]
-            return remote(sc["recv_z"].at[phase, 0], unit, ss, rs, here(me["xdp"] if even else me["ydp"]))
+            return remote(sc.recv_z.at[phase, 0], unit, ss, rs, here(me.xdp if even else me.ydp))
         if slot == 3:
             row = out[phase].at[:, core]
-            return remote(row, row, ss, rs, here(me["sib"]))
+            return remote(row, row, ss, rs, here(me.sib))
         if even:
             pair = out[phase].at[pl.ds(2 * py, 2), core]
-            return remote(pair, pair, ss, rs, here(me["ydp"]))
+            return remote(pair, pair, ss, rs, here(me.ydp))
         unit = out[phase].at[2 * (slot - 1) + px, core]
-        return remote(unit, unit, ss, rs, here(me["xdp"]))
+        return remote(unit, unit, ss, rs, here(me.xdp))
 
     def a_to_b(s):
-        acc, got = sc["acc"], sc["recv_a"]
-        pltpu.make_async_copy(got.at[s], acc.at[s], sc["a_own"].at[s]).wait()
-        whole = remote(got.at[s], got.at[s], sc["a_send"].at[s], sc["a_recv"].at[s], here(me["sib"]))
+        acc, got = sc.acc, sc.recv_a
+        pltpu.make_async_copy(got.at[s], acc.at[s], sc.a_own.at[s]).wait()
+        whole = remote(got.at[s], got.at[s], sc.a_send.at[s], sc.a_recv.at[s], here(me.sib))
         whole.wait_recv()
         for j in range(2):
             t = first(s, j, True)
@@ -264,8 +257,8 @@
         whole.wait_send()
 
     def b_to_c(s):
-        acc, got = sc["acc"], sc["recv_b"]
-        remote(got.at[s], got.at[s], sc["b_send"].at[s, 0], sc["b_recv"].at[s], here(me["xdp"])).wait_recv()
+        acc, got = sc.acc, sc.recv_b
+        remote(got.at[s], got.at[s], sc.b_send.at[s, 0], sc.b_recv.at[s], here(me.xdp)).wait_recv()
         away = flip(py) if s % 2 == 0 else flip(px)
         stay = py if s % 2 == 0 else px
         add_rows(acc.at[s, second(s, True)], got.at[s, away])
@@ -273,20 +266,20 @@
         add_rows(acc.at[s, kind], got.at[s, stay])
 
     def c_to_z(s):
-        acc, got = sc["acc"], sc["recv_c"]
+        acc, got = sc.acc, sc.recv_c
         phase, k = chunks[s]
-        remote(got.at[s], got.at[s], sc["c_send"].at[s], sc["c_recv"].at[s], here(me["xdp"])).wait_recv()
+        remote(got.at[s], got.at[s], sc.c_send.at[s], sc.c_recv.at[s], here(me.xdp)).wait_recv()
         add_rows(acc.at[s, kind], got.at[s])
         if k != 0:
             go(partial(send_z, s))
 
     def z_to_d(phase):
         s = phase * NB + NB - 1
-        acc, got = sc["acc"], sc["recv_z"]
+        acc, got = sc.acc, sc.recv_z
         for k in range(1, NB):
             remote(
-                got.at[phase, k], got.at[phase, k], sc["z_send"].at[phase, k],
-                sc["z_recv"].at[phase, k], here(dp),
+                got.at[phase, k], got.at[phase, k], sc.z_send.at[phase, k],
+                sc.z_recv.at[phase, k], here(dp),
             ).wait_recv()
         rows = acc.shape[2]
 
@@ -299,7 +292,7 @@
             got[phase, 0, at, :] = total.astype(jnp.bfloat16)
 
         unit = out[phase].at[kind, core]
-        own = pltpu.make_async_copy(got.at[phase, 0], unit, sc["d_own"].at[phase])
+        own = pltpu.make_async_copy(got.at[phase, 0], unit, sc.d_own.at[phase])
         own.start()
         go(partial(send_d, phase, 0))
         own.wait()
@@ -308,49 +301,96 @@
         even = phase % 2 == 0
         mate = 2 * py + flip(px) if even else 2 * flip(py) + px
         unit = out[phase].at[mate, core]
-        remote(unit, unit, sc["d_send"].at[phase, 0], sc["d_recv"].at[phase, 0], here(me["xdp"])).wait_recv()
+        remote(unit, unit, sc.d_send.at[phase, 0], sc.d_recv.at[phase, 0], here(me.xdp)).wait_recv()
         for slot in (1,) if even else (1, 2):
             go(partial(send_d, phase, slot))
 
     def d_third(phase):
         if phase % 2 == 0:
             pair = out[phase].at[pl.ds(2 * flip(py), 2), core]
-            remote(pair, pair, sc["d_send"].at[phase, 1], sc["d_recv"].at[phase, 1], here(me["ydp"])).wait_recv()
+            remote(pair, pair, sc.d_send.at[phase, 1], sc.d_recv.at[phase, 1], here(me.ydp)).wait_recv()
         else:
             for j in range(2):
                 unit = out[phase].at[2 * j + flip(px), core]
-                remote(unit, unit, sc["d_send"].at[phase, 1 + j], sc["d_recv"].at[phase, 1 + j], here(me["xdp"])).wait_recv()
+                remote(unit, unit, sc.d_send.at[phase, 1 + j], sc.d_recv.at[phase, 1 + j], here(me.xdp)).wait_recv()
         go(partial(send_d, phase, 3))
 
     def d_last(phase):
         row = out[phase].at[:, flip(core)]
-        remote(row, row, sc["d_send"].at[phase, 3], sc["d_recv"].at[phase, 3], here(me["sib"])).wait_recv()
+        remote(row, row, sc.d_send.at[phase, 3], sc.d_recv.at[phase, 3], here(me.sib)).wait_recv()
 
     def finish():
         for make in sends:
             make().wait_send()
 
-    steps = [partial(run_all, [partial(start_a, s) for s in range(n)])]
-    late = {}
+    table = {-1: [partial(start_a, s) for s in range(n)]}
+
+    def put(at, do):
+        table.setdefault(at, []).append(do)
+
+    for at, do in enumerate(beside):
+        put(at, do)
+    for s in range(n):
+        put(s + 3, partial(b_to_c, s))
+        put(s + 5, partial(c_to_z, s))
+        put(s, partial(a_to_b, s))
     for phase in range(phases):
-        end = (phase + 1) * NB - 1
-        for lag, do in ((4, z_to_d), (5, d_second), (6, d_third), (7, d_last)):
-            late.setdefault(end + lag, []).append(partial(do, phase))
-    for s in range(n + 8):
-        batch = []
-        if s < n:
-            batch.append(partial(a_to_b, s))
-        if 0 <= s - 1 < n:
-            batch.append(partial(b_to_c, s - 1))
-        if 0 <= s - 2 < n:
-            batch.append(partial(c_to_z, s - 2))
-        if s < len(beside):
-            batch.append(beside[s])
-        batch += late.get(s, [])
-        if batch:
-            steps.append(partial(run_all, batch))
+        end = (phase + 1) * NB - 1 + 5
+        for lag, do in ((2, z_to_d), (3, d_second), (4, d_third), (5, d_last)):
+            put(end + lag, partial(do, phase))
+    steps = [partial(run_all, table[at]) for at in sorted(table)]
     steps.append(finish)
     return steps
+
+
+def home_scratch():
+    D = pltpu.SemaphoreType.DMA
+    return dict(home_send=D((2,)), home_recv=D((2,)))
+
+
+def home_steps(me, rows_ref, home_ref, sc):
+    band, core = me.band, me.core
+    slot = lax.rem(band, 2)
+
+    def stays(s):
+        return jnp.logical_and(band // 2 == core, 2 * core + s == band)
+
+    def copy(s):
+        to = device(me.dp - core + band // 2, 2 * core + s)
+        return pltpu.make_async_remote_copy(
+            src_ref=rows_ref.at[s], dst_ref=home_ref.at[slot], send_sem=sc.home_send.at[s],
+            recv_sem=sc.home_recv.at[slot], device_id=to, device_id_type=MESH,
+        )
+
+    def begin():
+        for s in range(2):
+            pl.when(stays(s))(
+                lambda: pltpu.make_async_copy(
+                    rows_ref.at[s], home_ref.at[slot], sc.home_recv.at[slot]
+                ).start()
+            )
+            pl.when(jnp.logical_not(stays(s)))(lambda: copy(s).start())
+
+    def finish():
+        for s in range(2):
+            pl.when(jnp.logical_not(stays(s)))(lambda: copy(s).wait_send())
+        for i in range(2):
+            pltpu.make_async_copy(rows_ref.at[i], home_ref.at[i], sc.home_recv.at[i]).wait()
+
+    return begin, finish
+
+
+def group_barrier(me):
+    barrier = pltpu.get_barrier_semaphore()
+    peers = [(me.xdp, me.band), (me.ydp, me.band), (me.sib, me.band)]
+    for k in range(1, NB):
+        other = lax.rem(me.band + k, NB)
+        peers += [(me.dp, other), (me.sib, other)]
+    for dp, band in peers:
+        pl.semaphore_signal(
+            barrier, inc=1, device_id=device(dp, band), device_id_type=MESH
+        )
+    pl.semaphore_wait(barrier, len(peers))
 
 
 def reduce_sources(counts, refs):
@@ -384,9 +424,9 @@
 
 
 def small_steps(me, mods, images, small_ref, ada_ref, every_ref, bias_ref, cond_ref, sc):
-    dp, band, core, px, py, kind = (me[k] for k in ("dp", "band", "core", "px", "py", "kind"))
-    here = lambda d: {"dp": d, "band": band}
-    every, bias, got, cond = sc["s_every"], sc["s_bias"], sc["s_got"], sc["s_cond"]
+    dp, band, core, px, py, kind = me.dp, me.band, me.core, me.px, me.py, me.kind
+    here = lambda d: device(d, band)
+    every, bias, got, cond = sc.s_every, sc.s_bias, sc.s_got, sc.s_cond
     mod_rows = every.shape[2]
     flip = lambda v: 1 - v
 
@@ -396,44 +436,44 @@
         )
 
     def plain(index, src, dst, to):
-        return remote(src, dst, sc["s_send"].at[index], sc["s_recv"].at[index], to)
+        return remote(src, dst, sc.s_send.at[index], sc.s_recv.at[index], to)
 
     def core_copy():
-        return plain(0, small_ref, sc["s_core"], here(me["sib"]))
+        return plain(0, small_ref, sc.s_core, here(me.sib))
 
     def x_copies(mine):
         unit = every.at[band, kind if mine else 2 * py + flip(px)]
         return [
-            plain(1, unit, unit, here(me["xdp"])),
-            plain(2, bias.at[0], got.at[0], here(me["xdp"])),
+            plain(1, unit, unit, here(me.xdp)),
+            plain(2, bias.at[0], got.at[0], here(me.xdp)),
         ]
 
     def y_copies(mine):
         pair = every.at[band, pl.ds(2 * (py if mine else flip(py)), 2)]
         return [
-            plain(3, pair, pair, here(me["ydp"])),
-            plain(4, bias.at[1], got.at[1], here(me["ydp"])),
+            plain(3, pair, pair, here(me.ydp)),
+            plain(4, bias.at[1], got.at[1], here(me.ydp)),
         ]
 
     def z_copies(k, mine):
-        to = {"dp": dp, "band": lax.rem(band + k, NB)}
+        to = device(dp, lax.rem(band + k, NB))
         block = every.at[band if mine else lax.rem(band + NB - k, NB)]
         return [
-            remote(block, block, sc["sz_send"].at[0, k], sc["sz_recv"].at[0, k], to),
-            remote(bias.at[2], got.at[2 + k], sc["sz_send"].at[1, k], sc["sz_recv"].at[1, k], to),
+            remote(block, block, sc.sz_send.at[0, k], sc.sz_recv.at[0, k], to),
+            remote(bias.at[2], got.at[2 + k], sc.sz_send.at[1, k], sc.sz_recv.at[1, k], to),
         ]
 
     def cond_copy(k, mine):
-        to = {"dp": dp, "band": lax.rem(band + k, NB)}
+        to = device(dp, lax.rem(band + k, NB))
         block = cond.at[band if mine else lax.rem(band + NB - k, NB)]
-        return remote(block, block, sc["sc_send"].at[k], sc["sc_recv"].at[k], to)
+        return remote(block, block, sc.sc_send.at[k], sc.sc_recv.at[k], to)
 
     def begin():
         core_copy().start()
 
     def cores():
         core_copy().wait()
-        total = small_ref[...] + sc["s_core"][...]
+        total = small_ref[...] + sc.s_core[...]
         every[band, kind] = total[:mod_rows].astype(jnp.bfloat16)
         bias[0] = total[mod_rows:]
         for copy in x_copies(True):
@@ -466,7 +506,7 @@
                 copy.wait_recv()
         bias_ref[...] = bias[2] + got[3] + got[4] + got[5]
         every_ref[...] = every[...]
-        flat = sc["s_flat"]
+        flat = sc.s_flat
         for i in range(images):
             flat[i] = every[images * core + i, kind].astype(jnp.float32)
         parts = mods // 128
@@ -497,42 +537,49 @@
     phases = len(counts)
     at = sum(counts)
     source = reduce_sources(counts, refs)
-    small_ref, ada_ref = refs[at : at + 2]
-    out = refs[at + 2 : at + 2 + phases]
-    every_ref, bias_ref, cond_ref = refs[at + 2 + phases : at + 5 + phases]
-    sc = dict(zip(names, refs[at + 5 + phases :]))
-    reduce_barrier(me)
+    rows_ref, small_ref, ada_ref = refs[at : at + 3]
+    at += 3
+    out = refs[at : at + phases]
+    home_ref, every_ref, bias_ref, cond_ref = refs[at + phases : at + 4 + phases]
+    sc = SimpleNamespace(**dict(zip(names, refs[at + 4 + phases :])))
+    group_barrier(me)
     small = small_steps(me, mods, images, small_ref, ada_ref, every_ref, bias_ref, cond_ref, sc)
     small[0]()
+    depart, settle = home_steps(me, rows_ref, home_ref, sc)
+    depart()
     for step in reduce_steps(me, phases, source, out, sc, small[1:]):
         step()
-
-
-def reduce_last(grads, mod_part, bias_part, ada_weight, images, collective_id):
+    settle()
+
+
+def reduce_last(grads, rows, mod_part, bias_part, ada_weight, images, collective_id):
     phases = len(grads)
     half, width = grads[0][0].shape[-2:]
     counts = tuple(len(phase) for phase in grads)
     mod_rows, bias_rows = mod_part.shape[0], bias_part.shape[0]
     cond_cols = -(-ada_weight.shape[0] // 128) * 128
-    scratch = dict(**reduce_scratch(phases, half, width), **small_scratch(mod_rows, bias_rows, 8, cond_cols))
+    scratch = dict(
+        **reduce_scratch(phases, half, width), **small_scratch(mod_rows, bias_rows, 8, cond_cols), **home_scratch()
+    )
     any_, vmem = pl.BlockSpec(memory_space=pl.ANY), pl.BlockSpec(memory_space=pltpu.VMEM)
     outs = pl.pallas_call(
         partial(reduce_last_kernel, counts, ada_weight.shape[1], images, tuple(scratch)),
         out_shape=[jax.ShapeDtypeStruct((4, 2, half, width), jnp.bfloat16)] * phases
         + [
+            jax.ShapeDtypeStruct(rows.shape, rows.dtype),
             jax.ShapeDtypeStruct((NB, 4, mod_rows, 128), jnp.bfloat16),
             jax.ShapeDtypeStruct((bias_rows, 128), jnp.float32),
             jax.ShapeDtypeStruct((NB, 8, cond_cols), jnp.float32),
         ],
-        in_specs=[any_] * sum(counts) + [vmem] * 2,
-        out_specs=[any_] * phases + [vmem] * 3,
+        in_specs=[any_] * (sum(counts) + 1) + [vmem] * 2,
+        out_specs=[any_] * (phases + 1) + [vmem] * 3,
         scratch_shapes=list(scratch.values()),
         compiler_params=pltpu.CompilerParams(
             collective_id=collective_id, has_side_effects=True, vmem_limit_bytes=56 * 2**20
         ),
         name="reduce_last",
-    )(*[unit for phase in grads for unit in phase], jnp.concatenate([mod_part, bias_part]), ada_weight)
-    return outs[:phases], outs[phases], outs[phases + 1], outs[phases + 2]
+    )(*[unit for phase in grads for unit in phase], rows, jnp.concatenate([mod_part, bias_part]), ada_weight)
+    return outs[:phases], *outs[phases:]
 
 
 def reduce_attend_kernel(counts, band_slots, names, *refs):
@@ -540,17 +587,19 @@
     phases = len(counts)
     at = sum(counts)
     source = reduce_sources(counts, refs)
-    count_ref, q_ref, own_ref, far_ref, grad_ref, top_ref = refs[at : at + 6]
-    at += 6
+    rows_ref, count_ref, q_ref, own_ref, far_ref, grad_ref, top_ref = refs[at : at + 7]
+    at += 7
     out = refs[at : at + phases]
-    dq_ref, down_ref, dfar_ref = refs[at + phases : at + phases + 3]
-    sc = dict(zip(names, refs[at + phases + 3 :]))
-    qh, kh, vh, gh, stage, stage_sem = (sc[k] for k in ("qh", "kh", "vh", "gh", "stage", "stage_sem"))
+    home_ref, dq_ref, down_ref, dfar_ref = refs[at + phases : at + phases + 4]
+    sc = SimpleNamespace(**dict(zip(names, refs[at + phases + 4 :])))
+    qh, kh, vh, gh, stage, stage_sem = sc.qh, sc.kh, sc.vh, sc.gh, sc.stage, sc.stage_sem
     rows, width = q_ref.shape
     heads = qh.shape[0]
-    reduce_barrier(me)
+    group_barrier(me)
     steps = reduce_steps(me, phases, source, out, sc)
+    depart, settle = home_steps(me, rows_ref, home_ref, sc)
     steps[0]()
+    depart()
     keys, plain, ones = key_tail(count_ref[0], band_slots), flat_tail(0.0), flat_tail(1.0)
     loads = [(q_ref, 0, qh, 0, ones), (grad_ref, 0, gh, 0, plain)]
     for row0, ref in ((0, own_ref), (rows, far_ref)):
@@ -561,18 +610,21 @@
         return pltpu.make_async_copy(ref.at[:, pl.ds(column, width)], stage.at[i % 2], stage_sem.at[i % 2])
 
     load(0).start()
+    for step in steps[1:4]:
+        step()
     for i, (ref, column, heads_ref, row0, tail) in enumerate(loads):
         if i + 1 < len(loads):
             load(i + 1).start()
         load(i).wait()
         pack_heads(stage.at[i % 2], 0, heads_ref, row0, rows, tail)
-    rest = steps[1:]
+    rest = steps[4:]
+    inside = heads // 2
 
     @pl.loop(0, heads)
     def _(h):
         attend_head(h, qh, kh, vh, gh, top_ref)
-        for i, step in enumerate(rest[:heads]):
-            pl.when(h == i)(step)
+        for i, step in enumerate(rest[:inside]):
+            pl.when(h == 2 * i)(step)
 
     stores = [(qh, 0, dq_ref, 0)]
     for row0, ref in ((0, down_ref), (rows, dfar_ref)):
@@ -589,11 +641,12 @@
         store(i).start()
     for i in (len(stores) - 2, len(stores) - 1):
         store(i).wait()
-    for step in rest[heads:]:
+    for step in rest[inside:]:
         step()
-
-
-def reduce_attend(grads, count, query, own, far, grad, top, band_slots, collective_id):
+    settle()
+
+
+def reduce_attend(grads, rows_out, count, query, own, far, grad, top, band_slots, collective_id):
     phases = len(grads)
     half, width = grads[0][0].shape[-2:]
     counts = tuple(len(phase) for phase in grads)
@@ -608,6 +661,7 @@
         gh=pltpu.VMEM((heads, rows, LANES), bf),
         stage=pltpu.VMEM((2, rows, width), bf),
         stage_sem=pltpu.SemaphoreType.DMA((2,)),
+        **home_scratch(),
     )
     any_, vmem = pl.BlockSpec(memory_space=pl.ANY), pl.BlockSpec(memory_space=pltpu.VMEM)
     smem = pl.BlockSpec(memory_space=pltpu.SMEM)
@@ -615,22 +669,22 @@
         partial(reduce_attend_kernel, counts, band_slots, tuple(scratch)),
         out_shape=[jax.ShapeDtypeStruct((4, 2, half, width), bf)] * phases
         + [
+            jax.ShapeDtypeStruct(rows_out.shape, bf),
             jax.ShapeDtypeStruct((rows, width), bf),
             jax.ShapeDtypeStruct((rows, 2 * width), bf),
             jax.ShapeDtypeStruct((rows, 2 * width), bf),
         ],
-        in_specs=[any_] * sum(counts) + [smem] + [any_] * 4 + [vmem],
-        out_specs=[any_] * (phases + 3),
+        in_specs=[any_] * (sum(counts) + 1) + [smem] + [any_] * 4 + [vmem],
+        out_specs=[any_] * (phases + 4),
         scratch_shapes=list(scratch.values()),
         compiler_params=pltpu.CompilerParams(
             collective_id=collective_id, has_side_effects=True, vmem_limit_bytes=60 * 2**20
         ),
         name="reduce_attend",
-    )(*[unit for phase in grads for unit in phase], count, query, own, far, grad, top)
-    return outs[:phases], outs[phases], outs[phases + 1], outs[phases + 2]
-
-
-GATHER_ORDER = (1, 3, 2)
+    )(*[unit for phase in grads for unit in phase], rows_out, count, query, own, far, grad, top)
+    return outs[:phases], *outs[phases:]
+
+
 MOD_BLOCKS = 6
 BLOCK = 128
 
@@ -648,19 +702,22 @@
         own=V((rows, 2 * width), bf), far=V((rows, 2 * width), bf), mixed=V((rows, width), bf),
         attended=V((rows, width), f32), mlp_in=V((rows, width), bf), tops=V((heads, 8, rows), f32),
         qh=V((heads, rows, LANES), bf), kh=V((heads, 2 * rows, LANES), bf), vh=V((heads, 2 * rows, LANES), bf),
-        z_send=D((3, NB)), z_recv=D((3, NB)), a_send=D((9,)), a_recv=D((9,)), b_send=D((9, 2)), b_recv=D((9, 2)),
+        z_send=D((3, 2)), z_recv=D((3, NB)), f_send=D((3, NB)), a_send=D((9,)), a_recv=D((9,)), b_send=D((9, 2)), b_recv=D((9, 2)),
         c_send=D((9,)), c_recv=D((9,)), t_send=D((2, 2)), t_recv=D((2, 2)), m_send=D((2, 2)), m_recv=D((NB,)),
         local=D((4,)), kv_send=D((1,)), kv_recv=D((1,)), done=D((12,)),
     )
 
 
 def gather_steps(me, width, ins, outs, tok_in, tok_out, cot_in, cot_out, note_in, note_out, sc):
-    dp, band, core, px, py, kind = (me[k] for k in ("dp", "band", "core", "px", "py", "kind"))
+    dp, band, core, px, py, kind = me.dp, me.band, me.core, me.px, me.py, me.kind
     base = dp - core
-    dev = lambda d, b: {"dp": d, "band": b}
+    dev = lambda d, b: device(d, b)
     here = lambda d: dev(d, band)
     flip = lambda v: 1 - v
-    order = [(ph, k) for ph in range(3) for k in GATHER_ORDER]
+    low = band < 2
+    bands = (band + 1 - 2 * lax.rem(band, 2), jnp.where(low, 2, 1), jnp.where(low, 3, 0))
+    order = [(ph, b) for ph in range(3) for b in bands]
+    inside = jnp.logical_or(band == 1, band == 2)
     sends = []
 
     def remote(src, dst, ss, rs, to):
@@ -684,55 +741,56 @@
     def row(ph, b, h):
         return outs[ph].at[b, :, h] if ph == 2 else outs[ph].at[b, h]
 
-    def came(k):
-        return lax.rem(band + NB - k, NB)
-
-    def send_z(ph, k):
+    def own_z(ph, up):
         src = ins[ph].at[kind, core] if ph == 2 else ins[ph].at[core, :, cols(kind)]
         return remote(
-            src, unit(ph, band, kind, core), sc["z_send"].at[ph, k], sc["z_recv"].at[ph, k],
-            dev(dp, lax.rem(band + k, NB)),
+            src, unit(ph, band, kind, core), sc.z_send.at[ph, up], sc.z_recv.at[ph, band],
+            dev(dp, band - 1 + 2 * up),
         )
 
+    def pass_z(s):
+        ph, b = order[s]
+        u = unit(ph, b, kind, core)
+        return remote(
+            u, u, sc.f_send.at[ph, b], sc.z_recv.at[ph, b], dev(dp, jnp.where(b < band, band + 1, band - 1))
+        )
+
     def send_a(s):
-        ph, k = order[s]
-        u = unit(ph, came(k), kind, core)
-        return remote(u, u, sc["a_send"].at[s], sc["a_recv"].at[s], here(me["xdp"] if s % 2 == 0 else me["ydp"]))
+        ph, b = order[s]
+        u = unit(ph, b, kind, core)
+        return remote(u, u, sc.a_send.at[s], sc.a_recv.at[s], here(me.xdp if s % 2 == 0 else me.ydp))
 
     def b_copy(s, j, mine):
-        ph, k = order[s]
+        ph, b = order[s]
         if s % 2 == 0:
-            u = pair(ph, came(k), core, py if mine else flip(py))
-            to = me["ydp"]
+            u = pair(ph, b, core, py if mine else flip(py))
+            to = me.ydp
         else:
-            u = unit(ph, came(k), 2 * j + (px if mine else flip(px)), core)
-            to = me["xdp"]
-        return remote(u, u, sc["b_send"].at[s, j], sc["b_recv"].at[s, j], here(to))
+            u = unit(ph, b, 2 * j + (px if mine else flip(px)), core)
+            to = me.xdp
+        return remote(u, u, sc.b_send.at[s, j], sc.b_recv.at[s, j], here(to))
 
     def c_copy(s, mine):
-        ph, k = order[s]
-        u = row(ph, came(k), core if mine else flip(core))
-        return remote(u, u, sc["c_send"].at[s], sc["c_recv"].at[s], here(me["sib"]))
+        ph, b = order[s]
+        u = row(ph, b, core if mine else flip(core))
+        return remote(u, u, sc.c_send.at[s], sc.c_recv.at[s], here(me.sib))
 
     def z_start(ph):
-        for k in GATHER_ORDER:
-            go(partial(send_z, ph, k))
+        pl.when(band < NB - 1)(lambda: own_z(ph, 1).start())
+        pl.when(band > 0)(lambda: own_z(ph, 0).start())
 
     def z_wait(s):
-        ph, k = order[s]
-        u = unit(ph, came(k), kind, core)
-        remote(u, u, sc["z_send"].at[ph, k], sc["z_recv"].at[ph, k], here(dp)).wait_recv()
+        ph, b = order[s]
+        u = unit(ph, b, kind, core)
+        remote(u, u, sc.a_send.at[s], sc.z_recv.at[ph, b], here(dp)).wait_recv()
+        pl.when(inside)(lambda: pass_z(s).start())
         go(partial(send_a, s))
-        if k == GATHER_ORDER[1] and ph < 2:
-            z_start(ph + 1)
-        if k == GATHER_ORDER[2] and ph == 2:
-            move(1, cot_in, cot_out, sc["bounce_t"])
 
     def a_wait(s):
-        ph, k = order[s]
+        ph, b = order[s]
         got = 2 * py + flip(px) if s % 2 == 0 else 2 * flip(py) + px
-        u = unit(ph, came(k), got, core)
-        remote(u, u, sc["a_send"].at[s], sc["a_recv"].at[s], here(me["xdp"])).wait_recv()
+        u = unit(ph, b, got, core)
+        remote(u, u, sc.a_send.at[s], sc.a_recv.at[s], here(me.xdp)).wait_recv()
         for j in range(1 if s % 2 == 0 else 2):
             go(partial(b_copy, s, j, True))
 
@@ -748,7 +806,7 @@
 
     def image_copy(which, src, dst, i):
         to = dev(base + band // 2, 2 * core + i)
-        return remote(src.at[i], dst.at[slot], sc["t_send"].at[which, i], sc["t_recv"].at[which, slot], to)
+        return remote(src.at[i], dst.at[slot], sc.t_send.at[which, i], sc.t_recv.at[which, slot], to)
 
     def at_home(i):
         return jnp.logical_and(band // 2 == core, 2 * core + i == band)
@@ -759,12 +817,12 @@
             @pl.when(at_home(i))
             def _():
                 if bounce is None:
-                    pltpu.make_async_copy(src.at[i], dst.at[slot], sc["t_recv"].at[which, slot]).start()
+                    pltpu.make_async_copy(src.at[i], dst.at[slot], sc.t_recv.at[which, slot]).start()
                 else:
-                    inward = pltpu.make_async_copy(src.at[i], bounce, sc["local"].at[3])
+                    inward = pltpu.make_async_copy(src.at[i], bounce, sc.local.at[3])
                     inward.start()
                     inward.wait()
-                    pltpu.make_async_copy(bounce, dst.at[slot], sc["t_recv"].at[which, slot]).start()
+                    pltpu.make_async_copy(bounce, dst.at[slot], sc.t_recv.at[which, slot]).start()
 
             @pl.when(jnp.logical_not(at_home(i)))
             def _():
@@ -778,11 +836,11 @@
                 image_copy(which, src, dst, i).wait_send()
 
         for s in range(2):
-            pltpu.make_async_copy(dst.at[s], dst.at[s], sc["t_recv"].at[which, s]).wait()
+            pltpu.make_async_copy(dst.at[s], dst.at[s], sc.t_recv.at[which, s]).wait()
 
     def note_copy(i, c):
         return remote(
-            note_in.at[i], note_out.at[band], sc["m_send"].at[i, c], sc["m_recv"].at[band],
+            note_in.at[i], note_out.at[band], sc.m_send.at[i, c], sc.m_recv.at[band],
             dev(base + c, 2 * core + i),
         )
 
@@ -795,16 +853,15 @@
 
                 @pl.when(note_home(i, c))
                 def _():
-                    pltpu.make_async_copy(note_in.at[i], note_out.at[band], sc["m_recv"].at[band]).start()
+                    pltpu.make_async_copy(note_in.at[i], note_out.at[band], sc.m_recv.at[band]).start()
 
                 @pl.when(jnp.logical_not(note_home(i, c)))
                 def _():
                     note_copy(i, c).start()
 
-        move(0, tok_in, tok_out)
         z_start(0)
-        for ph, dst in enumerate((outs[0].at[band], sc["bounce_i"], sc["bounce_o"])):
-            pltpu.make_async_copy(ins[ph], dst, sc["local"].at[ph]).start()
+        for ph, dst in enumerate((outs[0].at[band], sc.bounce_i, sc.bounce_o)):
+            pltpu.make_async_copy(ins[ph], dst, sc.local.at[ph]).start()
 
     def arrived():
         for i in range(2):
@@ -815,25 +872,37 @@
                     note_copy(i, c).wait_send()
 
         for b in range(NB):
-            pltpu.make_async_copy(note_in.at[0], note_out.at[b], sc["m_recv"].at[b]).wait()
+            pltpu.make_async_copy(note_in.at[0], note_out.at[b], sc.m_recv.at[b]).wait()
         move_wait(0, tok_in, tok_out)
 
     def place():
-        for ph, dst in ((1, sc["bounce_i"]), (2, sc["bounce_o"])):
-            pltpu.make_async_copy(ins[ph], dst, sc["local"].at[ph]).wait()
-            pltpu.make_async_copy(dst, outs[ph].at[band], sc["local"].at[ph]).start()
+        for ph, dst in ((1, sc.bounce_i), (2, sc.bounce_o)):
+            pltpu.make_async_copy(ins[ph], dst, sc.local.at[ph]).wait()
+            pltpu.make_async_copy(dst, outs[ph].at[band], sc.local.at[ph]).start()
 
     def first_here():
-        pltpu.make_async_copy(ins[0], outs[0].at[band], sc["local"].at[0]).wait()
+        pltpu.make_async_copy(ins[0], outs[0].at[band], sc.local.at[0]).wait()
 
     def finish():
-        for ph, src in ((1, sc["bounce_i"]), (2, sc["bounce_o"])):
-            pltpu.make_async_copy(src, outs[ph].at[band], sc["local"].at[ph]).wait()
+        for ph, src in ((1, sc.bounce_i), (2, sc.bounce_o)):
+            pltpu.make_async_copy(src, outs[ph].at[band], sc.local.at[ph]).wait()
         move_wait(1, cot_in, cot_out)
+        for ph in range(3):
+            pl.when(band < NB - 1)(lambda: own_z(ph, 1).wait_send())
+            pl.when(band > 0)(lambda: own_z(ph, 0).wait_send())
+        for s in range(len(order)):
+            pl.when(inside)(lambda: pass_z(s).wait_send())
         for make in sends:
             make().wait_send()
 
-    return dict(
+    def images(which):
+        if which == 0:
+            move(0, tok_in, tok_out)
+        else:
+            move(1, cot_in, cot_out, sc.bounce_t)
+
+    return SimpleNamespace(
+        i=images, s=z_start,
         begin=begin, arrived=arrived, place=place, first_here=first_here, finish=finish,
         z=z_wait, a=a_wait, b=b_wait, c=c_wait,
     )
@@ -844,21 +913,13 @@
     qp_in, inner_in, outer_in, tok_in, cot_in, note_in, table_ref = refs[:7]
     (qp_out, inner_out, outer_out, cot_out, vec_out, residual_out, attn_out, query_out, own_out, far_out,
      tops_out, mixed_out, attended_out, mlp_out) = refs[7:21]
-    sc = dict(zip(names, refs[21:]))
-    rows, width = sc["residual"].shape
+    sc = SimpleNamespace(**dict(zip(names, refs[21:])))
+    rows, width = sc.residual.shape
     heads = width // HEAD_DIM
-    core = me["core"]
-    qp, tok, notes, vec = sc["qp"], sc["tok"], sc["notes"], sc["vec"]
-
-    barrier = pltpu.get_barrier_semaphore()
-    peers = [(me["xdp"], me["band"]), (me["ydp"], me["band"]), (me["sib"], me["band"])]
-    for k in range(1, NB):
-        other = lax.rem(me["band"] + k, NB)
-        peers += [(me["dp"], other), (me["sib"], other)]
-    for d, b in peers:
-        pl.semaphore_signal(barrier, inc=1, device_id={"dp": d, "band": b}, device_id_type=MESH)
-    pl.semaphore_wait(barrier, len(peers))
-
+    core = me.core
+    qp, tok, notes, vec = sc.qp, sc.tok, sc.notes, sc.vec
+
+    group_barrier(me)
     g = gather_steps(
         me, width, (qp_in, inner_in, outer_in), (qp, inner_out, outer_out), tok_in, tok, cot_in, cot_out,
         note_in, notes, sc,
@@ -866,17 +927,18 @@
     saves = []
 
     def save(src, dst):
-        copy = pltpu.make_async_copy(src, dst, sc["done"].at[len(saves)])
+        copy = pltpu.make_async_copy(src, dst, sc.done.at[len(saves)])
         copy.start()
         saves.append(copy)
 
-    def run(text):
-        for word in text.split():
-            g[word[0]](int(word[1:]))
-
-    g["begin"]()
-    g["place"]()
-    g["arrived"]()
+    def run(*words):
+        for do, index in words:
+            do(index)
+
+    g.begin()
+    g.place()
+    run((g.z, 0), (g.z, 1), (g.i, 0), (g.a, 0), (g.a, 1), (g.z, 2), (g.s, 1), (g.b, 0), (g.b, 1), (g.a, 2), (g.c, 0), (g.c, 1), (g.z, 3), (g.z, 4), (g.b, 2))
+    g.arrived()
     spread_notes(notes, vec, width)
     grid_rows = notes[0, 63:64, 0:1]
     grid_cols = notes[0, 63:64, 1:2]
@@ -904,15 +966,14 @@
             picks.append(part[0] + (part[1] + part[2]))
         token = tok[step // per_image, pl.ds(lax.rem(step, per_image) * BLOCK, BLOCK), :]
         residual = token.astype(jnp.float32) + jnp.concatenate(picks, 1)
-        sc["residual"][sub, :] = residual
+        sc.residual[sub, :] = residual
         normed = normalize(residual)[0]
-        sc["attn_in"][sub, :] = (normed * (1.0 + vec[1:2, :]) + vec[0:1, :]).astype(jnp.bfloat16)
-
-    save(sc["residual"], residual_out)
-    save(sc["attn_in"], attn_out)
-    run("z0 z1 a0 z2 a1 b0 a2 b1 c0 b2 c1")
-    g["first_here"]()
-    run("z3 c2")
+        sc.attn_in[sub, :] = (normed * (1.0 + vec[1:2, :]) + vec[0:1, :]).astype(jnp.bfloat16)
+
+    save(sc.residual, residual_out)
+    save(sc.attn_in, attn_out)
+    g.first_here()
+    run((g.c, 2))
     save(qp, qp_out)
     tile = width // 3
     full = NB * 2 * qp.shape[2]
@@ -928,66 +989,69 @@
 
     @pl.loop(0, 3)
     def _(step):
-        sc["own"][:, here(step)] = product(sc["attn_in"], width, step).astype(jnp.bfloat16)
-
-    run("z4 a3")
+        sc.own[:, here(step)] = product(sc.attn_in, width, step).astype(jnp.bfloat16)
+
+    run((g.a, 3), (g.z, 5), (g.s, 2))
 
     @pl.loop(0, 3)
     def _(step):
-        value = product(sc["attn_in"], 2 * width, step) + vec[7:8, here(step)]
-        sc["own"][:, here(step + 3)] = value.astype(jnp.bfloat16)
+        value = product(sc.attn_in, 2 * width, step) + vec[7:8, here(step)]
+        sc.own[:, here(step + 3)] = value.astype(jnp.bfloat16)
 
     swap = pltpu.make_async_remote_copy(
-        src_ref=sc["own"], dst_ref=sc["far"], send_sem=sc["kv_send"].at[0], recv_sem=sc["kv_recv"].at[0],
-        device_id={"dp": me["sib"], "band": me["band"]}, device_id_type=MESH,
+        src_ref=sc.own, dst_ref=sc.far, send_sem=sc.kv_send.at[0], recv_sem=sc.kv_recv.at[0],
+        device_id=device(me.sib, me.band), device_id_type=MESH,
     )
     swap.start()
-    run("z5 a4 b3")
+    run((g.a, 4), (g.b, 3))
 
     @pl.loop(0, 3)
     def _(step):
-        value = product(sc["attn_in"], 0, step) + vec[6:7, here(step)]
-        sc["query"][:, here(step)] = value.astype(jnp.bfloat16)
-
-    save(sc["query"], query_out)
-    save(sc["own"], own_out)
-    qh, kh, vh = sc["qh"], sc["kh"], sc["vh"]
+        value = product(sc.attn_in, 0, step) + vec[6:7, here(step)]
+        sc.query[:, here(step)] = value.astype(jnp.bfloat16)
+
+    save(sc.query, query_out)
+    save(sc.own, own_out)
+    run((g.a, 5), (g.b, 4), (g.c, 3), (g.z, 6))
+    qh, kh, vh = sc.qh, sc.kh, sc.vh
     keys, plain = key_tail(valid_count, band_slots), flat_tail(0.0)
-    pack_heads(sc["query"], 0, qh, 0, rows, flat_tail(1.0))
-    pack_heads(sc["own"], 0, kh, 0, rows, keys)
-    pack_heads(sc["own"], width, vh, 0, rows, plain)
+    pack_heads(sc.query, 0, qh, 0, rows, flat_tail(1.0))
+    pack_heads(sc.own, 0, kh, 0, rows, keys)
+    pack_heads(sc.own, width, vh, 0, rows, plain)
     swap.wait()
-    save(sc["far"], far_out)
-    pack_heads(sc["far"], 0, kh, rows, rows, keys)
-    pack_heads(sc["far"], width, vh, rows, rows, plain)
-    beside = ["z6 a5 b4 c3", "", "z7 a6 b5 c4", "", "", "z8 a7 b6 c5", "", "", "a8 b7 c6", "", "", "b8 c7", "", "", "c8"]
+    save(sc.far, far_out)
+    pack_heads(sc.far, 0, kh, rows, rows, keys)
+    pack_heads(sc.far, width, vh, rows, rows, plain)
+    beside = {
+        0: ((g.z, 7), (g.b, 5), (g.c, 4)), 2: ((g.a, 6), (g.z, 8), (g.i, 1)), 4: ((g.a, 7), (g.b, 6), (g.c, 5)), 7: ((g.a, 8), (g.b, 7), (g.c, 6)), 10: ((g.b, 8), (g.c, 7)),
+        13: ((g.c, 8),),
+    }
 
     @pl.loop(0, heads)
     def _(h):
-        attend_block(h, qh, kh, vh, sc["tops"])
-        for i, text in enumerate(beside):
-            if text:
-                pl.when(h == i)(partial(run, text))
-
-    unpack_heads(qh, 0, rows, sc["mixed"], 0)
-    save(sc["tops"], tops_out)
-    save(sc["mixed"], mixed_out)
+        attend_block(h, qh, kh, vh, sc.tops)
+        for i, words in beside.items():
+            pl.when(h == i)(partial(run, *words))
+
+    unpack_heads(qh, 0, rows, sc.mixed, 0)
+    save(sc.tops, tops_out)
+    save(sc.mixed, mixed_out)
 
     @pl.loop(0, 3)
     def _(step):
-        sc["attended"][:, here(step)] = product(sc["mixed"], 3 * width, step) + vec[8:9, here(step)]
-
-    save(sc["attended"], attended_out)
+        sc.attended[:, here(step)] = product(sc.mixed, 3 * width, step) + vec[8:9, here(step)]
+
+    save(sc.attended, attended_out)
 
     @pl.loop(0, rows // BLOCK)
     def _(step):
         sub = pl.ds(pl.multiple_of(step * BLOCK, BLOCK), BLOCK)
-        middle = sc["residual"][sub, :] + vec[2:3, :] * sc["attended"][sub, :]
+        middle = sc.residual[sub, :] + vec[2:3, :] * sc.attended[sub, :]
         normed = normalize(middle)[0]
-        sc["mlp_in"][sub, :] = (normed * (1.0 + vec[4:5, :]) + vec[3:4, :]).astype(jnp.bfloat16)
-
-    save(sc["mlp_in"], mlp_out)
-    g["finish"]()
+        sc.mlp_in[sub, :] = (normed * (1.0 + vec[4:5, :]) + vec[3:4, :]).astype(jnp.bfloat16)
+
+    save(sc.mlp_in, mlp_out)
+    g.finish()
     for copy in saves:
         copy.wait()
 
@@ -1058,24 +1122,6 @@
     ]
 
 
-def home_perm_back(dp_count, band_count, turn):
-    pairs = []
-    for dp in range(dp_count):
-        for band in range(band_count):
-            to_dp = dp - dp % 2 + band // 2
-            to_band = 2 * (dp % 2) + (band + turn) % 2
-            pairs.append((dp * band_count + band, to_dp * band_count + to_band))
-    return pairs
-
-
-def send_home(rows, band, perms):
-    odd = lax.rem(band, 2) == 1
-    first = jnp.where(odd, rows[1], rows[0])
-    second = jnp.where(odd, rows[0], rows[1])
-    got = [lax.ppermute(part, ("dp", "band"), perm) for part, perm in zip((first, second), perms)]
-    return jnp.stack([jnp.where(odd, got[1], got[0]), jnp.where(odd, got[0], got[1])])
-
-
 def position_parts(width):
     quarter = width // 4
     frequency = 10000.0 ** (-jnp.arange(quarter, dtype=jnp.float32) / quarter)
@@ -1134,7 +1180,6 @@
     hidden = inner_weight.shape[1]
     part_rows = qkv_weight.shape[0]
     siblings = pair_perm(dp_count, band_count)
-    homes = [home_perm_back(dp_count, band_count, turn) for turn in range(2)]
 
     condition_f = condition.astype(jnp.float32)
     activated = jax.nn.silu(condition_f).astype(jnp.bfloat16)
@@ -1182,7 +1227,6 @@
     hidden_act = jax.nn.gelu(hidden_pre, approximate=True).astype(jnp.bfloat16)
     mlp_out = jnp.dot(hidden_act, outer_full, preferred_element_type=jnp.float32) + outer_bias_full
     block_out = (middle + gate_two * mlp_out).astype(jnp.bfloat16)
-    block_home = send_home(block_out.reshape(images, band_slots, width), band, homes)
 
     grad_out = cotangent_here.reshape(rows, width).astype(jnp.float32) * is_valid[:, None].astype(
         jnp.float32
@@ -1211,8 +1255,8 @@
     grad_proj = rows_dot(mixed_rows, grad_attended).astype(jnp.bfloat16)
     grad_proj_bias = jnp.sum(grad_attended.astype(jnp.float32), 0)
     grad_mixed = lanes_dot(grad_attended, proj_full).astype(jnp.bfloat16)
-    (outer_sum, inner_sum), grad_query, own_terms, far_terms = reduce_attend(
-        [[grad_outer], grad_inner], valid_count, query_rows, key_value, other_key_value, grad_mixed, tops,
+    (outer_sum, inner_sum), block_home, grad_query, own_terms, far_terms = reduce_attend(
+        [[grad_outer], grad_inner], block_out.reshape(images, band_slots, width), valid_count, query_rows, key_value, other_key_value, grad_mixed, tops,
         band_slots, 1,
     )
     other_terms = lax.ppermute(far_terms, both, siblings)
@@ -1230,10 +1274,6 @@
     grad_shift_one = jnp.sum(grad_attn_in, 0)
     grad_scale_one = jnp.sum(grad_attn_in * normed_one, 0)
     grad_tokens = grad_middle + norm_back(grad_attn_in * (1.0 + scale_one), normed_one, inverse_one)
-    tokens_home = send_home(
-        grad_tokens.astype(jnp.bfloat16).reshape(images, band_slots, width), band, homes
-    ).astype(jnp.float32)
-
     part_mod = jnp.concatenate(
         [grad_shift_one, grad_scale_one, grad_gate_one, grad_shift_two, grad_scale_two, grad_gate_two]
     )
@@ -1242,9 +1282,11 @@
     part_bias = jnp.concatenate(
         [grad_query_bias, grad_value_bias, grad_proj_bias, grad_inner_bias, grad_outer_bias]
     ).reshape(-1, 128)
-    (first_sum,), every, bias_grads, grad_act = reduce_last(
-        [grad_first + [grad_proj.reshape(blocks)]], part_mod, part_bias, ada_weight, images, 2
-    )
+    (first_sum,), tokens_home, every, bias_grads, grad_act = reduce_last(
+        [grad_first + [grad_proj.reshape(blocks)]],
+        grad_tokens.astype(jnp.bfloat16).reshape(images, band_slots, width), part_mod, part_bias, ada_weight, images, 2
+    )
+    tokens_home = tokens_home.astype(jnp.float32)
     every = every_group(every, dp_count)
     bias_grads = over_groups(bias_grads, dp_count).reshape(-1)
     every = jnp.swapaxes(every, 1, 2).reshape(dp_count * images, -1)
@@ -1263,12 +1305,10 @@
     first_sum, inner_sum, outer_sum = [
         over_groups(piece, dp_count) for piece in (first_sum, inner_sum, outer_sum)
     ]
-    weight_sums = dict(
-        qkv=side_by_side([first_sum[t] for t in range(3)]),
-        proj=first_sum[3].reshape(part_rows, width).astype(jnp.float32),
-        inner=side_by_side([inner_sum[t] for t in range(4)]),
-        outer=outer_sum.reshape(4 * part_rows, width).astype(jnp.float32),
-    )
+    qkv_sum = side_by_side([first_sum[t] for t in range(3)])
+    proj_sum = first_sum[3].reshape(part_rows, width).astype(jnp.float32)
+    inner_sum = side_by_side([inner_sum[t] for t in range(4)])
+    outer_sum = outer_sum.reshape(4 * part_rows, width).astype(jnp.float32)
     bias_parts = []
     at = 0
     for piece in (query_bias, value_bias, proj_bias, inner_bias, outer_bias):
@@ -1281,14 +1321,14 @@
         grad_condition,
         grad_ada,
         grad_ada_bias,
-        weight_sums["qkv"],
+        qkv_sum,
         bias_parts[0],
         bias_parts[1],
-        weight_sums["proj"],
+        proj_sum,
         bias_parts[2],
-        weight_sums["inner"],
+        inner_sum,
         bias_parts[3],
-        weight_sums["outer"],
+        outer_sum,
         bias_parts[4],
     )
 

time: 705 us -> 615 us (0.87)
  Pallas kernels: 488 us -> 436 us
  waiting for transfers between devices: 16.6 us -> 0.01 us
  starting transfers between devices: 13.9 us -> 0.49 us
    pallas_call x1, Pallas kernels: 202 us -> 173 us  [forward_block(): pl.pallas_call(partial(forward_kernel, tuple(scratch), band_slots), out_s...]
    pallas_call x1, Pallas kernels: 178 us -> 152 us  [reduce_attend(): pl.pallas_call(partial(reduce_attend_kernel, counts, band_slots, tuple(sc...]
    ppermute x4 -> x0, waiting for transfers between devices: 16.6 us -> none  [send_home(): lax.ppermute(part, ('dp', 'band'), perm)]
    ppermute x4 -> x0, starting transfers between devices: 13.8 us -> none  [send_home(): lax.ppermute(part, ('dp', 'band'), perm)]
  transfers between devices with their start and end apart: 5 -> 1, of which waited for: 3 -> 0; matrix products, arithmetic and copies ran while one was open for 4% -> 3% of each run, Pallas kernels for 0% -> 0%
where the time goes in v5:
time: 615 us; the launch traced here: 603 us
  Pallas kernels  436 us (71%)
  matrix products  115 us (19%)
  other arithmetic  32.1 us (5%)
  local copies, waits for them, and re-layouts  17.8 us (3%)
    pallas_call x1, Pallas kernels, forward_block(): pl.pallas_call(partial(forward_kernel, tuple(scratch), band_slots), out_s...  173 us
    pallas_call x1, Pallas kernels, reduce_attend(): pl.pallas_call(partial(reduce_attend_kernel, counts, band_slots, tuple(sc...  152 us
    pallas_call x1, Pallas kernels, reduce_last(): pl.pallas_call(partial(reduce_last_kernel, counts, ada_weight.shape[1], i...  111 us
    dot_general x10, matrix products, rows_dot(): lax.dot_general(left, right, (((0,), (0,)), ((), ())), preferred_element_...  43.5 us
    dot_general x4, matrix products, lanes_dot(): lax.dot_general(left, right, (((1,), (1,)), ((), ())), preferred_element_...  40.9 us
    dot_general x1, matrix products, body(): jnp.dot(hidden_act, outer_full, preferred_element_type=jnp.float32)  15.6 us
  transfers between devices with their start and end apart: 1, of which 0 were waited for; matrix products, arithmetic and copies ran while one was open for 3% of the time, Pallas kernels for 0%

profile of v5, /device:TPU:1, one launch (start us, length us, event | category | flops | bytes accessed | tf_op | source)
XLA Modules:
  0.0 603.2 jit_solution(14639769422126646204)
XLA Ops:
  0.7 0.7 add_divide_fusion
  1.5 0.7 convert_element_type.195
  2.2 0.8 convert_dynamic-update-slice_fusion
  3.0 3.0 fusion.9
  6.9 0.7 sine_bitcast_fusion
  7.8 1.7 pad_maximum_fusion
  9.5 0.9 pad_maximum_fusion.1.refs_6_
  10.3 172.5 %forward_block.1 = (bf16[4,2,144,4608]{3,2,1,0:T(8,128)(2,1)}, bf16[4,2,144,4608]{3,2,1,0:T(8,128)(2,1)}, bf16[4,4,2,144,1152]{4,3,2,1,0:T(8,128)(2,1)}, bf16[2,...) custom-call(bf16[2,144,4608]{2,1,0:T(8,128)(2,1)} %bitcast.100, ...), custom_call_target="tpu_custom_call" | custom-call | tf_op jit(solution)/shard_map/forward_block/pallas_call | solution.py:1099
  182.9 1.6 multiply_reduce_fusion.10
  184.5 1.2 slice.114
  185.7 0.8 slice.112
  187.7 11.6 %fusion.42 = f32[512,4608]{1,0:T(8,128)} fusion(bf16[512,1152]{1,0:T(8,128)(2,1)} %get-tuple-element.39, bf16[1152,4608]{1,0:T(8,128)(2,1)} %bitcast.139), kind=kOutput, calls=%fused_computation.148 | convolution fusion | flops 5435817984 | bytes 21233664 | tf_op jit(solution)/shard_map/dot_general | solution.py:1226
  199.3 1.0 convert_reduce_fusion.1
  200.4 16.3 %convert_reduce_fusion = (f32[4608]{0:T(1024)}, bf16[512,4608]{1,0:T(8,128)(2,1)S(1)}) fusion(f32[512,4608]{1,0:T(8,128)} %fusion.42, f32[4608]{0:T(1024)S(1)} %add.137, bf16[512,1152]{1,0:T(8,128)(2,1)S(1)} %bitcast.123, bf16[4608,1152]{1,0:T(8,128)(2,1)} %bitcast.137), kind=kOutput, calls=%fused_computation.10 | convolution fusion | flops 5490077184 | bytes 25989120 | tf_op jit(solution)/shard_map/dot_general | solution.py:82
  216.7 3.2 convolution_convert_fusion.5
  219.9 3.2 convolution_convert_fusion.6
  223.2 3.2 convolution_convert_fusion.7
  226.4 3.2 convolution_convert_fusion.8
  229.6 0.8 reduce_sum.184
  230.4 0.7 broadcast_multiply_fusion.2
  231.1 2.4 fusion.39
  234.5 11.2 %multiply_reduce_fusion.1 = (f32[1152]{0:T(1024)}, f32[512]{0:T(512)S(1)}, f32[512]{0:T(512)S(1)}, f32[1152]{0:T(1024)}, f32[512,1152]{1,0:T(8,128)S(1)}) fusion(f32[512,1152]{1,0:T(8,128)S(1)} %get-tuple-element.86, f32[512]{0:T(512)S(1)} %add_rsqrt_fusion.1, f32[512]{0:T(512)S(1)} %get-tuple-element.116, f32[1152]{0:T(1024)S(1)} %copy-done.23, ...), kind=kOutput, calls=%fused_computation.40 | convolution fusion | flops 5441123328 | bytes 20076032 | tf_op jit(solution)/shard_map/dot_general | solution.py:82
  245.8 15.6 %multiply_reduce_fusion = (f32[1152]{0:T(1024)}, bf16[512,1152]{1,0:T(8,128)(2,1)}, f32[1152]{0:T(1024)}, bf16[512,1152]{1,0:T(8,128)(2,1)S(1)}, f32[512,1152]{1,0:T(8,128)}, /*index=5*/bf16[512,1152]{1,0:T(8,128)(2,1)S(1)}) fusion(bf16[2,256,1152]{2,1,0:T(8,128)(2,1)S(1)} %copy-done.10, f32[512]{0:T(512)S(1)} %copy-done.30, ...), kind=kOutput, calls=%fused_computation.39 | convolution fusion | flops 5472385024 | bytes 31906816 | tf_op jit(solution)/shard_map/dot_general | solution.py:1228
  261.5 13.0 %convolution_convert_fusion = bf16[4608,1152]{1,0:T(8,128)(2,1)} fusion(bf16[512,1152]{1,0:T(8,128)(2,1)S(1)} %get-tuple-element.103, f32[512,4608]{1,0:T(8,128)} %fusion.42, f32[4608]{0:T(1024)S(1)} %copy-done.19), kind=kOutput, calls=%fused_computation | convolution fusion | flops 5464719360 | bytes 21252096 | tf_op jit(solution)/shard_map/dot_general | solution.py:86
  274.5 4.6 convolution_convert_fusion.9.refs_10_
  279.1 151.9 %reduce_attend.1 = (bf16[4,2,144,1152]{3,2,1,0:T(8,128)(2,1)}, bf16[4,2,144,1152]{3,2,1,0:T(8,128)(2,1)}, bf16[2,256,1152]{2,1,0:T(8,128)(2,1)}, bf16[512,1152]{...) custom-call(bf16[4,4,2,144,1152]{4,3,2,1,0:T(8,128)(2,1)} %bitcast.99, ...), custom_call_target="tpu_custom_call" | custom-call | tf_op jit(solution)/shard_map/reduce_attend/pallas_call | solution.py:668
  431.6 3.2 fusion.40
  434.8 3.3 convolution_convert_fusion.1
  438.1 3.2 convolution_convert_fusion.4
  441.5 4.2 maximum_convert_fusion
  445.8 2.9 bitcast_convert_fusion
  448.7 2.4 add_convert_fusion
  451.4 3.2 convolution_convert_fusion.2
  454.6 3.2 convolution_convert_fusion.3
  457.9 8.7 %multiply_reduce_fusion.3 = (f32[1152]{0:T(1024)S(1)}, f32[512]{0:T(512)S(1)}, f32[512]{0:T(512)S(1)}, f32[1152]{0:T(1024)S(1)}, f32[512,1152]{1,0:T(8,128)S(1)}) fusion(f32[512,1152]{1,0:T(8,128)S(1)} %copy-done, f32[512]{0:T(512)S(1)} %copy-done.22, f32[512]{0:T(512)S(1)} %copy-done.21, f32[1152]{0:T(1024)S(1)} %get-tuple-element.73, ...), kind=kOutput, calls=%fused_computation.42 | convolution fusion | flops 4089246720 | bytes 16242176 | tf_op jit(solution)/shard_map/dot_general | solution.py:82
  466.8 2.0 multiply_reduce_fusion.2
  468.8 0.7 concatenate.80
  470.2 111.3 %reduce_last.1 = (bf16[4,2,144,1152]{3,2,1,0:T(8,128)(2,1)}, bf16[2,256,1152]{2,1,0:T(8,128)(2,1)}, bf16[4,4,64,128]{3,2,1,0:T(8,128)(2,1)}, f32[72,128]{1,0:T(8,128)}, f32[4,8,384]{2,1,0:T(8,128)}) custom-call(bf16[4,2,144,1152]{3,2,1,0:T(8,128)(2,1)} %bitcast.103, bf16[4,2,144,1152]{3,2,1,0:T(8,128)(2,1)} %bitcast.105, ...), custom_call_target="tpu_custom_call" | custom-call | tf_op jit(solution)/shard_map/reduce_last/pallas_call | solution.py:565
  581.5 1.0 copy.30
  582.7 0.8 slice_bitcast_fusion.2
  583.5 0.7 slice_bitcast_fusion
  584.3 1.9 fusion.41
  586.2 4.6 fusion.22
  590.7 1.2 bitcast_convert_fusion.1
  592.5 1.6 convert_element_type.236
  594.7 0.8 slice_bitcast_fusion.1
  599.5 2.2 maximum_convert_fusion.1
  601.7 1.0 copy.51
  (142 shorter events, 9.7 us)
Async XLA Ops:
  0.6 5.4 copy-start.12
  0.7 5.4 copy-start.35
  0.7 5.4 copy-start.31
  0.7 5.4 copy-start.32
  0.7 5.4 copy-start.33
  0.7 5.5 copy-start.34
  0.7 5.5 copy-start.29
  3.0 4.8 copy-start.5
  3.0 4.8 copy-start.11
  187.7 12.7 %copy-start.18 = (f32[4608]{0:T(1024)}, f32[4608]{0:T(1024)S(1)}, u32[]{:S(2)}) copy-start(f32[4608]{0:T(1024)S(1)} %add.137) | copy-start | bytes 55300
  187.7 11.6 %copy-start.10 = (bf16[2,256,1152]{2,1,0:T(8,128)(2,1)S(1)}, bf16[2,256,1152]{2,1,0:T(8,128)(2,1)}, u32[]{:S(2)}) copy-start(bf16[2,256,1152]{2,1,0:T(8,128)(2,1)} %get-tuple-element.42) | copy-start | bytes 3538948
  200.4 16.3 %copy-start.39 = (bf16[512,1152]{1,0:T(8,128)(2,1)S(1)}, bf16[512,1152]{1,0:T(8,128)(2,1)}, u32[]{:S(2)}) copy-start(bf16[512,1152]{1,0:T(8,128)(2,1)} %get-tuple-element.39) | copy-start | bytes 3538948
  216.7 9.7 %copy-start.40 = (bf16[512,4608]{1,0:T(8,128)(2,1)}, bf16[512,4608]{1,0:T(8,128)(2,1)S(1)}, u32[]{:S(2)}) copy-start(bf16[512,4608]{1,0:T(8,128)(2,1)S(1)} %get-tuple-element.81) | copy-start | bytes 14155780
  226.4 3.2 copy-start
  231.1 2.4 copy-start.20
  231.1 3.4 slice-start
  231.1 3.4 slice-start.1
  233.5 1.0 copy-start.23
  234.5 11.3 %copy-start.16 = (f32[1152]{0:T(1024)S(1)}, f32[1152]{0:T(1024)}, u32[]{:S(2)}) copy-start(f32[1152]{0:T(1024)} %get-tuple-element.76) | copy-start | bytes 13828
  234.5 11.3 %copy-start.19 = (f32[4608]{0:T(1024)S(1)}, f32[4608]{0:T(1024)}, u32[]{:S(2)}) copy-start(f32[4608]{0:T(1024)} %copy-done.18) | copy-start | bytes 55300
  234.5 11.3 %copy-start.24 = (f32[1152]{0:T(1024)S(1)}, f32[1152]{0:T(1024)}, u32[]{:S(2)}) copy-start(f32[1152]{0:T(1024)} %get-tuple-element.75) | copy-start | bytes 13828
  234.5 11.3 %copy-start.30 = (f32[512]{0:T(512)S(1)}, f32[512]{0:T(512)}, u32[]{:S(2)}) copy-start(f32[512]{0:T(512)} %fusion.31) | copy-start | bytes 6148
  261.5 13.1 %copy-start.41 = (bf16[512,1152]{1,0:T(8,128)(2,1)}, bf16[512,1152]{1,0:T(8,128)(2,1)S(1)}, u32[]{:S(2)}) copy-start(bf16[512,1152]{1,0:T(8,128)(2,1)S(1)} %get-tuple-element.98) | copy-start | bytes 3538948
  431.1 17.6 %collective-permute-start = (bf16[512,2304]{1,0:T(8,128)(2,1)}, bf16[512,2304]{1,0:T(8,128)(2,1)}, u32[]{:S(2)}, u32[]{:S(2)}) collective-permute-start(bf16[512,2304]{1,0:T(8,128)(2,1)} %get-tuple-element.55), channel_id=1, source_target_pairs={{0,4},{1,5},{2,6},{3,7},{4,0},{5,1},{6,2},{7,3},{8,12},{9,13},{10,... | collective-permute-start | bytes 7077896 | tf_op jit(solution)/shard_map/ppermute | solution.py:1262
  431.6 3.2 copy-start.38
  431.6 3.2 copy-start.42
  434.8 3.3 copy-start.8
  434.8 3.3 copy-start.36
  441.5 4.2 copy-start.2
  445.8 2.9 copy-start.3
  448.7 2.6 copy-start.37
  454.6 3.3 copy-start.9
  454.6 3.3 copy-start.21
  454.6 3.3 copy-start.22
  457.8 8.8 %copy-start.25 = (f32[1152]{0:T(1024)S(1)}, f32[1152]{0:T(1024)}, u32[]{:S(2)}) copy-start(f32[1152]{0:T(1024)} %get-tuple-element.97) | copy-start | bytes 13828
  457.8 8.8 %copy-start.17 = (f32[4608]{0:T(1024)S(1)}, f32[4608]{0:T(1024)}, u32[]{:S(2)}) copy-start(f32[4608]{0:T(1024)} %get-tuple-element.80) | copy-start | bytes 55300
  457.8 8.9 %copy-start.14 = (f32[1152]{0:T(1024)S(1)}, f32[1152]{0:T(1024)}, u32[]{:S(2)}) copy-start(f32[1152]{0:T(1024)} %get-tuple-element.78) | copy-start | bytes 13828
  457.8 8.9 %copy-start.1 = (f32[512,1152]{1,0:T(8,128)S(1)}, f32[512,1152]{1,0:T(8,128)}, u32[]{:S(2)}) copy-start(f32[512,1152]{1,0:T(8,128)} %get-tuple-element.45) | copy-start | bytes 7077892
  457.9 8.9 %copy-start.4 = (f32[512,1152]{1,0:T(8,128)S(1)}, f32[512,1152]{1,0:T(8,128)}, u32[]{:S(2)}) copy-start(f32[512,1152]{1,0:T(8,128)} %get-tuple-element.99) | copy-start | bytes 7077892
  466.7 2.1 copy-start.15
  466.7 2.1 copy-start.26
  466.8 2.1 copy-start.27
  466.8 2.1 copy-start.28
  590.7 1.8 copy-start.6
  590.7 4.9 copy-start.13
  599.5 2.2 copy-start.7

commit v6 on v5

--- a/solution.py
+++ b/solution.py
@@ -152,30 +152,40 @@
 REDUCE_ORDER = (1, 3, 2, 0)
 
 
-def reduce_scratch(phases, half, width):
+FRONT, BACK = 1, 2
+
+
+def reduce_scratch(plan, half, width):
     bf = jnp.bfloat16
-    n = phases * NB
+    n = NB * sum(1 for todo in plan if todo & FRONT)
+    m = len(plan)
     D = pltpu.SemaphoreType.DMA
-    return dict(
-        acc=pltpu.VMEM((n, 4, half, width), bf),
-        recv_a=pltpu.VMEM((n, 4, half, width), bf),
-        recv_b=pltpu.VMEM((n, 2, half, width), bf),
-        recv_c=pltpu.VMEM((n, half, width), bf),
-        recv_z=pltpu.VMEM((phases, NB, half, width), bf),
-        a_send=D((n,)), a_recv=D((n,)), a_own=D((n,)),
-        b_send=D((n, 2)), b_recv=D((n,)), c_send=D((n,)), c_recv=D((n,)),
-        z_send=D((phases, NB)), z_recv=D((phases, NB)),
-        d_send=D((phases, 4)), d_recv=D((phases, 4)), d_own=D((phases,)),
-    )
-
-
-def reduce_steps(me, phases, source, out, sc, beside=()):
+    scratch = dict(
+        recv_z=pltpu.VMEM((m, NB, half, width), bf), z_send=D((m, NB)), z_recv=D((m, NB)),
+        d_send=D((m, 6)), d_recv=D((m, 6)), d_own=D((m,)), part_sem=D((m,)),
+    )
+    if n:
+        scratch.update(
+            acc=pltpu.VMEM((n, 4, half, width), bf), recv_a=pltpu.VMEM((n, 4, half, width), bf),
+            recv_b=pltpu.VMEM((n, 2, half, width), bf), recv_c=pltpu.VMEM((n, half, width), bf),
+            a_send=D((n,)), a_recv=D((n,)), a_own=D((n,)),
+            b_send=D((n, 2, 2)), b_recv=D((n, 2, 2)), c_send=D((n, 2)), c_recv=D((n, 2)),
+        )
+    return scratch
+
+
+def reduce_steps(me, plan, source, out, parts_in, parts_out, sc, beside=(), ahead=3):
     dp, band, core, px, py, kind = me.dp, me.band, me.core, me.px, me.py, me.kind
     here = lambda d: device(d, band)
-    chunks = [(phase, k) for phase in range(phases) for k in REDUCE_ORDER]
+    fronts = [phase for phase, todo in enumerate(plan) if todo & FRONT]
+    backs = [phase for phase, todo in enumerate(plan) if todo & BACK]
+    chunks = [(phase, k) for phase in fronts for k in REDUCE_ORDER]
     n = len(chunks)
     flip = lambda v: 1 - v
     sends = []
+    rows = sc.recv_z.shape[2]
+    cut = rows // 32 * 16
+    spans = (pl.ds(0, cut), pl.ds(cut, rows - cut))
 
     def remote(src, dst, ss, rs, to):
         return pltpu.make_async_remote_copy(
@@ -185,62 +195,72 @@
     def go(make):
         make().start()
         sends.append(make)
+
+    def target(k):
+        return device(dp, lax.rem(band + k, NB))
 
     def start_a(s):
         phase, k = chunks[s]
         b = lax.rem(band + k, NB)
         for t in range(4):
             remote(
-                source(phase, b, t, flip(core)), sc.recv_a.at[s, t],
-                sc.a_send.at[s], sc.a_recv.at[s], here(me.sib),
+                source(phase, b, t, flip(core)), sc.recv_a.at[s, t], sc.a_send.at[s], sc.a_recv.at[s],
+                here(me.sib),
             ).start()
-            pltpu.make_async_copy(
-                source(phase, b, t, core), sc.acc.at[s, t], sc.a_own.at[s]
-            ).start()
-
-    def first(s, j, send):
-        if s % 2 == 0:
+            pltpu.make_async_copy(source(phase, b, t, core), sc.acc.at[s, t], sc.a_own.at[s]).start()
+
+    def first(half, j, send):
+        if half == 0:
             return 2 * j + (flip(px) if send else px)
         return 2 * (flip(py) if send else py) + j
 
-    def second(s, send):
-        if s % 2 == 0:
+    def second(half, send):
+        if half == 0:
             return 2 * (flip(py) if send else py) + px
         return 2 * py + (flip(px) if send else px)
 
-    def send_b(s, j):
+    def near(half):
+        return here(me.xdp if half == 0 else me.ydp)
+
+    def send_b(s, half, j):
         return remote(
-            sc.acc.at[s, first(s, j, True)], sc.recv_b.at[s, j], sc.b_send.at[s, j],
-            sc.b_recv.at[s], here(me.xdp if s % 2 == 0 else me.ydp),
+            sc.acc.at[s, first(half, j, True), spans[half]], sc.recv_b.at[s, j, spans[half]],
+            sc.b_send.at[s, half, j], sc.b_recv.at[s, half, j], near(half),
         )
 
-    def send_c(s):
+    def send_c(s, half):
         return remote(
-            sc.acc.at[s, second(s, True)], sc.recv_c.at[s], sc.c_send.at[s],
-            sc.c_recv.at[s], here(me.ydp if s % 2 == 0 else me.xdp),
+            sc.acc.at[s, second(half, True), spans[half]], sc.recv_c.at[s, spans[half]],
+            sc.c_send.at[s, half], sc.c_recv.at[s, half], near(1 - half),
         )
 
-    def send_z(s):
+    def send_z(phase, k, src):
+        return remote(src, sc.recv_z.at[phase, k], sc.z_send.at[phase, k], sc.z_recv.at[phase, k], target(k))
+
+    def unit_z(s):
         phase, k = chunks[s]
-        return remote(
-            sc.acc.at[s, kind], sc.recv_z.at[phase, k], sc.z_send.at[phase, k],
-            sc.z_recv.at[phase, k], device(dp, lax.rem(band + k, NB)),
-        )
-
-    def send_d(phase, slot):
-        ss, rs = sc.d_send.at[phase, slot], sc.d_recv.at[phase, slot]
-        even = phase % 2 == 0
+        return send_z(phase, k, sc.acc.at[s, kind])
+
+    def part_load(phase):
+        return pltpu.make_async_copy(parts_in[phase], sc.recv_z.at[phase, 0], sc.part_sem.at[phase])
+
+    def part_store(phase):
+        return pltpu.make_async_copy(sc.recv_z.at[phase, 0], parts_out[phase], sc.part_sem.at[phase])
+
+    def d_copy(phase, half, slot, mine):
+        ss, rs = sc.d_send.at[phase, 3 * half + slot], sc.d_recv.at[phase, 3 * half + slot]
+        span = spans[half]
         if slot == 0:
-            unit = out[phase].at[kind, core]
-            return remote(sc.recv_z.at[phase, 0], unit, ss, rs, here(me.xdp if even else me.ydp))
-        if slot == 3:
-            row = out[phase].at[:, core]
-            return remote(row, row, ss, rs, here(me.sib))
-        if even:
-            pair = out[phase].at[pl.ds(2 * py, 2), core]
-            return remote(pair, pair, ss, rs, here(me.ydp))
-        unit = out[phase].at[2 * (slot - 1) + px, core]
-        return remote(unit, unit, ss, rs, here(me.xdp))
+            src = sc.recv_z.at[phase, 0, span]
+            return remote(src, out[phase].at[kind, core, span], ss, rs, near(half))
+        j = slot - 1
+        t = 2 * (py if mine else flip(py)) + j if half == 0 else 2 * j + (px if mine else flip(px))
+        unit = out[phase].at[t, core, span]
+        return remote(unit, unit, ss, rs, near(1 - half))
+
+    def d_cross(phase, mine):
+        row = out[phase].at[:, core if mine else flip(core)]
+        return remote(row, row, sc.z_send.at[phase, 0], sc.z_recv.at[phase, 0], here(me.sib))
 
     def a_to_b(s):
         acc, got = sc.acc, sc.recv_a
@@ -248,78 +268,84 @@
         whole = remote(got.at[s], got.at[s], sc.a_send.at[s], sc.a_recv.at[s], here(me.sib))
         whole.wait_recv()
         for j in range(2):
-            t = first(s, j, True)
-            add_rows(acc.at[s, t], got.at[s, t])
-            go(partial(send_b, s, j))
+            for half in range(2):
+                t = first(half, j, True)
+                add_rows(acc.at[s, t, spans[half]], got.at[s, t, spans[half]])
+                go(partial(send_b, s, half, j))
         for j in range(2):
-            t = first(s, j, False)
-            add_rows(acc.at[s, t], got.at[s, t])
+            for half in range(2):
+                t = first(half, j, False)
+                add_rows(acc.at[s, t, spans[half]], got.at[s, t, spans[half]])
         whole.wait_send()
 
     def b_to_c(s):
         acc, got = sc.acc, sc.recv_b
-        remote(got.at[s], got.at[s], sc.b_send.at[s, 0], sc.b_recv.at[s], here(me.xdp)).wait_recv()
-        away = flip(py) if s % 2 == 0 else flip(px)
-        stay = py if s % 2 == 0 else px
-        add_rows(acc.at[s, second(s, True)], got.at[s, away])
-        go(partial(send_c, s))
-        add_rows(acc.at[s, kind], got.at[s, stay])
+        for half in range(2):
+            for j in range(2):
+                send_b(s, half, j).wait_recv()
+            away = flip(py) if half == 0 else flip(px)
+            t = second(half, True)
+            add_rows(acc.at[s, t, spans[half]], got.at[s, away, spans[half]])
+            go(partial(send_c, s, half))
+        for half in range(2):
+            stay = py if half == 0 else px
+            add_rows(acc.at[s, kind, spans[half]], got.at[s, stay, spans[half]])
 
     def c_to_z(s):
-        acc, got = sc.acc, sc.recv_c
         phase, k = chunks[s]
-        remote(got.at[s], got.at[s], sc.c_send.at[s], sc.c_recv.at[s], here(me.xdp)).wait_recv()
-        add_rows(acc.at[s, kind], got.at[s])
+        for half in range(2):
+            send_c(s, half).wait_recv()
+            add_rows(sc.acc.at[s, kind, spans[half]], sc.recv_c.at[s, spans[half]])
         if k != 0:
-            go(partial(send_z, s))
-
-    def z_to_d(phase):
-        s = phase * NB + NB - 1
-        acc, got = sc.acc, sc.recv_z
+            go(partial(unit_z, s))
+
+    def z_sum(phase):
+        got = sc.recv_z
         for k in range(1, NB):
             remote(
-                got.at[phase, k], got.at[phase, k], sc.z_send.at[phase, k],
-                sc.z_recv.at[phase, k], here(dp),
+                got.at[phase, k], got.at[phase, k], sc.z_send.at[phase, k], sc.z_recv.at[phase, k], here(dp)
             ).wait_recv()
-        rows = acc.shape[2]
+        s = NB * fronts.index(phase) + NB - 1
 
         @pl.loop(0, rows // 16)
         def _(step):
             at = pl.ds(pl.multiple_of(step * 16, 16), 16)
-            total = acc[s, kind, at, :].astype(jnp.float32)
+            total = sc.acc[s, kind, at, :].astype(jnp.float32)
             for k in range(1, NB):
                 total = total + got[phase, k, at, :].astype(jnp.float32)
             got[phase, 0, at, :] = total.astype(jnp.bfloat16)
 
-        unit = out[phase].at[kind, core]
-        own = pltpu.make_async_copy(got.at[phase, 0], unit, sc.d_own.at[phase])
-        own.start()
-        go(partial(send_d, phase, 0))
-        own.wait()
+        if not plan[phase] & BACK:
+            part_store(phase).start()
+
+    def d_first(phase):
+        if not plan[phase] & FRONT:
+            part_load(phase).wait()
+        own_copy = pltpu.make_async_copy(sc.recv_z.at[phase, 0], out[phase].at[kind, core], sc.d_own.at[phase])
+        own_copy.start()
+        for half in range(2):
+            go(partial(d_copy, phase, half, 0, True))
+        own_copy.wait()
 
     def d_second(phase):
-        even = phase % 2 == 0
-        mate = 2 * py + flip(px) if even else 2 * flip(py) + px
-        unit = out[phase].at[mate, core]
-        remote(unit, unit, sc.d_send.at[phase, 0], sc.d_recv.at[phase, 0], here(me.xdp)).wait_recv()
-        for slot in (1,) if even else (1, 2):
-            go(partial(send_d, phase, slot))
+        for half in range(2):
+            d_copy(phase, half, 0, False).wait_recv()
+            for slot in (1, 2):
+                go(partial(d_copy, phase, half, slot, True))
 
     def d_third(phase):
-        if phase % 2 == 0:
-            pair = out[phase].at[pl.ds(2 * flip(py), 2), core]
-            remote(pair, pair, sc.d_send.at[phase, 1], sc.d_recv.at[phase, 1], here(me.ydp)).wait_recv()
-        else:
-            for j in range(2):
-                unit = out[phase].at[2 * j + flip(px), core]
-                remote(unit, unit, sc.d_send.at[phase, 1 + j], sc.d_recv.at[phase, 1 + j], here(me.xdp)).wait_recv()
-        go(partial(send_d, phase, 3))
+        for half in range(2):
+            for slot in (1, 2):
+                d_copy(phase, half, slot, False).wait_recv()
+        go(partial(d_cross, phase, True))
 
     def d_last(phase):
-        row = out[phase].at[:, flip(core)]
-        remote(row, row, sc.d_send.at[phase, 3], sc.d_recv.at[phase, 3], here(me.sib)).wait_recv()
+        d_cross(phase, False).wait_recv()
 
     def finish():
+        for phase in fronts:
+            if not plan[phase] & BACK:
+                part_store(phase).wait()
         for make in sends:
             make().wait_send()
 
@@ -328,16 +354,23 @@
     def put(at, do):
         table.setdefault(at, []).append(do)
 
+    for phase in backs:
+        if not plan[phase] & FRONT:
+            put(-1, lambda phase=phase: part_load(phase).start())
     for at, do in enumerate(beside):
         put(at, do)
     for s in range(n):
-        put(s + 3, partial(b_to_c, s))
-        put(s + 5, partial(c_to_z, s))
+        put(s + ahead, partial(b_to_c, s))
+        put(s + ahead + 1, partial(c_to_z, s))
         put(s, partial(a_to_b, s))
-    for phase in range(phases):
-        end = (phase + 1) * NB - 1 + 5
-        for lag, do in ((2, z_to_d), (3, d_second), (4, d_third), (5, d_last)):
-            put(end + lag, partial(do, phase))
+    for phase, todo in enumerate(plan):
+        end = 0
+        if todo & FRONT:
+            end = NB * fronts.index(phase) + NB + ahead + 1
+            put(end, partial(z_sum, phase))
+        if todo & BACK:
+            for lag, do in ((0, d_first), (1, d_second), (2, d_third), (4, d_last)):
+                put(end + lag, partial(do, phase))
     steps = [partial(run_all, table[at]) for at in sorted(table)]
     steps.append(finish)
     return steps
@@ -393,19 +426,28 @@
     pl.semaphore_wait(barrier, len(peers))
 
 
-def reduce_sources(counts, refs):
-    grads = []
-    at = 0
-    for count in counts:
-        grads.append(refs[at : at + count])
-        at += count
+def reduce_refs(plan, counts, refs):
+    take = iter(refs)
+    grads = [[next(take) for _ in range(count)] for count in counts]
 
     def source(phase, b, t, h):
         if len(grads[phase]) == 1:
             return grads[phase][0].at[b, t, h]
         return grads[phase][t].at[b, h]
 
-    return source
+    return source, [next(take) if todo == BACK else None for todo in plan]
+
+
+def reduce_outs(plan, refs):
+    take = iter(refs)
+    out = [next(take) if todo & BACK else None for todo in plan]
+    return out, [next(take) if todo == FRONT else None for todo in plan]
+
+
+def reduce_shapes(plan, half, width):
+    bf = jnp.bfloat16
+    shapes = [jax.ShapeDtypeStruct((4, 2, half, width), bf) for todo in plan if todo & BACK]
+    return shapes + [jax.ShapeDtypeStruct((half, width), bf) for todo in plan if todo == FRONT]
 
 
 def small_scratch(mod_rows, bias_rows, cond_rows, cond_cols):
@@ -532,71 +574,71 @@
     return [begin, cores, over_x, over_y, over_z, conditions]
 
 
-def reduce_last_kernel(counts, mods, images, names, *refs):
+def reduce_last_kernel(plan, counts, mods, images, names, *refs):
     me = compass()
-    phases = len(counts)
-    at = sum(counts)
-    source = reduce_sources(counts, refs)
+    at = sum(counts) + sum(1 for todo in plan if todo == BACK)
+    source, parts = reduce_refs(plan, counts, refs)
     rows_ref, small_ref, ada_ref = refs[at : at + 3]
     at += 3
-    out = refs[at : at + phases]
-    home_ref, every_ref, bias_ref, cond_ref = refs[at + phases : at + 4 + phases]
-    sc = SimpleNamespace(**dict(zip(names, refs[at + 4 + phases :])))
+    out, given = reduce_outs(plan, refs[at:])
+    at += len(plan)
+    home_ref, every_ref, bias_ref, cond_ref = refs[at : at + 4]
+    sc = SimpleNamespace(**dict(zip(names, refs[at + 4 :])))
     group_barrier(me)
     small = small_steps(me, mods, images, small_ref, ada_ref, every_ref, bias_ref, cond_ref, sc)
     small[0]()
     depart, settle = home_steps(me, rows_ref, home_ref, sc)
+    steps = reduce_steps(me, plan, source, out, parts, given, sc, small[1:], 2)
+    steps[0]()
     depart()
-    for step in reduce_steps(me, phases, source, out, sc, small[1:]):
+    for step in steps[1:]:
         step()
     settle()
 
 
-def reduce_last(grads, rows, mod_part, bias_part, ada_weight, images, collective_id):
-    phases = len(grads)
-    half, width = grads[0][0].shape[-2:]
-    counts = tuple(len(phase) for phase in grads)
+def reduce_last(grads, parts, rows, mod_part, bias_part, ada_weight, images, collective_id):
+    plan, counts = (BACK, FRONT | BACK), (0, len(grads))
+    half, width = grads[0].shape[-2:]
     mod_rows, bias_rows = mod_part.shape[0], bias_part.shape[0]
     cond_cols = -(-ada_weight.shape[0] // 128) * 128
     scratch = dict(
-        **reduce_scratch(phases, half, width), **small_scratch(mod_rows, bias_rows, 8, cond_cols), **home_scratch()
+        **reduce_scratch(plan, half, width), **small_scratch(mod_rows, bias_rows, 8, cond_cols), **home_scratch()
     )
     any_, vmem = pl.BlockSpec(memory_space=pl.ANY), pl.BlockSpec(memory_space=pltpu.VMEM)
-    outs = pl.pallas_call(
-        partial(reduce_last_kernel, counts, ada_weight.shape[1], images, tuple(scratch)),
-        out_shape=[jax.ShapeDtypeStruct((4, 2, half, width), jnp.bfloat16)] * phases
+    return pl.pallas_call(
+        partial(reduce_last_kernel, plan, counts, ada_weight.shape[1], images, tuple(scratch)),
+        out_shape=reduce_shapes(plan, half, width)
         + [
             jax.ShapeDtypeStruct(rows.shape, rows.dtype),
             jax.ShapeDtypeStruct((NB, 4, mod_rows, 128), jnp.bfloat16),
             jax.ShapeDtypeStruct((bias_rows, 128), jnp.float32),
             jax.ShapeDtypeStruct((NB, 8, cond_cols), jnp.float32),
         ],
-        in_specs=[any_] * (sum(counts) + 1) + [vmem] * 2,
-        out_specs=[any_] * (phases + 1) + [vmem] * 3,
+        in_specs=[any_] * (len(grads) + 2) + [vmem] * 2,
+        out_specs=[any_] * 3 + [vmem] * 3,
         scratch_shapes=list(scratch.values()),
         compiler_params=pltpu.CompilerParams(
             collective_id=collective_id, has_side_effects=True, vmem_limit_bytes=56 * 2**20
         ),
         name="reduce_last",
-    )(*[unit for phase in grads for unit in phase], rows, jnp.concatenate([mod_part, bias_part]), ada_weight)
-    return outs[:phases], *outs[phases:]
-
-
-def reduce_attend_kernel(counts, band_slots, names, *refs):
+    )(*grads, parts, rows, jnp.concatenate([mod_part, bias_part]), ada_weight)
+
+
+def reduce_attend_kernel(plan, counts, band_slots, names, *refs):
     me = compass()
-    phases = len(counts)
-    at = sum(counts)
-    source = reduce_sources(counts, refs)
+    at = sum(counts) + sum(1 for todo in plan if todo == BACK)
+    source, parts = reduce_refs(plan, counts, refs)
     rows_ref, count_ref, q_ref, own_ref, far_ref, grad_ref, top_ref = refs[at : at + 7]
     at += 7
-    out = refs[at : at + phases]
-    home_ref, dq_ref, down_ref, dfar_ref = refs[at + phases : at + phases + 4]
-    sc = SimpleNamespace(**dict(zip(names, refs[at + phases + 4 :])))
+    out, given = reduce_outs(plan, refs[at:])
+    at += len(plan)
+    home_ref, dq_ref, down_ref, dfar_ref = refs[at : at + 4]
+    sc = SimpleNamespace(**dict(zip(names, refs[at + 4 :])))
     qh, kh, vh, gh, stage, stage_sem = sc.qh, sc.kh, sc.vh, sc.gh, sc.stage, sc.stage_sem
     rows, width = q_ref.shape
     heads = qh.shape[0]
     group_barrier(me)
-    steps = reduce_steps(me, phases, source, out, sc)
+    steps = reduce_steps(me, plan, source, out, parts, given, sc)
     depart, settle = home_steps(me, rows_ref, home_ref, sc)
     steps[0]()
     depart()
@@ -646,14 +688,13 @@
     settle()
 
 
-def reduce_attend(grads, rows_out, count, query, own, far, grad, top, band_slots, collective_id):
-    phases = len(grads)
-    half, width = grads[0][0].shape[-2:]
+def reduce_attend(plan, grads, parts, rows_out, count, query, own, far, grad, top, band_slots, collective_id):
+    half, width = grads[-1][0].shape[-2:]
     counts = tuple(len(phase) for phase in grads)
     rows = query.shape[0]
     heads = width // HEAD_DIM
     bf = jnp.bfloat16
-    scratch = reduce_scratch(phases, half, width)
+    scratch = reduce_scratch(plan, half, width)
     scratch.update(
         qh=pltpu.VMEM((heads, rows, LANES), bf),
         kh=pltpu.VMEM((heads, 2 * rows, LANES), bf),
@@ -665,24 +706,24 @@
     )
     any_, vmem = pl.BlockSpec(memory_space=pl.ANY), pl.BlockSpec(memory_space=pltpu.VMEM)
     smem = pl.BlockSpec(memory_space=pltpu.SMEM)
-    outs = pl.pallas_call(
-        partial(reduce_attend_kernel, counts, band_slots, tuple(scratch)),
-        out_shape=[jax.ShapeDtypeStruct((4, 2, half, width), bf)] * phases
+    units = [unit for phase in grads for unit in phase]
+    return pl.pallas_call(
+        partial(reduce_attend_kernel, plan, counts, band_slots, tuple(scratch)),
+        out_shape=reduce_shapes(plan, half, width)
         + [
             jax.ShapeDtypeStruct(rows_out.shape, bf),
             jax.ShapeDtypeStruct((rows, width), bf),
             jax.ShapeDtypeStruct((rows, 2 * width), bf),
             jax.ShapeDtypeStruct((rows, 2 * width), bf),
         ],
-        in_specs=[any_] * (sum(counts) + 1) + [smem] + [any_] * 4 + [vmem],
-        out_specs=[any_] * (phases + 4),
+        in_specs=[any_] * (len(units) + len(parts) + 1) + [smem] + [any_] * 4 + [vmem],
+        out_specs=[any_] * (len(plan) + 4),
         scratch_shapes=list(scratch.values()),
         compiler_params=pltpu.CompilerParams(
             collective_id=collective_id, has_side_effects=True, vmem_limit_bytes=60 * 2**20
         ),
         name="reduce_attend",
-    )(*[unit for phase in grads for unit in phase], rows_out, count, query, own, far, grad, top)
-    return outs[:phases], *outs[phases:]
+    )(*units, *parts, rows_out, count, query, own, far, grad, top)
 
 
 MOD_BLOCKS = 6
@@ -1255,8 +1296,8 @@
     grad_proj = rows_dot(mixed_rows, grad_attended).astype(jnp.bfloat16)
     grad_proj_bias = jnp.sum(grad_attended.astype(jnp.float32), 0)
     grad_mixed = lanes_dot(grad_attended, proj_full).astype(jnp.bfloat16)
-    (outer_sum, inner_sum), block_home, grad_query, own_terms, far_terms = reduce_attend(
-        [[grad_outer], grad_inner], block_out.reshape(images, band_slots, width), valid_count, query_rows, key_value, other_key_value, grad_mixed, tops,
+    outer_sum, inner_part, block_home, grad_query, own_terms, far_terms = reduce_attend(
+        (FRONT | BACK, FRONT), [[grad_outer], grad_inner], [], block_out.reshape(images, band_slots, width), valid_count, query_rows, key_value, other_key_value, grad_mixed, tops,
         band_slots, 1,
     )
     other_terms = lax.ppermute(far_terms, both, siblings)
@@ -1282,9 +1323,8 @@
     part_bias = jnp.concatenate(
         [grad_query_bias, grad_value_bias, grad_proj_bias, grad_inner_bias, grad_outer_bias]
     ).reshape(-1, 128)
-    (first_sum,), tokens_home, every, bias_grads, grad_act = reduce_last(
-        [grad_first + [grad_proj.reshape(blocks)]],
-        grad_tokens.astype(jnp.bfloat16).reshape(images, band_slots, width), part_mod, part_bias, ada_weight, images, 2
+    inner_sum, first_sum, tokens_home, every, bias_grads, grad_act = reduce_last(
+        grad_first + [grad_proj.reshape(blocks)], inner_part, grad_tokens.astype(jnp.bfloat16).reshape(images, band_slots, width), part_mod, part_bias, ada_weight, images, 2
     )
     tokens_home = tokens_home.astype(jnp.float32)
     every = every_group(every, dp_count)

time: 615 us -> 564 us (0.917); the launches traced: 603 us -> 560 us
  Pallas kernels: 436 us -> 390 us
    pallas_call x2, Pallas kernels: 263 us -> 218 us  [the longest x1 120 us: reduce_attend(): pl.pallas_call(partial(reduce_attend_kernel, plan, counts, band_slots, tu...]
  transfers between devices with their start and end apart: 1 -> 1, of which waited for: 0 -> 0; matrix products, arithmetic and copies ran while one was open for 3% -> 2% of each run, Pallas kernels for 0% -> 0%
where the time goes in v6:
time: 564 us; the launch traced here: 560 us
  Pallas kernels  390 us (69%)
  matrix products  118 us (21%)
  other arithmetic  31.7 us (6%)
  local copies, waits for them, and re-layouts  16 us (3%)
    pallas_call x1, Pallas kernels, forward_block(): pl.pallas_call(partial(forward_kernel, tuple(scratch), band_slots), out_s...  172 us
    pallas_call x1, Pallas kernels, reduce_attend(): pl.pallas_call(partial(reduce_attend_kernel, plan, counts, band_slots, tu...  120 us
    pallas_call x1, Pallas kernels, reduce_last(): pl.pallas_call(partial(reduce_last_kernel, plan, counts, ada_weight.shape...  98.8 us
    dot_general x10, matrix products, rows_dot(): lax.dot_general(left, right, (((0,), (0,)), ((), ())), preferred_element_...  47.1 us
    dot_general x4, matrix products, lanes_dot(): lax.dot_general(left, right, (((1,), (1,)), ((), ())), preferred_element_...  40.8 us
    dot_general x1, matrix products, body(): jnp.dot(hidden_act, outer_full, preferred_element_type=jnp.float32)  15.7 us
    dot_general x1, matrix products, body(): jnp.dot(mlp_in, inner_full, preferred_element_type=jnp.float32)  11.7 us
  transfers between devices with their start and end apart: 1, of which 0 were waited for; matrix products, arithmetic and copies ran while one was open for 2% of the time, Pallas kernels for 0%

profile of v6, /device:TPU:1, one launch (start us, length us, event | category | flops | bytes accessed | tf_op | source)
XLA Modules:
  0.0 560.3 jit_solution(9301637321149087648)
XLA Ops:
  0.7 0.7 add_divide_fusion
  1.5 0.7 convert_element_type.195
  2.2 0.8 convert_dynamic-update-slice_fusion
  3.0 3.0 fusion.9
  6.9 0.7 sine_bitcast_fusion
  7.8 1.7 pad_maximum_fusion
  9.5 0.9 pad_maximum_fusion.1.refs_6_
  10.3 171.8 %forward_block.1 = (bf16[4,2,144,4608]{3,2,1,0:T(8,128)(2,1)}, bf16[4,2,144,4608]{3,2,1,0:T(8,128)(2,1)}, bf16[4,4,2,144,1152]{4,3,2,1,0:T(8,128)(2,1)}, bf16[2,...) custom-call(bf16[2,144,4608]{2,1,0:T(8,128)(2,1)} %bitcast.100, ...), custom_call_target="tpu_custom_call" | custom-call | tf_op jit(solution)/shard_map/forward_block/pallas_call | solution.py:1140
  182.1 1.6 multiply_reduce_fusion.10
  183.8 1.2 slice.114
  185.0 0.8 slice.112
  187.1 11.7 %fusion.42 = f32[512,4608]{1,0:T(8,128)} fusion(bf16[512,1152]{1,0:T(8,128)(2,1)} %get-tuple-element.40, bf16[1152,4608]{1,0:T(8,128)(2,1)} %bitcast.141), kind=kOutput, calls=%fused_computation.148 | convolution fusion | flops 5435817984 | bytes 21233664 | tf_op jit(solution)/shard_map/dot_general | solution.py:1267
  198.8 1.0 convert_reduce_fusion.1
  199.8 15.9 %convert_reduce_fusion = (f32[4608]{0:T(1024)}, bf16[512,4608]{1,0:T(8,128)(2,1)}) fusion(f32[512,4608]{1,0:T(8,128)} %fusion.42, f32[4608]{0:T(1024)S(1)} %add.137, bf16[512,1152]{1,0:T(8,128)(2,1)S(1)} %bitcast.123, bf16[4608,1152]{1,0:T(8,128)(2,1)S(1)} %bitcast.140), kind=kOutput, calls=%fused_computation.10 | convolution fusion | flops 5490077184 | bytes 25989120 | tf_op jit(solution)/shard_map/dot_general | solution.py:82
  215.7 5.0 convolution_convert_fusion.5
  220.8 3.2 convolution_convert_fusion.6
  224.0 3.2 convolution_convert_fusion.7
  227.2 3.2 convolution_convert_fusion.8
  230.5 0.8 reduce_sum.184
  231.9 2.5 fusion.39
  235.5 11.2 %multiply_reduce_fusion.1 = (f32[1152]{0:T(1024)}, f32[512]{0:T(512)S(1)}, f32[512]{0:T(512)S(1)}, f32[1152]{0:T(1024)}, f32[512,1152]{1,0:T(8,128)S(1)}) fusion(f32[512,1152]{1,0:T(8,128)S(1)} %get-tuple-element.88, f32[512]{0:T(512)S(1)} %add_rsqrt_fusion.1, f32[512]{0:T(512)S(1)} %get-tuple-element.118, f32[1152]{0:T(1024)S(1)} %copy-done.25, ...), kind=kOutput, calls=%fused_computation.40 | convolution fusion | flops 5441123328 | bytes 20076032 | tf_op jit(solution)/shard_map/dot_general | solution.py:82
  246.8 15.7 %multiply_reduce_fusion = (f32[1152]{0:T(1024)}, bf16[512,1152]{1,0:T(8,128)(2,1)}, f32[1152]{0:T(1024)}, bf16[512,1152]{1,0:T(8,128)(2,1)S(1)}, f32[512,1152]{1,0:T(8,128)}, /*index=5*/bf16[512,1152]{1,0:T(8,128)(2,1)S(1)}) fusion(bf16[2,256,1152]{2,1,0:T(8,128)(2,1)S(1)} %copy-done.12, f32[512]{0:T(512)S(1)} %copy-done.32, ...), kind=kOutput, calls=%fused_computation.39 | convolution fusion | flops 5472385024 | bytes 31906816 | tf_op jit(solution)/shard_map/dot_general | solution.py:1269
  262.4 13.0 %convolution_convert_fusion = bf16[4608,1152]{1,0:T(8,128)(2,1)} fusion(bf16[512,1152]{1,0:T(8,128)(2,1)S(1)} %get-tuple-element.105, f32[512,4608]{1,0:T(8,128)} %fusion.42, f32[4608]{0:T(1024)S(1)} %copy-done.21), kind=kOutput, calls=%fused_computation | convolution fusion | flops 5464719360 | bytes 21252096 | tf_op jit(solution)/shard_map/dot_general | solution.py:86
  275.5 4.6 convolution_convert_fusion.9.refs_10_
  280.1 119.6 %reduce_attend.1 = (bf16[4,2,144,1152]{3,2,1,0:T(8,128)(2,1)}, bf16[144,1152]{1,0:T(8,128)(2,1)}, bf16[2,256,1152]{2,1,0:T(8,128)(2,1)}, bf16[512,1152]{1,0:T(8,...) custom-call(bf16[4,4,2,144,1152]{4,3,2,1,0:T(8,128)(2,1)} %bitcast.99, ...), custom_call_target="tpu_custom_call" | custom-call | tf_op jit(solution)/shard_map/reduce_attend/pallas_call | solution.py:710
  399.7 1.7 collective-permute-start
  401.4 1.5 convert_reduce_fusion.4
  402.9 5.1 convolution_convert_fusion.1
  408.0 3.2 convolution_convert_fusion.4
  411.2 2.9 bitcast_convert_fusion
  414.2 2.3 add_convert_fusion
  416.7 3.2 convolution_convert_fusion.2
  419.9 3.2 convolution_convert_fusion.3
  423.2 9.0 %multiply_reduce_fusion.3 = (f32[1152]{0:T(1024)S(1)}, f32[512]{0:T(512)S(1)}, f32[512]{0:T(512)S(1)}, f32[1152]{0:T(1024)S(1)}, f32[512,1152]{1,0:T(8,128)S(1)}) fusion(f32[512,1152]{1,0:T(8,128)S(1)} %copy-done, f32[512]{0:T(512)S(1)} %copy-done.24, f32[512]{0:T(512)S(1)} %copy-done.23, f32[1152]{0:T(1024)S(1)} %get-tuple-element.75, ...), kind=kOutput, calls=%fused_computation.42 | convolution fusion | flops 4089246720 | bytes 16242176 | tf_op jit(solution)/shard_map/dot_general | solution.py:82
  432.4 2.0 multiply_reduce_fusion.2
  434.4 0.7 concatenate.80
  435.7 98.8 %reduce_last.1 = (bf16[4,2,144,1152]{3,2,1,0:T(8,128)(2,1)}, bf16[4,2,144,1152]{3,2,1,0:T(8,128)(2,1)}, bf16[2,256,1152]{2,1,0:T(8,128)(2,1)}, bf16[4,4,64,128]{...) custom-call(bf16[4,2,144,1152]{3,2,1,0:T(8,128)(2,1)} %bitcast.103, bf16[4,2,144,1152]{3,2,1,0:T(8,128)(2,1)} %bitcast.105, ...), custom_call_target="tpu_custom_call" | custom-call | tf_op jit(solution)/shard_map/reduce_last/pallas_call | solution.py:608
  534.5 1.0 copy.30
  535.7 0.8 slice_bitcast_fusion.2
  536.5 0.7 slice_bitcast_fusion
  537.3 3.1 fusion.40
  540.6 4.6 fusion.22
  545.2 1.2 bitcast_convert_fusion.1
  546.9 1.6 convert_element_type.236
  549.1 0.8 slice_bitcast_fusion.1
  554.0 2.2 maximum_convert_fusion.1
  556.2 2.7 maximum_convert_fusion
  558.8 1.0 copy.51
  (147 shorter events, 9.9 us)
Async XLA Ops:
  0.6 5.4 copy-start.14
  0.7 5.4 copy-start.37
  0.7 5.4 copy-start.33
  0.7 5.4 copy-start.34
  0.7 5.4 copy-start.35
  0.7 5.5 copy-start.36
  0.7 5.5 copy-start.31
  3.0 4.8 copy-start.8
  3.0 4.8 copy-start.13
  187.0 12.8 %copy-start.20 = (f32[4608]{0:T(1024)}, f32[4608]{0:T(1024)S(1)}, u32[]{:S(2)}) copy-start(f32[4608]{0:T(1024)S(1)} %add.137) | copy-start | bytes 55300
  187.0 12.8 %slice-start = ((s8[10616832]{0:T(1024)(128)(4,1)}), s8[4194304]{0:T(1024)(128)(4,1)S(1)}, s32[]{:S(2)}) async-start(s8[10616832]{0:T(1024)(128)(4,1)} %bitcast.138), calls=%async_computation | async-start | bytes 8388608
  187.0 11.7 %copy-start.12 = (bf16[2,256,1152]{2,1,0:T(8,128)(2,1)S(1)}, bf16[2,256,1152]{2,1,0:T(8,128)(2,1)}, u32[]{:S(2)}) copy-start(bf16[2,256,1152]{2,1,0:T(8,128)(2,1)} %get-tuple-element.43) | copy-start | bytes 3538948
  187.0 12.7 %slice-start.1 = ((s8[10616832]{0:T(1024)(128)(4,1)}), s8[4194304]{0:T(1024)(128)(4,1)S(1)}, s32[]{:S(2)}) async-start(s8[10616832]{0:T(1024)(128)(4,1)} %bitcast.138), calls=%async_computation.1 | async-start | bytes 8388608
  187.1 12.7 %slice-start.2 = ((s8[10616832]{0:T(1024)(128)(4,1)}), s8[2228224]{0:T(1024)(128)(4,1)S(1)}, s32[]{:S(2)}) async-start(s8[10616832]{0:T(1024)(128)(4,1)} %bitcast.138), calls=%async_computation.2 | async-start | bytes 4456448
  215.7 5.0 copy-start.39
  215.7 5.0 copy-start.40
  227.2 3.2 copy-start
  231.9 2.5 copy-start.22
  231.9 3.5 slice-start.3
  231.9 3.5 slice-start.4
  234.4 1.0 copy-start.25
  235.4 11.3 %copy-start.18 = (f32[1152]{0:T(1024)S(1)}, f32[1152]{0:T(1024)}, u32[]{:S(2)}) copy-start(f32[1152]{0:T(1024)} %get-tuple-element.78) | copy-start | bytes 13828
  235.4 11.3 %copy-start.21 = (f32[4608]{0:T(1024)S(1)}, f32[4608]{0:T(1024)}, u32[]{:S(2)}) copy-start(f32[4608]{0:T(1024)} %copy-done.20) | copy-start | bytes 55300
  235.5 11.3 %copy-start.26 = (f32[1152]{0:T(1024)S(1)}, f32[1152]{0:T(1024)}, u32[]{:S(2)}) copy-start(f32[1152]{0:T(1024)} %get-tuple-element.77) | copy-start | bytes 13828
  235.5 11.3 %copy-start.32 = (f32[512]{0:T(512)S(1)}, f32[512]{0:T(512)}, u32[]{:S(2)}) copy-start(f32[512]{0:T(512)} %fusion.31) | copy-start | bytes 6148
  262.4 13.1 %copy-start.41 = (bf16[512,1152]{1,0:T(8,128)(2,1)}, bf16[512,1152]{1,0:T(8,128)(2,1)S(1)}, u32[]{:S(2)}) copy-start(bf16[512,1152]{1,0:T(8,128)(2,1)S(1)} %get-tuple-element.100) | copy-start | bytes 3538948
  399.7 14.5 %collective-permute-start = (bf16[512,2304]{1,0:T(8,128)(2,1)}, bf16[512,2304]{1,0:T(8,128)(2,1)}, u32[]{:S(2)}, u32[]{:S(2)}) collective-permute-start(bf16[512,2304]{1,0:T(8,128)(2,1)} %get-tuple-element.56), channel_id=1, source_target_pairs={{0,4},{1,5},{2,6},{3,7},{4,0},{5,1},{6,2},{7,3},{8,12},{9,13},{10,... | collective-permute-start | bytes 7077896 | tf_op jit(solution)/shard_map/ppermute | solution.py:1303
  402.9 5.1 copy-start.11
  402.9 5.1 copy-start.38
  408.0 3.2 copy-start.3
  411.2 2.9 copy-start.6
  419.9 3.2 copy-start.23
  419.9 3.2 copy-start.24
  423.2 9.0 %copy-start.27 = (f32[1152]{0:T(1024)S(1)}, f32[1152]{0:T(1024)}, u32[]{:S(2)}) copy-start(f32[1152]{0:T(1024)} %get-tuple-element.99) | copy-start | bytes 13828
  423.2 9.1 %copy-start.19 = (f32[4608]{0:T(1024)S(1)}, f32[4608]{0:T(1024)}, u32[]{:S(2)}) copy-start(f32[4608]{0:T(1024)} %get-tuple-element.82) | copy-start | bytes 55300
  423.2 9.1 %copy-start.16 = (f32[1152]{0:T(1024)S(1)}, f32[1152]{0:T(1024)}, u32[]{:S(2)}) copy-start(f32[1152]{0:T(1024)} %get-tuple-element.80) | copy-start | bytes 13828
  423.2 9.1 %copy-start.1 = (f32[512,1152]{1,0:T(8,128)S(1)}, f32[512,1152]{1,0:T(8,128)}, u32[]{:S(2)}) copy-start(f32[512,1152]{1,0:T(8,128)} %get-tuple-element.46) | copy-start | bytes 7077892
  423.2 9.1 %copy-start.7 = (f32[512,1152]{1,0:T(8,128)S(1)}, f32[512,1152]{1,0:T(8,128)}, u32[]{:S(2)}) copy-start(f32[512,1152]{1,0:T(8,128)} %get-tuple-element.101) | copy-start | bytes 7077892
  432.3 2.0 copy-start.17
  432.3 2.0 copy-start.28
  432.3 2.0 copy-start.29
  432.3 2.0 copy-start.30
  537.3 3.1 copy-start.2
  545.2 1.8 copy-start.9
  545.2 4.9 copy-start.15
  554.0 2.2 copy-start.4
  554.0 2.2 copy-start.5
  556.2 2.7 copy-start.10

commit v7 on v6

--- a/solution.py
+++ b/solution.py
@@ -431,9 +431,13 @@
     grads = [[next(take) for _ in range(count)] for count in counts]
 
     def source(phase, b, t, h):
-        if len(grads[phase]) == 1:
-            return grads[phase][0].at[b, t, h]
-        return grads[phase][t].at[b, h]
+        if len(grads[phase]) > 1:
+            return grads[phase][t].at[b, h]
+        whole = grads[phase][0]
+        if len(whole.shape) == 5:
+            return whole.at[b, t, h]
+        span = whole.shape[3] // 4
+        return whole.at[b, h, :, pl.ds(pl.multiple_of(t * span, 128), span)]
 
     return source, [next(take) if todo == BACK else None for todo in plan]
 
@@ -689,7 +693,7 @@
 
 
 def reduce_attend(plan, grads, parts, rows_out, count, query, own, far, grad, top, band_slots, collective_id):
-    half, width = grads[-1][0].shape[-2:]
+    half, width = grads[0][0].shape[-2:]
     counts = tuple(len(phase) for phase in grads)
     rows = query.shape[0]
     heads = width // HEAD_DIM
@@ -743,7 +747,7 @@
         own=V((rows, 2 * width), bf), far=V((rows, 2 * width), bf), mixed=V((rows, width), bf),
         attended=V((rows, width), f32), mlp_in=V((rows, width), bf), tops=V((heads, 8, rows), f32),
         qh=V((heads, rows, LANES), bf), kh=V((heads, 2 * rows, LANES), bf), vh=V((heads, 2 * rows, LANES), bf),
-        z_send=D((3, 2)), z_recv=D((3, NB)), f_send=D((3, NB)), a_send=D((9,)), a_recv=D((9,)), b_send=D((9, 2)), b_recv=D((9, 2)),
+        z_send=D((3, 2)), z_recv=D((3, NB)), f_send=D((3, NB)), a_send=D((9, 2)), a_recv=D((9, 2)), b_send=D((9, 2, 2)), b_recv=D((9, 2, 2)),
         c_send=D((9,)), c_recv=D((9,)), t_send=D((2, 2)), t_recv=D((2, 2)), m_send=D((2, 2)), m_recv=D((NB,)),
         local=D((4,)), kv_send=D((1,)), kv_recv=D((1,)), done=D((12,)),
     )
@@ -767,17 +771,22 @@
         )
 
     def go(make):
-        make().start()
+        for copy in make():
+            copy.start()
         sends.append(make)
+
+    size = ins[0].shape[1]
+    cut = size // 32 * 16
+    whole, spans = pl.ds(0, size), (pl.ds(0, cut), pl.ds(cut, size - cut))
 
     def cols(t, n=1):
         return pl.ds(pl.multiple_of(t * width, 128), n * width)
 
-    def unit(ph, b, t, h):
-        return outs[ph].at[b, t, h] if ph == 2 else outs[ph].at[b, h, :, cols(t)]
-
-    def pair(ph, b, h, y):
-        return outs[ph].at[b, pl.ds(2 * y, 2), h] if ph == 2 else outs[ph].at[b, h, :, cols(2 * y, 2)]
+    def unit(ph, b, t, h, span=whole):
+        return outs[ph].at[b, t, h, span] if ph == 2 else outs[ph].at[b, h, span, cols(t)]
+
+    def pair(ph, b, h, y, span):
+        return outs[ph].at[b, pl.ds(2 * y, 2), h, span] if ph == 2 else outs[ph].at[b, h, span, cols(2 * y, 2)]
 
     def row(ph, b, h):
         return outs[ph].at[b, :, h] if ph == 2 else outs[ph].at[b, h]
@@ -796,20 +805,22 @@
             u, u, sc.f_send.at[ph, b], sc.z_recv.at[ph, b], dev(dp, jnp.where(b < band, band + 1, band - 1))
         )
 
-    def send_a(s):
+    def a_copy(s, half, mine):
         ph, b = order[s]
-        u = unit(ph, b, kind, core)
-        return remote(u, u, sc.a_send.at[s], sc.a_recv.at[s], here(me.xdp if s % 2 == 0 else me.ydp))
-
-    def b_copy(s, j, mine):
+        near = 2 * py + flip(px) if half == 0 else 2 * flip(py) + px
+        u = unit(ph, b, kind if mine else near, core, spans[half])
+        return remote(u, u, sc.a_send.at[s, half], sc.a_recv.at[s, half], here(me.xdp if half == 0 else me.ydp))
+
+    def b_copies(s, half, mine):
         ph, b = order[s]
-        if s % 2 == 0:
-            u = pair(ph, b, core, py if mine else flip(py))
-            to = me.ydp
-        else:
-            u = unit(ph, b, 2 * j + (px if mine else flip(px)), core)
-            to = me.xdp
-        return remote(u, u, sc.b_send.at[s, j], sc.b_recv.at[s, j], here(to))
+        if half == 0:
+            u = pair(ph, b, core, py if mine else flip(py), spans[half])
+            return [remote(u, u, sc.b_send.at[s, half, 0], sc.b_recv.at[s, half, 0], here(me.ydp))]
+        copies = []
+        for j in range(2):
+            u = unit(ph, b, 2 * j + (px if mine else flip(px)), core, spans[half])
+            copies.append(remote(u, u, sc.b_send.at[s, half, j], sc.b_recv.at[s, half, j], here(me.xdp)))
+        return copies
 
     def c_copy(s, mine):
         ph, b = order[s]
@@ -823,22 +834,21 @@
     def z_wait(s):
         ph, b = order[s]
         u = unit(ph, b, kind, core)
-        remote(u, u, sc.a_send.at[s], sc.z_recv.at[ph, b], here(dp)).wait_recv()
+        remote(u, u, sc.f_send.at[ph, b], sc.z_recv.at[ph, b], here(dp)).wait_recv()
         pl.when(inside)(lambda: pass_z(s).start())
-        go(partial(send_a, s))
+        for half in range(2):
+            go(lambda half=half: [a_copy(s, half, True)])
 
     def a_wait(s):
-        ph, b = order[s]
-        got = 2 * py + flip(px) if s % 2 == 0 else 2 * flip(py) + px
-        u = unit(ph, b, got, core)
-        remote(u, u, sc.a_send.at[s], sc.a_recv.at[s], here(me.xdp)).wait_recv()
-        for j in range(1 if s % 2 == 0 else 2):
-            go(partial(b_copy, s, j, True))
+        for half in range(2):
+            a_copy(s, half, False).wait_recv()
+            go(partial(b_copies, s, half, True))
 
     def b_wait(s):
-        for j in range(1 if s % 2 == 0 else 2):
-            b_copy(s, j, False).wait_recv()
-        go(partial(c_copy, s, True))
+        for half in range(2):
+            for copy in b_copies(s, half, False):
+                copy.wait_recv()
+        go(lambda: [c_copy(s, True)])
 
     def c_wait(s):
         c_copy(s, False).wait_recv()
@@ -934,7 +944,8 @@
         for s in range(len(order)):
             pl.when(inside)(lambda: pass_z(s).wait_send())
         for make in sends:
-            make().wait_send()
+            for copy in make():
+                copy.wait_send()
 
     def images(which):
         if which == 0:
@@ -1155,6 +1166,116 @@
     )(qp, inner, outer, tok, cot, note, table)
 
 
+GELU_SCALE = 0.7978845608028654
+
+
+def mlp_kernel(band_slots, mlp_ref, inner_ref, outer_ref, vec_ref, bias_ref, residual_ref, attended_ref, cot_ref,
+               mixed_ref, proj_ref, out_ref, middle_ref, back_ref, proj_grad_ref, outer_grad_ref, inner_grad_ref,
+               bias_grad_ref, sums_ref, out_acc, back_acc, grad_mlp):
+    step = pl.program_id(0)
+    rows = mlp_ref.shape[0]
+    low = lambda value: value.astype(jnp.bfloat16)
+    line = lambda index: vec_ref[index : index + 1, :]
+
+    def grad_out(at):
+        slot = lax.rem(at + lax.broadcasted_iota(jnp.int32, (BLOCK, 1), 0), band_slots)
+        valid = jnp.where(slot.astype(jnp.float32) < vec_ref[15:16, 0:1], 1.0, 0.0)
+        return cot_ref[pl.ds(at, BLOCK), :].astype(jnp.float32) * valid
+
+    def add_line(index, values):
+        sums_ref[index : index + 1, :] += jnp.sum(values, 0, keepdims=True)
+
+    @pl.when(step == 0)
+    def _():
+        sums_ref[...] = jnp.zeros_like(sums_ref)
+
+        @pl.loop(0, rows // BLOCK)
+        def _(block):
+            at = pl.multiple_of(block * BLOCK, BLOCK)
+            grad = low(line(5) * grad_out(at))
+            grad_mlp[pl.ds(at, BLOCK), :] = grad
+            add_line(5, grad.astype(jnp.float32))
+            out_acc[pl.ds(at, BLOCK), :] = jnp.zeros((BLOCK, out_acc.shape[1]), jnp.float32)
+            back_acc[pl.ds(at, BLOCK), :] = jnp.zeros((BLOCK, out_acc.shape[1]), jnp.float32)
+
+    inner, outer, grad = inner_ref[...], outer_ref[...], grad_mlp[...]
+    pre = jnp.dot(mlp_ref[...], inner, preferred_element_type=jnp.float32) + bias_ref[...]
+    grad_hidden = lanes_dot(grad, outer)
+    square = pre * pre
+    bend = jnp.tanh(GELU_SCALE * (pre * (1.0 + 0.044715 * square)))
+    rise = 0.5 * (1.0 + bend)
+    hidden = low(pre * rise)
+    slope = rise + (0.5 * pre) * (1.0 - bend * bend) * (GELU_SCALE * (1.0 + 0.134145 * square))
+    grad_pre = low(slope * grad_hidden)
+    out_acc[...] += jnp.dot(hidden, outer, preferred_element_type=jnp.float32)
+    outer_grad_ref[...] = low(rows_dot(hidden, grad))
+    back_acc[...] += lanes_dot(grad_pre, inner)
+    inner_grad_ref[...] = low(rows_dot(mlp_ref[...], grad_pre))
+    bias_grad_ref[...] = jnp.broadcast_to(
+        jnp.sum(grad_pre.astype(jnp.float32), 0, keepdims=True), bias_grad_ref.shape
+    )
+
+    @pl.when(step == pl.num_programs(0) - 1)
+    def _():
+        @pl.loop(0, rows // BLOCK)
+        def _(block):
+            at = pl.multiple_of(block * BLOCK, BLOCK)
+            sub = pl.ds(at, BLOCK)
+            attended = attended_ref[sub, :]
+            middle = residual_ref[sub, :] + line(2) * attended
+            normed, inverse = normalize(middle)
+            mlp_out = out_acc[sub, :] + line(9)
+            out_ref[sub, :] = low(middle + line(5) * mlp_out)
+            grad_block = grad_out(at)
+            add_line(0, grad_block * mlp_out)
+            back = back_acc[sub, :]
+            add_line(1, back)
+            add_line(2, back * normed)
+            grad_middle = grad_block + norm_back(back * (1.0 + line(4)), normed, inverse)
+            middle_ref[sub, :] = grad_middle
+            add_line(3, grad_middle * attended)
+            grad_attended = low(line(2) * grad_middle)
+            add_line(4, grad_attended.astype(jnp.float32))
+            grad_mlp[sub, :] = grad_attended
+
+        proj_grad_ref[...] = low(rows_dot(mixed_ref[...], grad_mlp[...]))
+        back_ref[...] = low(lanes_dot(grad_mlp[...], proj_ref[...]))
+
+
+def feed_forward(mlp_in, inner, outer, vectors, inner_bias, residual, attended, cotangent, mixed, first, band_slots):
+    rows, width = mlp_in.shape
+    hidden = inner.shape[1]
+    tile = 512
+    bf, f32 = jnp.bfloat16, jnp.float32
+    S = jax.ShapeDtypeStruct
+    keep = lambda *shape: pl.BlockSpec(shape, lambda j: (0,) * len(shape))
+    return pl.pallas_call(
+        partial(mlp_kernel, band_slots),
+        grid=(hidden // tile,),
+        out_shape=[
+            S((rows, width), bf), S((rows, width), f32), S((rows, width), bf), S((width, width), bf),
+            S((hidden, width), bf), S((width, hidden), bf), S((8, hidden), f32), S((8, width), f32),
+        ],
+        in_specs=[
+            keep(rows, width), pl.BlockSpec((width, tile), lambda j: (0, j)), pl.BlockSpec((tile, width), lambda j: (j, 0)),
+            keep(16, width), pl.BlockSpec((1, tile), lambda j: (0, j)), keep(rows, width), keep(rows, width),
+            keep(rows, width), keep(rows, width), pl.BlockSpec((width, width), lambda j: (0, 3)),
+        ],
+        out_specs=[
+            keep(rows, width), keep(rows, width), keep(rows, width), keep(width, width),
+            pl.BlockSpec((tile, width), lambda j: (j, 0)), pl.BlockSpec((width, tile), lambda j: (0, j)),
+            pl.BlockSpec((8, tile), lambda j: (0, j)), keep(8, width),
+        ],
+        scratch_shapes=[pltpu.VMEM((rows, width), f32), pltpu.VMEM((rows, width), f32), pltpu.VMEM((rows, width), bf)],
+        compiler_params=pltpu.CompilerParams(vmem_limit_bytes=60 * 2**20),
+        cost_estimate=pl.CostEstimate(
+            flops=12 * rows * width * hidden, bytes_accessed=8 * width * hidden + 24 * rows * width,
+            transcendentals=rows * hidden,
+        ),
+        name="feed_forward",
+    )(mlp_in, inner, outer, vectors, inner_bias, residual, attended, cotangent, mixed, first)
+
+
 def pair_perm(dp_count, band_count):
     return [
         (dp * band_count + band, (dp ^ 1) * band_count + band)
@@ -1254,50 +1375,24 @@
     qkv_full = first_full[:, : 3 * width]
     proj_full = first_full[:, 3 * width :]
     scale_one, gate_one = vectors[1], vectors[2]
-    scale_two, gate_two = vectors[4], vectors[5]
-    outer_bias_full = vectors[9]
-    inner_bias_full = vectors[10:14].reshape(-1)
     condition_here = vectors[14]
     valid_count = vectors[15, :1].astype(jnp.int32)
     rows = images * band_slots
-    is_valid = jnp.arange(rows, dtype=jnp.int32) % band_slots < valid_count
+    inner_bias_row = vectors[10:14].reshape(1, -1)
+    (block_out, grad_middle, grad_mixed, grad_proj, grad_outer, grad_inner, grad_inner_bias, sums) = feed_forward(
+        mlp_in, inner_full, outer_full, vectors, inner_bias_row, residual, attended,
+        cotangent_here.reshape(rows, width), mixed_rows, first_full, band_slots,
+    )
+    blocks = (band_count, 2, part_rows // 2, width)
+    grad_outer = grad_outer.reshape(band_count, 4, 2, part_rows // 2, width)
+    grad_inner = grad_inner.reshape(band_count, 2, part_rows // 2, hidden)
+    grad_inner_bias = grad_inner_bias[0]
+    grad_gate_two, grad_shift_two, grad_scale_two, grad_gate_one, grad_proj_bias, grad_outer_bias = [
+        sums[index] for index in range(6)
+    ]
     normed_one, inverse_one = normalize(residual)
-    middle = residual + gate_one * attended
-    normed_two, inverse_two = normalize(middle)
-    hidden_pre = jnp.dot(mlp_in, inner_full, preferred_element_type=jnp.float32) + inner_bias_full
-    hidden_act = jax.nn.gelu(hidden_pre, approximate=True).astype(jnp.bfloat16)
-    mlp_out = jnp.dot(hidden_act, outer_full, preferred_element_type=jnp.float32) + outer_bias_full
-    block_out = (middle + gate_two * mlp_out).astype(jnp.bfloat16)
-
-    grad_out = cotangent_here.reshape(rows, width).astype(jnp.float32) * is_valid[:, None].astype(
-        jnp.float32
-    )
-    grad_gate_two = jnp.sum(grad_out * mlp_out, 0)
-    grad_mlp = (gate_two * grad_out).astype(jnp.bfloat16)
-    gelu_back = jax.vjp(partial(jax.nn.gelu, approximate=True), hidden_pre)[1]
-    blocks = (band_count, 2, part_rows // 2, width)
-    grad_outer = rows_dot(hidden_act, grad_mlp).astype(jnp.bfloat16).reshape(
-        band_count, 4, 2, part_rows // 2, width
-    )
-    grad_outer_bias = jnp.sum(grad_mlp.astype(jnp.float32), 0)
-    grad_hidden = lanes_dot(grad_mlp, outer_full)
-    grad_pre = gelu_back(grad_hidden)[0].astype(jnp.bfloat16)
-    grad_inner = [
-        rows_dot(mlp_in, grad_pre[:, t * width : (t + 1) * width]).astype(jnp.bfloat16).reshape(blocks)
-        for t in range(4)
-    ]
-    grad_inner_bias = jnp.sum(grad_pre.astype(jnp.float32), 0)
-    grad_mlp_in = lanes_dot(grad_pre, inner_full)
-    grad_shift_two = jnp.sum(grad_mlp_in, 0)
-    grad_scale_two = jnp.sum(grad_mlp_in * normed_two, 0)
-    grad_middle = grad_out + norm_back(grad_mlp_in * (1.0 + scale_two), normed_two, inverse_two)
-    grad_gate_one = jnp.sum(grad_middle * attended, 0)
-    grad_attended = (gate_one * grad_middle).astype(jnp.bfloat16)
-    grad_proj = rows_dot(mixed_rows, grad_attended).astype(jnp.bfloat16)
-    grad_proj_bias = jnp.sum(grad_attended.astype(jnp.float32), 0)
-    grad_mixed = lanes_dot(grad_attended, proj_full).astype(jnp.bfloat16)
     outer_sum, inner_part, block_home, grad_query, own_terms, far_terms = reduce_attend(
-        (FRONT | BACK, FRONT), [[grad_outer], grad_inner], [], block_out.reshape(images, band_slots, width), valid_count, query_rows, key_value, other_key_value, grad_mixed, tops,
+        (FRONT | BACK, FRONT), [[grad_outer], [grad_inner]], [], block_out.reshape(images, band_slots, width), valid_count, query_rows, key_value, other_key_value, grad_mixed, tops,
         band_slots, 1,
     )
     other_terms = lax.ppermute(far_terms, both, siblings)

time: 564 us -> 536 us (0.950)
  matrix products: 118 us -> 27.8 us
  Pallas kernels: 390 us -> 440 us
  local copies, waits for them, and re-layouts: 16 us -> 25.4 us
    pallas_call x0 -> x1, Pallas kernels: none -> 56.9 us  [feed_forward(): pl.pallas_call(partial(mlp_kernel, band_slots), grid=(hidden // tile,), o...]
    dot_general x10 -> x4, matrix products: 47.1 us -> 14.3 us  [rows_dot(): lax.dot_general(left, right, (((0,), (0,)), ((), ())), preferred_element_...]
    dot_general x4 -> x1, matrix products: 40.8 us -> 10.4 us  [lanes_dot(): lax.dot_general(left, right, (((1,), (1,)), ((), ())), preferred_element_...]
    dot_general x2 -> x0, matrix products: 27.4 us -> none  [the longest x1 15.7 us: body(): jnp.dot(hidden_act, outer_full, preferred_element_type=jnp.float32)]
    pallas_call x1, Pallas kernels: 172 us -> 165 us  [forward_block(): pl.pallas_call(partial(forward_kernel, tuple(scratch), band_slots), out_s...]
  transfers between devices with their start and end apart: 1 -> 1, of which waited for: 0 -> 0; matrix products, arithmetic and copies ran while one was open for 2% -> 3% of each run, Pallas kernels for 0% -> 0%
where the time goes in v7:
time: 536 us; the launch traced here: 527 us
  Pallas kernels  440 us (82%)
  other arithmetic  30.5 us (6%)
  matrix products  27.8 us (5%)
  local copies, waits for them, and re-layouts  25.4 us (5%)
    pallas_call x1, Pallas kernels, forward_block(): pl.pallas_call(partial(forward_kernel, tuple(scratch), band_slots), out_s...  165 us
    pallas_call x1, Pallas kernels, reduce_attend(): pl.pallas_call(partial(reduce_attend_kernel, plan, counts, band_slots, tu...  120 us
    pallas_call x1, Pallas kernels, reduce_last(): pl.pallas_call(partial(reduce_last_kernel, plan, counts, ada_weight.shape...  98.2 us
    pallas_call x1, Pallas kernels, feed_forward(): pl.pallas_call(partial(mlp_kernel, band_slots), grid=(hidden // tile,), o...  56.9 us
    dot_general x4, matrix products, rows_dot(): lax.dot_general(left, right, (((0,), (0,)), ((), ())), preferred_element_...  14.3 us
  transfers between devices with their start and end apart: 1, of which 0 were waited for; matrix products, arithmetic and copies ran while one was open for 3% of the time, Pallas kernels for 0%

profile of v7, /device:TPU:1, one launch (start us, length us, event | category | flops | bytes accessed | tf_op | source)
XLA Modules:
  0.0 527.0 jit_solution(12346564090470229808)
XLA Ops:
  0.7 0.7 add_divide_fusion
  1.5 0.7 convert_element_type.122
  2.2 0.8 convert_dynamic-update-slice_fusion
  3.0 3.0 fusion.2
  6.9 0.7 sine_bitcast_fusion
  7.8 1.7 pad_maximum_fusion
  9.5 0.9 pad_maximum_fusion.1.refs_6_
  10.3 165.1 %forward_block.1 = (bf16[4,2,144,4608]{3,2,1,0:T(8,128)(2,1)}, bf16[4,2,144,4608]{3,2,1,0:T(8,128)(2,1)}, bf16[4,4,2,144,1152]{4,3,2,1,0:T(8,128)(2,1)}, bf16[2,...) custom-call(bf16[2,144,4608]{2,1,0:T(8,128)(2,1)} %bitcast.77, ...), custom_call_target="tpu_custom_call" | custom-call | tf_op jit(solution)/shard_map/forward_block/pallas_call | solution.py:1151
  175.5 0.8 slice_bitcast_fusion.1
  176.3 1.2 slice.107
  178.7 56.9 %feed_forward.1 = (bf16[512,1152]{1,0:T(8,128)(2,1)}, f32[512,1152]{1,0:T(8,128)}, bf16[512,1152]{1,0:T(8,128)(2,1)}, bf16[1152,1152]{1,0:T(8,128)(2,1)}, bf16[4...) custom-call(bf16[512,1152]{1,0:T(8,128)(2,1)} %get-tuple-element.48.mlp_ref, ...), custom_call_target="tpu_custom_call" | custom-call | flops 32614907904 | bytes 56623104 | tf_op jit(solution)/shard_map/feed_forward/pallas_call | solution.py:1252
  235.7 119.5 %reduce_attend.1 = (bf16[4,2,144,1152]{3,2,1,0:T(8,128)(2,1)}, bf16[144,1152]{1,0:T(8,128)(2,1)}, bf16[2,256,1152]{2,1,0:T(8,128)(2,1)}, bf16[512,1152]{1,0:T(8,...) custom-call(bf16[4,4,2,144,1152]{4,3,2,1,0:T(8,128)(2,1)} %bitcast.75, ...), custom_call_target="tpu_custom_call" | custom-call | tf_op jit(solution)/shard_map/reduce_attend/pallas_call | solution.py:714
  355.2 1.5 collective-permute-start
  356.7 0.8 reduce_sum.81
  357.4 1.4 multiply_reduce_fusion.4
  359.1 1.7 slice_reduce_fusion.1
  360.7 1.6 slice_reduce_fusion
  362.3 1.3 broadcast_multiply_fusion.2
  363.5 1.3 constant_dynamic-update-slice_fusion.7
  364.9 1.1 multiply_reduce_fusion.2
  366.1 3.2 convolution_convert_fusion.2
  369.4 2.9 bitcast_convert_fusion
  372.3 2.2 add_convert_fusion
  374.7 3.3 convolution_convert_fusion
  378.0 3.2 convolution_convert_fusion.1
  381.4 10.4 %multiply_reduce_fusion = (f32[1152]{0:T(1024)}, f32[512]{0:T(512)}, f32[512]{0:T(512)}, f32[1152]{0:T(1024)}, f32[512,1152]{1,0:T(8,128)}) fusion(f32[512,1152]{1,0:T(8,128)S(1)} %copy-done, f32[512]{0:T(512)S(1)} %add_rsqrt_fusion, f32[512]{0:T(512)S(1)} %copy-done.18, f32[1152]{0:T(1024)S(1)} %copy-done.17, bf16[1152,4608]{1,0:T(8,128)(2,1)} %bitcast.109, ...), kind=kOutput, calls=%fused_computation.16 | convolution fusion | flops 4089246720 | bytes 16242176 | tf_op jit(solution)/shard_map/dot_general | solution.py:82
  391.9 4.9 concatenate.80
  396.7 1.4 select_maximum_fusion.refs_6_
  398.2 0.7 broadcast_multiply_fusion
  398.9 4.2 add_convert_fusion.1
  403.0 98.2 %reduce_last.1 = (bf16[4,2,144,1152]{3,2,1,0:T(8,128)(2,1)}, bf16[4,2,144,1152]{3,2,1,0:T(8,128)(2,1)}, bf16[2,256,1152]{2,1,0:T(8,128)(2,1)}, bf16[4,4,64,128]{...) custom-call(bf16[4,2,144,1152]{3,2,1,0:T(8,128)(2,1)} %bitcast.80, bf16[4,2,144,1152]{3,2,1,0:T(8,128)(2,1)} %bitcast.82, ...), custom_call_target="tpu_custom_call" | custom-call | tf_op jit(solution)/shard_map/reduce_last/pallas_call | solution.py:612
  501.2 1.0 copy.30
  502.5 0.8 slice_bitcast_fusion.3
  503.3 0.7 slice_bitcast_fusion
  504.0 3.1 fusion.21
  507.3 4.6 fusion.10
  511.9 1.2 bitcast_convert_fusion.1
  513.7 1.6 convert_element_type.141
  515.2 0.7 dynamic_slice.26
  515.9 0.8 slice_bitcast_fusion.2
  517.4 0.7 dynamic_slice.27
  518.1 0.7 dynamic_slice.28
  518.7 0.7 dynamic_slice.29
  519.4 0.7 dynamic_slice.31
  520.0 0.7 dynamic_slice.30
  520.7 2.2 maximum_convert_fusion.1
  522.9 2.7 maximum_convert_fusion
  525.6 1.0 copy.52
  (89 shorter events, 3.9 us)
Async XLA Ops:
  0.6 5.4 %copy-start.12 = (bf16[2,1152]{1,0:T(2,128)(2,1)S(1)}, bf16[2,1152]{1,0:T(2,128)(2,1)}, u32[]{:S(2)}) copy-start(bf16[2,1152]{1,0:T(2,128)(2,1)} %param.16) | copy-start | bytes 13828
  0.7 5.4 %copy-start.25 = (s32[2,2]{1,0:T(2,128)S(1)}, s32[2,2]{1,0:T(2,128)}, u32[]{:S(2)}) copy-start(s32[2,2]{1,0:T(2,128)} %param.17) | copy-start | bytes 52
  0.7 5.4 %copy-start.21 = (bf16[288]{0:T(512)(128)(2,1)S(1)}, bf16[288]{0:T(512)(128)(2,1)}, u32[]{:S(2)}) copy-start(bf16[288]{0:T(512)(128)(2,1)} %param.21) | copy-start | bytes 1732
  0.7 5.4 %copy-start.22 = (bf16[288]{0:T(512)(128)(2,1)S(1)}, bf16[288]{0:T(512)(128)(2,1)}, u32[]{:S(2)}) copy-start(bf16[288]{0:T(512)(128)(2,1)} %param.22) | copy-start | bytes 1732
  0.7 5.4 %copy-start.23 = (bf16[288]{0:T(512)(128)(2,1)S(1)}, bf16[288]{0:T(512)(128)(2,1)}, u32[]{:S(2)}) copy-start(bf16[288]{0:T(512)(128)(2,1)} %param.24) | copy-start | bytes 1732
  0.7 5.5 %copy-start.24 = (bf16[288]{0:T(512)(128)(2,1)S(1)}, bf16[288]{0:T(512)(128)(2,1)}, u32[]{:S(2)}) copy-start(bf16[288]{0:T(512)(128)(2,1)} %param.28) | copy-start | bytes 1732
  0.7 5.5 %copy-start.20 = (bf16[1152]{0:T(1024)(128)(2,1)S(1)}, bf16[1152]{0:T(1024)(128)(2,1)}, u32[]{:S(2)}) copy-start(bf16[1152]{0:T(1024)(128)(2,1)} %param.26) | copy-start | bytes 6916
  3.0 4.8 copy-start.6
  3.0 4.8 copy-start.10
  235.6 121.0 %copy-start = (f32[512,1152]{1,0:T(8,128)S(1)}, f32[512,1152]{1,0:T(8,128)}, u32[]{:S(2)}) copy-start(f32[512,1152]{1,0:T(8,128)} %get-tuple-element.52.residual_ref) | copy-start | bytes 7077892
  355.2 3.7 copy-start.9
  355.2 17.1 %collective-permute-start = (bf16[512,2304]{1,0:T(8,128)(2,1)}, bf16[512,2304]{1,0:T(8,128)(2,1)}, u32[]{:S(2)}, u32[]{:S(2)}) collective-permute-start(bf16[512,2304]{1,0:T(8,128)(2,1)} %get-tuple-element.69), channel_id=1, source_target_pairs={{0,4},{1,5},{2,6},{3,7},{4,0},{5,1},{6,2},{7,3},{8,12},{9,13},{10,... | collective-permute-start | bytes 7077896 | tf_op jit(solution)/shard_map/ppermute | solution.py:1398
  364.9 1.3 copy-start.26
  366.0 15.4 %copy-start.19 = (f32[512]{0:T(512)}, f32[512]{0:T(512)S(1)}, u32[]{:S(2)}) copy-start(f32[512]{0:T(512)S(1)} %add_rsqrt_fusion) | copy-start | bytes 6148
  366.1 3.2 copy-start.2
  369.4 2.9 copy-start.5
  378.0 3.3 copy-start.13
  378.0 3.3 copy-start.15
  378.0 3.3 copy-start.11
  378.0 3.4 copy-start.17
  378.0 3.4 copy-start.18
  381.4 10.5 %copy-start.14 = (f32[9216]{0:T(1024)}, f32[9216]{0:T(1024)S(1)}, u32[]{:S(2)}) copy-start(f32[9216]{0:T(1024)S(1)} %constant_dynamic-update-slice_fusion.8) | copy-start | bytes 110596
  381.4 10.4 %copy-start.16 = (f32[1152]{0:T(1024)S(1)}, f32[1152]{0:T(1024)}, u32[]{:S(2)}) copy-start(f32[1152]{0:T(1024)} %get-tuple-element.86) | copy-start | bytes 13828
  504.0 3.1 copy-start.1
  511.9 1.8 copy-start.7
  520.7 2.2 copy-start.3
  520.7 2.2 copy-start.4
  522.9 2.7 copy-start.8

commit v8 on v7

--- a/solution.py
+++ b/solution.py
@@ -174,7 +174,7 @@
     return scratch
 
 
-def reduce_steps(me, plan, source, out, parts_in, parts_out, sc, beside=(), ahead=3):
+def reduce_steps(me, plan, source, out, parts_in, parts_out, sc, beside=(), ahead=3, by_kind=False):
     dp, band, core, px, py, kind = me.dp, me.band, me.core, me.px, me.py, me.kind
     here = lambda d: device(d, band)
     fronts = [phase for phase, todo in enumerate(plan) if todo & FRONT]
@@ -199,10 +199,10 @@
     def target(k):
         return device(dp, lax.rem(band + k, NB))
 
-    def start_a(s):
+    def start_a(s, kinds=range(4)):
         phase, k = chunks[s]
         b = lax.rem(band + k, NB)
-        for t in range(4):
+        for t in kinds:
             remote(
                 source(phase, b, t, flip(core)), sc.recv_a.at[s, t], sc.a_send.at[s], sc.a_recv.at[s],
                 here(me.sib),
@@ -349,7 +349,7 @@
         for make in sends:
             make().wait_send()
 
-    table = {-1: [partial(start_a, s) for s in range(n)]}
+    table = {-1: [] if by_kind else [partial(start_a, s) for s in range(n)]}
 
     def put(at, do):
         table.setdefault(at, []).append(do)
@@ -370,9 +370,11 @@
             put(end, partial(z_sum, phase))
         if todo & BACK:
             for lag, do in ((0, d_first), (1, d_second), (2, d_third), (4, d_last)):
-                put(end + lag, partial(do, phase))
+                put(end + lag - (0 if todo & FRONT else 1), partial(do, phase))
     steps = [partial(run_all, table[at]) for at in sorted(table)]
     steps.append(finish)
+    if by_kind:
+        return steps, lambda kind: [start_a(s, (kind,)) for s in range(n)]
     return steps
 
 
@@ -578,54 +580,149 @@
     return [begin, cores, over_x, over_y, over_z, conditions]
 
 
-def reduce_last_kernel(plan, counts, mods, images, names, *refs):
+def put_lines(ref, first, values):
+    for i in range(values.shape[1] // 128):
+        ref[first + i : first + i + 1, :] = values[:, i * 128 : (i + 1) * 128]
+
+
+def reduce_last_kernel(plan, images, band_slots, names, *refs):
     me = compass()
-    at = sum(counts) + sum(1 for todo in plan if todo == BACK)
-    source, parts = reduce_refs(plan, counts, refs)
-    rows_ref, small_ref, ada_ref = refs[at : at + 3]
-    at += 3
-    out, given = reduce_outs(plan, refs[at:])
-    at += len(plan)
-    home_ref, every_ref, bias_ref, cond_ref = refs[at : at + 4]
-    sc = SimpleNamespace(**dict(zip(names, refs[at + 4 :])))
+    (proj_ref, part_ref, attn_hbm, query_hbm, own_hbm, other_hbm, first_hbm, residual_hbm, middle_hbm, vec_ref, sums_ref,
+     inner_bias_ref, ada_ref) = refs[:13]
+    inner_out, first_out, home_ref, every_ref, bias_ref, cond_ref = refs[13:19]
+    sc = SimpleNamespace(**dict(zip(names, refs[19:])))
+    rows, width = sc.attn.shape
+    lines = width // 128
+    small = sc.small
+    mod_rows = sc.s_every.shape[2]
+
+    def source(phase, b, t, h):
+        return proj_ref.at[b, h] if t == 3 else sc.grads.at[t, b, h]
+
+    loads = [
+        (attn_hbm, sc.attn), (query_hbm, sc.gqkv.at[:, pl.ds(0, width)]), (own_hbm, sc.gqkv.at[:, pl.ds(width, 2 * width)]),
+        (other_hbm, sc.other), (first_hbm.at[:, pl.ds(0, 3 * width)], sc.first), (residual_hbm, sc.residual),
+        (middle_hbm, sc.middle),
+    ]
+
+    def load(i):
+        return pltpu.make_async_copy(*loads[i], sc.load_sem.at[i])
+
+    for i in range(len(loads)):
+        load(i).start()
     group_barrier(me)
-    small = small_steps(me, mods, images, small_ref, ada_ref, every_ref, bias_ref, cond_ref, sc)
-    small[0]()
-    depart, settle = home_steps(me, rows_ref, home_ref, sc)
-    steps = reduce_steps(me, plan, source, out, parts, given, sc, small[1:], 2)
+    mods = MOD_BLOCKS * width
+    exchange = small_steps(me, mods, images, small, ada_ref, every_ref, bias_ref, cond_ref, sc)
+    depart, settle = home_steps(me, sc.tokens, home_ref, sc)
+    steps, start = reduce_steps(
+        me, plan, source, (inner_out, first_out), (part_ref, None), (None, None), sc, (), 2, True
+    )
+    start(3)
     steps[0]()
+    for i in range(4):
+        load(i).wait()
+
+    sc.sums[...] = jnp.zeros_like(sc.sums)
+
+    def add_line(index, values):
+        sc.sums[index : index + 1, :] += jnp.sum(values, 0, keepdims=True)
+
+    @pl.loop(0, rows // BLOCK)
+    def _(block):
+        sub = pl.ds(pl.multiple_of(block * BLOCK, BLOCK), BLOCK)
+        total = sc.gqkv[sub, width:].astype(jnp.float32) + sc.other[sub, :].astype(jnp.float32)
+        total = total.astype(jnp.bfloat16)
+        sc.gqkv[sub, width:] = total
+        add_line(1, total[:, width:].astype(jnp.float32))
+        add_line(0, sc.gqkv[sub, :width].astype(jnp.float32))
+
+    tile = width // 3
+    for t in range(3):
+
+        @pl.loop(0, 3)
+        def _(j):
+            at = pl.multiple_of(t * width + j * tile, 128)
+            value = rows_dot(sc.attn[...], sc.gqkv[:, pl.ds(at, tile)]).astype(jnp.bfloat16)
+            to = pl.ds(pl.multiple_of(j * tile, 128), tile)
+            sc.grads[t, :, :, :, to] = value.reshape(sc.grads.shape[1:4] + (tile,))
+
+        start(t)
+
+    load(4).wait()
+    for j in range(3):
+        steps[1 + j]()
+        sc.back[:, j * tile : (j + 1) * tile] = lanes_dot(sc.gqkv[...], sc.first[j * tile : (j + 1) * tile, :])
+    load(5).wait()
+    load(6).wait()
+
+    @pl.loop(0, rows // BLOCK)
+    def _(block):
+        at = pl.multiple_of(block * BLOCK, BLOCK)
+        sub = pl.ds(at, BLOCK)
+        normed, inverse = normalize(sc.residual[sub, :])
+        back = sc.back[sub, :]
+        add_line(2, back)
+        add_line(3, back * normed)
+        grad = sc.middle[sub, :] + norm_back(back * (1.0 + vec_ref[1:2, :]), normed, inverse)
+        per_image = band_slots // BLOCK
+        to = pl.ds(pl.multiple_of(lax.rem(block, per_image) * BLOCK, BLOCK), BLOCK)
+        sc.tokens[block // per_image, to, :] = grad.astype(jnp.bfloat16)
+
+    small[...] = jnp.zeros_like(small)
+    kept = [sc.sums[2:3, :], sc.sums[3:4, :]] + [sums_ref[i : i + 1, :] for i in (3, 1, 2, 0)]
+    for i, values in enumerate(kept + [0.5 * vec_ref[14:15, :]]):
+        put_lines(small, i * lines, values)
+    at = mod_rows
+    for values in (sc.sums[0:1, :], sc.sums[1:2, :], sums_ref[4:5, :], inner_bias_ref[0:1, :], sums_ref[5:6, :]):
+        put_lines(small, at, values)
+        at += values.shape[1] // 128
+    exchange[0]()
     depart()
-    for step in steps[1:]:
-        step()
+    rest = steps[4:]
+    for i in range(max(len(rest), len(exchange) - 1)):
+        if i + 1 < len(exchange):
+            exchange[i + 1]()
+        if i < len(rest):
+            rest[i]()
     settle()
 
 
-def reduce_last(grads, parts, rows, mod_part, bias_part, ada_weight, images, collective_id):
-    plan, counts = (BACK, FRONT | BACK), (0, len(grads))
-    half, width = grads[0].shape[-2:]
-    mod_rows, bias_rows = mod_part.shape[0], bias_part.shape[0]
+def reduce_last(proj, part, attn_in, query, own, other, first, residual, middle, vectors, sums, inner_bias, ada_weight,
+                images, band_slots, collective_id):
+    plan = (BACK, FRONT | BACK)
+    half, width = proj.shape[-2:]
+    rows = attn_in.shape[0]
+    bf, f32 = jnp.bfloat16, jnp.float32
+    V = pltpu.VMEM
+    mod_rows = -(-(MOD_BLOCKS + 1) * width // 2048) * 16
+    bias_rows = (4 * width + inner_bias.shape[1]) // 128
     cond_cols = -(-ada_weight.shape[0] // 128) * 128
     scratch = dict(
-        **reduce_scratch(plan, half, width), **small_scratch(mod_rows, bias_rows, 8, cond_cols), **home_scratch()
+        **reduce_scratch(plan, half, width), **small_scratch(mod_rows, bias_rows, 8, cond_cols), **home_scratch(),
+        attn=V((rows, width), bf), gqkv=V((rows, 3 * width), bf), other=V((rows, 2 * width), bf),
+        first=V((width, 3 * width), bf), residual=V((rows, width), f32), middle=V((rows, width), f32),
+        grads=V((3, NB, 2, half, width), bf), back=V((rows, width), f32), sums=V((8, width), f32),
+        tokens=V((images, band_slots, width), bf), small=V((mod_rows + bias_rows, 128), f32),
+        load_sem=pltpu.SemaphoreType.DMA((7,)),
     )
     any_, vmem = pl.BlockSpec(memory_space=pl.ANY), pl.BlockSpec(memory_space=pltpu.VMEM)
     return pl.pallas_call(
-        partial(reduce_last_kernel, plan, counts, ada_weight.shape[1], images, tuple(scratch)),
+        partial(reduce_last_kernel, plan, images, band_slots, tuple(scratch)),
         out_shape=reduce_shapes(plan, half, width)
         + [
-            jax.ShapeDtypeStruct(rows.shape, rows.dtype),
-            jax.ShapeDtypeStruct((NB, 4, mod_rows, 128), jnp.bfloat16),
-            jax.ShapeDtypeStruct((bias_rows, 128), jnp.float32),
-            jax.ShapeDtypeStruct((NB, 8, cond_cols), jnp.float32),
+            jax.ShapeDtypeStruct((images, band_slots, width), bf),
+            jax.ShapeDtypeStruct((NB, 4, mod_rows, 128), bf),
+            jax.ShapeDtypeStruct((bias_rows, 128), f32),
+            jax.ShapeDtypeStruct((NB, 8, cond_cols), f32),
         ],
-        in_specs=[any_] * (len(grads) + 2) + [vmem] * 2,
+        in_specs=[any_] * 9 + [vmem] * 4,
         out_specs=[any_] * 3 + [vmem] * 3,
         scratch_shapes=list(scratch.values()),
         compiler_params=pltpu.CompilerParams(
-            collective_id=collective_id, has_side_effects=True, vmem_limit_bytes=56 * 2**20
+            collective_id=collective_id, has_side_effects=True, vmem_limit_bytes=62 * 2**20
         ),
         name="reduce_last",
-    )(*grads, parts, rows, jnp.concatenate([mod_part, bias_part]), ada_weight)
+    )(proj, part, attn_in, query, own, other, first, residual, middle, vectors, sums, inner_bias, ada_weight)
 
 
 def reduce_attend_kernel(plan, counts, band_slots, names, *refs):
@@ -678,7 +775,13 @@
 
     def store(i):
         ref, column = stores[i][2:]
-        return pltpu.make_async_copy(stage.at[i % 2], ref.at[:, pl.ds(column, width)], stage_sem.at[i % 2])
+        target = ref.at[:, pl.ds(column, width)]
+        if ref is not dfar_ref:
+            return pltpu.make_async_copy(stage.at[i % 2], target, stage_sem.at[i % 2])
+        return pltpu.make_async_remote_copy(
+            src_ref=stage.at[i % 2], dst_ref=target, send_sem=sc.far_send.at[i % 2],
+            recv_sem=sc.far_recv.at[i % 2], device_id=device(me.sib, me.band), device_id_type=MESH,
+        )
 
     for i, (heads_ref, row0, ref, column) in enumerate(stores):
         if i >= 2:
@@ -706,6 +809,8 @@
         gh=pltpu.VMEM((heads, rows, LANES), bf),
         stage=pltpu.VMEM((2, rows, width), bf),
         stage_sem=pltpu.SemaphoreType.DMA((2,)),
+        far_send=pltpu.SemaphoreType.DMA((2,)),
+        far_recv=pltpu.SemaphoreType.DMA((2,)),
         **home_scratch(),
     )
     any_, vmem = pl.BlockSpec(memory_space=pl.ANY), pl.BlockSpec(memory_space=pltpu.VMEM)
@@ -1276,14 +1381,6 @@
     )(mlp_in, inner, outer, vectors, inner_bias, residual, attended, cotangent, mixed, first)
 
 
-def pair_perm(dp_count, band_count):
-    return [
-        (dp * band_count + band, (dp ^ 1) * band_count + band)
-        for dp in range(dp_count)
-        for band in range(band_count)
-    ]
-
-
 def position_parts(width):
     quarter = width // 4
     frequency = 10000.0 ** (-jnp.arange(quarter, dtype=jnp.float32) / quarter)
@@ -1332,7 +1429,6 @@
     outer_bias,
     cotangent,
 ):
-    both = ("dp", "band")
     dp_count = lax.axis_size("dp")
     band_count = lax.axis_size("band")
     images, band_slots, width = tokens.shape
@@ -1341,7 +1437,6 @@
     core = lax.rem(dp, 2)
     hidden = inner_weight.shape[1]
     part_rows = qkv_weight.shape[0]
-    siblings = pair_perm(dp_count, band_count)
 
     condition_f = condition.astype(jnp.float32)
     activated = jax.nn.silu(condition_f).astype(jnp.bfloat16)
@@ -1372,10 +1467,6 @@
     first_full = first_full.reshape(width, -1)
     inner_full = inner_full.reshape(width, hidden)
     outer_full = outer_full.reshape(hidden, width)
-    qkv_full = first_full[:, : 3 * width]
-    proj_full = first_full[:, 3 * width :]
-    scale_one, gate_one = vectors[1], vectors[2]
-    condition_here = vectors[14]
     valid_count = vectors[15, :1].astype(jnp.int32)
     rows = images * band_slots
     inner_bias_row = vectors[10:14].reshape(1, -1)
@@ -1386,40 +1477,13 @@
     blocks = (band_count, 2, part_rows // 2, width)
     grad_outer = grad_outer.reshape(band_count, 4, 2, part_rows // 2, width)
     grad_inner = grad_inner.reshape(band_count, 2, part_rows // 2, hidden)
-    grad_inner_bias = grad_inner_bias[0]
-    grad_gate_two, grad_shift_two, grad_scale_two, grad_gate_one, grad_proj_bias, grad_outer_bias = [
-        sums[index] for index in range(6)
-    ]
-    normed_one, inverse_one = normalize(residual)
-    outer_sum, inner_part, block_home, grad_query, own_terms, far_terms = reduce_attend(
+    outer_sum, inner_part, block_home, grad_query, own_terms, other_terms = reduce_attend(
         (FRONT | BACK, FRONT), [[grad_outer], [grad_inner]], [], block_out.reshape(images, band_slots, width), valid_count, query_rows, key_value, other_key_value, grad_mixed, tops,
         band_slots, 1,
     )
-    other_terms = lax.ppermute(far_terms, both, siblings)
-    grad_key_value = (own_terms.astype(jnp.float32) + other_terms.astype(jnp.float32)).astype(
-        jnp.bfloat16
-    )
-    grad_qkv = jnp.concatenate([grad_query, grad_key_value], -1)
-    grad_first = [
-        rows_dot(attn_in, part).astype(jnp.bfloat16).reshape(blocks)
-        for part in (grad_query, grad_key_value[:, :width], grad_key_value[:, width:])
-    ]
-    grad_attn_in = lanes_dot(grad_qkv, qkv_full)
-    grad_query_bias = jnp.sum(grad_query.astype(jnp.float32), 0)
-    grad_value_bias = jnp.sum(grad_key_value[:, width:].astype(jnp.float32), 0)
-    grad_shift_one = jnp.sum(grad_attn_in, 0)
-    grad_scale_one = jnp.sum(grad_attn_in * normed_one, 0)
-    grad_tokens = grad_middle + norm_back(grad_attn_in * (1.0 + scale_one), normed_one, inverse_one)
-    part_mod = jnp.concatenate(
-        [grad_shift_one, grad_scale_one, grad_gate_one, grad_shift_two, grad_scale_two, grad_gate_two]
-    )
-    part_mod = jnp.concatenate([part_mod, 0.5 * condition_here]).reshape(-1, 128)
-    part_mod = jnp.pad(part_mod, ((0, -part_mod.shape[0] % 16), (0, 0)))
-    part_bias = jnp.concatenate(
-        [grad_query_bias, grad_value_bias, grad_proj_bias, grad_inner_bias, grad_outer_bias]
-    ).reshape(-1, 128)
     inner_sum, first_sum, tokens_home, every, bias_grads, grad_act = reduce_last(
-        grad_first + [grad_proj.reshape(blocks)], inner_part, grad_tokens.astype(jnp.bfloat16).reshape(images, band_slots, width), part_mod, part_bias, ada_weight, images, 2
+        grad_proj.reshape(blocks), inner_part, attn_in, grad_query, own_terms, other_terms, first_full, residual,
+        grad_middle, vectors, sums, grad_inner_bias, ada_weight, images, band_slots, 2,
     )
     tokens_home = tokens_home.astype(jnp.float32)
     every = every_group(every, dp_count)

time: 536 us -> 519 us (0.968)
  Pallas kernels: 440 us -> 473 us
  matrix products: 27.8 us -> 7.58 us
  other arithmetic: 30.5 us -> 16.9 us
  local copies, waits for them, and re-layouts: 25.4 us -> 12.3 us
    pallas_call x1, Pallas kernels: 98.2 us -> 131 us  [reduce_last(): pl.pallas_call(partial(reduce_last_kernel, plan, images, band_slots, tupl...]
    dot_general x1 -> x0, matrix products: 10.4 us -> none  [lanes_dot(): lax.dot_general(left, right, (((1,), (1,)), ((), ())), preferred_element_...]
    dot_general x4 -> x1, matrix products: 14.3 us -> 4.57 us  [rows_dot(): lax.dot_general(left, right, (((0,), (0,)), ((), ())), preferred_element_...]
    convert_element_type x2 -> x0, other arithmetic: 6.4 us -> none  [the longest x1 4.2 us: body(): grad_tokens.astype(jnp.bfloat16).reshape(images, band_slots, width)]
  transfers between devices with their start and end apart: 1 -> 0, of which waited for: 0 -> 0; matrix products, arithmetic and copies ran while one was open for 3% -> 0% of each run, Pallas kernels for 0% -> 0%
where the time goes in v8:
time: 519 us; the launch traced here: 512 us
  Pallas kernels  473 us (91%)
  other arithmetic  16.9 us (3%)
  local copies, waits for them, and re-layouts  12.3 us (2%)
  matrix products  7.58 us (1%)
    pallas_call x1, Pallas kernels, forward_block(): pl.pallas_call(partial(forward_kernel, tuple(scratch), band_slots), out_s...  165 us
    pallas_call x1, Pallas kernels, reduce_last(): pl.pallas_call(partial(reduce_last_kernel, plan, images, band_slots, tupl...  131 us
    pallas_call x1, Pallas kernels, reduce_attend(): pl.pallas_call(partial(reduce_attend_kernel, plan, counts, band_slots, tu...  120 us
    pallas_call x1, Pallas kernels, feed_forward(): pl.pallas_call(partial(mlp_kernel, band_slots), grid=(hidden // tile,), o...  57.1 us

profile of v8, /device:TPU:1, one launch (start us, length us, event | category | flops | bytes accessed | tf_op | source)
XLA Modules:
  0.0 511.9 jit_solution(15206270657379436835)
XLA Ops:
  0.6 0.0 copy-start.7
  0.7 0.0 copy-start.13
  0.7 0.0 copy-start.9
  0.7 0.0 copy-start.10
  0.7 0.0 copy-start.11
  0.7 0.0 copy-start.12
  0.7 0.0 copy-start.8
  0.7 0.8 convert_dynamic-update-slice_fusion
  1.6 0.7 add_divide_fusion
  2.3 0.7 convert_element_type.93
  3.0 3.0 fusion
  6.0 0.0 copy-done.13
  6.0 0.0 copy-done.9
  6.1 0.0 copy-done.11
  6.2 0.0 copy-done.8
  6.2 0.6 copy.37
  6.9 0.7 sine_bitcast_fusion
  7.6 0.1 reduce-precision_convert_fusion.1
  7.7 0.9 pad_maximum_fusion.1.refs_6_
  8.6 0.0 copy-done.4
  8.6 1.7 pad_maximum_fusion
  10.3 165.3 %forward_block.1 = (bf16[4,2,144,4608]{3,2,1,0:T(8,128)(2,1)}, bf16[4,2,144,4608]{3,2,1,0:T(8,128)(2,1)}, bf16[4,4,2,144,1152]{4,3,2,1,0:T(8,128)(2,1)}, bf16[2,...) custom-call(bf16[2,144,4608]{2,1,0:T(8,128)(2,1)} %bitcast.63, ...), custom_call_target="tpu_custom_call" | custom-call | tf_op jit(solution)/shard_map/forward_block/pallas_call | solution.py:1256
  175.6 0.8 slice_bitcast_fusion.1
  176.3 0.6 copy.32
  177.0 57.1 %feed_forward.1 = (bf16[512,1152]{1,0:T(8,128)(2,1)}, f32[512,1152]{1,0:T(8,128)}, bf16[512,1152]{1,0:T(8,128)(2,1)}, bf16[1152,1152]{1,0:T(8,128)(2,1)}, bf16[4...) custom-call(bf16[512,1152]{1,0:T(8,128)(2,1)} %get-tuple-element.48.mlp_ref, ...), custom_call_target="tpu_custom_call" | custom-call | flops 32614907904 | bytes 56623104 | tf_op jit(solution)/shard_map/feed_forward/pallas_call | solution.py:1357
  234.1 1.2 slice.70
  235.9 120.1 %reduce_attend.1 = (bf16[4,2,144,1152]{3,2,1,0:T(8,128)(2,1)}, bf16[144,1152]{1,0:T(8,128)(2,1)}, bf16[2,256,1152]{2,1,0:T(8,128)(2,1)}, bf16[512,1152]{1,0:T(8,...) custom-call(bf16[4,4,2,144,1152]{4,3,2,1,0:T(8,128)(2,1)} %bitcast.61, ...), custom_call_target="tpu_custom_call" | custom-call | tf_op jit(solution)/shard_map/reduce_attend/pallas_call | solution.py:819
  356.0 130.8 %reduce_last.1 = (bf16[4,2,144,1152]{3,2,1,0:T(8,128)(2,1)}, bf16[4,2,144,1152]{3,2,1,0:T(8,128)(2,1)}, bf16[2,256,1152]{2,1,0:T(8,128)(2,1)}, bf16[4,4,64,128]{...) custom-call(bf16[4,2,144,1152]{3,2,1,0:T(8,128)(2,1)} %bitcast.64, ...), custom_call_target="tpu_custom_call" | custom-call | tf_op jit(solution)/shard_map/reduce_last/pallas_call | solution.py:709
  486.8 2.9 fusion.13
  489.7 2.7 maximum_convert_fusion
  492.4 2.2 maximum_convert_fusion.1
  494.5 1.2 bitcast_convert_fusion.1
  495.7 0.0 copy-done.5
  495.8 0.2 copy.36
  496.0 4.6 fusion.3
  500.6 1.6 convert_element_type.103
  502.1 0.1 convert_reduce_fusion
  502.2 0.7 dynamic_slice.26
  502.9 0.8 slice_bitcast_fusion.2
  503.7 0.1 reshape.253
  503.8 0.6 fusion.7
  504.4 0.7 dynamic_slice.27
  505.1 0.7 dynamic_slice.28
  505.7 0.7 dynamic_slice.29
  506.4 0.7 dynamic_slice.31
  507.0 0.7 dynamic_slice.30
  507.7 2.9 bitcast_convert_fusion
  510.6 1.0 copy.47
  (36 shorter events, 0.2 us)
Async XLA Ops:
  0.6 5.3 %copy-start.7 = (bf16[2,1152]{1,0:T(2,128)(2,1)S(1)}, bf16[2,1152]{1,0:T(2,128)(2,1)}, u32[]{:S(2)}) copy-start(bf16[2,1152]{1,0:T(2,128)(2,1)} %param.16) | copy-start | bytes 13828
  0.7 5.3 %copy-start.13 = (s32[2,2]{1,0:T(2,128)S(1)}, s32[2,2]{1,0:T(2,128)}, u32[]{:S(2)}) copy-start(s32[2,2]{1,0:T(2,128)} %param.17) | copy-start | bytes 52
  0.7 5.4 %copy-start.9 = (bf16[288]{0:T(512)(128)(2,1)S(1)}, bf16[288]{0:T(512)(128)(2,1)}, u32[]{:S(2)}) copy-start(bf16[288]{0:T(512)(128)(2,1)} %param.21) | copy-start | bytes 1732
  0.7 5.4 %copy-start.10 = (bf16[288]{0:T(512)(128)(2,1)S(1)}, bf16[288]{0:T(512)(128)(2,1)}, u32[]{:S(2)}) copy-start(bf16[288]{0:T(512)(128)(2,1)} %param.22) | copy-start | bytes 1732
  0.7 5.4 %copy-start.11 = (bf16[288]{0:T(512)(128)(2,1)S(1)}, bf16[288]{0:T(512)(128)(2,1)}, u32[]{:S(2)}) copy-start(bf16[288]{0:T(512)(128)(2,1)} %param.24) | copy-start | bytes 1732
  0.7 5.4 %copy-start.12 = (bf16[288]{0:T(512)(128)(2,1)S(1)}, bf16[288]{0:T(512)(128)(2,1)}, u32[]{:S(2)}) copy-start(bf16[288]{0:T(512)(128)(2,1)} %param.28) | copy-start | bytes 1732
  0.7 5.5 %copy-start.8 = (bf16[1152]{0:T(1024)(128)(2,1)S(1)}, bf16[1152]{0:T(1024)(128)(2,1)}, u32[]{:S(2)}) copy-start(bf16[1152]{0:T(1024)(128)(2,1)} %param.26) | copy-start | bytes 6916
  3.0 5.6 %copy-start.1 = (bf16[288,3456]{1,0:T(8,128)(2,1)S(1)}, bf16[288,3456]{1,0:T(8,128)(2,1)}, u32[]{:S(2)}) copy-start(bf16[288,3456]{1,0:T(8,128)(2,1)} %param.20) | copy-start | bytes 5971972
  3.0 5.6 %copy-start.4 = (bf16[288,1152]{1,0:T(8,128)(2,1)S(1)}, bf16[288,1152]{1,0:T(8,128)(2,1)}, u32[]{:S(2)}) copy-start(bf16[288,1152]{1,0:T(8,128)(2,1)} %param.23) | copy-start | bytes 1990660
  492.3 3.4 copy-start.5
  496.0 4.6 copy-start.2
  500.5 3.9 copy-start.6
  500.5 7.2 %copy-start = (bf16[4,2,144,1152]{3,2,1,0:T(8,128)(2,1)S(1)}, bf16[4,2,144,1152]{3,2,1,0:T(8,128)(2,1)}, u32[]{:S(2)}) copy-start(bf16[4,2,144,1152]{3,2,1,0:T(8,128)(2,1)} %get-tuple-element.81) | copy-start | bytes 7962628
  507.7 2.9 copy-start.3

commit v9 on v8

--- a/solution.py
+++ b/solution.py
@@ -374,7 +374,10 @@
     steps = [partial(run_all, table[at]) for at in sorted(table)]
     steps.append(finish)
     if by_kind:
-        return steps, lambda kind: [start_a(s, (kind,)) for s in range(n)]
+        return SimpleNamespace(
+            start=lambda kind: [start_a(s, (kind,)) for s in range(n)], a=a_to_b, b=b_to_c, c=c_to_z, sum=z_sum,
+            take=lambda phase: part_load(phase).start(), d1=d_first, d2=d_second, d3=d_third, d4=d_last, finish=finish,
+        )
     return steps
 
 
@@ -614,11 +617,13 @@
     mods = MOD_BLOCKS * width
     exchange = small_steps(me, mods, images, small, ada_ref, every_ref, bias_ref, cond_ref, sc)
     depart, settle = home_steps(me, sc.tokens, home_ref, sc)
-    steps, start = reduce_steps(
-        me, plan, source, (inner_out, first_out), (part_ref, None), (None, None), sc, (), 2, True
-    )
-    start(3)
-    steps[0]()
+    r = reduce_steps(me, plan, source, (inner_out, first_out), (part_ref, None), (None, None), sc, (), 2, True)
+
+    def run(*todo):
+        for do, index in todo:
+            do(index)
+
+    run((r.start, 3), (r.take, 0), (r.d1, 0))
     for i in range(4):
         load(i).wait()
 
@@ -637,21 +642,11 @@
         add_line(0, sc.gqkv[sub, :width].astype(jnp.float32))
 
     tile = width // 3
-    for t in range(3):
-
-        @pl.loop(0, 3)
-        def _(j):
-            at = pl.multiple_of(t * width + j * tile, 128)
-            value = rows_dot(sc.attn[...], sc.gqkv[:, pl.ds(at, tile)]).astype(jnp.bfloat16)
-            to = pl.ds(pl.multiple_of(j * tile, 128), tile)
-            sc.grads[t, :, :, :, to] = value.reshape(sc.grads.shape[1:4] + (tile,))
-
-        start(t)
-
     load(4).wait()
+    between = [(), ((r.d2, 0),), ()]
     for j in range(3):
-        steps[1 + j]()
         sc.back[:, j * tile : (j + 1) * tile] = lanes_dot(sc.gqkv[...], sc.first[j * tile : (j + 1) * tile, :])
+        run(*between[j])
     load(5).wait()
     load(6).wait()
 
@@ -676,15 +671,24 @@
     for values in (sc.sums[0:1, :], sc.sums[1:2, :], sums_ref[4:5, :], inner_bias_ref[0:1, :], sums_ref[5:6, :]):
         put_lines(small, at, values)
         at += values.shape[1] // 128
-    exchange[0]()
+    say = lambda i: exchange[i]()
     depart()
-    rest = steps[4:]
-    for i in range(max(len(rest), len(exchange) - 1)):
-        if i + 1 < len(exchange):
-            exchange[i + 1]()
-        if i < len(rest):
-            rest[i]()
+    run((r.d3, 0))
+    for t in range(3):
+
+        @pl.loop(0, 3)
+        def _(j):
+            at = pl.multiple_of(t * width + j * tile, 128)
+            value = rows_dot(sc.attn[...], sc.gqkv[:, pl.ds(at, tile)]).astype(jnp.bfloat16)
+            to = pl.ds(pl.multiple_of(j * tile, 128), tile)
+            sc.grads[t, :, :, :, to] = value.reshape(sc.grads.shape[1:4] + (tile,))
+
+        run((r.start, t), (say, t))
+
+    run((r.a, 0), (r.a, 1), (say, 3), (r.b, 0), (r.a, 2), (r.b, 1), (r.c, 0), (r.a, 3), (r.b, 2), (r.c, 1), (r.b, 3), (r.c, 2))
+    run((r.c, 3), (say, 4), (r.sum, 1), (r.d1, 1), (r.d2, 1), (r.d3, 1), (say, 5), (r.d4, 0), (r.d4, 1))
     settle()
+    r.finish()
 
 
 def reduce_last(proj, part, attn_in, query, own, other, first, residual, middle, vectors, sums, inner_bias, ada_weight,

time: 519 us -> 497 us (0.958); the launches traced: 512 us -> 497 us
  Pallas kernels: 473 us -> 458 us
    pallas_call x1, Pallas kernels: 131 us -> 116 us  [reduce_last(): pl.pallas_call(partial(reduce_last_kernel, plan, images, band_slots, tupl...]
where the time goes in v9:
time: 497 us
  Pallas kernels  458 us (92%)
  other arithmetic  16.9 us (3%)
  local copies, waits for them, and re-layouts  12.3 us (2%)
  matrix products  7.58 us (2%)
    pallas_call x1, Pallas kernels, forward_block(): pl.pallas_call(partial(forward_kernel, tuple(scratch), band_slots), out_s...  165 us
    pallas_call x1, Pallas kernels, reduce_attend(): pl.pallas_call(partial(reduce_attend_kernel, plan, counts, band_slots, tu...  120 us
    pallas_call x1, Pallas kernels, reduce_last(): pl.pallas_call(partial(reduce_last_kernel, plan, images, band_slots, tupl...  116 us
    pallas_call x1, Pallas kernels, feed_forward(): pl.pallas_call(partial(mlp_kernel, band_slots), grid=(hidden // tile,), o...  56.8 us

profile of v9, /device:TPU:1, one launch (start us, length us, event | category | flops | bytes accessed | tf_op | source)
XLA Modules:
  0.0 496.8 jit_solution(13582376428035494115)
XLA Ops:
  0.6 0.0 copy-start.7
  0.7 0.0 copy-start.13
  0.7 0.0 copy-start.9
  0.7 0.0 copy-start.10
  0.7 0.0 copy-start.11
  0.7 0.0 copy-start.12
  0.7 0.0 copy-start.8
  0.7 0.8 convert_dynamic-update-slice_fusion
  1.6 0.7 add_divide_fusion
  2.3 0.7 convert_element_type.93
  3.0 3.0 fusion
  6.0 0.0 copy-done.13
  6.0 0.0 copy-done.9
  6.1 0.0 copy-done.11
  6.2 0.0 copy-done.8
  6.2 0.6 copy.37
  6.9 0.7 sine_bitcast_fusion
  7.6 0.1 reduce-precision_convert_fusion.1
  7.7 0.9 pad_maximum_fusion.1.refs_6_
  8.6 0.0 copy-done.4
  8.6 1.7 pad_maximum_fusion
  10.3 165.3 %forward_block.1 = (bf16[4,2,144,4608]{3,2,1,0:T(8,128)(2,1)}, bf16[4,2,144,4608]{3,2,1,0:T(8,128)(2,1)}, bf16[4,4,2,144,1152]{4,3,2,1,0:T(8,128)(2,1)}, bf16[2,...) custom-call(bf16[2,144,4608]{2,1,0:T(8,128)(2,1)} %bitcast.63, ...), custom_call_target="tpu_custom_call" | custom-call | tf_op jit(solution)/shard_map/forward_block/pallas_call | solution.py:1260
  175.6 0.8 slice_bitcast_fusion.1
  176.3 0.6 copy.32
  177.0 56.8 %feed_forward.1 = (bf16[512,1152]{1,0:T(8,128)(2,1)}, f32[512,1152]{1,0:T(8,128)}, bf16[512,1152]{1,0:T(8,128)(2,1)}, bf16[1152,1152]{1,0:T(8,128)(2,1)}, bf16[4...) custom-call(bf16[512,1152]{1,0:T(8,128)(2,1)} %get-tuple-element.48.mlp_ref, ...), custom_call_target="tpu_custom_call" | custom-call | flops 32614907904 | bytes 56623104 | tf_op jit(solution)/shard_map/feed_forward/pallas_call | solution.py:1361
  233.8 1.2 slice.70
  235.6 120.2 %reduce_attend.1 = (bf16[4,2,144,1152]{3,2,1,0:T(8,128)(2,1)}, bf16[144,1152]{1,0:T(8,128)(2,1)}, bf16[2,256,1152]{2,1,0:T(8,128)(2,1)}, bf16[512,1152]{1,0:T(8,...) custom-call(bf16[4,4,2,144,1152]{4,3,2,1,0:T(8,128)(2,1)} %bitcast.61, ...), custom_call_target="tpu_custom_call" | custom-call | tf_op jit(solution)/shard_map/reduce_attend/pallas_call | solution.py:823
  355.8 116.2 %reduce_last.1 = (bf16[4,2,144,1152]{3,2,1,0:T(8,128)(2,1)}, bf16[4,2,144,1152]{3,2,1,0:T(8,128)(2,1)}, bf16[2,256,1152]{2,1,0:T(8,128)(2,1)}, bf16[4,4,64,128]{...) custom-call(bf16[4,2,144,1152]{3,2,1,0:T(8,128)(2,1)} %bitcast.64, ...), custom_call_target="tpu_custom_call" | custom-call | tf_op jit(solution)/shard_map/reduce_last/pallas_call | solution.py:713
  472.0 2.9 fusion.13
  474.9 2.7 maximum_convert_fusion
  477.5 2.2 maximum_convert_fusion.1
  479.7 1.2 bitcast_convert_fusion.1
  481.0 0.2 copy.36
  481.2 0.0 copy-start.2
  481.2 4.6 fusion.3
  485.8 1.6 convert_element_type.103
  487.3 0.1 convert_reduce_fusion
  487.4 0.7 dynamic_slice.26
  488.1 0.8 slice_bitcast_fusion.2
  488.9 0.1 reshape.253
  489.0 0.6 fusion.7
  489.6 0.7 dynamic_slice.27
  490.3 0.7 dynamic_slice.28
  490.9 0.7 dynamic_slice.29
  491.6 0.7 dynamic_slice.31
  492.2 0.7 dynamic_slice.30
  492.9 2.9 bitcast_convert_fusion
  495.8 1.0 copy.47
  (36 shorter events, 0.2 us)
Async XLA Ops:
  0.6 5.3 %copy-start.7 = (bf16[2,1152]{1,0:T(2,128)(2,1)S(1)}, bf16[2,1152]{1,0:T(2,128)(2,1)}, u32[]{:S(2)}) copy-start(bf16[2,1152]{1,0:T(2,128)(2,1)} %param.16) | copy-start | bytes 13828
  0.7 5.3 %copy-start.13 = (s32[2,2]{1,0:T(2,128)S(1)}, s32[2,2]{1,0:T(2,128)}, u32[]{:S(2)}) copy-start(s32[2,2]{1,0:T(2,128)} %param.17) | copy-start | bytes 52
  0.7 5.4 %copy-start.9 = (bf16[288]{0:T(512)(128)(2,1)S(1)}, bf16[288]{0:T(512)(128)(2,1)}, u32[]{:S(2)}) copy-start(bf16[288]{0:T(512)(128)(2,1)} %param.21) | copy-start | bytes 1732
  0.7 5.4 %copy-start.10 = (bf16[288]{0:T(512)(128)(2,1)S(1)}, bf16[288]{0:T(512)(128)(2,1)}, u32[]{:S(2)}) copy-start(bf16[288]{0:T(512)(128)(2,1)} %param.22) | copy-start | bytes 1732
  0.7 5.4 %copy-start.11 = (bf16[288]{0:T(512)(128)(2,1)S(1)}, bf16[288]{0:T(512)(128)(2,1)}, u32[]{:S(2)}) copy-start(bf16[288]{0:T(512)(128)(2,1)} %param.24) | copy-start | bytes 1732
  0.7 5.4 %copy-start.12 = (bf16[288]{0:T(512)(128)(2,1)S(1)}, bf16[288]{0:T(512)(128)(2,1)}, u32[]{:S(2)}) copy-start(bf16[288]{0:T(512)(128)(2,1)} %param.28) | copy-start | bytes 1732
  0.7 5.5 %copy-start.8 = (bf16[1152]{0:T(1024)(128)(2,1)S(1)}, bf16[1152]{0:T(1024)(128)(2,1)}, u32[]{:S(2)}) copy-start(bf16[1152]{0:T(1024)(128)(2,1)} %param.26) | copy-start | bytes 6916
  3.0 5.6 %copy-start.1 = (bf16[288,3456]{1,0:T(8,128)(2,1)S(1)}, bf16[288,3456]{1,0:T(8,128)(2,1)}, u32[]{:S(2)}) copy-start(bf16[288,3456]{1,0:T(8,128)(2,1)} %param.20) | copy-start | bytes 5971972
  3.0 5.6 %copy-start.4 = (bf16[288,1152]{1,0:T(8,128)(2,1)S(1)}, bf16[288,1152]{1,0:T(8,128)(2,1)}, u32[]{:S(2)}) copy-start(bf16[288,1152]{1,0:T(8,128)(2,1)} %param.23) | copy-start | bytes 1990660
  477.5 3.4 copy-start.5
  481.2 4.6 copy-start.2
  485.7 3.9 copy-start.6
  485.7 7.2 %copy-start = (bf16[4,2,144,1152]{3,2,1,0:T(8,128)(2,1)S(1)}, bf16[4,2,144,1152]{3,2,1,0:T(8,128)(2,1)}, u32[]{:S(2)}) copy-start(bf16[4,2,144,1152]{3,2,1,0:T(8,128)(2,1)} %get-tuple-element.81) | copy-start | bytes 7962628
  492.9 2.9 copy-start.3

commit v10 on v9

--- a/solution.py
+++ b/solution.py
@@ -3,6 +3,7 @@
 
 import jax
 import jax.numpy as jnp
+import numpy as np
 from jax import lax
 from jax.experimental import pallas as pl
 from jax.experimental.pallas import tpu as pltpu
@@ -1098,7 +1099,7 @@
 
     g.begin()
     g.place()
-    run((g.z, 0), (g.z, 1), (g.i, 0), (g.a, 0), (g.a, 1), (g.z, 2), (g.s, 1), (g.b, 0), (g.b, 1), (g.a, 2), (g.c, 0), (g.c, 1), (g.z, 3), (g.z, 4), (g.b, 2))
+    run((g.z, 0), (g.z, 1), (g.i, 0), (g.a, 0), (g.a, 1), (g.z, 2), (g.s, 1), (g.b, 0), (g.b, 1), (g.a, 2), (g.z, 3), (g.c, 0), (g.c, 1), (g.z, 4), (g.b, 2), (g.a, 3))
     g.arrived()
     spread_notes(notes, vec, width)
     grid_rows = notes[0, 63:64, 0:1]
@@ -1152,7 +1153,7 @@
     def _(step):
         sc.own[:, here(step)] = product(sc.attn_in, width, step).astype(jnp.bfloat16)
 
-    run((g.a, 3), (g.z, 5), (g.s, 2))
+    run((g.z, 5), (g.s, 2))
 
     @pl.loop(0, 3)
     def _(step):
@@ -1387,15 +1388,14 @@
 
 def position_parts(width):
     quarter = width // 4
-    frequency = 10000.0 ** (-jnp.arange(quarter, dtype=jnp.float32) / quarter)
-    angles = jnp.arange(128, dtype=jnp.float32)[:, None] * frequency
-    left = jnp.concatenate([jnp.sin(angles), jnp.cos(angles)], -1)
+    frequency = 10000.0 ** (-np.arange(quarter, dtype=np.float32) / np.float32(quarter))
+    angles = (np.arange(128, dtype=np.float32)[:, None] * frequency.astype(np.float32)).astype(np.float64)
+    left = np.concatenate([np.sin(angles), np.cos(angles)], -1).astype(np.float32)
     parts = []
     for _ in range(3):
-        part = lax.reduce_precision(left, 8, 7)
-        parts.append(part.astype(jnp.bfloat16))
-        left = left - part
-    return jnp.stack(parts)
+        parts.append(left.astype(jnp.bfloat16))
+        left = left - parts[-1].astype(np.float32)
+    return jnp.asarray(np.stack(parts))
 
 
 def over_groups(piece, dp_count):

time: 497 us -> 490 us (0.986)
  Pallas kernels: 458 us -> 453 us
    pallas_call x1, Pallas kernels: 165 us -> 159 us  [forward_block(): pl.pallas_call(partial(forward_kernel, tuple(scratch), band_slots), out_s...]
where the time goes in v10:
time: 490 us
  Pallas kernels  453 us (92%)
  other arithmetic  15.4 us (3%)
  local copies, waits for them, and re-layouts  12.3 us (3%)
  matrix products  7.42 us (2%)
    pallas_call x1, Pallas kernels, forward_block(): pl.pallas_call(partial(forward_kernel, tuple(scratch), band_slots), out_s...  159 us
    pallas_call x1, Pallas kernels, reduce_attend(): pl.pallas_call(partial(reduce_attend_kernel, plan, counts, band_slots, tu...  119 us
    pallas_call x1, Pallas kernels, reduce_last(): pl.pallas_call(partial(reduce_last_kernel, plan, images, band_slots, tupl...  117 us
    pallas_call x1, Pallas kernels, feed_forward(): pl.pallas_call(partial(mlp_kernel, band_slots), grid=(hidden // tile,), o...  56.8 us

profile of v10, /device:TPU:1, one launch (start us, length us, event | category | flops | bytes accessed | tf_op | source)
XLA Modules:
  0.0 489.5 jit_solution(15414659275654357329)
XLA Ops:
  0.6 0.0 copy-start.7
  0.7 0.0 copy-start.13
  0.7 0.0 copy-start.9
  0.7 0.0 copy-start.10
  0.7 0.0 copy-start.11
  0.7 0.0 copy-start.12
  0.7 0.0 copy-start.8
  0.7 0.0 copy-start.1
  0.7 0.0 copy-start.4
  0.8 1.0 convert_dynamic-update-slice_fusion
  1.7 0.7 add_divide_fusion
  2.4 0.7 convert_element_type.63
  3.1 2.9 fusion
  6.0 0.0 copy-done.7
  6.0 0.0 copy-done.9
  6.1 0.0 copy-done.11
  6.2 0.0 copy-done.8
  6.2 0.6 copy.38
  6.9 0.0 copy-done.4
  6.9 1.7 pad_maximum_fusion
  8.6 159.5 %forward_block.1 = (bf16[4,2,144,4608]{3,2,1,0:T(8,128)(2,1)}, bf16[4,2,144,4608]{3,2,1,0:T(8,128)(2,1)}, bf16[4,4,2,144,1152]{4,3,2,1,0:T(8,128)(2,1)}, bf16[2,...) custom-call(bf16[2,144,4608]{2,1,0:T(8,128)(2,1)} %bitcast.59, ...), custom_call_target="tpu_custom_call" | custom-call | tf_op jit(solution)/shard_map/forward_block/pallas_call | solution.py:1261
  168.0 0.8 slice_bitcast_fusion.1
  168.8 0.6 copy.33
  169.4 56.8 %feed_forward.1 = (bf16[512,1152]{1,0:T(8,128)(2,1)}, f32[512,1152]{1,0:T(8,128)}, bf16[512,1152]{1,0:T(8,128)(2,1)}, bf16[1152,1152]{1,0:T(8,128)(2,1)}, bf16[4...) custom-call(bf16[512,1152]{1,0:T(8,128)(2,1)} %get-tuple-element.48.mlp_ref, ...), custom_call_target="tpu_custom_call" | custom-call | flops 32614907904 | bytes 56623104 | tf_op jit(solution)/shard_map/feed_forward/pallas_call | solution.py:1362
  226.3 1.2 slice.70
  228.1 119.4 %reduce_attend.1 = (bf16[4,2,144,1152]{3,2,1,0:T(8,128)(2,1)}, bf16[144,1152]{1,0:T(8,128)(2,1)}, bf16[2,256,1152]{2,1,0:T(8,128)(2,1)}, bf16[512,1152]{1,0:T(8,...) custom-call(bf16[4,4,2,144,1152]{4,3,2,1,0:T(8,128)(2,1)} %bitcast.57, ...), custom_call_target="tpu_custom_call" | custom-call | tf_op jit(solution)/shard_map/reduce_attend/pallas_call | solution.py:824
  347.5 117.2 %reduce_last.1 = (bf16[4,2,144,1152]{3,2,1,0:T(8,128)(2,1)}, bf16[4,2,144,1152]{3,2,1,0:T(8,128)(2,1)}, bf16[2,256,1152]{2,1,0:T(8,128)(2,1)}, bf16[4,4,64,128]{...) custom-call(bf16[4,2,144,1152]{3,2,1,0:T(8,128)(2,1)} %bitcast.60, ...), custom_call_target="tpu_custom_call" | custom-call | tf_op jit(solution)/shard_map/reduce_last/pallas_call | solution.py:714
  464.6 2.9 fusion.11
  467.5 2.7 maximum_convert_fusion
  470.2 2.2 maximum_convert_fusion.1
  472.4 1.2 bitcast_convert_fusion.1
  473.6 0.0 copy-done.5
  473.6 0.2 copy.37
  473.9 4.6 fusion.1
  478.4 1.6 convert_element_type.70
  480.0 0.1 convert_reduce_fusion
  480.1 0.7 dynamic_slice.26
  480.8 0.8 slice_bitcast_fusion.2
  481.6 0.1 reshape.103
  481.7 0.6 fusion.5
  482.3 0.7 dynamic_slice.27
  482.9 0.7 dynamic_slice.28
  483.6 0.7 dynamic_slice.29
  484.2 0.7 dynamic_slice.31
  484.9 0.7 dynamic_slice.30
  485.6 2.9 bitcast_convert_fusion
  488.5 0.0 copy-done.3
  488.5 1.0 copy.48
  (32 shorter events, 0.2 us)
Async XLA Ops:
  0.6 5.3 %copy-start.7 = (bf16[2,1152]{1,0:T(2,128)(2,1)S(1)}, bf16[2,1152]{1,0:T(2,128)(2,1)}, u32[]{:S(2)}) copy-start(bf16[2,1152]{1,0:T(2,128)(2,1)} %param.17) | copy-start | bytes 13828
  0.7 5.4 %copy-start.13 = (s32[2,2]{1,0:T(2,128)S(1)}, s32[2,2]{1,0:T(2,128)}, u32[]{:S(2)}) copy-start(s32[2,2]{1,0:T(2,128)} %param.18) | copy-start | bytes 52
  0.7 5.4 %copy-start.9 = (bf16[288]{0:T(512)(128)(2,1)S(1)}, bf16[288]{0:T(512)(128)(2,1)}, u32[]{:S(2)}) copy-start(bf16[288]{0:T(512)(128)(2,1)} %param.22) | copy-start | bytes 1732
  0.7 5.4 %copy-start.10 = (bf16[288]{0:T(512)(128)(2,1)S(1)}, bf16[288]{0:T(512)(128)(2,1)}, u32[]{:S(2)}) copy-start(bf16[288]{0:T(512)(128)(2,1)} %param.23) | copy-start | bytes 1732
  0.7 5.4 %copy-start.11 = (bf16[288]{0:T(512)(128)(2,1)S(1)}, bf16[288]{0:T(512)(128)(2,1)}, u32[]{:S(2)}) copy-start(bf16[288]{0:T(512)(128)(2,1)} %param.25) | copy-start | bytes 1732
  0.7 5.5 %copy-start.12 = (bf16[288]{0:T(512)(128)(2,1)S(1)}, bf16[288]{0:T(512)(128)(2,1)}, u32[]{:S(2)}) copy-start(bf16[288]{0:T(512)(128)(2,1)} %param.29) | copy-start | bytes 1732
  0.7 5.5 %copy-start.8 = (bf16[1152]{0:T(1024)(128)(2,1)S(1)}, bf16[1152]{0:T(1024)(128)(2,1)}, u32[]{:S(2)}) copy-start(bf16[1152]{0:T(1024)(128)(2,1)} %param.27) | copy-start | bytes 6916
  0.7 6.2 %copy-start.1 = (bf16[288,3456]{1,0:T(8,128)(2,1)S(1)}, bf16[288,3456]{1,0:T(8,128)(2,1)}, u32[]{:S(2)}) copy-start(bf16[288,3456]{1,0:T(8,128)(2,1)} %param.21) | copy-start | bytes 5971972
  0.7 6.2 %copy-start.4 = (bf16[288,1152]{1,0:T(8,128)(2,1)S(1)}, bf16[288,1152]{1,0:T(8,128)(2,1)}, u32[]{:S(2)}) copy-start(bf16[288,1152]{1,0:T(8,128)(2,1)} %param.24) | copy-start | bytes 1990660
  470.2 3.4 copy-start.5
  473.8 4.6 copy-start.2
  478.4 3.9 copy-start.6
  478.4 7.2 %copy-start = (bf16[4,2,144,1152]{3,2,1,0:T(8,128)(2,1)S(1)}, bf16[4,2,144,1152]{3,2,1,0:T(8,128)(2,1)}, u32[]{:S(2)}) copy-start(bf16[4,2,144,1152]{3,2,1,0:T(8,128)(2,1)} %get-tuple-element.81) | copy-start | bytes 7962628
  485.6 2.9 copy-start.3

commit v11 on v10

--- a/solution.py
+++ b/solution.py
@@ -1279,13 +1279,21 @@
 GELU_SCALE = 0.7978845608028654
 
 
-def mlp_kernel(band_slots, mlp_ref, inner_ref, outer_ref, vec_ref, bias_ref, residual_ref, attended_ref, cot_ref,
-               mixed_ref, proj_ref, out_ref, middle_ref, back_ref, proj_grad_ref, outer_grad_ref, inner_grad_ref,
-               bias_grad_ref, sums_ref, out_acc, back_acc, grad_mlp):
+def mlp_kernel(band_slots, mlp_ref, inner_ref, outer_ref, vec_ref, bias_ref, residual_hbm, attended_hbm, cot_ref,
+               mixed_hbm, first_hbm, out_ref, middle_ref, back_ref, proj_grad_ref, outer_grad_ref, inner_grad_ref,
+               bias_grad_ref, sums_ref, out_acc, back_acc, grad_mlp, residual_ref, attended_ref, mixed_ref, proj_ref, late_sem):
     step = pl.program_id(0)
     rows = mlp_ref.shape[0]
     low = lambda value: value.astype(jnp.bfloat16)
     line = lambda index: vec_ref[index : index + 1, :]
+    width = mlp_ref.shape[1]
+    late = [
+        pltpu.make_async_copy(src, dst, late_sem.at[i])
+        for i, (src, dst) in enumerate(
+            ((residual_hbm, residual_ref), (attended_hbm, attended_ref), (mixed_hbm, mixed_ref),
+             (first_hbm.at[:, pl.ds(3 * width, width)], proj_ref))
+        )
+    ]
 
     def grad_out(at):
         slot = lax.rem(at + lax.broadcasted_iota(jnp.int32, (BLOCK, 1), 0), band_slots)
@@ -1298,6 +1306,8 @@
     @pl.when(step == 0)
     def _():
         sums_ref[...] = jnp.zeros_like(sums_ref)
+        for copy in late:
+            copy.start()
 
         @pl.loop(0, rows // BLOCK)
         def _(block):
@@ -1327,6 +1337,9 @@
 
     @pl.when(step == pl.num_programs(0) - 1)
     def _():
+        for copy in late:
+            copy.wait()
+
         @pl.loop(0, rows // BLOCK)
         def _(block):
             at = pl.multiple_of(block * BLOCK, BLOCK)
@@ -1359,6 +1372,7 @@
     bf, f32 = jnp.bfloat16, jnp.float32
     S = jax.ShapeDtypeStruct
     keep = lambda *shape: pl.BlockSpec(shape, lambda j: (0,) * len(shape))
+    any_ = pl.BlockSpec(memory_space=pl.ANY)
     return pl.pallas_call(
         partial(mlp_kernel, band_slots),
         grid=(hidden // tile,),
@@ -1368,15 +1382,18 @@
         ],
         in_specs=[
             keep(rows, width), pl.BlockSpec((width, tile), lambda j: (0, j)), pl.BlockSpec((tile, width), lambda j: (j, 0)),
-            keep(16, width), pl.BlockSpec((1, tile), lambda j: (0, j)), keep(rows, width), keep(rows, width),
-            keep(rows, width), keep(rows, width), pl.BlockSpec((width, width), lambda j: (0, 3)),
+            keep(16, width), pl.BlockSpec((1, tile), lambda j: (0, j)), any_, any_, keep(rows, width), any_, any_,
         ],
         out_specs=[
             keep(rows, width), keep(rows, width), keep(rows, width), keep(width, width),
             pl.BlockSpec((tile, width), lambda j: (j, 0)), pl.BlockSpec((width, tile), lambda j: (0, j)),
             pl.BlockSpec((8, tile), lambda j: (0, j)), keep(8, width),
         ],
-        scratch_shapes=[pltpu.VMEM((rows, width), f32), pltpu.VMEM((rows, width), f32), pltpu.VMEM((rows, width), bf)],
+        scratch_shapes=[
+            pltpu.VMEM((rows, width), f32), pltpu.VMEM((rows, width), f32), pltpu.VMEM((rows, width), bf),
+            pltpu.VMEM((rows, width), f32), pltpu.VMEM((rows, width), f32), pltpu.VMEM((rows, width), bf),
+            pltpu.VMEM((width, width), bf), pltpu.SemaphoreType.DMA((4,)),
+        ],
         compiler_params=pltpu.CompilerParams(vmem_limit_bytes=60 * 2**20),
         cost_estimate=pl.CostEstimate(
             flops=12 * rows * width * hidden, bytes_accessed=8 * width * hidden + 24 * rows * width,

time: 490 us -> 487 us (level)
  no operation moved by 1% of the time
where the time goes in v11:
time: 487 us
  Pallas kernels  450 us (92%)
  other arithmetic  15.4 us (3%)
  local copies, waits for them, and re-layouts  12.3 us (3%)
  matrix products  7.42 us (2%)
    pallas_call x1, Pallas kernels, forward_block(): pl.pallas_call(partial(forward_kernel, tuple(scratch), band_slots), out_s...  159 us
    pallas_call x1, Pallas kernels, reduce_attend(): pl.pallas_call(partial(reduce_attend_kernel, plan, counts, band_slots, tu...  119 us
    pallas_call x1, Pallas kernels, reduce_last(): pl.pallas_call(partial(reduce_last_kernel, plan, images, band_slots, tupl...  117 us
    pallas_call x1, Pallas kernels, feed_forward(): pl.pallas_call(partial(mlp_kernel, band_slots), grid=(hidden // tile,), o...  54.1 us

profile of v11, /device:TPU:1, one launch (start us, length us, event | category | flops | bytes accessed | tf_op | source)
XLA Modules:
  0.0 486.8 jit_solution(2251793284710088104)
XLA Ops:
  0.6 0.0 copy-start.7
  0.7 0.0 copy-start.13
  0.7 0.0 copy-start.9
  0.7 0.0 copy-start.10
  0.7 0.0 copy-start.11
  0.7 0.0 copy-start.12
  0.7 0.0 copy-start.8
  0.7 0.0 copy-start.1
  0.7 0.0 copy-start.4
  0.8 1.0 convert_dynamic-update-slice_fusion
  1.7 0.7 add_divide_fusion
  2.4 0.7 convert_element_type.63
  3.1 2.9 fusion
  6.0 0.0 copy-done.7
  6.0 0.0 copy-done.13
  6.0 0.0 copy-done.9
  6.1 0.0 copy-done.11
  6.2 0.0 copy-done.8
  6.2 0.6 copy.38
  6.9 0.0 copy-done.4
  6.9 1.7 pad_maximum_fusion
  8.6 159.5 %forward_block.1 = (bf16[4,2,144,4608]{3,2,1,0:T(8,128)(2,1)}, bf16[4,2,144,4608]{3,2,1,0:T(8,128)(2,1)}, bf16[4,4,2,144,1152]{4,3,2,1,0:T(8,128)(2,1)}, bf16[2,...) custom-call(bf16[2,144,4608]{2,1,0:T(8,128)(2,1)} %bitcast.59, ...), custom_call_target="tpu_custom_call" | custom-call | tf_op jit(solution)/shard_map/forward_block/pallas_call | solution.py:1261
  168.0 0.8 slice_bitcast_fusion.1
  168.8 0.6 copy.33
  169.4 54.1 %feed_forward.1 = (bf16[512,1152]{1,0:T(8,128)(2,1)}, f32[512,1152]{1,0:T(8,128)}, bf16[512,1152]{1,0:T(8,128)(2,1)}, bf16[1152,1152]{1,0:T(8,128)(2,1)}, bf16[4...) custom-call(bf16[512,1152]{1,0:T(8,128)(2,1)} %get-tuple-element.48.mlp_ref, ...), custom_call_target="tpu_custom_call" | custom-call | flops 32614907904 | bytes 56623104 | tf_op jit(solution)/shard_map/feed_forward/pallas_call | solution.py:1376
  223.5 1.2 slice.70
  225.4 119.4 %reduce_attend.1 = (bf16[4,2,144,1152]{3,2,1,0:T(8,128)(2,1)}, bf16[144,1152]{1,0:T(8,128)(2,1)}, bf16[2,256,1152]{2,1,0:T(8,128)(2,1)}, bf16[512,1152]{1,0:T(8,...) custom-call(bf16[4,4,2,144,1152]{4,3,2,1,0:T(8,128)(2,1)} %bitcast.57, ...), custom_call_target="tpu_custom_call" | custom-call | tf_op jit(solution)/shard_map/reduce_attend/pallas_call | solution.py:824
  344.8 117.2 %reduce_last.1 = (bf16[4,2,144,1152]{3,2,1,0:T(8,128)(2,1)}, bf16[4,2,144,1152]{3,2,1,0:T(8,128)(2,1)}, bf16[2,256,1152]{2,1,0:T(8,128)(2,1)}, bf16[4,4,64,128]{...) custom-call(bf16[4,2,144,1152]{3,2,1,0:T(8,128)(2,1)} %bitcast.60, ...), custom_call_target="tpu_custom_call" | custom-call | tf_op jit(solution)/shard_map/reduce_last/pallas_call | solution.py:714
  461.9 2.9 fusion.11
  464.8 2.7 maximum_convert_fusion
  467.5 2.2 maximum_convert_fusion.1
  469.7 1.2 bitcast_convert_fusion.1
  470.9 0.2 copy.37
  471.1 4.6 fusion.1
  475.7 1.6 convert_element_type.70
  477.3 0.1 convert_reduce_fusion
  477.4 0.7 dynamic_slice.26
  478.0 0.8 slice_bitcast_fusion.2
  478.8 0.1 reshape.103
  478.9 0.6 fusion.5
  479.6 0.7 dynamic_slice.27
  480.2 0.7 dynamic_slice.28
  480.9 0.7 dynamic_slice.29
  481.5 0.7 dynamic_slice.31
  482.2 0.7 dynamic_slice.30
  482.9 2.9 bitcast_convert_fusion
  485.8 0.0 copy-done.3
  485.8 1.0 copy.48
  (32 shorter events, 0.2 us)
Async XLA Ops:
  0.6 5.3 %copy-start.7 = (bf16[2,1152]{1,0:T(2,128)(2,1)S(1)}, bf16[2,1152]{1,0:T(2,128)(2,1)}, u32[]{:S(2)}) copy-start(bf16[2,1152]{1,0:T(2,128)(2,1)} %param.17) | copy-start | bytes 13828
  0.7 5.4 %copy-start.13 = (s32[2,2]{1,0:T(2,128)S(1)}, s32[2,2]{1,0:T(2,128)}, u32[]{:S(2)}) copy-start(s32[2,2]{1,0:T(2,128)} %param.18) | copy-start | bytes 52
  0.7 5.4 %copy-start.9 = (bf16[288]{0:T(512)(128)(2,1)S(1)}, bf16[288]{0:T(512)(128)(2,1)}, u32[]{:S(2)}) copy-start(bf16[288]{0:T(512)(128)(2,1)} %param.22) | copy-start | bytes 1732
  0.7 5.4 %copy-start.10 = (bf16[288]{0:T(512)(128)(2,1)S(1)}, bf16[288]{0:T(512)(128)(2,1)}, u32[]{:S(2)}) copy-start(bf16[288]{0:T(512)(128)(2,1)} %param.23) | copy-start | bytes 1732
  0.7 5.4 %copy-start.11 = (bf16[288]{0:T(512)(128)(2,1)S(1)}, bf16[288]{0:T(512)(128)(2,1)}, u32[]{:S(2)}) copy-start(bf16[288]{0:T(512)(128)(2,1)} %param.25) | copy-start | bytes 1732
  0.7 5.5 %copy-start.12 = (bf16[288]{0:T(512)(128)(2,1)S(1)}, bf16[288]{0:T(512)(128)(2,1)}, u32[]{:S(2)}) copy-start(bf16[288]{0:T(512)(128)(2,1)} %param.29) | copy-start | bytes 1732
  0.7 5.5 %copy-start.8 = (bf16[1152]{0:T(1024)(128)(2,1)S(1)}, bf16[1152]{0:T(1024)(128)(2,1)}, u32[]{:S(2)}) copy-start(bf16[1152]{0:T(1024)(128)(2,1)} %param.27) | copy-start | bytes 6916
  0.7 6.2 %copy-start.1 = (bf16[288,3456]{1,0:T(8,128)(2,1)S(1)}, bf16[288,3456]{1,0:T(8,128)(2,1)}, u32[]{:S(2)}) copy-start(bf16[288,3456]{1,0:T(8,128)(2,1)} %param.21) | copy-start | bytes 5971972
  0.7 6.2 %copy-start.4 = (bf16[288,1152]{1,0:T(8,128)(2,1)S(1)}, bf16[288,1152]{1,0:T(8,128)(2,1)}, u32[]{:S(2)}) copy-start(bf16[288,1152]{1,0:T(8,128)(2,1)} %param.24) | copy-start | bytes 1990660
  467.5 3.4 copy-start.5
  471.1 4.6 copy-start.2
  475.7 3.9 copy-start.6
  475.7 7.2 %copy-start = (bf16[4,2,144,1152]{3,2,1,0:T(8,128)(2,1)S(1)}, bf16[4,2,144,1152]{3,2,1,0:T(8,128)(2,1)}, u32[]{:S(2)}) copy-start(bf16[4,2,144,1152]{3,2,1,0:T(8,128)(2,1)} %get-tuple-element.81) | copy-start | bytes 7962628
  482.9 2.9 copy-start.3

commit v12 on v11

--- a/solution.py
+++ b/solution.py
@@ -592,7 +592,7 @@
 def reduce_last_kernel(plan, images, band_slots, names, *refs):
     me = compass()
     (proj_ref, part_ref, attn_hbm, query_hbm, own_hbm, other_hbm, first_hbm, residual_hbm, middle_hbm, vec_ref, sums_ref,
-     inner_bias_ref, ada_ref) = refs[:13]
+     inner_bias_ref, ada_hbm) = refs[:13]
     inner_out, first_out, home_ref, every_ref, bias_ref, cond_ref = refs[13:19]
     sc = SimpleNamespace(**dict(zip(names, refs[19:])))
     rows, width = sc.attn.shape
@@ -606,7 +606,7 @@
     loads = [
         (attn_hbm, sc.attn), (query_hbm, sc.gqkv.at[:, pl.ds(0, width)]), (own_hbm, sc.gqkv.at[:, pl.ds(width, 2 * width)]),
         (other_hbm, sc.other), (first_hbm.at[:, pl.ds(0, 3 * width)], sc.first), (residual_hbm, sc.residual),
-        (middle_hbm, sc.middle),
+        (middle_hbm, sc.middle), (ada_hbm, sc.ada),
     ]
 
     def load(i):
@@ -616,7 +616,7 @@
         load(i).start()
     group_barrier(me)
     mods = MOD_BLOCKS * width
-    exchange = small_steps(me, mods, images, small, ada_ref, every_ref, bias_ref, cond_ref, sc)
+    exchange = small_steps(me, mods, images, small, sc.ada, every_ref, bias_ref, cond_ref, sc)
     depart, settle = home_steps(me, sc.tokens, home_ref, sc)
     r = reduce_steps(me, plan, source, (inner_out, first_out), (part_ref, None), (None, None), sc, (), 2, True)
 
@@ -650,6 +650,7 @@
         run(*between[j])
     load(5).wait()
     load(6).wait()
+    load(7).wait()
 
     @pl.loop(0, rows // BLOCK)
     def _(block):
@@ -708,7 +709,7 @@
         first=V((width, 3 * width), bf), residual=V((rows, width), f32), middle=V((rows, width), f32),
         grads=V((3, NB, 2, half, width), bf), back=V((rows, width), f32), sums=V((8, width), f32),
         tokens=V((images, band_slots, width), bf), small=V((mod_rows + bias_rows, 128), f32),
-        load_sem=pltpu.SemaphoreType.DMA((7,)),
+        load_sem=pltpu.SemaphoreType.DMA((8,)), ada=V(ada_weight.shape, bf),
     )
     any_, vmem = pl.BlockSpec(memory_space=pl.ANY), pl.BlockSpec(memory_space=pltpu.VMEM)
     return pl.pallas_call(
@@ -720,7 +721,7 @@
             jax.ShapeDtypeStruct((bias_rows, 128), f32),
             jax.ShapeDtypeStruct((NB, 8, cond_cols), f32),
         ],
-        in_specs=[any_] * 9 + [vmem] * 4,
+        in_specs=[any_] * 9 + [vmem] * 3 + [any_],
         out_specs=[any_] * 3 + [vmem] * 3,
         scratch_shapes=list(scratch.values()),
         compiler_params=pltpu.CompilerParams(

time: 487 us -> 487 us (level)
  no operation moved by 1% of the time
where the time goes in v12:
time: 487 us
  Pallas kernels  450 us (92%)
  other arithmetic  15.4 us (3%)
  local copies, waits for them, and re-layouts  12.3 us (3%)
  matrix products  7.42 us (2%)
    pallas_call x1, Pallas kernels, forward_block(): pl.pallas_call(partial(forward_kernel, tuple(scratch), band_slots), out_s...  159 us
    pallas_call x1, Pallas kernels, reduce_attend(): pl.pallas_call(partial(reduce_attend_kernel, plan, counts, band_slots, tu...  119 us
    pallas_call x1, Pallas kernels, reduce_last(): pl.pallas_call(partial(reduce_last_kernel, plan, images, band_slots, tupl...  117 us
    pallas_call x1, Pallas kernels, feed_forward(): pl.pallas_call(partial(mlp_kernel, band_slots), grid=(hidden // tile,), o...  54.1 us

profile of v12, /device:TPU:1, one launch (start us, length us, event | category | flops | bytes accessed | tf_op | source)
XLA Modules:
  0.0 486.6 jit_solution(3064154027533589298)
XLA Ops:
  0.6 0.0 copy-start.7
  0.7 0.0 copy-start.13
  0.7 0.0 copy-start.9
  0.7 0.0 copy-start.10
  0.7 0.0 copy-start.11
  0.7 0.0 copy-start.12
  0.7 0.0 copy-start.8
  0.7 0.0 copy-start.1
  0.7 0.0 copy-start.4
  0.8 1.0 convert_dynamic-update-slice_fusion
  1.7 0.7 add_divide_fusion
  2.4 0.7 convert_element_type.63
  3.1 2.9 fusion
  6.0 0.0 copy-done.7
  6.0 0.0 copy-done.13
  6.0 0.0 copy-done.9
  6.1 0.0 copy-done.10
  6.2 0.0 copy-done.12
  6.2 0.6 copy.38
  6.9 1.7 pad_maximum_fusion
  8.6 159.5 %forward_block.1 = (bf16[4,2,144,4608]{3,2,1,0:T(8,128)(2,1)}, bf16[4,2,144,4608]{3,2,1,0:T(8,128)(2,1)}, bf16[4,4,2,144,1152]{4,3,2,1,0:T(8,128)(2,1)}, bf16[2,...) custom-call(bf16[2,144,4608]{2,1,0:T(8,128)(2,1)} %bitcast.59, ...), custom_call_target="tpu_custom_call" | custom-call | tf_op jit(solution)/shard_map/forward_block/pallas_call | solution.py:1262
  168.0 0.8 slice_bitcast_fusion.1
  168.8 0.6 copy.33
  169.4 54.1 %feed_forward.1 = (bf16[512,1152]{1,0:T(8,128)(2,1)}, f32[512,1152]{1,0:T(8,128)}, bf16[512,1152]{1,0:T(8,128)(2,1)}, bf16[1152,1152]{1,0:T(8,128)(2,1)}, bf16[4...) custom-call(bf16[512,1152]{1,0:T(8,128)(2,1)} %get-tuple-element.48.mlp_ref, ...), custom_call_target="tpu_custom_call" | custom-call | flops 32614907904 | bytes 56623104 | tf_op jit(solution)/shard_map/feed_forward/pallas_call | solution.py:1377
  223.5 1.2 slice.70
  225.4 119.4 %reduce_attend.1 = (bf16[4,2,144,1152]{3,2,1,0:T(8,128)(2,1)}, bf16[144,1152]{1,0:T(8,128)(2,1)}, bf16[2,256,1152]{2,1,0:T(8,128)(2,1)}, bf16[512,1152]{1,0:T(8,...) custom-call(bf16[4,4,2,144,1152]{4,3,2,1,0:T(8,128)(2,1)} %bitcast.57, ...), custom_call_target="tpu_custom_call" | custom-call | tf_op jit(solution)/shard_map/reduce_attend/pallas_call | solution.py:825
  344.8 117.0 %reduce_last.1 = (bf16[4,2,144,1152]{3,2,1,0:T(8,128)(2,1)}, bf16[4,2,144,1152]{3,2,1,0:T(8,128)(2,1)}, bf16[2,256,1152]{2,1,0:T(8,128)(2,1)}, bf16[4,4,64,128]{...) custom-call(bf16[4,2,144,1152]{3,2,1,0:T(8,128)(2,1)} %bitcast.60, ...), custom_call_target="tpu_custom_call" | custom-call | tf_op jit(solution)/shard_map/reduce_last/pallas_call | solution.py:715
  461.7 2.9 fusion.11
  464.6 2.7 maximum_convert_fusion
  467.3 2.2 maximum_convert_fusion.1
  469.5 1.2 bitcast_convert_fusion.1
  470.7 0.2 copy.37
  470.9 4.6 fusion.1
  475.5 0.0 copy-done.2
  475.5 1.6 convert_element_type.70
  477.1 0.1 convert_reduce_fusion
  477.2 0.7 dynamic_slice.26
  477.9 0.8 slice_bitcast_fusion.2
  478.7 0.1 reshape.103
  478.8 0.6 fusion.5
  479.4 0.7 dynamic_slice.27
  480.0 0.7 dynamic_slice.28
  480.7 0.7 dynamic_slice.29
  481.3 0.7 dynamic_slice.31
  482.0 0.7 dynamic_slice.30
  482.7 2.9 bitcast_convert_fusion
  485.6 0.0 copy-done.3
  485.6 1.0 copy.48
  (32 shorter events, 0.2 us)
Async XLA Ops:
  0.6 5.3 %copy-start.7 = (bf16[2,1152]{1,0:T(2,128)(2,1)S(1)}, bf16[2,1152]{1,0:T(2,128)(2,1)}, u32[]{:S(2)}) copy-start(bf16[2,1152]{1,0:T(2,128)(2,1)} %param.17) | copy-start | bytes 13828
  0.7 5.4 %copy-start.13 = (s32[2,2]{1,0:T(2,128)S(1)}, s32[2,2]{1,0:T(2,128)}, u32[]{:S(2)}) copy-start(s32[2,2]{1,0:T(2,128)} %param.18) | copy-start | bytes 52
  0.7 5.4 %copy-start.9 = (bf16[288]{0:T(512)(128)(2,1)S(1)}, bf16[288]{0:T(512)(128)(2,1)}, u32[]{:S(2)}) copy-start(bf16[288]{0:T(512)(128)(2,1)} %param.22) | copy-start | bytes 1732
  0.7 5.4 %copy-start.10 = (bf16[288]{0:T(512)(128)(2,1)S(1)}, bf16[288]{0:T(512)(128)(2,1)}, u32[]{:S(2)}) copy-start(bf16[288]{0:T(512)(128)(2,1)} %param.23) | copy-start | bytes 1732
  0.7 5.4 %copy-start.11 = (bf16[288]{0:T(512)(128)(2,1)S(1)}, bf16[288]{0:T(512)(128)(2,1)}, u32[]{:S(2)}) copy-start(bf16[288]{0:T(512)(128)(2,1)} %param.25) | copy-start | bytes 1732
  0.7 5.5 %copy-start.12 = (bf16[288]{0:T(512)(128)(2,1)S(1)}, bf16[288]{0:T(512)(128)(2,1)}, u32[]{:S(2)}) copy-start(bf16[288]{0:T(512)(128)(2,1)} %param.29) | copy-start | bytes 1732
  0.7 5.5 %copy-start.8 = (bf16[1152]{0:T(1024)(128)(2,1)S(1)}, bf16[1152]{0:T(1024)(128)(2,1)}, u32[]{:S(2)}) copy-start(bf16[1152]{0:T(1024)(128)(2,1)} %param.27) | copy-start | bytes 6916
  0.7 6.2 %copy-start.1 = (bf16[288,3456]{1,0:T(8,128)(2,1)S(1)}, bf16[288,3456]{1,0:T(8,128)(2,1)}, u32[]{:S(2)}) copy-start(bf16[288,3456]{1,0:T(8,128)(2,1)} %param.21) | copy-start | bytes 5971972
  0.7 6.2 %copy-start.4 = (bf16[288,1152]{1,0:T(8,128)(2,1)S(1)}, bf16[288,1152]{1,0:T(8,128)(2,1)}, u32[]{:S(2)}) copy-start(bf16[288,1152]{1,0:T(8,128)(2,1)} %param.24) | copy-start | bytes 1990660
  467.3 3.4 copy-start.5
  470.9 4.6 copy-start.2
  475.5 3.9 copy-start.6
  475.5 7.2 %copy-start = (bf16[4,2,144,1152]{3,2,1,0:T(8,128)(2,1)S(1)}, bf16[4,2,144,1152]{3,2,1,0:T(8,128)(2,1)}, u32[]{:S(2)}) copy-start(bf16[4,2,144,1152]{3,2,1,0:T(8,128)(2,1)} %get-tuple-element.81) | copy-start | bytes 7962628
  482.7 2.9 copy-start.3
